TPU v7x, 32 devices: a whole 2x2x4 slice. The times are simulated.
32 devices in a mesh: dp: 4 (over z), gx: 2 (over x), gy: 4 (over y, core).
Axes of the slice: x: 2, y: 2, z: 4, core: 2. Of those that a mesh axis runs over, the one named last changes fastest.
Arguments:
- tokens: bfloat16 [960, 32768], P('gy', ('dp', 'gx')), may hold values from -6 to 6
- doc_start: int32 [32768], P(('dp', 'gx', 'gy')), may hold values from 0 to 32256, as said below
- cotangent: bfloat16 [960, 32768], P('gy', ('dp', 'gx')), may hold values from -6 to 6
- attn_gain: float32 [960], replicated, may hold values from 0.5 to 1.5
- mlp_gain: float32 [960], replicated, may hold values from 0.5 to 1.5
- w_qkv: bfloat16 [960, 1600], P('gy', 'gx'), may hold values from -0.1875 to 0.1875
- w_out: bfloat16 [960, 960], P('gx', 'gy'), may hold values from -2.5 to 2.5
- w_gate: bfloat16 [960, 2560], P('gy', 'gx'), may hold values from -0.1875 to 0.1875
- w_up: bfloat16 [960, 2560], P('gy', 'gx'), may hold values from -0.1875 to 0.1875
- w_down: bfloat16 [2560, 960], P('gx', 'gy'), may hold values from -0.125 to 0.125
Outputs:
- result: bfloat16 [960, 32768], P('gy', ('dp', 'gx'))
- input_grad: bfloat16 [960, 32768], P('gy', ('dp', 'gx'))
- grad_qkv: float32 [960, 1600], P('gy', 'gx')
- grad_out: float32 [960, 960], P('gx', 'gy')
- grad_gate: float32 [960, 2560], P('gy', 'gx')
- grad_up: float32 [960, 2560], P('gy', 'gx')
- grad_down: float32 [2560, 960], P('gx', 'gy')
- grad_attn_gain: float32 [960], replicated
- grad_mlp_gain: float32 [960], replicated
Inputs may be any that keep to these rules, and one draw needn't show every extreme that they name: `doc_start`: each value is the index of the first token of its token's document. Documents lie inside aligned blocks of 2048 tokens, three to a block; the middle one holds 256 to 1024 tokens and contains the block's tokens 1024 - 1 and 1024; the others hold 512 to 896 tokens.
All inputs are finite; a program needn't handle non-finite values.
Results may differ from a plain program's by a relative error of at most 0.014.
Values may be sent and summed in bfloat16 or wider, within the bound.
No kernel may reach another device: no remote copies, remote signals or barrier semaphores. Data moves between devices by JAX's collectives and lax.ppermute only.
A program may use at most 256 MiB of HBM per device.

v0:
```python
import jax
import jax.numpy as jnp
from jax import lax
from jax.sharding import PartitionSpec as P

HEADS = 15
KV_HEADS = 5
HEAD = 64


EPS = 1e-05
THETA = 100000.0
NEG = -1e30


def passed_along(shard, axis, by):
    peers = lax.axis_size(axis)
    pairs = [(i, i + by) for i in range(peers) if 0 <= i + by < peers]
    return lax.ppermute(shard, axis, pairs)


def contract(left, right, left_dim, right_dim):
    return lax.dot_general(
        left, right, (((left_dim,), (right_dim,)), ((), ())), preferred_element_type=jnp.float32
    )


def frequencies():
    half_size = HEAD // 2
    return jnp.power(THETA, -jnp.arange(half_size, dtype=jnp.float32) / half_size)


def rotate(values, cosine_table, sine_table):
    half_size = values.shape[-1] // 2
    front_half = values[..., :half_size]
    back_half = values[..., half_size:]
    return jnp.concatenate(
        [
            front_half * cosine_table - back_half * sine_table,
            back_half * cosine_table + front_half * sine_table,
        ],
        axis=-1,
    )


def rotate_back(gradient, cosine_table, sine_table):
    half_size = gradient.shape[-1] // 2
    front_half = gradient[..., :half_size]
    back_half = gradient[..., half_size:]
    return jnp.concatenate(
        [
            front_half * cosine_table + back_half * sine_table,
            back_half * cosine_table - front_half * sine_table,
        ],
        axis=-1,
    )


def rms_norm(values, gain_row):
    norm_scale = lax.rsqrt(jnp.mean(values * values, axis=1, keepdims=True) + EPS)
    return (norm_scale, (values * norm_scale * gain_row).astype(jnp.bfloat16))


def norm_back(values, norm_scale, gain_row, gradient):
    weighted = gradient * gain_row
    inner_sum = jnp.mean(weighted * values, axis=1, keepdims=True)
    values_grad = (
        norm_scale * weighted - values * (norm_scale * norm_scale * norm_scale) * inner_sum
    )
    return (values_grad, jnp.sum(gradient * values * norm_scale, axis=0))


def gather_wide(parts):
    return (
        lax.all_gather(parts[0], "gx", axis=1, tiled=True),
        lax.all_gather(parts[1], "gx", axis=0, tiled=True),
        lax.all_gather(parts[2], "gx", axis=1, tiled=True),
        lax.all_gather(parts[3], "gx", axis=1, tiled=True),
        lax.all_gather(parts[4], "gx", axis=0, tiled=True),
    )


def gather_narrow(parts):
    return (
        lax.all_gather(parts[0], "gy", axis=0, tiled=True),
        lax.all_gather(parts[1], "gy", axis=1, tiled=True),
        lax.all_gather(parts[2], "gy", axis=0, tiled=True),
        lax.all_gather(parts[3], "gy", axis=0, tiled=True),
        lax.all_gather(parts[4], "gy", axis=1, tiled=True),
    )


def scatter_wide(parts):
    return (
        lax.psum_scatter(parts[0], "gx", scatter_dimension=1, tiled=True),
        lax.psum_scatter(parts[1], "gx", scatter_dimension=0, tiled=True),
        lax.psum_scatter(parts[2], "gx", scatter_dimension=1, tiled=True),
        lax.psum_scatter(parts[3], "gx", scatter_dimension=1, tiled=True),
        lax.psum_scatter(parts[4], "gx", scatter_dimension=0, tiled=True),
    )


def scatter_narrow(parts):
    return (
        lax.psum_scatter(parts[0], "gy", scatter_dimension=0, tiled=True),
        lax.psum_scatter(parts[1], "gy", scatter_dimension=1, tiled=True),
        lax.psum_scatter(parts[2], "gy", scatter_dimension=0, tiled=True),
        lax.psum_scatter(parts[3], "gy", scatter_dimension=0, tiled=True),
        lax.psum_scatter(parts[4], "gy", scatter_dimension=1, tiled=True),
    )


def on_device(
    tokens, doc_start, cotangent, attn_gain, mlp_gain, w_qkv, w_out, w_gate, w_up, w_down
):
    block_rows = doc_start.shape[0]
    group_size = HEADS // KV_HEADS
    query_width = HEADS * HEAD
    kv_width = KV_HEADS * HEAD
    score_scale = HEAD ** (-0.5)
    inputs_cols, upstream_cols = (
        lax.all_to_all(tokens, "gy", split_axis=1, concat_axis=0, tiled=True),
        lax.all_to_all(cotangent, "gy", split_axis=1, concat_axis=0, tiled=True),
    )
    inputs = inputs_cols.T
    upstream = upstream_cols.T
    local_parts = (w_qkv, w_out, w_gate, w_up, w_down)
    full_parts = gather_wide(gather_narrow(local_parts))
    full_qkv, full_out, full_gate, full_up, full_down = full_parts
    residual_in = inputs.astype(jnp.float32)
    scale_one, normed_one = rms_norm(residual_in, attn_gain)
    projected = jnp.dot(normed_one, full_qkv, preferred_element_type=jnp.float32).astype(
        jnp.bfloat16
    )
    first_row = lax.axis_index(("dp", "gx", "gy")) * block_rows
    query_places = first_row + jnp.arange(block_rows, dtype=jnp.int32)
    key_places = first_row - block_rows + jnp.arange(2 * block_rows, dtype=jnp.int32)
    allowed = (key_places[None, :] >= doc_start[:, None]) & (
        key_places[None, :] <= query_places[:, None]
    )
    angle = (query_places - doc_start).astype(jnp.float32)[:, None] * frequencies()[None, :]
    cosine_table = jnp.cos(angle)[:, None, :]
    sine_table = jnp.sin(angle)[:, None, :]
    queries = rotate(
        projected[:, :query_width].astype(jnp.float32).reshape(block_rows, HEADS, HEAD),
        cosine_table,
        sine_table,
    ).astype(jnp.bfloat16)
    own_keys = rotate(
        projected[:, query_width : query_width + kv_width]
        .astype(jnp.float32)
        .reshape(block_rows, KV_HEADS, HEAD),
        cosine_table,
        sine_table,
    ).astype(jnp.bfloat16)
    own_values = projected[:, query_width + kv_width :].reshape(block_rows, KV_HEADS, HEAD)
    prior_keys, prior_values = passed_along((own_keys, own_values), "gy", 1)
    key_rows = jnp.concatenate([prior_keys, own_keys], axis=0).transpose(1, 0, 2)
    value_rows = jnp.concatenate([prior_values, own_values], axis=0).transpose(1, 0, 2)
    grouped = queries.reshape(block_rows, KV_HEADS, group_size, HEAD).transpose(1, 0, 2, 3)

    def scores_of(query_part, key_part):
        scores = (
            jnp.einsum("qrd,kd->rqk", query_part, key_part, preferred_element_type=jnp.float32)
            * score_scale
        )
        return jnp.where(allowed[None], scores, NEG)

    def forward_group(items):
        query_part, key_part, value_part = items
        masked = scores_of(query_part, key_part)
        row_max = jnp.max(masked, axis=-1, keepdims=True)
        exp_scores = jnp.exp(masked - row_max)
        row_total = jnp.sum(exp_scores, axis=-1, keepdims=True)
        soft_rows = exp_scores / row_total
        mixed_rows = jnp.einsum(
            "rqk,kd->qrd",
            soft_rows.astype(jnp.bfloat16),
            value_part,
            preferred_element_type=jnp.float32,
        )
        return (mixed_rows.astype(jnp.bfloat16), (row_max + jnp.log(row_total))[..., 0])

    def backward_group(items):
        query_part, key_part, value_part, log_total, grad_part = items
        masked = scores_of(query_part, key_part)
        soft_rows = jnp.exp(masked - log_total[..., None])
        prob_grads = jnp.einsum(
            "qrd,kd->rqk", grad_part, value_part, preferred_element_type=jnp.float32
        )
        inner_sum = jnp.sum(soft_rows * prob_grads, axis=-1, keepdims=True)
        score_grads = (soft_rows * (prob_grads - inner_sum)).astype(jnp.bfloat16)
        query_grads = (
            jnp.einsum("rqk,kd->qrd", score_grads, key_part, preferred_element_type=jnp.float32)
            * score_scale
        )
        key_grads = (
            jnp.einsum("rqk,qrd->kd", score_grads, query_part, preferred_element_type=jnp.float32)
            * score_scale
        )
        value_grads = jnp.einsum(
            "rqk,qrd->kd",
            soft_rows.astype(jnp.bfloat16),
            grad_part,
            preferred_element_type=jnp.float32,
        )
        return (query_grads, key_grads, value_grads)

    mixed_parts, log_totals = lax.map(forward_group, (grouped, key_rows, value_rows))
    mixed = mixed_parts.transpose(1, 0, 2, 3).reshape(block_rows, query_width)
    residual_mid = residual_in + jnp.dot(mixed, full_out, preferred_element_type=jnp.float32)
    scale_two, normed_two = rms_norm(residual_mid, mlp_gain)
    gate = jnp.dot(normed_two, full_gate, preferred_element_type=jnp.float32)
    up_part = jnp.dot(normed_two, full_up, preferred_element_type=jnp.float32)
    sigmoid_gate = jax.nn.sigmoid(gate)
    silu_gate = gate * sigmoid_gate
    hidden = (silu_gate * up_part).astype(jnp.bfloat16)
    result = (residual_mid + jnp.dot(hidden, full_down, preferred_element_type=jnp.float32)).astype(
        jnp.bfloat16
    )
    hidden_grad = contract(upstream, full_down, 1, 1)
    grad_down = contract(hidden, upstream, 0, 0)
    gate_grad = (hidden_grad * up_part * sigmoid_gate * (1.0 + gate * (1.0 - sigmoid_gate))).astype(
        jnp.bfloat16
    )
    up_grad = (hidden_grad * silu_gate).astype(jnp.bfloat16)
    normed_two_grad = contract(gate_grad, full_gate, 1, 1) + contract(up_grad, full_up, 1, 1)
    grad_gate = contract(normed_two, gate_grad, 0, 0)
    grad_up = contract(normed_two, up_grad, 0, 0)
    mid_grad, gain_two = norm_back(residual_mid, scale_two, mlp_gain, normed_two_grad)
    mid_grad = mid_grad + upstream.astype(jnp.float32)
    branch_grad = mid_grad.astype(jnp.bfloat16)
    mixed_grad = contract(branch_grad, full_out, 1, 1).astype(jnp.bfloat16)
    grad_out = contract(mixed, branch_grad, 0, 0)
    mixed_grad_parts = mixed_grad.reshape(block_rows, KV_HEADS, group_size, HEAD).transpose(
        1, 0, 2, 3
    )
    query_parts, key_parts, value_parts = lax.map(
        backward_group, (grouped, key_rows, value_rows, log_totals, mixed_grad_parts)
    )
    key_grads = key_parts.transpose(1, 0, 2)
    value_grads = value_parts.transpose(1, 0, 2)
    sent_keys, sent_values = (
        passed_along(key_grads[:block_rows].astype(jnp.bfloat16), "gy", -1).astype(jnp.float32),
        passed_along(value_grads[:block_rows].astype(jnp.bfloat16), "gy", -1).astype(jnp.float32),
    )
    own_key_grad = key_grads[block_rows:] + sent_keys
    own_value_grad = value_grads[block_rows:] + sent_values
    query_grad = query_parts.transpose(1, 0, 2, 3).reshape(block_rows, HEADS, HEAD)
    projected_grad = jnp.concatenate(
        [
            rotate_back(query_grad, cosine_table, sine_table).reshape(block_rows, query_width),
            rotate_back(own_key_grad, cosine_table, sine_table).reshape(block_rows, kv_width),
            own_value_grad.reshape(block_rows, kv_width),
        ],
        axis=1,
    ).astype(jnp.bfloat16)
    normed_one_grad = contract(projected_grad, full_qkv, 1, 1)
    grad_qkv = contract(normed_one, projected_grad, 0, 0)
    in_grad, gain_one = norm_back(residual_in, scale_one, attn_gain, normed_one_grad)
    in_grad = in_grad + mid_grad
    result_cols, grad_cols = (
        lax.all_to_all(result.T, "gy", split_axis=0, concat_axis=1, tiled=True),
        lax.all_to_all(
            in_grad.astype(jnp.bfloat16).T, "gy", split_axis=0, concat_axis=1, tiled=True
        ),
    )
    full_grads = (grad_qkv, grad_out, grad_gate, grad_up, grad_down)
    shard_grads = scatter_narrow(scatter_wide(full_grads))
    shard_qkv, shard_out, shard_gate, shard_up, shard_down = lax.psum(
        (shard_grads[0], shard_grads[1], shard_grads[2], shard_grads[3], shard_grads[4]), "dp"
    )
    gain_one, gain_two = lax.psum((gain_one, gain_two), ("dp", "gx", "gy"))
    return (
        result_cols,
        grad_cols,
        shard_qkv,
        shard_out,
        shard_gate,
        shard_up,
        shard_down,
        gain_one,
        gain_two,
    )


def solution(mesh):
    placed = (
        P("gy", ("dp", "gx")),
        P(("dp", "gx", "gy")),
        P("gy", ("dp", "gx")),
        P(),
        P(),
        P("gy", "gx"),
        P("gx", "gy"),
        P("gy", "gx"),
        P("gy", "gx"),
        P("gx", "gy"),
    )
    return jax.shard_map(
        on_device,
        mesh=mesh,
        in_specs=placed,
        out_specs=(
            P("gy", ("dp", "gx")),
            P("gy", ("dp", "gx")),
            P("gy", "gx"),
            P("gx", "gy"),
            P("gy", "gx"),
            P("gy", "gx"),
            P("gx", "gy"),
            P(),
            P(),
        ),
        check_vma=False,
    )
```

profile of v0, /device:TPU:0, one launch (start us, length us, event | category | flops | bytes accessed | tf_op | source)
XLA Modules:
  0.0 1728.5 jit_solution(6253090190570335351)
XLA Ops:
  9.5 22.9 %all-gather.27.cloned.1.call-done = bf16[4,240,800]{1,2,0:T(8,128)(2,1)} async-done(((bf16[1,240,800]{1,2,0:T(8,128)(2,1)}), bf16[4,240,800]{1,2,0:T(8,128)(2,1)}) %all-gather.27.cloned.1.call-update) | async-done | bytes 1536016 | tf_op jit(solution)/shard_map/all_gather | solution.py:85
  38.2 13.4 all_gather.32
  61.8 26.2 %all-gather.15.cloned.1.call-done = bf16[960,1280]{1,0:T(8,128)(2,1)} async-done(((bf16[240,1280]{1,0:T(8,128)(2,1)}), bf16[960,1280]{1,0:T(8,128)(2,1)}) %all-gather.15.cloned.1.call-update) | async-done | bytes 2457616 | tf_op jit(solution)/shard_map/all_gather | solution.py:87
  96.8 20.6 %all-to-all-done = bf16[240,4,1024]{2,0,1:T(8,128)(2,1)S(1)} async-done(((bf16[240,4,1024]{2,0,1:T(8,128)(2,1)}), bf16[240,4,1024]{2,0,1:T(8,128)(2,1)S(1)}, u32[]{:S(2)}, u32[]{:S(2)}) %all-to-all-start) | async-done | bytes 1966112 | tf_op jit(solution)/shard_map/all_to_all | solution.py:122
  124.8 11.6 all-gather.11.cloned.1.call-done
  146.0 18.3 %all-gather.23.cloned.1.call-done = bf16[1280,960]{0,1:T(8,128)(2,1)} async-done(((bf16[1280,240]{0,1:T(8,128)(2,1)}), bf16[1280,960]{0,1:T(8,128)(2,1)}) %all-gather.23.cloned.1.call-update) | async-done | bytes 2457616 | tf_op jit(solution)/shard_map/all_gather | solution.py:89
  171.8 197.8 %while.28 = (s32[]{:T(128)}, bf16[5,1024,3,64]{1,3,2,0:T(8,128)(2,1)}, f32[5,3,1024]{2,1,0:T(4,128)}, bf16[5,2048,64]{1,2,0:T(8,128)(2,1)}, bf16[5,2048,64]{1,2,...) while((s32[]{:T(128)}, ...), condition=%wide.region_4.5_spmd.clone, body=%wide.region_1.4_spmd.clone.sunk | while | flops 1692595200 | bytes 85317736 | solution.py:209
  174.0 11.9 fusion.137
  197.4 13.0 fusion.139
  212.8 11.9 fusion.137
  224.7 11.4 fusion.138
  236.1 12.9 fusion.139
  251.4 11.9 fusion.137
  274.8 15.2 fusion.139
  292.4 11.9 fusion.137
  315.7 12.9 fusion.139
  331.0 12.2 fusion.137
  343.2 12.8 fusion.138
  356.0 13.0 fusion.139
  401.6 20.2 %multiply_convert_fusion = (bf16[1024,2560]{1,0:T(8,128)(2,1)}, bf16[1024,2560]{1,0:T(8,128)(2,1)}, bf16[1024,2560]{1,0:T(8,128)(2,1)}) fusion(f32[1024,2560]{1,0:T(8,128)} %fusion.81, f32[1024,2560]{1,0:T(8,128)} %fusion.82, bf16[960,1024]{1,0:T(8,128)(2,1)} %bitcast.24, bf16[2560,960]{0,1:T(8,128)(2,1)} %all-gather.25.cloned.1.call-done), kind=kOutput, calls=%fused_computation.69 | convolution fusion | flops 5072486400 | bytes 43581440 | tf_op jit(solution)/shard_map/dot_general | solution.py:23
  459.3 365.5 %while.29 = (s32[]{:T(128)}, f32[5,1024,3,64]{1,3,2,0:T(8,128)}, f32[5,2048,64]{1,2,0:T(8,128)}, f32[5,2048,64]{1,2,0:T(8,128)}, bf16[5,2048,64]{1,2,0:T(8,128)(...) while((s32[]{:T(128)}, f32[5,1024,3,64]{1,3,2,0:T(8,128)}, ...), condition=%wide.region_9.10_spmd.clone, body=%wide.region_7.9_spmd.clone.sunk | while | flops 4127519744 | bytes 233022832 | solution.py:238
  463.3 12.1 fusion.148
  475.4 12.4 fusion.153
  487.7 17.7 %fusion.149 = (f32[3,1024]{1,0:T(4,128)}, f32[2048,1024,3]{1,0,2:T(8,128)}) fusion(f32[2048,1024,3]{1,0,2:T(8,128)} %fusion.148, f32[3,1024]{1,0:T(4,128)S(1)} %dynamic-slice_bitcast_fusion.2, pred[1024,2048]{0,1:T(8,128)(4,1)S(1)} %compare_and_fusion.5, bf16[5,1024,3,64]{1,3,2,0:T(8,128)(2,1)} %get-tuple-element.439, s32[]{:T(128)S(6)} %copy.93, ...), kind=kOutput, calls=%fused_computation.26.clone.1 | convolution fusion | flops 836760576 | bytes 53109760 | tf_op jit(solution)/shard_map/while/body/eval_jaxpr/qrd,kd->rqk/dot_general | solution.py:188
  505.5 17.5 %fusion.150 = bf16[3,1024,2048]{1,2,0:T(8,128)(2,1)S(1)} fusion(f32[2048,1024,3]{1,0,2:T(8,128)} %get-tuple-element.373, f32[2048,1024,3]{1,0,2:T(8,128)} %fusion.148, f32[3,1024]{1,0:T(4,128)} %get-tuple-element.374, f32[3,1024]{1,0:T(4,128)S(1)} %dynamic-slice_bitcast_fusion.2, pred[1024,2048]{0,1:T(8,128)(4,1)S(1)} %compare_and_fusion.5), kind=kLoop, calls=%fused_computation.28.clone.1 | loop fusion | flops 37748736 | bytes 65036288 | tf_op jit(solution)/shard_map/while/body/eval_jaxpr/convert_element_type | solution.py:192
  548.2 12.4 fusion.153
  560.6 17.8 %fusion.149 = (f32[3,1024]{1,0:T(4,128)}, f32[2048,1024,3]{1,0,2:T(8,128)}) fusion(f32[2048,1024,3]{1,0,2:T(8,128)} %fusion.148, f32[3,1024]{1,0:T(4,128)S(1)} %dynamic-slice_bitcast_fusion.2, pred[1024,2048]{0,1:T(8,128)(4,1)S(1)} %compare_and_fusion.5, bf16[5,1024,3,64]{1,3,2,0:T(8,128)(2,1)} %get-tuple-element.439, s32[]{:T(128)S(6)} %copy.93, ...), kind=kOutput, calls=%fused_computation.26.clone.1 | convolution fusion | flops 836760576 | bytes 53109760 | tf_op jit(solution)/shard_map/while/body/eval_jaxpr/qrd,kd->rqk/dot_general | solution.py:188
  578.4 17.4 %fusion.150 = bf16[3,1024,2048]{1,2,0:T(8,128)(2,1)S(1)} fusion(f32[2048,1024,3]{1,0,2:T(8,128)} %get-tuple-element.373, f32[2048,1024,3]{1,0,2:T(8,128)} %fusion.148, f32[3,1024]{1,0:T(4,128)} %get-tuple-element.374, f32[3,1024]{1,0:T(4,128)S(1)} %dynamic-slice_bitcast_fusion.2, pred[1024,2048]{0,1:T(8,128)(4,1)S(1)} %compare_and_fusion.5), kind=kLoop, calls=%fused_computation.28.clone.1 | loop fusion | flops 37748736 | bytes 65036288 | tf_op jit(solution)/shard_map/while/body/eval_jaxpr/convert_element_type | solution.py:192
  621.1 12.4 fusion.153
  633.5 17.8 %fusion.149 = (f32[3,1024]{1,0:T(4,128)}, f32[2048,1024,3]{1,0,2:T(8,128)}) fusion(f32[2048,1024,3]{1,0,2:T(8,128)} %fusion.148, f32[3,1024]{1,0:T(4,128)S(1)} %dynamic-slice_bitcast_fusion.2, pred[1024,2048]{0,1:T(8,128)(4,1)S(1)} %compare_and_fusion.5, bf16[5,1024,3,64]{1,3,2,0:T(8,128)(2,1)} %get-tuple-element.439, s32[]{:T(128)S(6)} %copy.93, ...), kind=kOutput, calls=%fused_computation.26.clone.1 | convolution fusion | flops 836760576 | bytes 53109760 | tf_op jit(solution)/shard_map/while/body/eval_jaxpr/qrd,kd->rqk/dot_general | solution.py:188
  651.2 17.4 %fusion.150 = bf16[3,1024,2048]{1,2,0:T(8,128)(2,1)S(1)} fusion(f32[2048,1024,3]{1,0,2:T(8,128)} %get-tuple-element.373, f32[2048,1024,3]{1,0,2:T(8,128)} %fusion.148, f32[3,1024]{1,0:T(4,128)} %get-tuple-element.374, f32[3,1024]{1,0:T(4,128)S(1)} %dynamic-slice_bitcast_fusion.2, pred[1024,2048]{0,1:T(8,128)(4,1)S(1)} %compare_and_fusion.5), kind=kLoop, calls=%fused_computation.28.clone.1 | loop fusion | flops 37748736 | bytes 65036288 | tf_op jit(solution)/shard_map/while/body/eval_jaxpr/convert_element_type | solution.py:192
  693.9 12.4 fusion.153
  706.3 17.8 %fusion.149 = (f32[3,1024]{1,0:T(4,128)}, f32[2048,1024,3]{1,0,2:T(8,128)}) fusion(f32[2048,1024,3]{1,0,2:T(8,128)} %fusion.148, f32[3,1024]{1,0:T(4,128)S(1)} %dynamic-slice_bitcast_fusion.2, pred[1024,2048]{0,1:T(8,128)(4,1)S(1)} %compare_and_fusion.5, bf16[5,1024,3,64]{1,3,2,0:T(8,128)(2,1)} %get-tuple-element.439, s32[]{:T(128)S(6)} %copy.93, ...), kind=kOutput, calls=%fused_computation.26.clone.1 | convolution fusion | flops 836760576 | bytes 53109760 | tf_op jit(solution)/shard_map/while/body/eval_jaxpr/qrd,kd->rqk/dot_general | solution.py:188
  724.1 17.4 %fusion.150 = bf16[3,1024,2048]{1,2,0:T(8,128)(2,1)S(1)} fusion(f32[2048,1024,3]{1,0,2:T(8,128)} %get-tuple-element.373, f32[2048,1024,3]{1,0,2:T(8,128)} %fusion.148, f32[3,1024]{1,0:T(4,128)} %get-tuple-element.374, f32[3,1024]{1,0:T(4,128)S(1)} %dynamic-slice_bitcast_fusion.2, pred[1024,2048]{0,1:T(8,128)(4,1)S(1)} %compare_and_fusion.5), kind=kLoop, calls=%fused_computation.28.clone.1 | loop fusion | flops 37748736 | bytes 65036288 | tf_op jit(solution)/shard_map/while/body/eval_jaxpr/convert_element_type | solution.py:192
  766.7 12.4 fusion.153
  779.1 17.7 %fusion.149 = (f32[3,1024]{1,0:T(4,128)}, f32[2048,1024,3]{1,0,2:T(8,128)}) fusion(f32[2048,1024,3]{1,0,2:T(8,128)} %fusion.148, f32[3,1024]{1,0:T(4,128)S(1)} %dynamic-slice_bitcast_fusion.2, pred[1024,2048]{0,1:T(8,128)(4,1)S(1)} %compare_and_fusion.5, bf16[5,1024,3,64]{1,3,2,0:T(8,128)(2,1)} %get-tuple-element.439, s32[]{:T(128)S(6)} %copy.93, ...), kind=kOutput, calls=%fused_computation.26.clone.1 | convolution fusion | flops 836760576 | bytes 53109760 | tf_op jit(solution)/shard_map/while/body/eval_jaxpr/qrd,kd->rqk/dot_general | solution.py:188
  796.8 17.4 %fusion.150 = bf16[3,1024,2048]{1,2,0:T(8,128)(2,1)S(1)} fusion(f32[2048,1024,3]{1,0,2:T(8,128)} %get-tuple-element.373, f32[2048,1024,3]{1,0,2:T(8,128)} %fusion.148, f32[3,1024]{1,0:T(4,128)} %get-tuple-element.374, f32[3,1024]{1,0:T(4,128)S(1)} %dynamic-slice_bitcast_fusion.2, pred[1024,2048]{0,1:T(8,128)(4,1)S(1)} %compare_and_fusion.5), kind=kLoop, calls=%fused_computation.28.clone.1 | loop fusion | flops 37748736 | bytes 65036288 | tf_op jit(solution)/shard_map/while/body/eval_jaxpr/convert_element_type | solution.py:192
  886.2 57.7 %reduce-scatter.15.cloned.1.call-done = f32[960,800]{0,1:T(8,128)} async-done(((f32[960,1600]{0,1:T(8,128)}), f32[960,800]{0,1:T(8,128)}) %reduce-scatter.15.cloned.1.call-update) | async-done | bytes 3072016 | tf_op jit(solution)/shard_map/reduce_scatter | solution.py:95
  948.8 112.1 %reduce-scatter.23.cloned.1.call-done = f32[960,1280]{1,0:T(8,128)} async-done(((f32[960,2560]{1,0:T(8,128)}), f32[960,1280]{1,0:T(8,128)}) %reduce-scatter.23.cloned.1.call-update) | async-done | bytes 4915216 | tf_op jit(solution)/shard_map/reduce_scatter | solution.py:98
  1061.0 117.2 %reduce-scatter.19.cloned.1.call-done = f32[960,1280]{1,0:T(8,128)} async-done(((f32[960,2560]{1,0:T(8,128)}), f32[960,1280]{1,0:T(8,128)}) %reduce-scatter.19.cloned.1.call-update) | async-done | bytes 4915216 | tf_op jit(solution)/shard_map/reduce_scatter | solution.py:97
  1178.2 116.9 %reduce-scatter.27.cloned.1.call-done = f32[1280,960]{0,1:T(8,128)} async-done(((f32[2560,960]{0,1:T(8,128)}), f32[1280,960]{0,1:T(8,128)}) %reduce-scatter.27.cloned.1.call-update) | async-done | bytes 4915216 | tf_op jit(solution)/shard_map/reduce_scatter | solution.py:99
  1295.2 33.2 %reduce-scatter.33.cloned.1.call-done = f32[240,480]{1,0:T(8,128)} async-done(((f32[960,480]{1,0:T(8,128)}), f32[240,480]{1,0:T(8,128)}) %reduce-scatter.33.cloned.1.call-update) | async-done | bytes 460816
  1330.4 40.3 %reduce-scatter.31.cloned.1.call-done = f32[240,800]{1,0:T(8,128)} async-done(((f32[960,800]{1,0:T(8,128)}), f32[240,800]{1,0:T(8,128)}) %reduce-scatter.31.cloned.1.call-update) | async-done | bytes 768016
  1373.0 49.5 %reduce-scatter.25.cloned.1.call-done = f32[240,1280]{1,0:T(8,128)} async-done(((f32[960,1280]{1,0:T(8,128)}), f32[240,1280]{1,0:T(8,128)}) %reduce-scatter.25.cloned.1.call-update) | async-done | bytes 1228816 | tf_op jit(solution)/shard_map/reduce_scatter | solution.py:108
  1422.6 51.7 %reduce-scatter.21.cloned.1.call-done = f32[240,1280]{1,0:T(8,128)} async-done(((f32[960,1280]{1,0:T(8,128)}), f32[240,1280]{1,0:T(8,128)}) %reduce-scatter.21.cloned.1.call-update) | async-done | bytes 1228816 | tf_op jit(solution)/shard_map/reduce_scatter | solution.py:107
  1474.2 52.0 %reduce-scatter.29.cloned.1.call-done = f32[1280,240]{0,1:T(8,128)} async-done(((f32[1280,960]{0,1:T(8,128)}), f32[1280,240]{0,1:T(8,128)}) %reduce-scatter.29.cloned.1.call-update) | async-done | bytes 1228816 | tf_op jit(solution)/shard_map/reduce_scatter | solution.py:109
  1571.9 59.5 %all-reduce = (f32[960]{0:T(1024)}, f32[960]{0:T(1024)}) all-reduce(f32[960]{0:T(1024)S(1)} %multiply_reduce_fusion.1, f32[960]{0:T(1024)S(1)} %copy-done.47), channel_id=1, replica_groups=mesh['dp'=4,'gx'=2,'gy'=4] {'dp','gx','gy'}, use_global_device_ids=true, to_apply=%region_27.28 | all-reduce | flops 1920 | bytes 15360 | tf_op jit(solution)/shard_map/psum | solution.py:273
  1635.9 77.0 %all-reduce.4.cloned.1.call-done = (f32[240,800]{0,1:T(8,128)}, f32[480,240]{1,0:T(8,128)}, f32[240,1280]{1,0:T(8,128)}, f32[240,1280]{1,0:T(8,128)}, f32[1280,240]{0,1:T(8,128)}) async-done(((f32[240,800]{0,1:T(8,128)}, f32[480,240]{1,0:T(8,128)}, f32[240,1280]{1,0:T(8,128)}, f32[240,1280]{1,0:T(8,128)}, f32[1280,240]{0,1:T(8,128)}), (f32[240,800]{0,1:T(8,128)}, f32[480,240]{1,0:T(8,128)}, ...) | async-done | bytes 4915216 | tf_op jit(solution)/shard_map/psum | solution.py:270
  (333 shorter events, 410.5 us)
Async XLA Ops:
  7.2 25.2 %all-gather.27.cloned.1.call-start = ((), (), s32[]{:S(2)}) async-start(), calls=%async_computation.30 | async-start | bytes 2048000 | tf_op jit(solution)/shard_map/all_gather | solution.py:85
  7.9 53.8 %all-gather.19.cloned.1.call-start = ((), (), s32[]{:S(2)}) async-start(), calls=%async_computation.18 | async-start | bytes 3072000 | tf_op jit(solution)/shard_map/all_gather | solution.py:88
  8.7 79.3 %all-gather.15.cloned.1.call-start = ((), (), s32[]{:S(2)}) async-start(), calls=%async_computation.16 | async-start | bytes 3072000 | tf_op jit(solution)/shard_map/all_gather | solution.py:87
  9.4 28.7 %copy-start.33 = (bf16[480,240]{1,0:T(8,128)(2,1)S(1)}, bf16[480,240]{1,0:T(8,128)(2,1)}, u32[]{:S(2)}) copy-start(bf16[480,240]{1,0:T(8,128)(2,1)} %param.20) | copy-start | bytes 691204
  9.4 126.9 %all-gather.11.cloned.1.call-start = ((), (), s32[]{:S(2)}) async-start(), calls=%async_computation.14 | async-start | bytes 4915200 | tf_op jit(solution)/shard_map/all_gather | solution.py:75
  37.4 126.8 %all-gather.23.cloned.1.call-start = ((), (), s32[]{:S(2)}) async-start(), calls=%async_computation.20 | async-start | bytes 3072000 | tf_op jit(solution)/shard_map/all_gather | solution.py:89
  38.0 331.6 %all-gather.13.cloned.1.call-start = ((), (), s32[]{:S(2)}) async-start(), calls=%async_computation.15 | async-start | bytes 2949120 | tf_op jit(solution)/shard_map/all_gather | solution.py:76
  51.6 36.3 %copy-start.15 = (bf16[240,4096]{1,0:T(8,128)(2,1)S(1)}, bf16[240,4096]{1,0:T(8,128)(2,1)}, u32[]{:S(2)}) copy-start(bf16[240,4096]{1,0:T(8,128)(2,1)} %param.14) | copy-start | bytes 5898244
  53.0 327.0 %all-gather.21.cloned.1.call-start = ((), (), s32[]{:S(2)}) async-start(), calls=%async_computation.19 | async-start | bytes 7372800 | tf_op jit(solution)/shard_map/all_gather | solution.py:78
  61.7 329.1 %all-gather.17.cloned.1.call-start = ((), (), s32[]{:S(2)}) async-start(), calls=%async_computation.17 | async-start | bytes 7372800 | tf_op jit(solution)/shard_map/all_gather | solution.py:77
  89.4 28.0 %all-to-all-start = ((bf16[240,4,1024]{2,0,1:T(8,128)(2,1)}), bf16[240,4,1024]{2,0,1:T(8,128)(2,1)S(1)}, u32[]{:S(2)}, u32[]{:S(2)}) async-start(bf16[240,4,1024]{2,0,1:T(8,128)(2,1)} %bitcast.312), calls=%async_computation | async-start | bytes 3932160 | tf_op jit(solution)/shard_map/all_to_all | solution.py:122
  96.2 26.8 %copy-start.45 = (f32[960]{0:T(1024)S(1)}, f32[960]{0:T(1024)}, u32[]{:S(2)}) copy-start(f32[960]{0:T(1024)} %param.17) | copy-start | bytes 11524
  96.8 71.6 %copy-start.10 = (f32[1024,32]{0,1:T(8,128)}, f32[1024,32]{0,1:T(8,128)S(1)}, u32[]{:S(2)}) copy-start(f32[1024,32]{0,1:T(8,128)S(1)} %get-tuple-element.230) | copy-start | bytes 393220
  96.8 71.6 %copy-start.12 = (f32[1024,32]{0,1:T(8,128)}, f32[1024,32]{0,1:T(8,128)S(1)}, u32[]{:S(2)}) copy-start(f32[1024,32]{0,1:T(8,128)S(1)} %get-tuple-element.231) | copy-start | bytes 393220
  117.4 283.9 %all-to-all-start.2 = ((bf16[240,4,1024]{2,0,1:T(8,128)(2,1)}), bf16[240,4,1024]{2,0,1:T(8,128)(2,1)}, u32[]{:S(2)}, u32[]{:S(2)}) async-start(bf16[240,4,1024]{2,0,1:T(8,128)(2,1)} %bitcast.310), calls=%async_computation.2 | async-start | bytes 3932160 | tf_op jit(solution)/shard_map/all_to_all | solution.py:123
  121.9 279.6 %all-gather.25.cloned.1.call-start = ((), (), s32[]{:S(2)}) async-start(), calls=%async_computation.21 | async-start | bytes 7372800 | tf_op jit(solution)/shard_map/all_gather | solution.py:79
  123.0 19.4 %copy-start.36 = (f32[1024]{0:T(1024)}, f32[1024]{0:T(1024)S(1)}, u32[]{:S(2)}) copy-start(f32[1024]{0:T(1024)S(1)} %get-tuple-element.233) | copy-start | bytes 12292
  144.1 26.4 %collective-permute-start.1 = (bf16[1024,5,64]{0,2,1:T(8,128)(2,1)S(1)}, bf16[1024,5,64]{0,2,1:T(8,128)(2,1)S(1)}, u32[]{:S(2)}, u32[]{:S(2)}) collective-permute-start(bf16[1024,5,64]{0,2,1:T(8,128)(2,1)S(1)} %pad_maximum_fusion.4), channel_id=1, source_target_pairs={{0,1},{1,2},{2,3},{4,5},{5,6},{6,7},{8,9},{9,10},{10,11},{12,13},{... | collective-permute-start | bytes 1966088 | tf_op jit(solution)/shard_map/ppermute | solution.py:19
  164.3 719.0 %reduce-scatter.17.cloned.1.call-start = ((), (), s32[]{:S(2)}) async-start(), calls=%async_computation.23 | async-start | bytes 5898240 | tf_op jit(solution)/shard_map/reduce_scatter | solution.py:96
  166.0 4.6 collective-permute-start
  171.8 197.9 %copy-start.1 = (bf16[240,4,1024]{2,0,1:T(8,128)(2,1)S(1)}, bf16[240,4,1024]{2,0,1:T(8,128)(2,1)}, u32[]{:S(2)}) copy-start(bf16[240,4,1024]{2,0,1:T(8,128)(2,1)} %copy-done) | copy-start | bytes 5898244
  376.2 66.7 %copy-start.34 = (f32[1024]{0:T(1024)}, f32[1024]{0:T(1024)S(1)}, u32[]{:S(2)}) copy-start(f32[1024]{0:T(1024)S(1)} %get-tuple-element.235) | copy-start | bytes 12292
  376.2 66.7 %copy-start.40 = (f32[1024]{0:T(1024)}, f32[1024]{0:T(1024)S(1)}, u32[]{:S(2)}) copy-start(f32[1024]{0:T(1024)S(1)} %get-tuple-element.234) | copy-start | bytes 12292
  421.8 10.7 copy-start.4
  421.8 10.7 copy-start.49
  421.8 10.7 copy-start.50
  452.7 491.2 %reduce-scatter.15.cloned.1.call-start = ((), (), s32[]{:S(2)}) async-start(), calls=%async_computation.22 | async-start | bytes 9830400 | tf_op jit(solution)/shard_map/reduce_scatter | solution.py:95
  459.3 370.9 %copy-start.11 = (f32[1024,32]{0,1:T(8,128)S(1)}, f32[1024,32]{0,1:T(8,128)}, u32[]{:S(2)}) copy-start(f32[1024,32]{0,1:T(8,128)} %copy-done.10) | copy-start | bytes 393220
  826.2 11.9 collective-permute-start.2
  828.9 12.5 collective-permute-start.3
  833.3 9.6 copy-start.17
  833.3 9.6 copy-start.16
  850.6 210.3 %reduce-scatter.23.cloned.1.call-start = ((), (), s32[]{:S(2)}) async-start(), calls=%async_computation.26 | async-start | bytes 14745600 | tf_op jit(solution)/shard_map/reduce_scatter | solution.py:98
  862.4 315.8 %reduce-scatter.19.cloned.1.call-start = ((), (), s32[]{:S(2)}) async-start(), calls=%async_computation.24 | async-start | bytes 14745600 | tf_op jit(solution)/shard_map/reduce_scatter | solution.py:97
  872.5 422.6 %reduce-scatter.27.cloned.1.call-start = ((), (), s32[]{:S(2)}) async-start(), calls=%async_computation.28 | async-start | bytes 14745600 | tf_op jit(solution)/shard_map/reduce_scatter | solution.py:99
  883.2 445.2 %reduce-scatter.33.cloned.1.call-start = ((), (), s32[]{:S(2)}) async-start(), calls=%async_computation.32 | async-start | bytes 2457600
  886.2 484.5 %reduce-scatter.31.cloned.1.call-start = ((), (), s32[]{:S(2)}) async-start(), calls=%async_computation.31 | async-start | bytes 4300800
  948.7 473.9 %reduce-scatter.25.cloned.1.call-start = ((), (), s32[]{:S(2)}) async-start(), calls=%async_computation.27 | async-start | bytes 6144000 | tf_op jit(solution)/shard_map/reduce_scatter | solution.py:108
  1060.9 413.3 %reduce-scatter.21.cloned.1.call-start = ((), (), s32[]{:S(2)}) async-start(), calls=%async_computation.25 | async-start | bytes 6144000 | tf_op jit(solution)/shard_map/reduce_scatter | solution.py:107
  1178.2 348.1 %reduce-scatter.29.cloned.1.call-start = ((), (), s32[]{:S(2)}) async-start(), calls=%async_computation.29 | async-start | bytes 6144000 | tf_op jit(solution)/shard_map/reduce_scatter | solution.py:109
  1295.2 231.1 %copy-start.2 = (bf16[240,4,1024]{2,0,1:T(8,128)(2,1)S(1)}, bf16[240,4,1024]{2,0,1:T(8,128)(2,1)}, u32[]{:S(2)}) copy-start(bf16[240,4,1024]{2,0,1:T(8,128)(2,1)} %copy-done) | copy-start | bytes 5898244
  1295.2 417.7 %all-reduce.4.cloned.1.call-start = ((), (), s32[]{:S(2)}) async-start(), calls=%async_computation.33 | async-start | bytes 9994240 | tf_op jit(solution)/shard_map/psum | solution.py:270
  1536.7 28.9 %all-to-all-start.1 = ((bf16[4,240,1024]{2,1,0:T(8,128)(2,1)}), bf16[4,240,1024]{2,1,0:T(8,128)(2,1)}, u32[]{:S(2)}, u32[]{:S(2)}) async-start(bf16[4,240,1024]{2,1,0:T(8,128)(2,1)} %bitcast.330), calls=%async_computation.1 | async-start | bytes 3932160 | tf_op jit(solution)/shard_map/all_to_all | solution.py:263
  1541.3 8.8 copy-start.5
  1541.3 8.8 copy-start.7
  1541.3 8.8 copy-start.35
  1541.3 8.8 copy-start.37
  1565.6 68.7 %all-to-all-start.3 = ((bf16[4,240,1024]{2,1,0:T(8,128)(2,1)}), bf16[4,240,1024]{2,1,0:T(8,128)(2,1)S(1)}, u32[]{:S(2)}, u32[]{:S(2)}) async-start(bf16[4,240,1024]{2,1,0:T(8,128)(2,1)} %bitcast.313), calls=%async_computation.3 | async-start | bytes 3932160 | tf_op jit(solution)/shard_map/all_to_all | solution.py:264
  (63 other events, 238.3 us)
Sparse Core Ops, SparseCore 0:
  9.6 22.7 all-gather.26
  33.9 27.7 all-gather.18
  63.3 24.6 all-gather.14
  89.9 46.3 all-gather.10
  137.7 26.4 all-gather.22
  166.2 35.9 all-gather.12
  203.7 64.8 all-gather.20
  270.2 64.8 all-gather.16
  336.7 64.8 all-gather.24
  452.8 63.6 reduce-scatter.16
  850.8 93.0 reduce-scatter.14
  946.1 114.7 reduce-scatter.22
  1063.3 114.7 reduce-scatter.18
  1180.3 114.7 reduce-scatter.26
  1297.7 30.6 reduce-scatter.32
  1330.8 39.8 reduce-scatter.30
  1373.3 49.2 reduce-scatter.24
  1425.0 49.1 reduce-scatter.20
  1477.0 49.1 reduce-scatter.28
  1529.4 183.4 all-reduce.3
where the time goes:
time: 1740 us; the launch traced here: 1730 us
  waiting for transfers between devices  837 us (48%)
  matrix products  518 us (30%)
  other arithmetic  197 us (11%)
  blocking collectives  72.9 us (4%)
  local copies, waits for them, and re-layouts  64.2 us (4%)
  starting transfers between devices  23.5 us (1%)
    reduce_scatter x1, waiting for transfers between devices, scatter_wide(): lax.psum_scatter(parts[2], 'gx', scatter_dimension=1, tiled=True)  117 us
    reduce_scatter x1, waiting for transfers between devices, scatter_wide(): lax.psum_scatter(parts[4], 'gx', scatter_dimension=0, tiled=True)  117 us
    dot_general x10, matrix products, scores_of(): jnp.einsum('qrd,kd->rqk', query_part, key_part, preferred_element_type=jn...  117 us
    reduce_scatter x1, waiting for transfers between devices, scatter_wide(): lax.psum_scatter(parts[3], 'gx', scatter_dimension=1, tiled=True)  112 us
    dot_general x10, matrix products, contract(): lax.dot_general(left, right, (((left_dim,), (right_dim,)), ((), ())), pre...  97.7 us
    dot_general x5, matrix products, backward_group(): jnp.einsum('qrd,kd->rqk', grad_part, value_part, preferred_element_type=j...  88.9 us
    convert_element_type x5, other arithmetic, backward_group(): score_grads = (soft_rows * (prob_grads - inner_sum)).astype(jnp.bfloat16)  87.2 us
    psum x1, waiting for transfers between devices, on_device(): lax.psum((shard_grads[0], shard_grads[1], shard_grads[2], shard_grads[3],...  77 us
  transfers between devices with their start and end apart: 28, of which 20 were waited for; matrix products, arithmetic and copies ran while one was open for 41% of the time, Pallas kernels for 0%

commit v1 on v0

v1 whole, which is shorter than its diff:
```python
import functools

import jax
import jax.numpy as jnp
from jax import lax
from jax.experimental import pallas as pl
from jax.experimental.pallas import tpu as pltpu
from jax.sharding import PartitionSpec as P

HEADS = 15
KV_HEADS = 5
GROUP = HEADS // KV_HEADS
HEAD = 64
HALF = HEAD // 2
PRIOR = 512
TILE = 256

EPS = 1e-05
THETA = 100000.0
NEG = -1e30

BF = jnp.bfloat16
F32 = jnp.float32


def swap(value, axis, by):
    peers = lax.axis_size(axis)
    return lax.ppermute(value, axis, [(i, i ^ by) for i in range(peers)])


def dot(left, right, left_dim, right_dim):
    return lax.dot_general(
        left, right, (((left_dim,), (right_dim,)), ((), ())), preferred_element_type=F32
    )


def add(left, right):
    return (left.astype(F32) + right.astype(F32)).astype(BF)


def frequencies():
    return jnp.power(THETA, -jnp.arange(HALF, dtype=F32) / HALF)


def to_tokens(shard):
    peers = lax.axis_size("gy")
    me = lax.axis_index("gy")
    rows = shard.shape[1] // peers
    blocks = []
    for by in range(peers):
        piece = lax.dynamic_slice_in_dim(shard, (me ^ by) * rows, rows, 1)
        blocks.append(swap(piece, "gy", by) if by else piece)
    return jnp.concatenate(blocks, axis=0)


def to_features(full):
    peers = lax.axis_size("gy")
    me = lax.axis_index("gy")
    block, rows = full.shape[0] // peers, full.shape[1]
    out = jnp.zeros((block, rows * peers), full.dtype)
    for by in range(peers):
        piece = full[by * block : (by + 1) * block]
        piece = swap(piece, "gy", by) if by else piece
        out = lax.dynamic_update_slice_in_dim(out, piece, (me ^ by) * rows, 1)
    return out


def reorder(vector):
    peers = lax.axis_size("gy")
    me = lax.axis_index("gy")
    block = vector.shape[0] // peers
    return jnp.concatenate(
        [lax.dynamic_slice_in_dim(vector, (me ^ by) * block, block, 0) for by in range(peers)]
    )


def gather_x(block, dim):
    if lax.axis_size("gx") == 2:
        return [block, swap(block, "gx", 1)]
    whole = lax.all_gather(block, "gx", axis=dim, tiled=True)
    half = whole.shape[dim] // 2
    return [
        lax.slice_in_dim(whole, 0, half, axis=dim),
        lax.slice_in_dim(whole, half, 2 * half, axis=dim),
    ]


def reduce_x(chunks, dim):
    if lax.axis_size("gx") == 2:
        return add(chunks[0], swap(chunks[1], "gx", 1))
    return lax.psum_scatter(
        jnp.concatenate(chunks, axis=dim), "gx", scatter_dimension=dim, tiled=True
    )


def gather_blocks(shard, dim):
    far = swap(shard, "gy", 2)
    own = gather_x(shard, dim)
    far = gather_x(far, dim)
    return [
        [own[c], swap(own[c], "gy", 1), far[c], swap(far[c], "gy", 1)] for c in range(2)
    ]


def join_x(chunks, dim):
    if lax.axis_size("gx") == 2:
        first = lax.axis_index("gx") == 0
        low = jnp.where(first, chunks[0], chunks[1])
        high = jnp.where(first, chunks[1], chunks[0])
        return jnp.concatenate([low, high], axis=dim)
    return jnp.concatenate(chunks, axis=dim)


def split_x(whole, dim):
    half = whole.shape[dim] // 2
    if lax.axis_size("gx") == 2:
        me = lax.axis_index("gx")
        return [
            lax.dynamic_slice_in_dim(whole, me * half, half, dim),
            lax.dynamic_slice_in_dim(whole, (1 - me) * half, half, dim),
        ]
    return [
        lax.slice_in_dim(whole, 0, half, axis=dim),
        lax.slice_in_dim(whole, half, 2 * half, axis=dim),
    ]


def sum_z(value):
    peers = lax.axis_size("dp")
    if peers != 4:
        return lax.psum(value.astype(F32), "dp")
    me = lax.axis_index("dp")
    inner = add(value, lax.ppermute(value, "dp", [(0, 1), (3, 2)]))
    total = add(inner, lax.ppermute(inner, "dp", [(1, 2), (2, 1)]))
    outer = lax.ppermute(total, "dp", [(1, 0), (2, 3)])
    return jnp.where((me == 0) | (me == 3), outer, total).astype(F32)


def reduce_blocks(chunks, dim):
    near, far = [], []
    for blocks in chunks:
        near.append(add(blocks[0], swap(blocks[1], "gy", 1)))
        far.append(add(blocks[2], swap(blocks[3], "gy", 1)))
    far = reduce_x(far, dim)
    near = reduce_x(near, dim)
    return sum_z(add(near, swap(far, "gy", 2)))


def reduce_joined(blocks, dim):
    near = add(blocks[0], swap(blocks[1], "gy", 1))
    far = add(blocks[2], swap(blocks[3], "gy", 1))
    far = reduce_x(split_x(far, dim), dim)
    near = reduce_x(split_x(near, dim), dim)
    return sum_z(add(near, swap(far, "gy", 2)))


def sum_all(value):
    for axis in ("gy", "gx", "dp"):
        by = 1
        while by < lax.axis_size(axis):
            value = value + swap(value, axis, by)
            by *= 2
    return value


RANGES = ((0, 768), (0, 1024), (512, 1280), (512, 1536))


def fill_bias(starts_ref, bias_ref):
    offset = 0
    for tile, (low, high) in enumerate(RANGES):
        size = high - low
        place = lax.broadcasted_iota(jnp.int32, (size, TILE), 0) + (low - PRIOR)
        query = lax.broadcasted_iota(jnp.int32, (size, TILE), 1) + tile * TILE
        start = starts_ref[:, tile * TILE : (tile + 1) * TILE]
        allowed = (place >= start) & (place <= query)
        bias_ref[offset : offset + size, :] = jnp.where(allowed, 0.0, NEG)
        offset += size


BIAS_ROWS = sum(high - low for low, high in RANGES)


def turned(prior_ref, own_ref, out_ref):
    out_ref[:PRIOR, :] = prior_ref[...].astype(F32).T.astype(BF)
    out_ref[PRIOR:, :] = own_ref[...].astype(F32).T.astype(BF)


def forward_kernel(
    starts_ref, q_ref, kp_ref, ko_ref, vp_ref, vo_ref, mixed_ref, lse_ref, keys, values, bias
):
    @pl.when(pl.program_id(0) == 0)
    def _():
        fill_bias(starts_ref, bias)

    turned(kp_ref, ko_ref, keys)
    values[:, :PRIOR] = vp_ref[...]
    values[:, PRIOR:] = vo_ref[...]
    offset = 0
    for tile, (low, high) in enumerate(RANGES):
        size = high - low
        lanes = slice(tile * TILE, (tile + 1) * TILE)
        for head in range(GROUP):
            rows = slice(head * HEAD, (head + 1) * HEAD)
            scores = dot(keys[low:high, :], q_ref[rows, lanes], 1, 0)
            scores = scores + bias[offset : offset + size, :]
            top = jnp.max(scores, axis=0, keepdims=True)
            weights = jnp.exp(scores - top)
            total = jnp.sum(weights, axis=0, keepdims=True)
            out = dot(values[:, low:high], weights.astype(BF), 1, 0)
            mixed_ref[rows, lanes] = (out / total).astype(BF)
            lse_ref[0, head : head + 1, lanes] = top + jnp.log(total)
        offset += size


def attention_forward(starts, queries, prior_k, own_k, prior_v, own_v):
    count = queries.shape[1]
    wide = GROUP * HEAD
    prior = pl.BlockSpec((HEAD, PRIOR), lambda g: (g, 0))
    own = pl.BlockSpec((HEAD, count), lambda g: (g, 0))
    return pl.pallas_call(
        forward_kernel,
        grid=(KV_HEADS,),
        in_specs=[
            pl.BlockSpec((1, count), lambda g: (0, 0)),
            pl.BlockSpec((wide, count), lambda g: (g, 0)),
            prior,
            own,
            prior,
            own,
        ],
        out_specs=[
            pl.BlockSpec((wide, count), lambda g: (g, 0)),
            pl.BlockSpec((1, 8, count), lambda g: (g, 0, 0)),
        ],
        out_shape=[
            jax.ShapeDtypeStruct((HEADS * HEAD, count), BF),
            jax.ShapeDtypeStruct((KV_HEADS, 8, count), F32),
        ],
        scratch_shapes=[
            pltpu.VMEM((PRIOR + count, HEAD), BF),
            pltpu.VMEM((HEAD, PRIOR + count), BF),
            pltpu.VMEM((BIAS_ROWS, TILE), F32),
        ],
        compiler_params=pltpu.CompilerParams(vmem_limit_bytes=40 * 2**20),
        cost_estimate=pl.CostEstimate(
            flops=2 * 2 * HEADS * BIAS_ROWS * TILE * 256,
            bytes_accessed=8 * 2**20,
            transcendentals=HEADS * BIAS_ROWS * TILE,
        ),
        name="attend_forward",
    )(starts, queries, prior_k, own_k, prior_v, own_v)


def backward_kernel(
    starts_ref,
    cos_ref,
    sin_ref,
    q_ref,
    kp_ref,
    ko_ref,
    vp_ref,
    vo_ref,
    mixed_ref,
    lse_ref,
    grad_ref,
    dq_ref,
    dkp_ref,
    dko_ref,
    dvp_ref,
    dvo_ref,
    keys,
    turned_keys,
    turned_values,
    dk,
    dv,
    bias,
):
    @pl.when(pl.program_id(0) == 0)
    def _():
        fill_bias(starts_ref, bias)

    turned(kp_ref, ko_ref, turned_keys)
    turned(vp_ref, vo_ref, turned_values)
    keys[:, :PRIOR] = kp_ref[...]
    keys[:, PRIOR:] = ko_ref[...]
    dk[...] = jnp.zeros_like(dk)
    dv[...] = jnp.zeros_like(dv)
    offset = 0
    for tile, (low, high) in enumerate(RANGES):
        size = high - low
        lanes = slice(tile * TILE, (tile + 1) * TILE)
        for head in range(GROUP):
            rows = slice(head * HEAD, (head + 1) * HEAD)
            query = q_ref[rows, lanes]
            grad = grad_ref[rows, lanes]
            inner = jnp.sum(
                grad.astype(F32) * mixed_ref[rows, lanes].astype(F32), axis=0, keepdims=True
            )
            lse = lse_ref[0, head : head + 1, lanes]
            scores = dot(turned_keys[low:high, :], query, 1, 0)
            weights = jnp.exp(scores + bias[offset : offset + size, :] - lse)
            prob_grad = dot(turned_values[low:high, :], grad, 1, 0)
            score_grad = (weights * (prob_grad - inner)).astype(BF)
            weights = weights.astype(BF)
            dv[low:high, :] += dot(weights, grad, 1, 1)
            dk[low:high, :] += dot(score_grad, query, 1, 1)
            dq = dot(keys[:, low:high], score_grad, 1, 0) * HEAD ** (-0.5)
            cosine, sine = cos_ref[:, lanes], sin_ref[:, lanes]
            front, back = dq[:HALF], dq[HALF:]
            base = head * HEAD
            dq_ref[base : base + HALF, lanes] = (front * cosine + back * sine).astype(BF)
            dq_ref[base + HALF : base + HEAD, lanes] = (back * cosine - front * sine).astype(BF)
        offset += size
    dkp_ref[...] = dk[:PRIOR, :].T.astype(BF)
    dvp_ref[...] = dv[:PRIOR, :].T.astype(BF)
    dko_ref[...] = dk[PRIOR:, :].T
    dvo_ref[...] = dv[PRIOR:, :].T


def attention_backward(
    starts, cosine, sine, queries, prior_k, own_k, prior_v, own_v, mixed, lse, grads
):
    count = queries.shape[1]
    wide = GROUP * HEAD
    prior = pl.BlockSpec((HEAD, PRIOR), lambda g: (g, 0))
    own = pl.BlockSpec((HEAD, count), lambda g: (g, 0))
    heads = pl.BlockSpec((wide, count), lambda g: (g, 0))
    table = pl.BlockSpec((HALF, count), lambda g: (0, 0))
    return pl.pallas_call(
        backward_kernel,
        grid=(KV_HEADS,),
        in_specs=[
            pl.BlockSpec((1, count), lambda g: (0, 0)),
            table,
            table,
            heads,
            prior,
            own,
            prior,
            own,
            heads,
            pl.BlockSpec((1, 8, count), lambda g: (g, 0, 0)),
            heads,
        ],
        out_specs=[heads, prior, own, prior, own],
        out_shape=[
            jax.ShapeDtypeStruct((HEADS * HEAD, count), BF),
            jax.ShapeDtypeStruct((KV_HEADS * HEAD, PRIOR), BF),
            jax.ShapeDtypeStruct((KV_HEADS * HEAD, count), F32),
            jax.ShapeDtypeStruct((KV_HEADS * HEAD, PRIOR), BF),
            jax.ShapeDtypeStruct((KV_HEADS * HEAD, count), F32),
        ],
        scratch_shapes=[
            pltpu.VMEM((HEAD, PRIOR + count), BF),
            pltpu.VMEM((PRIOR + count, HEAD), BF),
            pltpu.VMEM((PRIOR + count, HEAD), BF),
            pltpu.VMEM((PRIOR + count, HEAD), F32),
            pltpu.VMEM((PRIOR + count, HEAD), F32),
            pltpu.VMEM((BIAS_ROWS, TILE), F32),
        ],
        compiler_params=pltpu.CompilerParams(vmem_limit_bytes=44 * 2**20),
        cost_estimate=pl.CostEstimate(
            flops=5 * 2 * HEADS * BIAS_ROWS * TILE * 256,
            bytes_accessed=16 * 2**20,
            transcendentals=HEADS * BIAS_ROWS * TILE,
        ),
        name="attend_backward",
    )(starts, cosine, sine, queries, prior_k, own_k, prior_v, own_v, mixed, lse, grads)


def mlp_kernel(first, *refs):
    normed_ref, up_ref, base_ref = refs[:3]
    refs = refs[3:]
    if not first:
        grad_in_ref, refs = refs[0], refs[1:]
    gates, ups, downs = refs[0:4], refs[4:8], refs[8:12]
    out_ref, grad_out_ref = refs[12:14]
    gate_grads, up_grads, down_grads = refs[14:18], refs[18:22], refs[22:26]
    total_ref, grad_total_ref = refs[26:28]
    step = pl.program_id(0)
    last = pl.num_programs(0) - 1

    @pl.when(step == 0)
    def _():
        total_ref[...] = base_ref[...]
        if first:
            grad_total_ref[...] = jnp.zeros_like(grad_total_ref)
        else:
            grad_total_ref[...] = grad_in_ref[...]

    normed = normed_ref[...]
    block = normed.shape[0] // 4
    w_gate = jnp.concatenate([ref[...] for ref in gates], axis=0)
    w_up = jnp.concatenate([ref[...] for ref in ups], axis=0)
    gate = dot(w_gate, normed, 0, 0)
    up = dot(w_up, normed, 0, 0)
    sigmoid = 1.0 / (1.0 + jnp.exp(-gate))
    silu = gate * sigmoid
    hidden = (silu * up).astype(BF)
    hidden_grad = dot(downs[0][...], up_ref[:block, :], 1, 0)
    for j in range(1, 4):
        hidden_grad += dot(downs[j][...], up_ref[j * block : (j + 1) * block, :], 1, 0)
    gate_grad = (hidden_grad * up * (sigmoid * (1.0 + gate * (1.0 - sigmoid)))).astype(BF)
    up_grad = (hidden_grad * silu).astype(BF)
    for j in range(4):
        rows = slice(j * block, (j + 1) * block)
        total_ref[rows, :] += dot(downs[j][...], hidden, 0, 0)
        down_grads[j][...] = dot(hidden, up_ref[rows, :], 1, 1).astype(BF)
    grad_total_ref[...] += dot(w_gate, gate_grad, 1, 0) + dot(w_up, up_grad, 1, 0)
    made = dot(normed, gate_grad, 1, 1).astype(BF)
    for j in range(4):
        gate_grads[j][...] = made[j * block : (j + 1) * block]
    made = dot(normed, up_grad, 1, 1).astype(BF)
    for j in range(4):
        up_grads[j][...] = made[j * block : (j + 1) * block]

    @pl.when(step == last)
    def _():
        out_ref[...] = total_ref[...].astype(out_ref.dtype)
        grad_out_ref[...] = grad_total_ref[...]


def mlp_chunk(normed, upstream, base, grad_in, gates, ups, downs):
    first = grad_in is None
    width, count = normed.shape
    block, size = gates[0].shape
    tile = TILE
    whole = pl.BlockSpec((width, count), lambda i: (0, 0), pipeline_mode=pl.Buffered(1))
    across = pl.BlockSpec((block, tile), lambda i: (0, i))
    down = pl.BlockSpec((tile, block), lambda i: (i, 0))
    operands = [normed, upstream, base] + ([] if first else [grad_in])
    return pl.pallas_call(
        functools.partial(mlp_kernel, first),
        grid=(size // tile,),
        in_specs=[whole] * len(operands) + [across] * 8 + [down] * 4,
        out_specs=[whole, whole] + [across] * 8 + [down] * 4,
        out_shape=[
            jax.ShapeDtypeStruct((width, count), F32 if first else BF),
            jax.ShapeDtypeStruct((width, count), F32),
        ]
        + [jax.ShapeDtypeStruct((block, size), BF)] * 8
        + [jax.ShapeDtypeStruct((size, block), BF)] * 4,
        scratch_shapes=[pltpu.VMEM((width, count), F32), pltpu.VMEM((width, count), F32)],
        compiler_params=pltpu.CompilerParams(vmem_limit_bytes=56 * 2**20),
        cost_estimate=pl.CostEstimate(
            flops=9 * 2 * width * count * size,
            bytes_accessed=30 * 2**20,
            transcendentals=size * count,
        ),
        name="feed_forward",
    )(*operands, *gates, *ups, *downs)


def norm_scale_of(values):
    return lax.rsqrt(jnp.mean(values * values, axis=0, keepdims=True) + EPS)


def norm_back(values, scale, gain, gradient):
    weighted = gradient * gain
    inner = jnp.mean(weighted * values, axis=0, keepdims=True)
    values_grad = scale * weighted - values * (scale * scale * scale) * inner
    return (values_grad, jnp.sum(gradient * values * scale, axis=1))


def rotate(values, cosine, sine):
    heads = values.shape[0] // HEAD
    count = values.shape[1]
    pairs = values.astype(F32).reshape(heads, 2, HALF, count)
    front, back = pairs[:, 0], pairs[:, 1]
    return jnp.stack(
        [front * cosine - back * sine, back * cosine + front * sine], axis=1
    ).reshape(heads * HEAD, count)


def on_device(
    tokens, doc_start, cotangent, attn_gain, mlp_gain, w_qkv, w_out, w_gate, w_up, w_down
):
    count = doc_start.shape[0]
    query_width = HEADS * HEAD
    kv_width = KV_HEADS * HEAD
    score_scale = HEAD ** (-0.5)

    inputs = to_tokens(tokens)
    qkv_chunks = gather_blocks(w_qkv, 1)
    full_qkv = join_x([jnp.concatenate(blocks, axis=0) for blocks in qkv_chunks], 1)
    out_chunks = gather_blocks(w_out, 0)
    full_out = join_x([jnp.concatenate(blocks, axis=1) for blocks in out_chunks], 0)
    upstream = to_tokens(cotangent)
    gate_chunks = gather_blocks(w_gate, 1)
    up_chunks = gather_blocks(w_up, 1)
    down_chunks = gather_blocks(w_down, 0)

    attn_gain = reorder(attn_gain)[:, None]
    mlp_gain = reorder(mlp_gain)[:, None]

    residual = inputs.astype(F32)
    scale_one = norm_scale_of(residual)
    normed_one = (residual * scale_one * attn_gain).astype(BF)
    projected = dot(full_qkv, normed_one, 0, 0).astype(BF)

    first_row = lax.axis_index(("dp", "gx", "gy")) * count
    places = first_row + jnp.arange(count, dtype=jnp.int32)
    angle = frequencies()[:, None] * (places - doc_start).astype(F32)[None, :]
    cosine, sine = jnp.cos(angle), jnp.sin(angle)
    starts = (doc_start - first_row)[None, :]

    queries = (rotate(projected[:query_width], cosine, sine) * score_scale).astype(BF)
    own_k = rotate(projected[query_width : query_width + kv_width], cosine, sine).astype(BF)
    own_v = projected[query_width + kv_width :]
    peers = lax.axis_size("gy")
    ahead = [(i, i + 1) for i in range(0, peers, 2)]
    behind = [(i + 1, i) for i in range(0, peers, 2)]
    prior_k = lax.ppermute(own_k[:, count - PRIOR :], "gy", ahead)
    prior_v = lax.ppermute(own_v[:, count - PRIOR :], "gy", ahead)

    mixed, lse = attention_forward(starts, queries, prior_k, own_k, prior_v, own_v)

    middle = residual + dot(full_out, mixed, 0, 0)
    scale_two = norm_scale_of(middle)
    normed_two = (middle * scale_two * mlp_gain).astype(BF)

    made = mlp_chunk(
        normed_two, upstream, middle, None, gate_chunks[0], up_chunks[0], down_chunks[0]
    )
    later = mlp_chunk(
        normed_two, upstream, made[0], made[1], gate_chunks[1], up_chunks[1], down_chunks[1]
    )
    result, normed_two_grad = later[0], later[1]
    shard_gate = reduce_blocks([made[2:6], later[2:6]], 1)
    shard_up = reduce_blocks([made[6:10], later[6:10]], 1)
    shard_down = reduce_blocks([made[10:14], later[10:14]], 0)
    result_shard = to_features(result)

    mid_grad, gain_two = norm_back(middle, scale_two, mlp_gain, normed_two_grad)
    mid_grad = mid_grad + upstream.astype(F32)
    branch_grad = mid_grad.astype(BF)
    mixed_grad = dot(full_out, branch_grad, 1, 0).astype(BF)
    grad_out = dot(mixed, branch_grad, 1, 1).astype(BF)
    width = grad_out.shape[1]
    block = width // 4
    shard_out = reduce_joined([grad_out[:, j * block : (j + 1) * block] for j in range(4)], 0)

    dq, dkp, dko, dvp, dvo = attention_backward(
        starts, cosine, sine, queries, prior_k, own_k, prior_v, own_v, mixed, lse, mixed_grad
    )
    sent_k = lax.ppermute(dkp, "gy", behind).astype(F32)
    sent_v = lax.ppermute(dvp, "gy", behind).astype(F32)
    zeros = jnp.zeros((kv_width, count - PRIOR), F32)
    dk = dko + jnp.concatenate([zeros, sent_k], axis=1)
    dv = dvo + jnp.concatenate([zeros, sent_v], axis=1)
    projected_grad = jnp.concatenate(
        [dq, rotate(dk, cosine, -sine).astype(BF), dv.astype(BF)], axis=0
    )
    grad_qkv = dot(normed_one, projected_grad, 1, 1).astype(BF)
    shard_qkv = reduce_joined([grad_qkv[j * block : (j + 1) * block] for j in range(4)], 1)
    normed_one_grad = dot(full_qkv, projected_grad, 1, 0)
    in_grad, gain_one = norm_back(residual, scale_one, attn_gain, normed_one_grad)
    grad_shard = to_features((in_grad + mid_grad).astype(BF))
    gain_one = sum_all(reorder(gain_one))
    gain_two = sum_all(reorder(gain_two))
    return (
        result_shard,
        grad_shard,
        shard_qkv,
        shard_out,
        shard_gate,
        shard_up,
        shard_down,
        gain_one,
        gain_two,
    )


def solution(mesh):
    placed = (
        P("gy", ("dp", "gx")),
        P(("dp", "gx", "gy")),
        P("gy", ("dp", "gx")),
        P(),
        P(),
        P("gy", "gx"),
        P("gx", "gy"),
        P("gy", "gx"),
        P("gy", "gx"),
        P("gx", "gy"),
    )
    return jax.shard_map(
        on_device,
        mesh=mesh,
        in_specs=placed,
        out_specs=(
            P("gy", ("dp", "gx")),
            P("gy", ("dp", "gx")),
            P("gy", "gx"),
            P("gx", "gy"),
            P("gy", "gx"),
            P("gy", "gx"),
            P("gx", "gy"),
            P(),
            P(),
        ),
        check_vma=False,
    )
```

time: 1740 us -> 671 us (0.39)
  waiting for transfers between devices: 837 us -> 242 us
  matrix products: 518 us -> 24.9 us
  Pallas kernels: 0 us -> 147 us
  other arithmetic: 197 us -> 76 us
  starting transfers between devices: 23.5 us -> 97.6 us
  blocking collectives: 72.9 us -> 0 us
    reduce_scatter x8 -> x0, waiting for transfers between devices: 557 us -> none  [the longest x1 117 us: scatter_wide(): lax.psum_scatter(parts[2], 'gx', scatter_dimension=1, tiled=True)]
    dot_general x50 -> x6, matrix products: 518 us -> 24.9 us  [dot(): lax.dot_general(left, right, (((left_dim,), (right_dim,)), ((), ())), pre...]
    ppermute x4 -> x107, waiting for transfers between devices: 7.61 us -> 242 us  [the longest x88 171 us: swap(): return lax.ppermute(value, axis, [(i, i ^ by) for i in range(peers)])]
    pallas_call x0 -> x4, Pallas kernels: none -> 147 us  [the longest x2 71.1 us: mlp_chunk(): pl.pallas_call(functools.partial(mlp_kernel, first), grid=(size // tile,)...]
    ppermute x4 -> x107, starting transfers between devices: 6.25 us -> 97.6 us  [the longest x88 63.5 us: swap(): return lax.ppermute(value, axis, [(i, i ^ by) for i in range(peers)])]
    all_gather x9 -> x0, waiting for transfers between devices: 87.7 us -> none  [the longest x1 26.2 us: gather_narrow(): lax.all_gather(parts[2], 'gy', axis=0, tiled=True)]
    psum x1 -> x0, waiting for transfers between devices: 77 us -> none  [on_device(): lax.psum((shard_grads[0], shard_grads[1], shard_grads[2], shard_grads[3],...]
    unnamed x22 -> x0, waiting for transfers between devices: 76.3 us -> none
  transfers between devices with their start and end apart: 28 -> 107, of which waited for: 20 -> 38; matrix products, arithmetic and copies ran while one was open for 41% -> 25% of each run, Pallas kernels for 0% -> 22%
where the time goes in v1:
time: 671 us; the launch traced here: 661 us
  waiting for transfers between devices  242 us (36%)
  Pallas kernels  147 us (22%)
  starting transfers between devices  97.6 us (15%)
  other arithmetic  76 us (11%)
  local copies, waits for them, and re-layouts  71.3 us (11%)
  matrix products  24.9 us (4%)
    ppermute x88, waiting for transfers between devices, swap(): return lax.ppermute(value, axis, [(i, i ^ by) for i in range(peers)])  171 us
    pallas_call x2, Pallas kernels, mlp_chunk(): pl.pallas_call(functools.partial(mlp_kernel, first), grid=(size // tile,)...  71.1 us
    ppermute x88, starting transfers between devices, swap(): return lax.ppermute(value, axis, [(i, i ^ by) for i in range(peers)])  63.5 us
    ppermute x5, waiting for transfers between devices, sum_z(): outer = lax.ppermute(total, 'dp', [(1, 0), (2, 3)])  46.6 us
    pallas_call x1, Pallas kernels, attention_backward(): pl.pallas_call(backward_kernel, grid=(KV_HEADS,), in_specs=[pl.BlockSpec(...  38.4 us
    convert_element_type x28, other arithmetic, add(): return (left.astype(F32) + right.astype(F32)).astype(BF)  38.4 us
    pallas_call x1, Pallas kernels, attention_forward(): pl.pallas_call(forward_kernel, grid=(KV_HEADS,), in_specs=[pl.BlockSpec((...  37.5 us
    dot_general x6, matrix products, dot(): lax.dot_general(left, right, (((left_dim,), (right_dim,)), ((), ())), pre...  24.9 us
  transfers between devices with their start and end apart: 107, of which 38 were waited for; matrix products, arithmetic and copies ran while one was open for 25% of the time, Pallas kernels for 22%

profile of v1, /device:TPU:0, one launch (start us, length us, event | category | flops | bytes accessed | tf_op | source)
XLA Modules:
  0.0 660.8 jit_solution(8687785983717755129)
XLA Ops:
  0.6 3.0 collective-permute-start.4
  6.5 4.2 collective-permute-done.4
  12.9 2.6 constant_dynamic-slice_fusion.11
  22.3 3.2 collective-permute-done.8
  30.1 5.9 collective-permute-done.1
  36.5 8.2 %collective-permute-done.2 = bf16[240,1024]{1,0:T(8,128)(2,1)S(1)} collective-permute-done((bf16[240,1024]{1,0:T(8,128)(2,1)}, bf16[240,1024]{1,0:T(8,128)(2,1)S(1)}, u32[]{:S(2)}, u32[]{:S(2)}) %collective-permute-start.2) | collective-permute-done | bytes 491552 | tf_op jit(solution)/shard_map/ppermute | solution.py:28
  49.0 8.0 %collective-permute-done.20 = bf16[240,1024]{1,0:T(8,128)(2,1)S(1)} collective-permute-done((bf16[240,1024]{1,0:T(8,128)(2,1)}, bf16[240,1024]{1,0:T(8,128)(2,1)S(1)}, u32[]{:S(2)}, u32[]{:S(2)}) %collective-permute-start.20) | collective-permute-done | bytes 491552 | tf_op jit(solution)/shard_map/ppermute | solution.py:28
  60.0 5.7 collective-permute-done.21
  68.4 10.8 %collective-permute-done.29 = bf16[1280,240]{0,1:T(8,128)(2,1)} collective-permute-done((bf16[1280,240]{0,1:T(8,128)(2,1)}, bf16[1280,240]{0,1:T(8,128)(2,1)}, u32[]{:S(2)}, u32[]{:S(2)}) %collective-permute-start.29) | collective-permute-done | bytes 614432 | tf_op jit(solution)/shard_map/ppermute | solution.py:28
  89.4 3.9 broadcast_select_fusion.3
  95.1 3.9 broadcast_select_fusion.1
  99.1 5.1 convolution_convert_fusion
  107.9 3.0 collective-permute-start.17
  124.4 37.5 %attend_forward.1 = (bf16[960,1024]{1,0:T(8,128)(2,1)S(1)}, f32[5,8,1024]{2,1,0:T(8,128)S(1)}) custom-call(s32[1,1024]{1,0:T(1,128)S(1)} %bitcast.16, bf16[960,1024]{1,0:T(8,128)(2,1)S(1)} %bitcast.11, bf16[320,512]{1,0:T(8,128)(2,1)} %collective-permute-done.17.kp_ref, bf16[320,1024]{1,0:T(8,128)(2,1)S(1)} %bitcast.14, ...), custom_call_target="tpu_custom_call" | custom-call | flops 14092861440 | bytes 8388608 | tf_op jit(solution)/shard_map/attend_forward/pallas_call | solution.py:221
  166.0 3.6 multiply_reduce_fusion.2
  172.2 6.7 %collective-permute-done.35.refs_8_ = bf16[240,1280]{1,0:T(8,128)(2,1)} collective-permute-done((bf16[240,1280]{1,0:T(8,128)(2,1)S(1)}, bf16[240,1280]{1,0:T(8,128)(2,1)}, u32[]{:S(2)}, u32[]{:S(2)}) %collective-permute-start.35) | collective-permute-done | bytes 614432 | tf_op jit(solution)/shard_map/ppermute | solution.py:28
  179.4 12.6 %collective-permute-done.33.refs_6_ = bf16[240,1280]{1,0:T(8,128)(2,1)} collective-permute-done((bf16[240,1280]{1,0:T(8,128)(2,1)}, bf16[240,1280]{1,0:T(8,128)(2,1)}, u32[]{:S(2)}, u32[]{:S(2)}) %collective-permute-start.33) | collective-permute-done | bytes 614432 | tf_op jit(solution)/shard_map/ppermute | solution.py:28
  192.0 12.2 %collective-permute-done.37.refs_10_ = bf16[240,1280]{1,0:T(8,128)(2,1)} collective-permute-done((bf16[240,1280]{1,0:T(8,128)(2,1)}, bf16[240,1280]{1,0:T(8,128)(2,1)}, u32[]{:S(2)}, u32[]{:S(2)}) %collective-permute-start.37) | collective-permute-done | bytes 614432 | tf_op jit(solution)/shard_map/ppermute | solution.py:28
  204.2 35.4 %feed_forward.2 = (f32[960,1024]{1,0:T(8,128)}, f32[960,1024]{1,0:T(8,128)}, bf16[240,1280]{1,0:T(8,128)(2,1)}, bf16[240,1280]{1,0:T(8,128)(2,1)}, bf16[240,1280...) custom-call(bf16[960,1024]{1,0:T(8,128)(2,1)} %multiply_convert_fusi, ...), custom_call_target="tpu_custom_call" | custom-call | flops 22649241600 | bytes 31457280 | tf_op jit(solution)/shard_map/feed_forward/pallas_call | solution.py:433
  246.6 35.7 %feed_forward.3 = (bf16[960,1024]{1,0:T(8,128)(2,1)}, f32[960,1024]{1,0:T(8,128)}, bf16[240,1280]{1,0:T(8,128)(2,1)}, bf16[240,1280]{1,0:T(8,128)(2,1)}, bf16[24...) custom-call(bf16[960,1024]{1,0:T(8,128)(2,1)} %multiply_convert_fusi, ...), custom_call_target="tpu_custom_call" | custom-call | flops 22649241600 | bytes 31457280 | tf_op jit(solution)/shard_map/feed_forward/pallas_call | solution.py:433
  282.4 3.8 multiply_reduce_fusion
  286.3 3.8 convert_add_fusion.1
  290.2 3.5 convolution_convert_fusion.3.grad_ref
  293.7 38.4 %attend_backward.1 = (bf16[960,1024]{1,0:T(8,128)(2,1)S(1)}, bf16[320,512]{1,0:T(8,128)(2,1)}, f32[320,1024]{1,0:T(8,128)S(1)}, bf16[320,512]{1,0:T(8,128)(2,1)}, f32[320,1024]{1,0:T(8,128)S(1)}) custom-call(s32[1,1024]{1,0:T(1,128)S(1)} %bitcast.17, f32[32,1024]{1,0:T(8,128)S(1)} %get-tuple-element.139.cos_ref, f32[32,1024]{1,0:T(8,128)S(1)} %get-tuple-element.138.sin_ref, ...), custom_call_target="tpu_custom_call" | custom-call | flops 35232153600 | bytes 16777216 | tf_op jit(solution)/shard_map/attend_backward/pallas_call | solution.py:330
  338.7 2.6 collective-permute-start.91
  355.6 5.5 fusion.9
  361.9 5.0 convolution_convert_fusion.1
  379.8 2.6 collective-permute-start.106
  392.9 8.8 %collective-permute-done.44 = bf16[240,1024]{1,0:T(8,128)(2,1)S(1)} collective-permute-done((bf16[240,1024]{1,0:T(8,128)(2,1)}, bf16[240,1024]{1,0:T(8,128)(2,1)S(1)}, u32[]{:S(2)}, u32[]{:S(2)}) %collective-permute-start.44) | collective-permute-done | bytes 491552 | tf_op jit(solution)/shard_map/ppermute | solution.py:28
  401.8 9.7 %collective-permute-done.45 = bf16[240,1024]{1,0:T(8,128)(2,1)S(1)} collective-permute-done((bf16[240,1024]{1,0:T(8,128)(2,1)}, bf16[240,1024]{1,0:T(8,128)(2,1)S(1)}, u32[]{:S(2)}, u32[]{:S(2)}) %collective-permute-start.45) | collective-permute-done | bytes 491552 | tf_op jit(solution)/shard_map/ppermute | solution.py:28
  431.0 3.8 collective-permute-done.62
  446.3 2.8 collective-permute-done.63
  449.9 3.4 collective-permute-start.64
  460.5 5.5 collective-permute-done.92
  469.3 9.9 %collective-permute-done.82 = bf16[240,1280]{1,0:T(8,128)(2,1)} collective-permute-done((bf16[240,1280]{1,0:T(8,128)(2,1)}, bf16[240,1280]{1,0:T(8,128)(2,1)}, u32[]{:S(2)}, u32[]{:S(2)}) %collective-permute-start.82) | collective-permute-done | bytes 614432 | tf_op jit(solution)/shard_map/ppermute | solution.py:28
  483.8 8.6 %collective-permute-done.72 = bf16[240,1280]{1,0:T(8,128)(2,1)} collective-permute-done((bf16[240,1280]{1,0:T(8,128)(2,1)}, bf16[240,1280]{1,0:T(8,128)(2,1)}, u32[]{:S(2)}, u32[]{:S(2)}) %collective-permute-start.72) | collective-permute-done | bytes 614432 | tf_op jit(solution)/shard_map/ppermute | solution.py:28
  496.5 9.0 %collective-permute-done.89 = bf16[1280,240]{0,1:T(8,128)(2,1)S(1)} collective-permute-done((bf16[1280,240]{0,1:T(8,128)(2,1)}, bf16[1280,240]{0,1:T(8,128)(2,1)S(1)}, u32[]{:S(2)}, u32[]{:S(2)}) %collective-permute-start.89) | collective-permute-done | bytes 614432 | tf_op jit(solution)/shard_map/ppermute | solution.py:28
  508.6 6.2 collective-permute-done.54
  518.0 5.8 collective-permute-done.66
  532.5 8.3 %collective-permute-done.83 = bf16[240,1280]{1,0:T(8,128)(2,1)S(1)} collective-permute-done((bf16[240,1280]{1,0:T(8,128)(2,1)}, bf16[240,1280]{1,0:T(8,128)(2,1)S(1)}, u32[]{:S(2)}, u32[]{:S(2)}) %collective-permute-start.83) | collective-permute-done | bytes 614432 | tf_op jit(solution)/shard_map/ppermute | solution.py:28
  543.7 6.2 collective-permute-done.52
  549.8 4.3 collective-permute-start.94
  554.2 6.6 collective-permute-done.55
  569.3 20.7 %collective-permute-done.56 = bf16[240,800]{1,0:T(8,128)(2,1)S(1)} collective-permute-done((bf16[240,800]{1,0:T(8,128)(2,1)S(1)}, bf16[240,800]{1,0:T(8,128)(2,1)S(1)}, u32[]{:S(2)}, u32[]{:S(2)}) %collective-permute-start.56) | collective-permute-done | bytes 384032 | tf_op jit(solution)/shard_map/ppermute | solution.py:133
  604.9 12.2 %collective-permute-done.58 = bf16[240,800]{1,0:T(8,128)(2,1)S(1)} collective-permute-done((bf16[240,800]{1,0:T(8,128)(2,1)S(1)}, bf16[240,800]{1,0:T(8,128)(2,1)S(1)}, u32[]{:S(2)}, u32[]{:S(2)}) %collective-permute-start.58) | collective-permute-done | bytes 384032 | tf_op jit(solution)/shard_map/ppermute | solution.py:135
  626.9 4.5 collective-permute-done.96
  633.2 14.1 %collective-permute-done.86 = bf16[240,1280]{1,0:T(8,128)(2,1)} collective-permute-done((bf16[240,1280]{1,0:T(8,128)(2,1)}, bf16[240,1280]{1,0:T(8,128)(2,1)}, u32[]{:S(2)}, u32[]{:S(2)}) %collective-permute-start.86) | collective-permute-done | bytes 614432 | tf_op jit(solution)/shard_map/ppermute | solution.py:135
  649.5 10.0 %collective-permute-done.76 = bf16[240,1280]{1,0:T(8,128)(2,1)S(1)} collective-permute-done((bf16[240,1280]{1,0:T(8,128)(2,1)}, bf16[240,1280]{1,0:T(8,128)(2,1)S(1)}, u32[]{:S(2)}, u32[]{:S(2)}) %collective-permute-start.76) | collective-permute-done | bytes 614432 | tf_op jit(solution)/shard_map/ppermute | solution.py:135
  (468 shorter events, 221.7 us)
Async XLA Ops:
  26.1 31.0 %collective-permute-start.20 = (bf16[240,1024]{1,0:T(8,128)(2,1)}, bf16[240,1024]{1,0:T(8,128)(2,1)S(1)}, u32[]{:S(2)}, u32[]{:S(2)}) collective-permute-start(bf16[240,1024]{1,0:T(8,128)(2,1)} %get-tuple-element.126), channel_id=1, source_target_pairs={{0,2},{1,3},{2,0},{3,1},{4,6},{5,7},{6,4},{7,5},{8,10},{9,11},{10,... | collective-permute-start | bytes 1474568 | tf_op jit(solution)/shard_map/ppermute | solution.py:28
  27.9 37.8 %collective-permute-start.21 = (bf16[240,1024]{1,0:T(8,128)(2,1)}, bf16[240,1024]{1,0:T(8,128)(2,1)}, u32[]{:S(2)}, u32[]{:S(2)}) collective-permute-start(bf16[240,1024]{1,0:T(8,128)(2,1)} %get-tuple-element.125), channel_id=1, source_target_pairs={{0,3},{1,2},{2,1},{3,0},{4,7},{5,6},{6,5},{7,4},{8,11},{9,10},{10,... | collective-permute-start | bytes 1474568 | tf_op jit(solution)/shard_map/ppermute | solution.py:28
  36.0 43.2 %collective-permute-start.29 = (bf16[1280,240]{0,1:T(8,128)(2,1)}, bf16[1280,240]{0,1:T(8,128)(2,1)}, u32[]{:S(2)}, u32[]{:S(2)}) collective-permute-start(bf16[1280,240]{0,1:T(8,128)(2,1)} %param.19), channel_id=1, source_target_pairs={{0,2},{1,3},{2,0},{3,1},{4,6},{5,7},{6,4},{7,5},{8,10},{9,11},{10,... | collective-permute-start | bytes 1843208 | tf_op jit(solution)/shard_map/ppermute | solution.py:28
  44.7 34.6 %collective-permute-start.28 = (bf16[1280,240]{0,1:T(8,128)(2,1)}, bf16[1280,240]{0,1:T(8,128)(2,1)}, u32[]{:S(2)}, u32[]{:S(2)}) collective-permute-start(bf16[1280,240]{0,1:T(8,128)(2,1)} %param.19), channel_id=1, source_target_pairs={{0,1},{1,0},{2,3},{3,2},{4,5},{5,4},{6,7},{7,6},{8,9},{9,8},{10,11... | collective-permute-start | bytes 1843208 | tf_op jit(solution)/shard_map/ppermute | solution.py:28
  46.4 33.4 %collective-permute-start.39 = (bf16[1280,240]{0,1:T(8,128)(2,1)}, bf16[1280,240]{0,1:T(8,128)(2,1)}, u32[]{:S(2)}, u32[]{:S(2)}) collective-permute-start(bf16[1280,240]{0,1:T(8,128)(2,1)} %param.19), channel_id=1, source_target_pairs={{0,4},{4,0},{1,5},{5,1},{2,6},{6,2},{3,7},{7,3},{8,12},{12,8},{9,1... | collective-permute-start | bytes 1843208 | tf_op jit(solution)/shard_map/ppermute | solution.py:28
  57.1 22.8 %collective-permute-start.15 = (bf16[240,800]{0,1:T(8,128)(2,1)}, bf16[240,800]{0,1:T(8,128)(2,1)}, u32[]{:S(2)}, u32[]{:S(2)}) collective-permute-start(bf16[240,800]{0,1:T(8,128)(2,1)} %copy-done.67), channel_id=1, source_target_pairs={{0,4},{4,0},{1,5},{5,1},{2,6},{6,2},{3,7},{7,3},{8,12},{12,8},{9,1... | collective-permute-start | bytes 1152008 | tf_op jit(solution)/shard_map/ppermute | solution.py:28
  65.7 23.6 %collective-permute-start.9 = (bf16[480,240]{1,0:T(8,128)(2,1)}, bf16[480,240]{1,0:T(8,128)(2,1)}, u32[]{:S(2)}, u32[]{:S(2)}) collective-permute-start(bf16[480,240]{1,0:T(8,128)(2,1)} %collective-permute-done.8), channel_id=1, source_target_pairs={{0,1},{1,0},{2,3},{3,2},{4,5},{5,4},{6,7},{7,6},{8,9},{9,8},{10,11... | collective-permute-start | bytes 691208 | tf_op jit(solution)/shard_map/ppermute | solution.py:28
  89.3 25.9 %collective-permute-start.30 = (bf16[1280,240]{0,1:T(8,128)(2,1)}, bf16[1280,240]{0,1:T(8,128)(2,1)}, u32[]{:S(2)}, u32[]{:S(2)}) collective-permute-start(bf16[1280,240]{0,1:T(8,128)(2,1)} %collective-permute-done.29), channel_id=1, source_target_pairs={{0,1},{1,0},{2,3},{3,2},{4,5},{5,4},{6,7},{7,6},{8,9},{9,8},{10,11... | collective-permute-start | bytes 1843208 | tf_op jit(solution)/shard_map/ppermute | solution.py:28
  93.3 25.6 %collective-permute-start.41 = (bf16[1280,240]{0,1:T(8,128)(2,1)}, bf16[1280,240]{0,1:T(8,128)(2,1)}, u32[]{:S(2)}, u32[]{:S(2)}) collective-permute-start(bf16[1280,240]{0,1:T(8,128)(2,1)} %collective-permute-done.29), channel_id=1, source_target_pairs={{0,4},{4,0},{1,5},{5,1},{2,6},{6,2},{3,7},{7,3},{8,12},{12,8},{9,1... | collective-permute-start | bytes 1843208 | tf_op jit(solution)/shard_map/ppermute | solution.py:28
  95.0 26.0 %collective-permute-start.40 = (bf16[1280,240]{0,1:T(8,128)(2,1)}, bf16[1280,240]{0,1:T(8,128)(2,1)}, u32[]{:S(2)}, u32[]{:S(2)}) collective-permute-start(bf16[1280,240]{0,1:T(8,128)(2,1)} %collective-permute-done.39), channel_id=1, source_target_pairs={{0,1},{1,0},{2,3},{3,2},{4,5},{5,4},{6,7},{7,6},{8,9},{9,8},{10,11... | collective-permute-start | bytes 1843208 | tf_op jit(solution)/shard_map/ppermute | solution.py:28
  115.2 46.7 %collective-permute-start.23 = (bf16[240,1280]{1,0:T(8,128)(2,1)}, bf16[240,1280]{1,0:T(8,128)(2,1)}, u32[]{:S(2)}, u32[]{:S(2)}) collective-permute-start(bf16[240,1280]{1,0:T(8,128)(2,1)} %refs_3_.1), channel_id=1, source_target_pairs={{0,2},{1,3},{2,0},{3,1},{4,6},{5,7},{6,4},{7,5},{8,10},{9,11},{10,... | collective-permute-start | bytes 1843208 | tf_op jit(solution)/shard_map/ppermute | solution.py:28
  118.9 44.8 %collective-permute-start.22 = (bf16[240,1280]{1,0:T(8,128)(2,1)}, bf16[240,1280]{1,0:T(8,128)(2,1)}, u32[]{:S(2)}, u32[]{:S(2)}) collective-permute-start(bf16[240,1280]{1,0:T(8,128)(2,1)} %refs_3_.1), channel_id=1, source_target_pairs={{0,1},{1,0},{2,3},{3,2},{4,5},{5,4},{6,7},{7,6},{8,9},{9,8},{10,11... | collective-permute-start | bytes 1843208 | tf_op jit(solution)/shard_map/ppermute | solution.py:28
  121.1 42.6 %collective-permute-start.26 = (bf16[240,1280]{1,0:T(8,128)(2,1)}, bf16[240,1280]{1,0:T(8,128)(2,1)}, u32[]{:S(2)}, u32[]{:S(2)}) collective-permute-start(bf16[240,1280]{1,0:T(8,128)(2,1)} %refs_7_.1), channel_id=1, source_target_pairs={{0,2},{1,3},{2,0},{3,1},{4,6},{5,7},{6,4},{7,5},{8,10},{9,11},{10,... | collective-permute-start | bytes 1843208 | tf_op jit(solution)/shard_map/ppermute | solution.py:28
  123.8 40.3 %collective-permute-start.25 = (bf16[240,1280]{1,0:T(8,128)(2,1)}, bf16[240,1280]{1,0:T(8,128)(2,1)S(1)}, u32[]{:S(2)}, u32[]{:S(2)}) collective-permute-start(bf16[240,1280]{1,0:T(8,128)(2,1)} %refs_7_.1), channel_id=1, source_target_pairs={{0,1},{1,0},{2,3},{3,2},{4,5},{5,4},{6,7},{7,6},{8,9},{9,8},{10,11... | collective-permute-start | bytes 1843208 | tf_op jit(solution)/shard_map/ppermute | solution.py:28
  124.0 40.3 %collective-permute-start.31 = (bf16[240,1280]{1,0:T(8,128)(2,1)}, bf16[240,1280]{1,0:T(8,128)(2,1)}, u32[]{:S(2)}, u32[]{:S(2)}) collective-permute-start(bf16[240,1280]{1,0:T(8,128)(2,1)} %refs_3_.1), channel_id=1, source_target_pairs={{0,4},{4,0},{1,5},{5,1},{2,6},{6,2},{3,7},{7,3},{8,12},{12,8},{9,1... | collective-permute-start | bytes 1843208 | tf_op jit(solution)/shard_map/ppermute | solution.py:28
  163.7 28.3 %collective-permute-start.33 = (bf16[240,1280]{1,0:T(8,128)(2,1)}, bf16[240,1280]{1,0:T(8,128)(2,1)}, u32[]{:S(2)}, u32[]{:S(2)}) collective-permute-start(bf16[240,1280]{1,0:T(8,128)(2,1)} %collective-permute-done.23.refs_5_), channel_id=1, source_target_pairs={{0,4},{4,0},{1,5},{5,1},{2,6},{6,2},{3,7},{7,3},{8,12},{12,8},{9,1... | collective-permute-start | bytes 1843208 | tf_op jit(solution)/shard_map/ppermute | solution.py:28
  164.3 39.9 %collective-permute-start.37 = (bf16[240,1280]{1,0:T(8,128)(2,1)}, bf16[240,1280]{1,0:T(8,128)(2,1)}, u32[]{:S(2)}, u32[]{:S(2)}) collective-permute-start(bf16[240,1280]{1,0:T(8,128)(2,1)} %collective-permute-done.26.refs_9_), channel_id=1, source_target_pairs={{0,4},{4,0},{1,5},{5,1},{2,6},{6,2},{3,7},{7,3},{8,12},{12,8},{9,1... | collective-permute-start | bytes 1843208 | tf_op jit(solution)/shard_map/ppermute | solution.py:28
  178.8 67.8 %collective-permute-start.32 = (bf16[240,1280]{1,0:T(8,128)(2,1)}, bf16[240,1280]{1,0:T(8,128)(2,1)}, u32[]{:S(2)}, u32[]{:S(2)}) collective-permute-start(bf16[240,1280]{1,0:T(8,128)(2,1)} %collective-permute-done.31.refs_4_), channel_id=1, source_target_pairs={{0,1},{1,0},{2,3},{3,2},{4,5},{5,4},{6,7},{7,6},{8,9},{9,8},{10,11... | collective-permute-start | bytes 1843208 | tf_op jit(solution)/shard_map/ppermute | solution.py:28
  178.8 67.8 %collective-permute-start.36 = (bf16[240,1280]{1,0:T(8,128)(2,1)}, bf16[240,1280]{1,0:T(8,128)(2,1)}, u32[]{:S(2)}, u32[]{:S(2)}) collective-permute-start(bf16[240,1280]{1,0:T(8,128)(2,1)} %collective-permute-done.35.refs_8_), channel_id=1, source_target_pairs={{0,1},{1,0},{2,3},{3,2},{4,5},{5,4},{6,7},{7,6},{8,9},{9,8},{10,11... | collective-permute-start | bytes 1843208 | tf_op jit(solution)/shard_map/ppermute | solution.py:28
  179.3 64.6 %collective-permute-start.42 = (bf16[1280,240]{0,1:T(8,128)(2,1)}, bf16[1280,240]{0,1:T(8,128)(2,1)}, u32[]{:S(2)}, u32[]{:S(2)}) collective-permute-start(bf16[1280,240]{0,1:T(8,128)(2,1)} %collective-permute-done.41), channel_id=1, source_target_pairs={{0,1},{1,0},{2,3},{3,2},{4,5},{5,4},{6,7},{7,6},{8,9},{9,8},{10,11... | collective-permute-start | bytes 1843208 | tf_op jit(solution)/shard_map/ppermute | solution.py:28
  192.0 54.6 %collective-permute-start.34 = (bf16[240,1280]{1,0:T(8,128)(2,1)}, bf16[240,1280]{1,0:T(8,128)(2,1)}, u32[]{:S(2)}, u32[]{:S(2)}) collective-permute-start(bf16[240,1280]{1,0:T(8,128)(2,1)} %collective-permute-done.33.refs_6_), channel_id=1, source_target_pairs={{0,1},{1,0},{2,3},{3,2},{4,5},{5,4},{6,7},{7,6},{8,9},{9,8},{10,11... | collective-permute-start | bytes 1843208 | tf_op jit(solution)/shard_map/ppermute | solution.py:28
  204.2 42.4 %collective-permute-start.38 = (bf16[240,1280]{1,0:T(8,128)(2,1)}, bf16[240,1280]{1,0:T(8,128)(2,1)}, u32[]{:S(2)}, u32[]{:S(2)}) collective-permute-start(bf16[240,1280]{1,0:T(8,128)(2,1)} %collective-permute-done.37.refs_10_), channel_id=1, source_target_pairs={{0,1},{1,0},{2,3},{3,2},{4,5},{5,4},{6,7},{7,6},{8,9},{9,8},{10,11... | collective-permute-start | bytes 1843208 | tf_op jit(solution)/shard_map/ppermute | solution.py:28
  243.9 102.5 %collective-permute-start.90 = (bf16[1280,240]{0,1:T(8,128)(2,1)}, bf16[1280,240]{0,1:T(8,128)(2,1)}, u32[]{:S(2)}, u32[]{:S(2)}) collective-permute-start(bf16[1280,240]{0,1:T(8,128)(2,1)} %copy.39), channel_id=1, source_target_pairs={{0,1},{1,0},{2,3},{3,2},{4,5},{5,4},{6,7},{7,6},{8,9},{9,8},{10,11... | collective-permute-start | bytes 1843208 | tf_op jit(solution)/shard_map/ppermute | solution.py:28
  246.6 102.4 %collective-permute-start.87 = (bf16[1280,240]{0,1:T(8,128)(2,1)}, bf16[1280,240]{0,1:T(8,128)(2,1)}, u32[]{:S(2)}, u32[]{:S(2)}) collective-permute-start(bf16[1280,240]{0,1:T(8,128)(2,1)} %copy.33), channel_id=1, source_target_pairs={{0,1},{1,0},{2,3},{3,2},{4,5},{5,4},{6,7},{7,6},{8,9},{9,8},{10,11... | collective-permute-start | bytes 1843208 | tf_op jit(solution)/shard_map/ppermute | solution.py:28
  338.7 73.1 %collective-permute-start.91 = (bf16[1280,240]{0,1:T(8,128)(2,1)}, bf16[1280,240]{0,1:T(8,128)(2,1)}, u32[]{:S(2)}, u32[]{:S(2)}) collective-permute-start(bf16[1280,240]{0,1:T(8,128)(2,1)} %copy.41), channel_id=1, source_target_pairs={{0,1},{1,0},{2,3},{3,2},{4,5},{5,4},{6,7},{7,6},{8,9},{9,8},{10,11... | collective-permute-start | bytes 1843208 | tf_op jit(solution)/shard_map/ppermute | solution.py:28
  347.7 39.9 %collective-permute-start.59 = (bf16[960,240]{1,0:T(8,128)(2,1)}, bf16[960,240]{1,0:T(8,128)(2,1)S(1)}, u32[]{:S(2)}, u32[]{:S(2)}) collective-permute-start(bf16[960,240]{1,0:T(8,128)(2,1)} %get-tuple-element.113), channel_id=1, source_target_pairs={{0,1},{1,0},{2,3},{3,2},{4,5},{5,4},{6,7},{7,6},{8,9},{9,8},{10,11... | collective-permute-start | bytes 1382408 | tf_op jit(solution)/shard_map/ppermute | solution.py:28
  349.0 39.0 %collective-permute-start.61 = (bf16[960,240]{1,0:T(8,128)(2,1)}, bf16[960,240]{1,0:T(8,128)(2,1)}, u32[]{:S(2)}, u32[]{:S(2)}) collective-permute-start(bf16[960,240]{1,0:T(8,128)(2,1)} %get-tuple-element.114), channel_id=1, source_target_pairs={{0,1},{1,0},{2,3},{3,2},{4,5},{5,4},{6,7},{7,6},{8,9},{9,8},{10,11... | collective-permute-start | bytes 1382408 | tf_op jit(solution)/shard_map/ppermute | solution.py:28
  385.4 37.0 %collective-permute-start.88 = (bf16[1280,240]{0,1:T(8,128)(2,1)}, bf16[1280,240]{0,1:T(8,128)(2,1)}, u32[]{:S(2)}, u32[]{:S(2)}) collective-permute-start(bf16[1280,240]{0,1:T(8,128)(2,1)} %copy.35), channel_id=1, source_target_pairs={{0,1},{1,0},{2,3},{3,2},{4,5},{5,4},{6,7},{7,6},{8,9},{9,8},{10,11... | collective-permute-start | bytes 1843208 | tf_op jit(solution)/shard_map/ppermute | solution.py:28
  388.3 23.2 %collective-permute-start.45 = (bf16[240,1024]{1,0:T(8,128)(2,1)}, bf16[240,1024]{1,0:T(8,128)(2,1)S(1)}, u32[]{:S(2)}, u32[]{:S(2)}) collective-permute-start(bf16[240,1024]{1,0:T(8,128)(2,1)} %get-tuple-element.119), channel_id=1, source_target_pairs={{0,3},{1,2},{2,1},{3,0},{4,7},{5,6},{6,5},{7,4},{8,11},{9,10},{10,... | collective-permute-start | bytes 1474568 | tf_op jit(solution)/shard_map/ppermute | solution.py:28
  414.9 34.4 %collective-permute-start.51 = (bf16[240,1600]{1,0:T(8,128)(2,1)}, bf16[240,1600]{1,0:T(8,128)(2,1)}, u32[]{:S(2)}, u32[]{:S(2)}) collective-permute-start(bf16[240,1600]{1,0:T(8,128)(2,1)} %get-tuple-element.109), channel_id=1, source_target_pairs={{0,1},{1,0},{2,3},{3,2},{4,5},{5,4},{6,7},{7,6},{8,9},{9,8},{10,11... | collective-permute-start | bytes 2304008 | tf_op jit(solution)/shard_map/ppermute | solution.py:28
  443.2 26.0 %collective-permute-start.80 = (bf16[240,1280]{1,0:T(8,128)(2,1)}, bf16[240,1280]{1,0:T(8,128)(2,1)}, u32[]{:S(2)}, u32[]{:S(2)}) collective-permute-start(bf16[240,1280]{1,0:T(8,128)(2,1)} %get-tuple-element.68), channel_id=1, source_target_pairs={{0,1},{1,0},{2,3},{3,2},{4,5},{5,4},{6,7},{7,6},{8,9},{9,8},{10,11... | collective-permute-start | bytes 1843208 | tf_op jit(solution)/shard_map/ppermute | solution.py:28
  446.3 84.1 %collective-permute-start.77 = (bf16[240,1280]{1,0:T(8,128)(2,1)}, bf16[240,1280]{1,0:T(8,128)(2,1)}, u32[]{:S(2)}, u32[]{:S(2)}) collective-permute-start(bf16[240,1280]{1,0:T(8,128)(2,1)} %get-tuple-element.64), channel_id=1, source_target_pairs={{0,1},{1,0},{2,3},{3,2},{4,5},{5,4},{6,7},{7,6},{8,9},{9,8},{10,11... | collective-permute-start | bytes 1843208 | tf_op jit(solution)/shard_map/ppermute | solution.py:28
  449.1 33.2 %collective-permute-start.70 = (bf16[240,1280]{1,0:T(8,128)(2,1)}, bf16[240,1280]{1,0:T(8,128)(2,1)}, u32[]{:S(2)}, u32[]{:S(2)}) collective-permute-start(bf16[240,1280]{1,0:T(8,128)(2,1)} %get-tuple-element.60), channel_id=1, source_target_pairs={{0,1},{1,0},{2,3},{3,2},{4,5},{5,4},{6,7},{7,6},{8,9},{9,8},{10,11... | collective-permute-start | bytes 1843208 | tf_op jit(solution)/shard_map/ppermute | solution.py:28
  466.0 26.4 %collective-permute-start.72 = (bf16[240,1280]{1,0:T(8,128)(2,1)}, bf16[240,1280]{1,0:T(8,128)(2,1)}, u32[]{:S(2)}, u32[]{:S(2)}) collective-permute-start(bf16[240,1280]{1,0:T(8,128)(2,1)} %add_convert_fusion.25), channel_id=1, source_target_pairs={{0,4},{4,0},{1,5},{5,1},{2,6},{6,2},{3,7},{7,3},{8,12},{12,8},{9,1... | collective-permute-start | bytes 1843208 | tf_op jit(solution)/shard_map/ppermute | solution.py:28
  469.2 93.9 %collective-permute-start.67 = (bf16[240,1280]{1,0:T(8,128)(2,1)}, bf16[240,1280]{1,0:T(8,128)(2,1)}, u32[]{:S(2)}, u32[]{:S(2)}) collective-permute-start(bf16[240,1280]{1,0:T(8,128)(2,1)} %get-tuple-element.56), channel_id=1, source_target_pairs={{0,1},{1,0},{2,3},{3,2},{4,5},{5,4},{6,7},{7,6},{8,9},{9,8},{10,11... | collective-permute-start | bytes 1843208 | tf_op jit(solution)/shard_map/ppermute | solution.py:28
  479.2 26.2 %collective-permute-start.89 = (bf16[1280,240]{0,1:T(8,128)(2,1)}, bf16[1280,240]{0,1:T(8,128)(2,1)S(1)}, u32[]{:S(2)}, u32[]{:S(2)}) collective-permute-start(bf16[1280,240]{0,1:T(8,128)(2,1)} %copy.37), channel_id=1, source_target_pairs={{0,4},{4,0},{1,5},{5,1},{2,6},{6,2},{3,7},{7,3},{8,12},{12,8},{9,1... | collective-permute-start | bytes 1843208 | tf_op jit(solution)/shard_map/ppermute | solution.py:28
  482.3 32.4 %collective-permute-start.54 = (bf16[240,800]{1,0:T(8,128)(2,1)}, bf16[240,800]{1,0:T(8,128)(2,1)}, u32[]{:S(2)}, u32[]{:S(2)}) collective-permute-start(bf16[240,800]{1,0:T(8,128)(2,1)} %constant_dynamic-slice_fusion.2), channel_id=1, source_target_pairs={{0,4},{4,0},{1,5},{5,1},{2,6},{6,2},{3,7},{7,3},{8,12},{12,8},{9,1... | collective-permute-start | bytes 1152008 | tf_op jit(solution)/shard_map/ppermute | solution.py:28
  505.5 25.6 %collective-permute-start.79 = (bf16[240,1280]{1,0:T(8,128)(2,1)}, bf16[240,1280]{1,0:T(8,128)(2,1)}, u32[]{:S(2)}, u32[]{:S(2)}) collective-permute-start(bf16[240,1280]{1,0:T(8,128)(2,1)} %add_convert_fusion.19), channel_id=1, source_target_pairs={{0,4},{4,0},{1,5},{5,1},{2,6},{6,2},{3,7},{7,3},{8,12},{12,8},{9,1... | collective-permute-start | bytes 1843208 | tf_op jit(solution)/shard_map/ppermute | solution.py:28
  525.2 39.3 %collective-permute-start.69 = (bf16[240,1280]{1,0:T(8,128)(2,1)}, bf16[240,1280]{1,0:T(8,128)(2,1)}, u32[]{:S(2)}, u32[]{:S(2)}) collective-permute-start(bf16[240,1280]{1,0:T(8,128)(2,1)} %add_convert_fusion.28), channel_id=1, source_target_pairs={{0,4},{4,0},{1,5},{5,1},{2,6},{6,2},{3,7},{7,3},{8,12},{12,8},{9,1... | collective-permute-start | bytes 1843208 | tf_op jit(solution)/shard_map/ppermute | solution.py:28
  531.0 33.5 %collective-permute-start.73 = (bf16[240,1280]{1,0:T(8,128)(2,1)}, bf16[240,1280]{1,0:T(8,128)(2,1)S(1)}, u32[]{:S(2)}, u32[]{:S(2)}) collective-permute-start(bf16[240,1280]{1,0:T(8,128)(2,1)} %add_convert_fusion.24), channel_id=1, source_target_pairs={{0,2},{1,3},{2,0},{3,1},{4,6},{5,7},{6,4},{7,5},{8,10},{9,11},{10,... | collective-permute-start | bytes 1843208 | tf_op jit(solution)/shard_map/ppermute | solution.py:28
  549.8 42.4 %collective-permute-start.94 = (bf16[1280,240]{0,1:T(8,128)(2,1)S(1)}, bf16[1280,240]{0,1:T(8,128)(2,1)}, u32[]{:S(2)}, u32[]{:S(2)}) collective-permute-start(bf16[1280,240]{0,1:T(8,128)(2,1)S(1)} %copy-done.62), channel_id=1, source_target_pairs={{0,8},{24,16},{1,9},{25,17},{2,10},{26,18},{3,11},{27,19},{4,12},{... | collective-permute-start | bytes 1843208 | tf_op jit(solution)/shard_map/ppermute | solution.py:133
  560.7 34.7 %collective-permute-start.84 = (bf16[240,1280]{1,0:T(8,128)(2,1)S(1)}, bf16[240,1280]{1,0:T(8,128)(2,1)}, u32[]{:S(2)}, u32[]{:S(2)}) collective-permute-start(bf16[240,1280]{1,0:T(8,128)(2,1)S(1)} %add_convert_fusion.14), channel_id=1, source_target_pairs={{0,8},{24,16},{1,9},{25,17},{2,10},{26,18},{3,11},{27,19},{4,12},{... | collective-permute-start | bytes 1843208 | tf_op jit(solution)/shard_map/ppermute | solution.py:133
  563.2 26.8 %collective-permute-start.56 = (bf16[240,800]{1,0:T(8,128)(2,1)S(1)}, bf16[240,800]{1,0:T(8,128)(2,1)S(1)}, u32[]{:S(2)}, u32[]{:S(2)}) collective-permute-start(bf16[240,800]{1,0:T(8,128)(2,1)S(1)} %add_convert_fusion.34), channel_id=1, source_target_pairs={{0,8},{24,16},{1,9},{25,17},{2,10},{26,18},{3,11},{27,19},{4,12},{... | collective-permute-start | bytes 1152008 | tf_op jit(solution)/shard_map/ppermute | solution.py:133
  567.0 35.0 %collective-permute-start.74 = (bf16[240,1280]{1,0:T(8,128)(2,1)}, bf16[240,1280]{1,0:T(8,128)(2,1)}, u32[]{:S(2)}, u32[]{:S(2)}) collective-permute-start(bf16[240,1280]{1,0:T(8,128)(2,1)} %add_convert_fusion.23), channel_id=1, source_target_pairs={{0,8},{24,16},{1,9},{25,17},{2,10},{26,18},{3,11},{27,19},{4,12},{... | collective-permute-start | bytes 1843208 | tf_op jit(solution)/shard_map/ppermute | solution.py:133
  594.8 23.5 %collective-permute-start.95 = (bf16[1280,240]{0,1:T(8,128)(2,1)}, bf16[1280,240]{0,1:T(8,128)(2,1)S(1)}, u32[]{:S(2)}, u32[]{:S(2)}) collective-permute-start(bf16[1280,240]{0,1:T(8,128)(2,1)} %copy.49), channel_id=1, source_target_pairs={{8,16},{16,8},{9,17},{17,9},{10,18},{18,10},{11,19},{19,11},{12,20... | collective-permute-start | bytes 1843208 | tf_op jit(solution)/shard_map/ppermute | solution.py:134
  596.7 23.5 %collective-permute-start.85 = (bf16[240,1280]{1,0:T(8,128)(2,1)S(1)}, bf16[240,1280]{1,0:T(8,128)(2,1)}, u32[]{:S(2)}, u32[]{:S(2)}) collective-permute-start(bf16[240,1280]{1,0:T(8,128)(2,1)S(1)} %add_convert_fusion.13), channel_id=1, source_target_pairs={{8,16},{16,8},{9,17},{17,9},{10,18},{18,10},{11,19},{19,11},{12,20... | collective-permute-start | bytes 1843208 | tf_op jit(solution)/shard_map/ppermute | solution.py:134
  622.3 25.0 %collective-permute-start.86 = (bf16[240,1280]{1,0:T(8,128)(2,1)}, bf16[240,1280]{1,0:T(8,128)(2,1)}, u32[]{:S(2)}, u32[]{:S(2)}) collective-permute-start(bf16[240,1280]{1,0:T(8,128)(2,1)} %add_convert_fusion.12), channel_id=1, source_target_pairs={{8,0},{16,24},{9,1},{17,25},{10,2},{18,26},{11,3},{19,27},{12,4},{... | collective-permute-start | bytes 1843208 | tf_op jit(solution)/shard_map/ppermute | solution.py:135
  625.6 33.9 %collective-permute-start.76 = (bf16[240,1280]{1,0:T(8,128)(2,1)}, bf16[240,1280]{1,0:T(8,128)(2,1)S(1)}, u32[]{:S(2)}, u32[]{:S(2)}) collective-permute-start(bf16[240,1280]{1,0:T(8,128)(2,1)} %add_convert_fusion.21), channel_id=1, source_target_pairs={{8,0},{16,24},{9,1},{17,25},{10,2},{18,26},{11,3},{19,27},{12,4},{... | collective-permute-start | bytes 1843208 | tf_op jit(solution)/shard_map/ppermute | solution.py:135
  (142 other events, 1970.0 us)

commit v2 on v1

v2 whole, which is shorter than its diff:
```python
import functools

import jax
import jax.numpy as jnp
from jax import lax
from jax.experimental import pallas as pl
from jax.experimental.pallas import tpu as pltpu
from jax.sharding import PartitionSpec as P

HEADS = 15
KV_HEADS = 5
GROUP = HEADS // KV_HEADS
HEAD = 64
HALF = HEAD // 2
PRIOR = 512
TILE = 256

EPS = 1e-05
THETA = 100000.0
NEG = -1e30

TINY = pl.CostEstimate(flops=1000, bytes_accessed=1000, transcendentals=0)

BF = jnp.bfloat16
F32 = jnp.float32


def swap(value, axis, by):
    peers = lax.axis_size(axis)
    return lax.ppermute(value, axis, [(i, i ^ by) for i in range(peers)])


def dot(left, right, left_dim, right_dim):
    return lax.dot_general(
        left, right, (((left_dim,), (right_dim,)), ((), ())), preferred_element_type=F32
    )


def add(left, right):
    return (left.astype(F32) + right.astype(F32)).astype(BF)


def frequencies():
    return jnp.power(THETA, -jnp.arange(HALF, dtype=F32) / HALF)


def after(value, *earlier):
    return lax.optimization_barrier((value, earlier))[0]


def ordered(mine, theirs, bit, axis):
    return jnp.where(
        bit == 0,
        jnp.concatenate([mine, theirs], axis=axis),
        jnp.concatenate([theirs, mine], axis=axis),
    )


def tokens_far(shard):
    me = lax.axis_index("gy")
    pair = shard.shape[1] // 2
    other = lax.dynamic_slice_in_dim(shard, (1 - me // 2) * pair, pair, 1)
    return swap(other, "gy", 2)


def tokens_near(shard, far):
    me = lax.axis_index("gy")
    rows = far.shape[1] // 2
    own, mate = (me % 2) * rows, (1 - me % 2) * rows
    base = (me // 2) * 2 * rows
    sent = jnp.concatenate(
        [
            lax.dynamic_slice_in_dim(shard, base + mate, rows, 1),
            lax.dynamic_slice_in_dim(far, mate, rows, 1),
        ],
        axis=0,
    )
    got = swap(sent, "gy", 1)
    return (
        lax.dynamic_slice_in_dim(shard, base + own, rows, 1),
        got,
        lax.dynamic_slice_in_dim(far, own, rows, 1),
    )


def to_features(full):
    me = lax.axis_index("gy")
    block = full.shape[0] // 4
    sent = jnp.concatenate([full[block : 2 * block], full[3 * block :]], axis=0)
    got = swap(sent, "gy", 1)
    near = ordered(full[:block], got[:block], me % 2, 1)
    far = ordered(full[2 * block : 3 * block], got[block:], me % 2, 1)
    return near, swap(far, "gy", 2)


def assemble(near, far):
    return ordered(near, far, lax.axis_index("gy") // 2, 1)


def reorder(vector):
    me = lax.axis_index("gy")
    block = vector.shape[0] // 4
    return jnp.concatenate(
        [lax.dynamic_slice_in_dim(vector, (me ^ by) * block, block, 0) for by in range(4)]
    )


def gather_x(block):
    if lax.axis_size("gx") == 2:
        return [block, swap(block, "gx", 1)]
    whole = lax.all_gather(block, "gx", axis=1, tiled=True)
    half = whole.shape[1] // 2
    return [whole[:, :half], whole[:, half:]]


def split_x(whole):
    half = whole.shape[-1] // 2
    if lax.axis_size("gx") == 2:
        me = lax.axis_index("gx")
        return [
            lax.dynamic_slice_in_dim(whole, me * half, half, whole.ndim - 1),
            lax.dynamic_slice_in_dim(whole, (1 - me) * half, half, whole.ndim - 1),
        ]
    return [whole[..., :half], whole[..., half:]]


def reduce_x(chunks, dim=-1):
    if lax.axis_size("gx") == 2:
        return add(chunks[0], swap(chunks[1], "gx", 1))
    dim = chunks[0].ndim + dim
    return lax.psum_scatter(
        jnp.concatenate(chunks, axis=dim), "gx", scatter_dimension=dim, tiled=True
    )


def sum_z(value):
    peers = lax.axis_size("dp")
    if peers != 4:
        return lax.psum(value.astype(F32), "dp")
    me = lax.axis_index("dp")
    inner = add(value, lax.ppermute(value, "dp", [(0, 1), (3, 2)]))
    total = add(inner, lax.ppermute(inner, "dp", [(1, 2), (2, 1)]))
    outer = lax.ppermute(total, "dp", [(1, 0), (2, 3)])
    return jnp.where((me == 0) | (me == 3), outer, total).astype(F32)


def sum_all(value):
    for axis in ("gy", "gx", "dp"):
        by = 1
        while by < lax.axis_size(axis):
            value = value + swap(value, axis, by)
            by *= 2
    return value


RANGES = ((0, 768), (0, 1024), (512, 1280), (512, 1536))


def fill_bias(starts_ref, bias_ref):
    offset = 0
    for tile, (low, high) in enumerate(RANGES):
        size = high - low
        place = lax.broadcasted_iota(jnp.int32, (size, TILE), 0) + (low - PRIOR)
        query = lax.broadcasted_iota(jnp.int32, (size, TILE), 1) + tile * TILE
        start = starts_ref[:, tile * TILE : (tile + 1) * TILE]
        allowed = (place >= start) & (place <= query)
        bias_ref[offset : offset + size, :] = jnp.where(allowed, 0.0, NEG)
        offset += size


BIAS_ROWS = sum(high - low for low, high in RANGES)


def turned(prior, own, out_ref):
    out_ref[:PRIOR, :] = prior.astype(F32).T.astype(BF)
    out_ref[PRIOR:, :] = own.astype(F32).T.astype(BF)


def forward_kernel(
    starts_ref, q_ref, prior_ref, own_ref, mixed_ref, lse_ref, keys, values, bias
):
    @pl.when(pl.program_id(0) == 0)
    def _():
        fill_bias(starts_ref, bias)

    turned(prior_ref[0, :HEAD, :], own_ref[0, :HEAD, :], keys)
    values[:, :PRIOR] = prior_ref[0, HEAD:, :]
    values[:, PRIOR:] = own_ref[0, HEAD:, :]
    offset = 0
    for tile, (low, high) in enumerate(RANGES):
        size = high - low
        lanes = slice(tile * TILE, (tile + 1) * TILE)
        for head in range(GROUP):
            rows = slice(head * HEAD, (head + 1) * HEAD)
            scores = dot(keys[low:high, :], q_ref[rows, lanes], 1, 0)
            scores = scores + bias[offset : offset + size, :]
            top = jnp.max(scores, axis=0, keepdims=True)
            weights = jnp.exp(scores - top)
            total = jnp.sum(weights, axis=0, keepdims=True)
            out = dot(values[:, low:high], weights.astype(BF), 1, 0)
            mixed_ref[rows, lanes] = (out / total).astype(BF)
            lse_ref[0, head : head + 1, lanes] = top + jnp.log(total)
        offset += size


def attention_forward(starts, queries, prior_kv, own_kv):
    count = queries.shape[1]
    wide = GROUP * HEAD
    prior = pl.BlockSpec((1, 2 * HEAD, PRIOR), lambda g: (g, 0, 0))
    own = pl.BlockSpec((1, 2 * HEAD, count), lambda g: (g, 0, 0))
    return pl.pallas_call(
        forward_kernel,
        grid=(KV_HEADS,),
        in_specs=[
            pl.BlockSpec((1, count), lambda g: (0, 0)),
            pl.BlockSpec((wide, count), lambda g: (g, 0)),
            prior,
            own,
        ],
        out_specs=[
            pl.BlockSpec((wide, count), lambda g: (g, 0)),
            pl.BlockSpec((1, 8, count), lambda g: (g, 0, 0)),
        ],
        out_shape=[
            jax.ShapeDtypeStruct((HEADS * HEAD, count), BF),
            jax.ShapeDtypeStruct((KV_HEADS, 8, count), F32),
        ],
        scratch_shapes=[
            pltpu.VMEM((PRIOR + count, HEAD), BF),
            pltpu.VMEM((HEAD, PRIOR + count), BF),
            pltpu.VMEM((BIAS_ROWS, TILE), F32),
        ],
        compiler_params=pltpu.CompilerParams(vmem_limit_bytes=40 * 2**20),
        cost_estimate=TINY,
        name="attend_forward",
    )(starts, queries, prior_kv, own_kv)


def backward_kernel(
    starts_ref,
    cos_ref,
    sin_ref,
    q_ref,
    prior_ref,
    own_ref,
    mixed_ref,
    lse_ref,
    grad_ref,
    dq_ref,
    dprior_ref,
    down_ref,
    keys,
    turned_keys,
    turned_values,
    dk,
    dv,
    bias,
):
    @pl.when(pl.program_id(0) == 0)
    def _():
        fill_bias(starts_ref, bias)

    turned(prior_ref[0, :HEAD, :], own_ref[0, :HEAD, :], turned_keys)
    turned(prior_ref[0, HEAD:, :], own_ref[0, HEAD:, :], turned_values)
    keys[:, :PRIOR] = prior_ref[0, :HEAD, :]
    keys[:, PRIOR:] = own_ref[0, :HEAD, :]
    dk[...] = jnp.zeros_like(dk)
    dv[...] = jnp.zeros_like(dv)
    offset = 0
    for tile, (low, high) in enumerate(RANGES):
        size = high - low
        lanes = slice(tile * TILE, (tile + 1) * TILE)
        for head in range(GROUP):
            rows = slice(head * HEAD, (head + 1) * HEAD)
            query = q_ref[rows, lanes]
            grad = grad_ref[rows, lanes]
            inner = jnp.sum(
                grad.astype(F32) * mixed_ref[rows, lanes].astype(F32), axis=0, keepdims=True
            )
            lse = lse_ref[0, head : head + 1, lanes]
            scores = dot(turned_keys[low:high, :], query, 1, 0)
            weights = jnp.exp(scores + bias[offset : offset + size, :] - lse)
            prob_grad = dot(turned_values[low:high, :], grad, 1, 0)
            score_grad = (weights * (prob_grad - inner)).astype(BF)
            weights = weights.astype(BF)
            dv[low:high, :] += dot(weights, grad, 1, 1)
            dk[low:high, :] += dot(score_grad, query, 1, 1)
            dq = dot(keys[:, low:high], score_grad, 1, 0) * HEAD ** (-0.5)
            cosine, sine = cos_ref[:, lanes], sin_ref[:, lanes]
            front, back = dq[:HALF], dq[HALF:]
            base = head * HEAD
            dq_ref[base : base + HALF, lanes] = (front * cosine + back * sine).astype(BF)
            dq_ref[base + HALF : base + HEAD, lanes] = (back * cosine - front * sine).astype(BF)
        offset += size
    dprior_ref[0, :HEAD, :] = dk[:PRIOR, :].T.astype(BF)
    dprior_ref[0, HEAD:, :] = dv[:PRIOR, :].T.astype(BF)
    down_ref[0, :HEAD, :] = dk[PRIOR:, :].T
    down_ref[0, HEAD:, :] = dv[PRIOR:, :].T


def attention_backward(
    starts, cosine, sine, queries, prior_kv, own_kv, mixed, lse, grads
):
    count = queries.shape[1]
    wide = GROUP * HEAD
    prior = pl.BlockSpec((1, 2 * HEAD, PRIOR), lambda g: (g, 0, 0))
    own = pl.BlockSpec((1, 2 * HEAD, count), lambda g: (g, 0, 0))
    heads = pl.BlockSpec((wide, count), lambda g: (g, 0))
    table = pl.BlockSpec((HALF, count), lambda g: (0, 0))
    return pl.pallas_call(
        backward_kernel,
        grid=(KV_HEADS,),
        in_specs=[
            pl.BlockSpec((1, count), lambda g: (0, 0)),
            table,
            table,
            heads,
            prior,
            own,
            heads,
            pl.BlockSpec((1, 8, count), lambda g: (g, 0, 0)),
            heads,
        ],
        out_specs=[heads, prior, own],
        out_shape=[
            jax.ShapeDtypeStruct((HEADS * HEAD, count), BF),
            jax.ShapeDtypeStruct((KV_HEADS, 2 * HEAD, PRIOR), BF),
            jax.ShapeDtypeStruct((KV_HEADS, 2 * HEAD, count), F32),
        ],
        scratch_shapes=[
            pltpu.VMEM((HEAD, PRIOR + count), BF),
            pltpu.VMEM((PRIOR + count, HEAD), BF),
            pltpu.VMEM((PRIOR + count, HEAD), BF),
            pltpu.VMEM((PRIOR + count, HEAD), F32),
            pltpu.VMEM((PRIOR + count, HEAD), F32),
            pltpu.VMEM((BIAS_ROWS, TILE), F32),
        ],
        compiler_params=pltpu.CompilerParams(vmem_limit_bytes=44 * 2**20),
        cost_estimate=TINY,
        name="attend_backward",
    )(starts, cosine, sine, queries, prior_kv, own_kv, mixed, lse, grads)


def mlp_kernel(first, *refs):
    normed_ref, up_ref, base_ref = refs[:3]
    refs = refs[3:]
    if not first:
        grad_in_ref, refs = refs[0], refs[1:]
    blocks = refs[0:4]
    out_ref, grad_out_ref, keep_ref, send_ref, total_ref, grad_total_ref = refs[4:]
    step = pl.program_id(0)
    last = pl.num_programs(0) - 1

    @pl.when(step == 0)
    def _():
        total_ref[...] = base_ref[...]
        if first:
            grad_total_ref[...] = jnp.zeros_like(grad_total_ref)
        else:
            grad_total_ref[...] = grad_in_ref[...]

    normed = normed_ref[...]
    upstream = up_ref[...]
    block = normed.shape[0] // 4
    w_gate = jnp.concatenate([ref[:block] for ref in blocks], axis=0)
    w_up = jnp.concatenate([ref[block : 2 * block] for ref in blocks], axis=0)
    w_down = jnp.concatenate([ref[2 * block :] for ref in blocks], axis=0)
    gate = dot(w_gate, normed, 0, 0)
    up = dot(w_up, normed, 0, 0)
    hidden_grad = dot(w_down, upstream, 0, 0)
    sigmoid = 1.0 / (1.0 + jnp.exp(-gate))
    silu = gate * sigmoid
    hidden = (silu * up).astype(BF)
    gate_grad = (hidden_grad * up * (sigmoid * (1.0 + gate * (1.0 - sigmoid)))).astype(BF)
    up_grad = (hidden_grad * silu).astype(BF)
    total_ref[...] += dot(w_down, hidden, 1, 0)
    grad_total_ref[...] += dot(w_gate, gate_grad, 1, 0) + dot(w_up, up_grad, 1, 0)
    for place, (left, right) in enumerate(
        ((normed, gate_grad), (normed, up_grad), (upstream, hidden))
    ):
        made = dot(left, right, 1, 1).astype(BF)
        rows = slice(place * block, (place + 1) * block)
        keep_ref[0, rows, :] = made[:block]
        send_ref[0, rows, :] = made[block : 2 * block]
        keep_ref[1, rows, :] = made[2 * block : 3 * block]
        send_ref[1, rows, :] = made[3 * block :]

    @pl.when(step == last)
    def _():
        out_ref[...] = total_ref[...].astype(out_ref.dtype)
        grad_out_ref[...] = grad_total_ref[...]


def mlp_chunk(normed, upstream, base, grad_in, blocks):
    first = grad_in is None
    width, count = normed.shape
    rows, size = blocks[0].shape
    tile = TILE
    whole = pl.BlockSpec((width, count), lambda i: (0, 0), pipeline_mode=pl.Buffered(1))
    across = pl.BlockSpec((rows, tile), lambda i: (0, i))
    made = pl.BlockSpec((2, rows, tile), lambda i: (0, 0, i))
    operands = [normed, upstream, base] + ([] if first else [grad_in])
    return pl.pallas_call(
        functools.partial(mlp_kernel, first),
        grid=(size // tile,),
        in_specs=[whole] * len(operands) + [across] * 4,
        out_specs=[whole, whole, made, made],
        out_shape=[
            jax.ShapeDtypeStruct((width, count), F32 if first else BF),
            jax.ShapeDtypeStruct((width, count), F32),
            jax.ShapeDtypeStruct((2, rows, size), BF),
            jax.ShapeDtypeStruct((2, rows, size), BF),
        ],
        scratch_shapes=[pltpu.VMEM((width, count), F32), pltpu.VMEM((width, count), F32)],
        compiler_params=pltpu.CompilerParams(vmem_limit_bytes=56 * 2**20),
        cost_estimate=TINY,
        name="feed_forward",
    )(*operands, *blocks)


VMEM = pl.BlockSpec(memory_space=pltpu.VMEM)
SMEM = pl.BlockSpec(memory_space=pltpu.SMEM)
Q_WIDTH = HEADS * HEAD
KV_WIDTH = KV_HEADS * HEAD
QKV_WIDTH = Q_WIDTH + 2 * KV_WIDTH
QKV_PART = QKV_WIDTH // 2
OUT_PART = Q_WIDTH // 2


def place_of(flip_ref, half, size):
    return pl.ds(pl.multiple_of((flip_ref[0] ^ half) * size, 16), size)


def stacked(refs, columns):
    return jnp.concatenate([ref[:, columns] for ref in refs], axis=0)


QKV_COLUMNS = slice(0, QKV_PART)
OUT_COLUMNS = slice(QKV_PART, QKV_PART + OUT_PART)


def norm_scale_of(values):
    return lax.rsqrt(jnp.mean(values * values, axis=0, keepdims=True) + EPS)


def norm_back(values, scale, gain, gradient):
    weighted = gradient * gain
    inner = jnp.mean(weighted * values, axis=0, keepdims=True)
    values_grad = scale * weighted - values * (scale * scale * scale) * inner
    return (values_grad, jnp.sum(gradient * values * scale, axis=1, keepdims=True))


def project_kernel(flip_ref, near_ref, got_ref, far_ref, gain_ref, cos_ref, sin_ref, *refs):
    weights = refs[:8]
    x_ref, normed_ref, q_ref, own_ref, prior_ref, made = refs[8:]
    block = near_ref.shape[0]
    x_ref[:block, :] = near_ref[...]
    x_ref[block : 2 * block, :] = got_ref[:block, :]
    x_ref[2 * block : 3 * block, :] = far_ref[...]
    x_ref[3 * block :, :] = got_ref[block:, :]
    x = x_ref[...].astype(F32)
    normed = (x * norm_scale_of(x) * gain_ref[...]).astype(BF)
    normed_ref[...] = normed
    for half in range(2):
        weight = stacked(weights[4 * half : 4 * half + 4], QKV_COLUMNS)
        made[place_of(flip_ref, half, QKV_PART), :] = dot(weight, normed, 0, 0).astype(BF)
    cosine, sine = cos_ref[...], sin_ref[...]
    count = cosine.shape[1]

    def rotated(base, scale):
        front = made[base : base + HALF, :].astype(F32)
        back = made[base + HALF : base + HEAD, :].astype(F32)
        return (
            ((front * cosine - back * sine) * scale).astype(BF),
            ((back * cosine + front * sine) * scale).astype(BF),
        )

    for head in range(HEADS):
        base = head * HEAD
        front, back = rotated(base, HEAD ** (-0.5))
        q_ref[base : base + HALF, :] = front
        q_ref[base + HALF : base + HEAD, :] = back
    for head in range(KV_HEADS):
        front, back = rotated(Q_WIDTH + head * HEAD, 1.0)
        base = Q_WIDTH + KV_WIDTH + head * HEAD
        value = made[base : base + HEAD, :]
        own_ref[head, :HALF, :] = front
        own_ref[head, HALF:HEAD, :] = back
        own_ref[head, HEAD:, :] = value
        prior_ref[head, :HALF, :] = front[:, count - PRIOR :]
        prior_ref[head, HALF:HEAD, :] = back[:, count - PRIOR :]
        prior_ref[head, HEAD:, :] = value[:, count - PRIOR :]


def call_whole(kernel, name, ins, outs, scratch=()):
    return pl.pallas_call(
        kernel,
        in_specs=[SMEM] + [VMEM] * (len(ins) - 1),
        out_specs=[VMEM] * len(outs),
        out_shape=[jax.ShapeDtypeStruct(shape, kind) for shape, kind in outs],
        scratch_shapes=list(scratch),
        compiler_params=pltpu.CompilerParams(vmem_limit_bytes=56 * 2**20),
        cost_estimate=TINY,
        name=name,
    )(*ins)


def project(flip, pieces, gain, cosine, sine, weights):
    block, count = pieces[0].shape
    width = 4 * block
    return call_whole(
        project_kernel,
        "project",
        (flip, *pieces, gain, cosine, sine, *weights),
        (
            ((width, count), BF),
            ((width, count), BF),
            ((Q_WIDTH, count), BF),
            ((KV_HEADS, 2 * HEAD, count), BF),
            ((KV_HEADS, 2 * HEAD, PRIOR), BF),
        ),
        (pltpu.VMEM((QKV_WIDTH, count), BF),),
    )


def branch_kernel(flip_ref, x_ref, gain_ref, mixed_ref, *refs):
    weights = refs[:8]
    middle_ref, normed_ref = refs[8:]
    middle = x_ref[...].astype(F32)
    for half in range(2):
        weight = stacked(weights[4 * half : 4 * half + 4], OUT_COLUMNS)
        middle = middle + dot(weight, mixed_ref[place_of(flip_ref, half, OUT_PART), :], 1, 0)
    middle_ref[...] = middle
    normed_ref[...] = (middle * norm_scale_of(middle) * gain_ref[...]).astype(BF)


def branch(flip, inputs, gain, mixed, weights):
    shape = inputs.shape
    return call_whole(
        branch_kernel,
        "branch",
        (flip, inputs, gain, mixed, *weights),
        ((shape, F32), (shape, BF)),
    )


def store_blocks(keep_ref, send_ref, half, made):
    block = made.shape[0] // 4
    keep_ref[half, 0] = made[:block]
    send_ref[half, 0] = made[block : 2 * block]
    keep_ref[half, 1] = made[2 * block : 3 * block]
    send_ref[half, 1] = made[3 * block :]


def branch_back_kernel(flip_ref, grad_ref, middle_ref, up_ref, gain_ref, mixed_ref, *refs):
    weights = refs[:8]
    mid_grad_ref, mixed_grad_ref, gain_grad_ref, keep_ref, send_ref = refs[8:]
    middle = middle_ref[...]
    mid_grad, gain_grad = norm_back(
        middle, norm_scale_of(middle), gain_ref[...], grad_ref[...]
    )
    gain_grad_ref[...] = gain_grad
    mid_grad = mid_grad + up_ref[...].astype(F32)
    mid_grad_ref[...] = mid_grad
    branch_grad = mid_grad.astype(BF)
    for half in range(2):
        place = place_of(flip_ref, half, OUT_PART)
        weight = stacked(weights[4 * half : 4 * half + 4], OUT_COLUMNS)
        mixed_grad_ref[place, :] = dot(weight, branch_grad, 0, 0).astype(BF)
        made = dot(branch_grad, mixed_ref[place, :], 1, 1).astype(BF)
        store_blocks(keep_ref, send_ref, half, made)


def branch_back(flip, grad, middle, upstream, gain, mixed, weights):
    width, count = middle.shape
    parts = (2, 2, width // 4, OUT_PART)
    return call_whole(
        branch_back_kernel,
        "branch_back",
        (flip, grad, middle, upstream, gain, mixed, *weights),
        (
            ((width, count), F32),
            ((Q_WIDTH, count), BF),
            ((width, 1), F32),
            (parts, BF),
            (parts, BF),
        ),
    )


def qkv_grad_kernel(
    flip_ref, normed_ref, dq_ref, own_ref, prior_ref, cos_ref, sin_ref, made_ref, keep_ref, send_ref
):
    made_ref[:Q_WIDTH, :] = dq_ref[...]
    count = own_ref.shape[2]
    cosine, sine = cos_ref[...], sin_ref[...]
    for head in range(KV_HEADS):
        sent = prior_ref[head].astype(F32)
        both = jnp.concatenate(
            [own_ref[head, :, : count - PRIOR], own_ref[head, :, count - PRIOR :] + sent], axis=1
        )
        front, back = both[:HALF], both[HALF:HEAD]
        base = Q_WIDTH + head * HEAD
        made_ref[base : base + HALF, :] = (front * cosine + back * sine).astype(BF)
        made_ref[base + HALF : base + HEAD, :] = (back * cosine - front * sine).astype(BF)
        base += KV_WIDTH
        made_ref[base : base + HEAD, :] = both[HEAD:].astype(BF)
    normed = normed_ref[...]
    block = normed.shape[0] // 4
    for half in range(2):
        grads = made_ref[place_of(flip_ref, half, QKV_PART), :]
        for number in range(4):
            rows = normed[number * block : (number + 1) * block]
            target = send_ref if number % 2 else keep_ref
            target[half, number // 2] = dot(grads, rows, 1, 1).astype(BF)


def qkv_grad(flip, normed, dq, own, prior, cosine, sine):
    width, count = normed.shape
    parts = (2, 2, QKV_PART, width // 4)
    return call_whole(
        qkv_grad_kernel,
        "qkv_grad",
        (flip, normed, dq, own, prior, cosine, sine),
        (((QKV_WIDTH, count), BF), (parts, BF), (parts, BF)),
    )


def input_grad_kernel(flip_ref, grads_ref, x_ref, gain_ref, mid_grad_ref, *refs):
    weights = refs[:8]
    out_ref, gain_grad_ref = refs[8:]
    total = jnp.zeros(x_ref.shape, F32)
    for half in range(2):
        weight = stacked(weights[4 * half : 4 * half + 4], QKV_COLUMNS)
        total = total + dot(weight, grads_ref[place_of(flip_ref, half, QKV_PART), :], 1, 0)
    x = x_ref[...].astype(F32)
    grad, gain_grad = norm_back(x, norm_scale_of(x), gain_ref[...], total)
    gain_grad_ref[...] = gain_grad
    out_ref[...] = (grad + mid_grad_ref[...]).astype(BF)


def input_grad(flip, grads, inputs, gain, mid_grad, weights):
    width, count = inputs.shape
    return call_whole(
        input_grad_kernel,
        "input_grad",
        (flip, grads, inputs, gain, mid_grad, *weights),
        (((width, count), BF), ((width, 1), F32)),
    )


def attention_halves(shard, cut):
    if lax.axis_size("gx") == 2:
        return [shard, swap(shard, "gx", 1)]
    peers = lax.axis_size("gx")
    block, width = shard.shape
    whole = lax.all_gather(shard, "gx", axis=1, tiled=True)
    whole = whole.reshape(block, 2, peers // 2, width)
    return [
        jnp.concatenate(
            [
                whole[:, c, :, :cut].reshape(block, peers // 2 * cut),
                whole[:, c, :, cut:].reshape(block, peers // 2 * (width - cut)),
            ],
            axis=1,
        )
        for c in range(2)
    ]


def on_device(
    tokens, doc_start, cotangent, attn_gain, mlp_gain, w_qkv, w_out, w_gate, w_up, w_down
):
    count = doc_start.shape[0]
    block = w_qkv.shape[0]
    pairs_x = lax.axis_size("gx") == 2
    flip = lax.axis_index("gx") if pairs_x else jnp.int32(0)
    flip = jnp.reshape(flip, (1,)).astype(jnp.int32)

    shard = jnp.concatenate([w_qkv, w_out.T], axis=1)
    shard_far = swap(shard, "gy", 2)
    inputs_far = tokens_far(tokens)
    near_halves = attention_halves(shard, w_qkv.shape[1])
    far_halves = attention_halves(shard_far, w_qkv.shape[1])
    weights = []
    for near, far in zip(near_halves, far_halves):
        weights += [near, swap(near, "gy", 1), far, swap(far, "gy", 1)]
    pieces = tokens_near(tokens, inputs_far)

    ff_shard = jnp.concatenate([w_gate, w_up, w_down.T], axis=0)
    ff_shard = after(ff_shard, inputs_far, *near_halves, *far_halves)
    ff_far = swap(ff_shard, "gy", 2)
    ff_near_halves = gather_x(ff_shard)
    ff_mate = swap(ff_shard, "gy", 1)

    attn_gain = reorder(attn_gain)[:, None]
    mlp_gain = reorder(mlp_gain)[:, None]

    first_row = lax.axis_index(("dp", "gx", "gy")) * count
    places = first_row + jnp.arange(count, dtype=jnp.int32)
    angle = frequencies()[:, None] * (places - doc_start).astype(F32)[None, :]
    cosine, sine = jnp.cos(angle), jnp.sin(angle)
    starts = (doc_start - first_row)[None, :]

    inputs, normed_one, queries, own_kv, sent_kv = project(
        flip, pieces, attn_gain, cosine, sine, weights
    )
    cotangent = after(cotangent, sent_kv)
    upstream_far = tokens_far(cotangent)
    peers = lax.axis_size("gy")
    ahead = [(i, i + 1) for i in range(0, peers, 2)]
    behind = [(i + 1, i) for i in range(0, peers, 2)]
    prior_kv = lax.ppermute(sent_kv, "gy", ahead)
    mixed, lse = attention_forward(starts, queries, prior_kv, own_kv)

    ff_far, ff_other, upstream_far = after((ff_far, ff_near_halves[1], upstream_far), mixed)
    ff_far_halves = gather_x(ff_far)
    ff_own = ff_near_halves[0] if pairs_x else after(ff_near_halves[0], mixed)
    ff_blocks = [
        [ff_own, ff_mate if pairs_x else swap(ff_own, "gy", 1)],
        [ff_other, swap(ff_other, "gy", 1)],
    ]
    for blocks, far in zip(ff_blocks, ff_far_halves):
        blocks += [far, swap(far, "gy", 1)]
    near, got, far = tokens_near(cotangent, upstream_far)
    upstream = jnp.concatenate([near, got[:block], far, got[block:]], axis=0)
    middle, normed_two = branch(flip, inputs, mlp_gain, mixed, weights)

    made = mlp_chunk(normed_two, upstream, middle, None, ff_blocks[0])
    later = mlp_chunk(normed_two, upstream, made[0], made[1], ff_blocks[1])
    result, normed_two_grad = later[0], later[1]

    first_half = add(made[2], swap(made[3], "gy", 1))
    second_half = add(later[2], swap(later[3], "gy", 1))
    split = 432
    low = reduce_x([first_half[:, :split], second_half[:, :split]])
    high_parts = [part[0, split:] for part in (first_half, second_half)]
    high_far = [swap(part[1, split:], "gy", 2) for part in (first_half, second_half)]

    mid_grad, mixed_grad, gain_two, out_keep, out_send = branch_back(
        flip, normed_two_grad, middle, upstream, mlp_gain, mixed, weights
    )
    result_near, result_far = to_features(result)
    out_paired = add(out_keep, swap(out_send, "gy", 1))
    mixed_grad = after(mixed_grad, first_half, second_half, out_paired)
    out_far = swap(out_paired[1], "gx", 1) if pairs_x else out_paired[1]

    dq, sent_grad, own_grad = attention_backward(
        starts, cosine, sine, queries, prior_kv, own_kv, mixed, lse, mixed_grad
    )
    prior_grad = lax.ppermute(sent_grad, "gy", behind)
    own_grad = after(own_grad, low, high_far)
    out_far, result_far = after((out_far, result_far), dq)
    out_both = (
        add(out_paired[0], out_far) if pairs_x else reduce_x([out_paired[0], out_far])
    )
    sum_out = sum_z(add(out_both[0], swap(out_both[1], "gy", 2)))
    low = add(low[0], swap(low[1], "gy", 2))
    high = reduce_x([add(mine, theirs) for mine, theirs in zip(high_parts, high_far)])
    ff_sum = jnp.concatenate([sum_z(low), sum_z(high)], axis=0)
    grads, qkv_keep, qkv_send = qkv_grad(
        flip, normed_one, dq, own_grad, prior_grad, cosine, sine
    )
    qkv_mate = swap(qkv_send, "gy", 1)
    grads = after(grads, qkv_mate)
    paired = add(qkv_keep, qkv_mate)
    both = reduce_x([paired[0], paired[1]], -2)
    sum_qkv = sum_z(add(both[0], swap(both[1], "gy", 2)))
    in_grad, gain_one = input_grad(flip, grads, inputs, attn_gain, mid_grad, weights)
    grad_near, grad_far = to_features(in_grad)
    gains = sum_all(jnp.stack([reorder(gain_one[:, 0]), reorder(gain_two[:, 0])]))
    return (
        assemble(result_near, result_far),
        assemble(grad_near, grad_far),
        sum_qkv.T,
        sum_out.T,
        ff_sum[:block],
        ff_sum[block : 2 * block],
        ff_sum[2 * block :].T,
        gains[0],
        gains[1],
    )


def solution(mesh):
    placed = (
        P("gy", ("dp", "gx")),
        P(("dp", "gx", "gy")),
        P("gy", ("dp", "gx")),
        P(),
        P(),
        P("gy", "gx"),
        P("gx", "gy"),
        P("gy", "gx"),
        P("gy", "gx"),
        P("gx", "gy"),
    )
    return jax.shard_map(
        on_device,
        mesh=mesh,
        in_specs=placed,
        out_specs=(
            P("gy", ("dp", "gx")),
            P("gy", ("dp", "gx")),
            P("gy", "gx"),
            P("gx", "gy"),
            P("gy", "gx"),
            P("gy", "gx"),
            P("gx", "gy"),
            P(),
            P(),
        ),
        check_vma=False,
    )
```

time: 671 us -> 507 us (0.76)
  waiting for transfers between devices: 242 us -> 174 us
  Pallas kernels: 147 us -> 199 us
  local copies, waits for them, and re-layouts: 71.3 us -> 25.7 us
  other arithmetic: 76 us -> 36.2 us
  starting transfers between devices: 97.6 us -> 62.5 us
  matrix products: 24.9 us -> 0 us
    pallas_call x0 -> x5, Pallas kernels: none -> 55.4 us  [call_whole(): pl.pallas_call(kernel, in_specs=[SMEM] + [VMEM] * (len(ins) - 1), out_spe...]
    ppermute x88 -> x40, starting transfers between devices: 63.5 us -> 28.3 us  [swap(): return lax.ppermute(value, axis, [(i, i ^ by) for i in range(peers)])]
    ppermute x88 -> x40, waiting for transfers between devices: 171 us -> 141 us  [swap(): return lax.ppermute(value, axis, [(i, i ^ by) for i in range(peers)])]
    ppermute x17 -> x0, local copies, waits for them, and re-layouts: 26.2 us -> none  [the longest x14 24.5 us: swap(): return lax.ppermute(value, axis, [(i, i ^ by) for i in range(peers)])]
    dot_general x6 -> x0, matrix products: 24.9 us -> none  [dot(): lax.dot_general(left, right, (((left_dim,), (right_dim,)), ((), ())), pre...]
    ppermute x5 -> x4, waiting for transfers between devices: 46.6 us -> 24.9 us  [sum_z(): outer = lax.ppermute(total, 'dp', [(1, 0), (2, 3)])]
    convert_element_type x28 -> x20, other arithmetic: 38.4 us -> 20 us  [add(): return (left.astype(F32) + right.astype(F32)).astype(BF)]
    ppermute x5 -> x4, waiting for transfers between devices: 24 us -> 6.49 us  [sum_z(): inner = add(value, lax.ppermute(value, 'dp', [(0, 1), (3, 2)]))]
  transfers between devices with their start and end apart: 107 -> 54, of which waited for: 38 -> 19; matrix products, arithmetic and copies ran while one was open for 25% -> 11% of each run, Pallas kernels for 22% -> 40%
where the time goes in v2:
time: 507 us; the launch traced here: 500 us
  Pallas kernels  199 us (39%)
  waiting for transfers between devices  174 us (34%)
  starting transfers between devices  62.5 us (12%)
  other arithmetic  36.2 us (7%)
  local copies, waits for them, and re-layouts  25.7 us (5%)
    ppermute x40, waiting for transfers between devices, swap(): return lax.ppermute(value, axis, [(i, i ^ by) for i in range(peers)])  141 us
    pallas_call x2, Pallas kernels, mlp_chunk(): pl.pallas_call(functools.partial(mlp_kernel, first), grid=(size // tile,)...  68.9 us
    pallas_call x5, Pallas kernels, call_whole(): pl.pallas_call(kernel, in_specs=[SMEM] + [VMEM] * (len(ins) - 1), out_spe...  55.4 us
    pallas_call x1, Pallas kernels, attention_backward(): pl.pallas_call(backward_kernel, grid=(KV_HEADS,), in_specs=[pl.BlockSpec(...  38.4 us
    pallas_call x1, Pallas kernels, attention_forward(): pl.pallas_call(forward_kernel, grid=(KV_HEADS,), in_specs=[pl.BlockSpec((...  36.5 us
    ppermute x40, starting transfers between devices, swap(): return lax.ppermute(value, axis, [(i, i ^ by) for i in range(peers)])  28.3 us
    ppermute x4, waiting for transfers between devices, sum_z(): outer = lax.ppermute(total, 'dp', [(1, 0), (2, 3)])  24.9 us
    ppermute x4, starting transfers between devices, sum_z(): inner = add(value, lax.ppermute(value, 'dp', [(0, 1), (3, 2)]))  22.5 us
  transfers between devices with their start and end apart: 54, of which 19 were waited for; matrix products, arithmetic and copies ran while one was open for 11% of the time, Pallas kernels for 40%

profile of v2, /device:TPU:0, one launch (start us, length us, event | category | flops | bytes accessed | tf_op | source)
XLA Modules:
  0.0 499.9 jit_solution(10987915092685158977)
XLA Ops:
  0.7 2.3 constant_dynamic-slice_fusion.7
  3.0 3.0 collective-permute-start
  6.5 1.6 collective-permute-start.5
  8.6 2.0 constant_dynamic-slice_fusion.8
  10.6 11.3 %collective-permute-done.5.refs_4_ = bf16[240,1280]{1,0:T(8,128)(2,1)S(1)} collective-permute-done((bf16[240,1280]{1,0:T(8,128)(2,1)S(1)}, bf16[240,1280]{1,0:T(8,128)(2,1)S(1)}, u32[]{:S(2)}, u32[]{:S(2)}) %collective-permute-start.5) | collective-permute-done | bytes 614432 | tf_op jit(solution)/shard_map/ppermute | solution.py:30
  21.9 19.2 %collective-permute-done.3.refs_2_ = bf16[240,1280]{1,0:T(8,128)(2,1)S(1)} collective-permute-done((bf16[240,1280]{1,0:T(8,128)(2,1)S(1)}, bf16[240,1280]{1,0:T(8,128)(2,1)S(1)}, u32[]{:S(2)}, u32[]{:S(2)}) %collective-permute-start.3) | collective-permute-done | bytes 614432 | tf_op jit(solution)/shard_map/ppermute | solution.py:30
  41.1 1.7 collective-permute-start.7
  42.8 2.0 constant_dynamic-slice_fusion.5
  47.9 8.4 %collective-permute-done.7.refs_6_ = bf16[240,1280]{1,0:T(8,128)(2,1)} collective-permute-done((bf16[240,1280]{1,0:T(8,128)(2,1)S(1)}, bf16[240,1280]{1,0:T(8,128)(2,1)}, u32[]{:S(2)}, u32[]{:S(2)}) %collective-permute-start.7) | collective-permute-done | bytes 614432 | tf_op jit(solution)/shard_map/ppermute | solution.py:30
  57.7 1.5 collective-permute-start.10
  62.4 10.5 %project.1 = (bf16[960,1024]{1,0:T(8,128)(2,1)}, bf16[960,1024]{1,0:T(8,128)(2,1)}, bf16[960,1024]{1,0:T(8,128)(2,1)}, bf16[5,128,1024]{2,1,0:T(8,128)(2,1)}, bf16[5,128,512]{2,1,0:T(8,128)(2,1)}) custom-call(s32[1]{0:T(128)} %bitcast.flip_ref, bf16[240,1024]{1,0:T(8,128)(2,1)} %get-tuple-element.128.near_ref, ...), custom_call_target="tpu_custom_call" | custom-call | flops 1000 | bytes 1000 | tf_op jit(solution)/shard_map/project/pallas_call | solution.py:496
  73.6 2.5 collective-permute-start.9
  76.1 1.7 collective-permute-done.9.prior_ref
  79.1 36.5 %attend_forward.1 = (bf16[960,1024]{1,0:T(8,128)(2,1)S(1)}, f32[5,8,1024]{2,1,0:T(8,128)S(1)}) custom-call(s32[1,1024]{1,0:T(1,128)S(1)} %bitcast.65, bf16[960,1024]{1,0:T(8,128)(2,1)S(1)} %copy-done.2, bf16[5,128,512]{2,1,0:T(8,128)(2,1)S(1)} %collective-permute-done.9.prior_ref, bf16[5,128,1024]{2,1,0:T(8,128)(2,1)S(1)} %copy-done.3), custom_call_target="tpu_custom_call" | custom-call | flops 1000 | bytes 1000 | tf_op jit(solution)/shard_map/attend_forward/pallas_call | solution.py:211
  115.6 3.2 collective-permute-done.12
  122.7 35.8 %collective-permute-done.17.refs_6_ = bf16[720,1280]{1,0:T(8,128)(2,1)} collective-permute-done((bf16[720,1280]{1,0:T(8,128)(2,1)}, bf16[720,1280]{1,0:T(8,128)(2,1)}, u32[]{:S(2)}, u32[]{:S(2)}) %collective-permute-start.17) | collective-permute-done | bytes 1843232 | tf_op jit(solution)/shard_map/ppermute | solution.py:30
  159.6 9.5 %branch.1 = (f32[960,1024]{1,0:T(8,128)}, bf16[960,1024]{1,0:T(8,128)(2,1)}) custom-call(s32[1]{0:T(128)} %bitcast.flip_ref, bf16[960,1024]{1,0:T(8,128)(2,1)} %get-tuple-element.49.x_ref, f32[960,1]{1,0:T(8,128)} %copy.25.gain_ref, bf16[960,1024]{1,0:T(8,128)(2,1)} %copy-done, bf16[240,1280]{1,0:T(8,128)(2,1)} %copy-done.8, bf16[240,1280]{1,0:T(8,128)(2,1)} %copy-done.11, ...), custom_call_target="tpu_custom_call" | custom-call | flops 1000 | bytes 1000 | tf_op jit(solution)/shard_map/branch/pallas_call | solution.py:496
  171.8 34.3 %feed_forward.2 = (f32[960,1024]{1,0:T(8,128)}, f32[960,1024]{1,0:T(8,128)}, bf16[2,720,1280]{2,1,0:T(8,128)(2,1)}, bf16[2,720,1280]{2,1,0:T(8,128)(2,1)}) custom-call(bf16[960,1024]{1,0:T(8,128)(2,1)} %get-tuple-element.54.refs_0_, bf16[960,1024]{1,0:T(8,128)(2,1)} %pad_maximum_fusion.refs_1_.up_ref, f32[960,1024]{1,0:T(8,128)} %get-tuple-element.58.refs_2_.middle_ref, ...), custom_call_target="tpu_custom_call" | custom-call | flops 1000 | bytes 1000 | tf_op jit(solution)/shard_map/feed_forward/pallas_call | solution.py:403
  206.6 34.5 %feed_forward.3 = (bf16[960,1024]{1,0:T(8,128)(2,1)}, f32[960,1024]{1,0:T(8,128)}, bf16[2,720,1280]{2,1,0:T(8,128)(2,1)}, bf16[2,720,1280]{2,1,0:T(8,128)(2,1)}) custom-call(bf16[960,1024]{1,0:T(8,128)(2,1)} %get-tuple-element.54.refs_0_, bf16[960,1024]{1,0:T(8,128)(2,1)} %pad_maximum_fusion.refs_1_.up_ref, f32[960,1024]{1,0:T(8,128)} %get-tuple-element.60.refs_2_, ...), custom_call_target="tpu_custom_call" | custom-call | flops 1000 | bytes 1000 | tf_op jit(solution)/shard_map/feed_forward/pallas_call | solution.py:403
  241.3 13.6 %branch_back.1 = (f32[960,1024]{1,0:T(8,128)}, bf16[960,1024]{1,0:T(8,128)(2,1)}, f32[960,1]{1,0:T(8,128)}, bf16[2,2,240,480]{3,2,1,0:T(8,128)(2,1)}, bf16[2,2,240,480]{3,2,1,0:T(8,128)(2,1)}) custom-call(s32[1]{0:T(128)} %bitcast.flip_ref, f32[960,1024]{1,0:T(8,128)} %get-tuple-element.64.grad_ref, f32[960,1024]{1,0:T(8,128)} %get-tuple-element.58.refs_2_.middle_ref, ...), custom_call_target="tpu_custom_call" | custom-call | flops 1000 | bytes 1000 | tf_op jit(solution)/shard_map/branch_back/pallas_call | solution.py:496
  258.6 1.8 add_convert_fusion.6
  265.1 3.1 add_convert_fusion.1
  268.3 3.0 add_convert_fusion
  271.3 1.5 slice.146
  275.6 38.4 %attend_backward.1 = (bf16[960,1024]{1,0:T(8,128)(2,1)S(1)}, bf16[5,128,512]{2,1,0:T(8,128)(2,1)S(1)}, f32[5,128,1024]{2,1,0:T(8,128)}) custom-call(s32[1,1024]{1,0:T(1,128)S(1)} %bitcast.66, f32[32,1024]{1,0:T(8,128)S(1)} %copy-done.6, f32[32,1024]{1,0:T(8,128)S(1)} %copy-done.5, bf16[960,1024]{1,0:T(8,128)(2,1)S(1)} %copy-done.2, ...), custom_call_target="tpu_custom_call" | custom-call | flops 1000 | bytes 1000 | tf_op jit(solution)/shard_map/attend_backward/pallas_call | solution.py:310
  317.7 6.7 %collective-permute-done.37 = bf16[240,480]{1,0:T(8,128)(2,1)S(1)} collective-permute-done((bf16[240,480]{1,0:T(8,128)(2,1)S(1)}, bf16[240,480]{1,0:T(8,128)(2,1)S(1)}, u32[]{:S(2)}, u32[]{:S(2)}) %collective-permute-start.37) | collective-permute-done | bytes 230432 | tf_op jit(solution)/shard_map/ppermute | solution.py:30
  324.5 3.5 collective-permute-start.38
  335.5 3.3 collective-permute-done.26
  338.8 5.6 %collective-permute-done.45 = bf16[288,1280]{1,0:T(8,128)(2,1)S(1)} collective-permute-done((bf16[288,1280]{1,0:T(8,128)(2,1)S(1)}, bf16[288,1280]{1,0:T(8,128)(2,1)S(1)}, u32[]{:S(2)}, u32[]{:S(2)}) %collective-permute-start.45) | collective-permute-done | bytes 737312 | tf_op jit(solution)/shard_map/ppermute | solution.py:30
  344.6 1.9 collective-permute-start.46
  346.5 2.2 add_convert_fusion.2
  351.9 8.9 %qkv_grad.1 = (bf16[1600,1024]{1,0:T(8,128)(2,1)}, bf16[2,2,800,240]{3,2,1,0:T(8,128)(2,1)}, bf16[2,2,800,240]{3,2,1,0:T(8,128)(2,1)}) custom-call(s32[1]{0:T(128)} %bitcast.flip_ref, bf16[960,1024]{1,0:T(8,128)(2,1)} %get-tuple-element.76.normed_ref, bf16[960,1024]{1,0:T(8,128)(2,1)} %copy-done.7, f32[5,128,1024]{2,1,0:T(8,128)} %get-tuple-element.78.own_ref, ...), custom_call_target="tpu_custom_call" | custom-call | flops 1000 | bytes 1000 | tf_op jit(solution)/shard_map/qkv_grad/pallas_call | solution.py:496
  362.6 2.0 maximum_select_fusion
  368.2 5.8 %collective-permute-done.41 = bf16[432,1280]{1,0:T(8,128)(2,1)} collective-permute-done((bf16[432,1280]{1,0:T(8,128)(2,1)}, bf16[432,1280]{1,0:T(8,128)(2,1)}, u32[]{:S(2)}, u32[]{:S(2)}) %collective-permute-start.41) | collective-permute-done | bytes 1105952 | tf_op jit(solution)/shard_map/ppermute | solution.py:30
  375.5 13.2 %collective-permute-start.42 = (bf16[432,1280]{1,0:T(8,128)(2,1)S(1)}, bf16[432,1280]{1,0:T(8,128)(2,1)S(1)}, u32[]{:S(2)}, u32[]{:S(2)}) collective-permute-start(bf16[432,1280]{1,0:T(8,128)(2,1)S(1)} %fusion), channel_id=1, source_target_pairs={{0,8},{24,16},{1,9},{25,17},{2,10},{26,18},{3,11},{27,19},{4,12},{... | collective-permute-start | bytes 3317768 | tf_op jit(solution)/shard_map/ppermute | solution.py:141
  388.7 13.0 %input_grad.1 = (bf16[960,1024]{1,0:T(8,128)(2,1)}, f32[960,1]{1,0:T(8,128)}) custom-call(s32[1]{0:T(128)} %bitcast.flip_ref, bf16[1600,1024]{1,0:T(8,128)(2,1)} %get-tuple-element.82.grads_ref, bf16[960,1024]{1,0:T(8,128)(2,1)} %get-tuple-element.49.x_ref, f32[960,1]{1,0:T(8,128)} %copy.24.gain_ref, f32[960,1024]{1,0:T(8,128)} %get-tuple-element.83.mid_grad_ref, ...), custom_call_target="tpu_custom_call" | custom-call | flops 1000 | bytes 1000 | tf_op jit(solution)/shard_map/input_grad/pallas_call | solution.py:496
  403.1 1.8 add_convert_fusion.3
  406.6 2.1 collective-permute-done.50
  409.5 16.9 %collective-permute-done.51 = f32[2,960]{1,0:T(2,128)S(1)} collective-permute-done((f32[2,960]{1,0:T(2,128)S(1)}, f32[2,960]{1,0:T(2,128)S(1)}, u32[]{:S(2)}, u32[]{:S(2)}) %collective-permute-start.51) | collective-permute-done | bytes 7712 | tf_op jit(solution)/shard_map/ppermute | solution.py:30
  426.6 3.4 collective-permute-done.52
  431.2 3.4 collective-permute-done.53
  437.9 5.5 %collective-permute-done.33 = bf16[800,240]{1,0:T(8,128)(2,1)S(1)} collective-permute-done((bf16[800,240]{1,0:T(8,128)(2,1)S(1)}, bf16[800,240]{1,0:T(8,128)(2,1)S(1)}, u32[]{:S(2)}, u32[]{:S(2)}) %collective-permute-start.33) | collective-permute-done | bytes 384032 | tf_op jit(solution)/shard_map/ppermute | solution.py:30
  443.5 4.0 collective-permute-start.34
  449.4 5.1 %collective-permute-done.34 = bf16[800,240]{1,0:T(8,128)(2,1)S(1)} collective-permute-done((bf16[800,240]{1,0:T(8,128)(2,1)S(1)}, bf16[800,240]{1,0:T(8,128)(2,1)S(1)}, u32[]{:S(2)}, u32[]{:S(2)}) %collective-permute-start.34) | collective-permute-done | bytes 384032 | tf_op jit(solution)/shard_map/ppermute | solution.py:141
  458.6 10.8 %collective-permute-done.31 = bf16[240,2048]{1,0:T(8,128)(2,1)S(1)} collective-permute-done((bf16[240,2048]{1,0:T(8,128)(2,1)S(1)}, bf16[240,2048]{1,0:T(8,128)(2,1)S(1)}, u32[]{:S(2)}, u32[]{:S(2)}) %collective-permute-start.31) | collective-permute-done | bytes 983072 | tf_op jit(solution)/shard_map/ppermute | solution.py:30
  469.5 2.0 maximum_select_fusion.1
  471.5 24.9 %collective-permute-done.36 = bf16[800,240]{1,0:T(8,128)(2,1)S(1)} collective-permute-done((bf16[800,240]{1,0:T(8,128)(2,1)S(1)}, bf16[800,240]{1,0:T(8,128)(2,1)S(1)}, u32[]{:S(2)}, u32[]{:S(2)}) %collective-permute-start.36) | collective-permute-done | bytes 384032 | tf_op jit(solution)/shard_map/ppermute | solution.py:143
  497.5 1.9 pad_maximum_fusion.2
  (210 shorter events, 67.6 us)
Async XLA Ops:
  3.0 39.8 %collective-permute-start = (bf16[240,2048]{1,0:T(8,128)(2,1)}, bf16[240,2048]{1,0:T(8,128)(2,1)}, u32[]{:S(2)}, u32[]{:S(2)}) collective-permute-start(bf16[240,2048]{1,0:T(8,128)(2,1)} %constant_dynamic-slice_fusion.7), channel_id=1, source_target_pairs={{0,2},{1,3},{2,0},{3,1},{4,6},{5,7},{6,4},{7,5},{8,10},{9,11},{10,... | collective-permute-start | bytes 2949128 | tf_op jit(solution)/shard_map/ppermute | solution.py:30
  6.5 15.4 %collective-permute-start.5 = (bf16[240,1280]{1,0:T(8,128)(2,1)S(1)}, bf16[240,1280]{1,0:T(8,128)(2,1)S(1)}, u32[]{:S(2)}, u32[]{:S(2)}) collective-permute-start(bf16[240,1280]{1,0:T(8,128)(2,1)S(1)} %pad_maximum_fusion.7.refs_0_), channel_id=1, source_target_pairs={{0,4},{4,0},{1,5},{5,1},{2,6},{6,2},{3,7},{7,3},{8,12},{12,8},{9,1... | collective-permute-start | bytes 1843208 | tf_op jit(solution)/shard_map/ppermute | solution.py:30
  8.1 33.0 %collective-permute-start.3 = (bf16[240,1280]{1,0:T(8,128)(2,1)S(1)}, bf16[240,1280]{1,0:T(8,128)(2,1)S(1)}, u32[]{:S(2)}, u32[]{:S(2)}) collective-permute-start(bf16[240,1280]{1,0:T(8,128)(2,1)S(1)} %pad_maximum_fusion.7.refs_0_), channel_id=1, source_target_pairs={{0,2},{1,3},{2,0},{3,1},{4,6},{5,7},{6,4},{7,5},{8,10},{9,11},{10,... | collective-permute-start | bytes 1843208 | tf_op jit(solution)/shard_map/ppermute | solution.py:30
  8.6 49.1 %collective-permute-start.2 = (bf16[240,1280]{1,0:T(8,128)(2,1)S(1)}, bf16[240,1280]{1,0:T(8,128)(2,1)S(1)}, u32[]{:S(2)}, u32[]{:S(2)}) collective-permute-start(bf16[240,1280]{1,0:T(8,128)(2,1)S(1)} %pad_maximum_fusion.7.refs_0_), channel_id=1, source_target_pairs={{0,1},{1,0},{2,3},{3,2},{4,5},{5,4},{6,7},{7,6},{8,9},{9,8},{10,11... | collective-permute-start | bytes 1843208 | tf_op jit(solution)/shard_map/ppermute | solution.py:30
  21.9 37.3 %collective-permute-start.6 = (bf16[240,1280]{1,0:T(8,128)(2,1)S(1)}, bf16[240,1280]{1,0:T(8,128)(2,1)S(1)}, u32[]{:S(2)}, u32[]{:S(2)}) collective-permute-start(bf16[240,1280]{1,0:T(8,128)(2,1)S(1)} %collective-permute-done.5.refs_4_), channel_id=1, source_target_pairs={{0,1},{1,0},{2,3},{3,2},{4,5},{5,4},{6,7},{7,6},{8,9},{9,8},{10,11... | collective-permute-start | bytes 1843208 | tf_op jit(solution)/shard_map/ppermute | solution.py:30
  41.1 15.1 %collective-permute-start.7 = (bf16[240,1280]{1,0:T(8,128)(2,1)S(1)}, bf16[240,1280]{1,0:T(8,128)(2,1)}, u32[]{:S(2)}, u32[]{:S(2)}) collective-permute-start(bf16[240,1280]{1,0:T(8,128)(2,1)S(1)} %collective-permute-done.3.refs_2_), channel_id=1, source_target_pairs={{0,4},{4,0},{1,5},{5,1},{2,6},{6,2},{3,7},{7,3},{8,12},{12,8},{9,1... | collective-permute-start | bytes 1843208 | tf_op jit(solution)/shard_map/ppermute | solution.py:30
  45.9 15.7 %collective-permute-start.1 = (bf16[480,1024]{1,0:T(8,128)(2,1)}, bf16[480,1024]{1,0:T(8,128)(2,1)}, u32[]{:S(2)}, u32[]{:S(2)}) collective-permute-start(bf16[480,1024]{1,0:T(8,128)(2,1)} %pad_maximum_fusion.3), channel_id=1, source_target_pairs={{0,1},{1,0},{2,3},{3,2},{4,5},{5,4},{6,7},{7,6},{8,9},{9,8},{10,11... | collective-permute-start | bytes 2949128 | tf_op jit(solution)/shard_map/ppermute | solution.py:30
  47.4 14.2 %collective-permute-start.4 = (bf16[240,1280]{1,0:T(8,128)(2,1)S(1)}, bf16[240,1280]{1,0:T(8,128)(2,1)}, u32[]{:S(2)}, u32[]{:S(2)}) collective-permute-start(bf16[240,1280]{1,0:T(8,128)(2,1)S(1)} %collective-permute-done.3.refs_2_), channel_id=1, source_target_pairs={{0,1},{1,0},{2,3},{3,2},{4,5},{5,4},{6,7},{7,6},{8,9},{9,8},{10,11... | collective-permute-start | bytes 1843208 | tf_op jit(solution)/shard_map/ppermute | solution.py:30
  56.2 62.5 %collective-permute-start.11 = (bf16[720,1280]{1,0:T(8,128)(2,1)}, bf16[720,1280]{1,0:T(8,128)(2,1)}, u32[]{:S(2)}, u32[]{:S(2)}) collective-permute-start(bf16[720,1280]{1,0:T(8,128)(2,1)} %pad_maximum_fusion.1.refs_3_), channel_id=1, source_target_pairs={{0,4},{4,0},{1,5},{5,1},{2,6},{6,2},{3,7},{7,3},{8,12},{12,8},{9,1... | collective-permute-start | bytes 5529608 | tf_op jit(solution)/shard_map/ppermute | solution.py:30
  57.7 61.1 %collective-permute-start.10 = (bf16[720,1280]{1,0:T(8,128)(2,1)}, bf16[720,1280]{1,0:T(8,128)(2,1)}, u32[]{:S(2)}, u32[]{:S(2)}) collective-permute-start(bf16[720,1280]{1,0:T(8,128)(2,1)} %pad_maximum_fusion.1.refs_3_), channel_id=1, source_target_pairs={{0,2},{1,3},{2,0},{3,1},{4,6},{5,7},{6,4},{7,5},{8,10},{9,11},{10,... | collective-permute-start | bytes 5529608 | tf_op jit(solution)/shard_map/ppermute | solution.py:30
  73.0 45.8 %collective-permute-start.12 = (bf16[240,2048]{1,0:T(8,128)(2,1)S(1)}, bf16[240,2048]{1,0:T(8,128)(2,1)S(1)}, u32[]{:S(2)}, u32[]{:S(2)}) collective-permute-start(bf16[240,2048]{1,0:T(8,128)(2,1)S(1)} %constant_dynamic-slice_fusion.2), channel_id=1, source_target_pairs={{0,2},{1,3},{2,0},{3,1},{4,6},{5,7},{6,4},{7,5},{8,10},{9,11},{10,... | collective-permute-start | bytes 2949128 | tf_op jit(solution)/shard_map/ppermute | solution.py:30
  73.6 4.2 collective-permute-start.9
  118.8 39.7 %collective-permute-start.17 = (bf16[720,1280]{1,0:T(8,128)(2,1)}, bf16[720,1280]{1,0:T(8,128)(2,1)}, u32[]{:S(2)}, u32[]{:S(2)}) collective-permute-start(bf16[720,1280]{1,0:T(8,128)(2,1)} %collective-permute-done.10.refs_5_), channel_id=1, source_target_pairs={{0,4},{4,0},{1,5},{5,1},{2,6},{6,2},{3,7},{7,3},{8,12},{12,8},{9,1... | collective-permute-start | bytes 5529608 | tf_op jit(solution)/shard_map/ppermute | solution.py:30
  119.7 52.0 %collective-permute-start.14 = (bf16[720,1280]{1,0:T(8,128)(2,1)}, bf16[720,1280]{1,0:T(8,128)(2,1)}, u32[]{:S(2)}, u32[]{:S(2)}) collective-permute-start(bf16[720,1280]{1,0:T(8,128)(2,1)} %pad_maximum_fusion.1.refs_3_), channel_id=1, source_target_pairs={{0,1},{1,0},{2,3},{3,2},{4,5},{5,4},{6,7},{7,6},{8,9},{9,8},{10,11... | collective-permute-start | bytes 5529608 | tf_op jit(solution)/shard_map/ppermute | solution.py:30
  119.7 52.0 %collective-permute-start.15 = (bf16[720,1280]{1,0:T(8,128)(2,1)}, bf16[720,1280]{1,0:T(8,128)(2,1)}, u32[]{:S(2)}, u32[]{:S(2)}) collective-permute-start(bf16[720,1280]{1,0:T(8,128)(2,1)} %collective-permute-done.10.refs_5_), channel_id=1, source_target_pairs={{0,1},{1,0},{2,3},{3,2},{4,5},{5,4},{6,7},{7,6},{8,9},{9,8},{10,11... | collective-permute-start | bytes 5529608 | tf_op jit(solution)/shard_map/ppermute | solution.py:30
  122.2 46.8 %collective-permute-start.13 = (bf16[480,1024]{1,0:T(8,128)(2,1)}, bf16[480,1024]{1,0:T(8,128)(2,1)}, u32[]{:S(2)}, u32[]{:S(2)}) collective-permute-start(bf16[480,1024]{1,0:T(8,128)(2,1)} %pad_maximum_fusion.4), channel_id=1, source_target_pairs={{0,1},{1,0},{2,3},{3,2},{4,5},{5,4},{6,7},{7,6},{8,9},{9,8},{10,11... | collective-permute-start | bytes 2949128 | tf_op jit(solution)/shard_map/ppermute | solution.py:30
  122.2 84.4 %collective-permute-start.16 = (bf16[720,1280]{1,0:T(8,128)(2,1)}, bf16[720,1280]{1,0:T(8,128)(2,1)}, u32[]{:S(2)}, u32[]{:S(2)}) collective-permute-start(bf16[720,1280]{1,0:T(8,128)(2,1)} %collective-permute-done.11.refs_4_), channel_id=1, source_target_pairs={{0,1},{1,0},{2,3},{3,2},{4,5},{5,4},{6,7},{7,6},{8,9},{9,8},{10,11... | collective-permute-start | bytes 5529608 | tf_op jit(solution)/shard_map/ppermute | solution.py:30
  158.5 48.1 %collective-permute-start.18 = (bf16[720,1280]{1,0:T(8,128)(2,1)}, bf16[720,1280]{1,0:T(8,128)(2,1)}, u32[]{:S(2)}, u32[]{:S(2)}) collective-permute-start(bf16[720,1280]{1,0:T(8,128)(2,1)} %collective-permute-done.17.refs_6_), channel_id=1, source_target_pairs={{0,1},{1,0},{2,3},{3,2},{4,5},{5,4},{6,7},{7,6},{8,9},{9,8},{10,11... | collective-permute-start | bytes 5529608 | tf_op jit(solution)/shard_map/ppermute | solution.py:30
  206.1 59.0 %collective-permute-start.23 = (bf16[2,720,1280]{2,1,0:T(8,128)(2,1)}, bf16[2,720,1280]{2,1,0:T(8,128)(2,1)}, u32[]{:S(2)}, u32[]{:S(2)}) collective-permute-start(bf16[2,720,1280]{2,1,0:T(8,128)(2,1)} %get-tuple-element.70), channel_id=1, source_target_pairs={{0,1},{1,0},{2,3},{3,2},{4,5},{5,4},{6,7},{7,6},{8,9},{9,8},{10,11... | collective-permute-start | bytes 11059208 | tf_op jit(solution)/shard_map/ppermute | solution.py:30
  241.1 27.1 %collective-permute-start.24 = (bf16[2,720,1280]{2,1,0:T(8,128)(2,1)}, bf16[2,720,1280]{2,1,0:T(8,128)(2,1)}, u32[]{:S(2)}, u32[]{:S(2)}) collective-permute-start(bf16[2,720,1280]{2,1,0:T(8,128)(2,1)} %get-tuple-element.72), channel_id=1, source_target_pairs={{0,1},{1,0},{2,3},{3,2},{4,5},{5,4},{6,7},{7,6},{8,9},{9,8},{10,11... | collective-permute-start | bytes 11059208 | tf_op jit(solution)/shard_map/ppermute | solution.py:30
  254.8 3.8 collective-permute-start.20
  257.3 4.8 collective-permute-start.19
  261.2 52.7 %collective-permute-start.21 = (bf16[2,240,480]{2,1,0:T(8,128)(2,1)}, bf16[2,240,480]{2,1,0:T(8,128)(2,1)}, u32[]{:S(2)}, u32[]{:S(2)}) collective-permute-start(bf16[2,240,480]{2,1,0:T(8,128)(2,1)} %slice_bitcast_fusion.10), channel_id=1, source_target_pairs={{0,4},{4,0},{1,5},{5,1},{2,6},{6,2},{3,7},{7,3},{8,12},{12,8},{9,1... | collective-permute-start | bytes 1382408 | tf_op jit(solution)/shard_map/ppermute | solution.py:30
  263.9 50.0 %collective-permute-start.22 = (bf16[240,2048]{1,0:T(8,128)(2,1)S(1)}, bf16[240,2048]{1,0:T(8,128)(2,1)S(1)}, u32[]{:S(2)}, u32[]{:S(2)}) collective-permute-start(bf16[240,2048]{1,0:T(8,128)(2,1)S(1)} %maximum_select_fusion.3), channel_id=1, source_target_pairs={{0,2},{1,3},{2,0},{3,1},{4,6},{5,7},{6,4},{7,5},{8,10},{9,11},{10,... | collective-permute-start | bytes 2949128 | tf_op jit(solution)/shard_map/ppermute | solution.py:30
  273.7 54.3 %collective-permute-start.27 = (bf16[288,1280]{1,0:T(8,128)(2,1)}, bf16[288,1280]{1,0:T(8,128)(2,1)}, u32[]{:S(2)}, u32[]{:S(2)}) collective-permute-start(bf16[288,1280]{1,0:T(8,128)(2,1)} %slice_bitcast_fusion.7), channel_id=1, source_target_pairs={{0,2},{1,3},{2,0},{3,1},{4,6},{5,7},{6,4},{7,5},{8,10},{9,11},{10,... | collective-permute-start | bytes 2211848 | tf_op jit(solution)/shard_map/ppermute | solution.py:30
  274.6 71.9 %collective-permute-start.25 = (bf16[2,432,1280]{2,1,0:T(8,128)(2,1)}, bf16[2,432,1280]{2,1,0:T(8,128)(2,1)}, u32[]{:S(2)}, u32[]{:S(2)}) collective-permute-start(bf16[2,432,1280]{2,1,0:T(8,128)(2,1)} %slice.146), channel_id=1, source_target_pairs={{0,4},{4,0},{1,5},{5,1},{2,6},{6,2},{3,7},{7,3},{8,12},{12,8},{9,1... | collective-permute-start | bytes 6635528 | tf_op jit(solution)/shard_map/ppermute | solution.py:30
  315.5 9.0 %collective-permute-start.37 = (bf16[240,480]{1,0:T(8,128)(2,1)S(1)}, bf16[240,480]{1,0:T(8,128)(2,1)S(1)}, u32[]{:S(2)}, u32[]{:S(2)}) collective-permute-start(bf16[240,480]{1,0:T(8,128)(2,1)S(1)} %slice_bitcast_fusion.13), channel_id=1, source_target_pairs={{0,2},{1,3},{2,0},{3,1},{4,6},{5,7},{6,4},{7,5},{8,10},{9,11},{10,... | collective-permute-start | bytes 691208 | tf_op jit(solution)/shard_map/ppermute | solution.py:30
  317.0 21.8 %collective-permute-start.26 = (bf16[288,1280]{1,0:T(8,128)(2,1)S(1)}, bf16[288,1280]{1,0:T(8,128)(2,1)S(1)}, u32[]{:S(2)}, u32[]{:S(2)}) collective-permute-start(bf16[288,1280]{1,0:T(8,128)(2,1)S(1)} %slice_bitcast_fusion.8), channel_id=1, source_target_pairs={{0,2},{1,3},{2,0},{3,1},{4,6},{5,7},{6,4},{7,5},{8,10},{9,11},{10,... | collective-permute-start | bytes 2211848 | tf_op jit(solution)/shard_map/ppermute | solution.py:30
  324.5 7.2 %collective-permute-start.38 = (bf16[240,480]{1,0:T(8,128)(2,1)S(1)}, bf16[240,480]{1,0:T(8,128)(2,1)S(1)}, u32[]{:S(2)}, u32[]{:S(2)}) collective-permute-start(bf16[240,480]{1,0:T(8,128)(2,1)S(1)} %fusion.6), channel_id=1, source_target_pairs={{0,8},{24,16},{1,9},{25,17},{2,10},{26,18},{3,11},{27,19},{4,12},{... | collective-permute-start | bytes 691208 | tf_op jit(solution)/shard_map/ppermute | solution.py:141
  329.3 15.0 %collective-permute-start.45 = (bf16[288,1280]{1,0:T(8,128)(2,1)S(1)}, bf16[288,1280]{1,0:T(8,128)(2,1)S(1)}, u32[]{:S(2)}, u32[]{:S(2)}) collective-permute-start(bf16[288,1280]{1,0:T(8,128)(2,1)S(1)} %fusion.2), channel_id=1, source_target_pairs={{0,4},{4,0},{1,5},{5,1},{2,6},{6,2},{3,7},{7,3},{8,12},{12,8},{9,1... | collective-permute-start | bytes 2211848 | tf_op jit(solution)/shard_map/ppermute | solution.py:30
  332.8 18.3 %collective-permute-start.28 = (bf16[5,128,512]{2,1,0:T(8,128)(2,1)S(1)}, bf16[5,128,512]{2,1,0:T(8,128)(2,1)S(1)}, u32[]{:S(2)}, u32[]{:S(2)}) collective-permute-start(bf16[5,128,512]{2,1,0:T(8,128)(2,1)S(1)} %get-tuple-element.79), channel_id=1, source_target_pairs={{1,0},{3,2},{5,4},{7,6},{9,8},{11,10},{13,12},{15,14},{17,16},{19,... | collective-permute-start | bytes 1966088 | tf_op jit(solution)/shard_map/ppermute | solution.py:751
  334.2 30.4 %collective-permute-start.40 = (bf16[240,480]{1,0:T(8,128)(2,1)S(1)}, bf16[240,480]{1,0:T(8,128)(2,1)S(1)}, u32[]{:S(2)}, u32[]{:S(2)}) collective-permute-start(bf16[240,480]{1,0:T(8,128)(2,1)S(1)} %add_convert_fusion.12), channel_id=1, source_target_pairs={{8,0},{16,24},{9,1},{17,25},{10,2},{18,26},{11,3},{19,27},{12,4},{... | collective-permute-start | bytes 691208 | tf_op jit(solution)/shard_map/ppermute | solution.py:143
  344.6 16.3 %collective-permute-start.46 = (bf16[288,1280]{1,0:T(8,128)(2,1)S(1)}, bf16[288,1280]{1,0:T(8,128)(2,1)S(1)}, u32[]{:S(2)}, u32[]{:S(2)}) collective-permute-start(bf16[288,1280]{1,0:T(8,128)(2,1)S(1)} %add_convert_fusion.9), channel_id=1, source_target_pairs={{0,8},{24,16},{1,9},{25,17},{2,10},{26,18},{3,11},{27,19},{4,12},{... | collective-permute-start | bytes 2211848 | tf_op jit(solution)/shard_map/ppermute | solution.py:141
  349.7 24.3 %collective-permute-start.41 = (bf16[432,1280]{1,0:T(8,128)(2,1)}, bf16[432,1280]{1,0:T(8,128)(2,1)}, u32[]{:S(2)}, u32[]{:S(2)}) collective-permute-start(bf16[432,1280]{1,0:T(8,128)(2,1)} %slice_bitcast_fusion.1), channel_id=1, source_target_pairs={{0,2},{1,3},{2,0},{3,1},{4,6},{5,7},{6,4},{7,5},{8,10},{9,11},{10,... | collective-permute-start | bytes 3317768 | tf_op jit(solution)/shard_map/ppermute | solution.py:30
  360.9 27.8 %collective-permute-start.29 = (bf16[2,2,800,240]{3,2,1,0:T(8,128)(2,1)}, bf16[2,2,800,240]{3,2,1,0:T(8,128)(2,1)}, u32[]{:S(2)}, u32[]{:S(2)}) collective-permute-start(bf16[2,2,800,240]{3,2,1,0:T(8,128)(2,1)} %get-tuple-element.81), channel_id=1, source_target_pairs={{0,1},{1,0},{2,3},{3,2},{4,5},{5,4},{6,7},{7,6},{8,9},{9,8},{10,11... | collective-permute-start | bytes 4608008 | tf_op jit(solution)/shard_map/ppermute | solution.py:30
  361.9 3.7 collective-permute-start.47
  366.9 42.4 %collective-permute-start.48 = (bf16[288,1280]{1,0:T(8,128)(2,1)S(1)}, bf16[288,1280]{1,0:T(8,128)(2,1)S(1)}, u32[]{:S(2)}, u32[]{:S(2)}) collective-permute-start(bf16[288,1280]{1,0:T(8,128)(2,1)S(1)} %add_convert_fusion.7), channel_id=1, source_target_pairs={{8,0},{16,24},{9,1},{17,25},{10,2},{18,26},{11,3},{19,27},{12,4},{... | collective-permute-start | bytes 2211848 | tf_op jit(solution)/shard_map/ppermute | solution.py:143
  375.5 60.8 %collective-permute-start.42 = (bf16[432,1280]{1,0:T(8,128)(2,1)S(1)}, bf16[432,1280]{1,0:T(8,128)(2,1)S(1)}, u32[]{:S(2)}, u32[]{:S(2)}) collective-permute-start(bf16[432,1280]{1,0:T(8,128)(2,1)S(1)} %fusion), channel_id=1, source_target_pairs={{0,8},{24,16},{1,9},{25,17},{2,10},{26,18},{3,11},{27,19},{4,12},{... | collective-permute-start | bytes 3317768 | tf_op jit(solution)/shard_map/ppermute | solution.py:141
  405.8 28.8 %collective-permute-start.32 = (bf16[2,800,240]{2,1,0:T(8,128)(2,1)S(1)}, bf16[2,800,240]{2,1,0:T(8,128)(2,1)S(1)}, u32[]{:S(2)}, u32[]{:S(2)}) collective-permute-start(bf16[2,800,240]{2,1,0:T(8,128)(2,1)S(1)} %slice_bitcast_fusion.3), channel_id=1, source_target_pairs={{0,4},{4,0},{1,5},{5,1},{2,6},{6,2},{3,7},{7,3},{8,12},{12,8},{9,1... | collective-permute-start | bytes 2304008 | tf_op jit(solution)/shard_map/ppermute | solution.py:30
  408.7 17.6 %collective-permute-start.51 = (f32[2,960]{1,0:T(2,128)S(1)}, f32[2,960]{1,0:T(2,128)S(1)}, u32[]{:S(2)}, u32[]{:S(2)}) collective-permute-start(f32[2,960]{1,0:T(2,128)S(1)} %fusion.16), channel_id=1, source_target_pairs={{0,4},{4,0},{1,5},{5,1},{2,6},{6,2},{3,7},{7,3},{8,12},{12,8},{9,1... | collective-permute-start | bytes 23048 | tf_op jit(solution)/shard_map/ppermute | solution.py:30
  430.0 4.5 collective-permute-start.53
  431.1 16.4 %collective-permute-start.30 = (bf16[480,1024]{1,0:T(8,128)(2,1)S(1)}, bf16[480,1024]{1,0:T(8,128)(2,1)S(1)}, u32[]{:S(2)}, u32[]{:S(2)}) collective-permute-start(bf16[480,1024]{1,0:T(8,128)(2,1)S(1)} %pad_maximum_fusion.6), channel_id=1, source_target_pairs={{0,1},{1,0},{2,3},{3,2},{4,5},{5,4},{6,7},{7,6},{8,9},{9,8},{10,11... | collective-permute-start | bytes 2949128 | tf_op jit(solution)/shard_map/ppermute | solution.py:30
  434.8 8.6 %collective-permute-start.33 = (bf16[800,240]{1,0:T(8,128)(2,1)S(1)}, bf16[800,240]{1,0:T(8,128)(2,1)S(1)}, u32[]{:S(2)}, u32[]{:S(2)}) collective-permute-start(bf16[800,240]{1,0:T(8,128)(2,1)S(1)} %slice_bitcast_fusion.11), channel_id=1, source_target_pairs={{0,2},{1,3},{2,0},{3,1},{4,6},{5,7},{6,4},{7,5},{8,10},{9,11},{10,... | collective-permute-start | bytes 1152008 | tf_op jit(solution)/shard_map/ppermute | solution.py:30
  436.6 18.6 %collective-permute-start.43 = (bf16[432,1280]{1,0:T(8,128)(2,1)S(1)}, bf16[432,1280]{1,0:T(8,128)(2,1)S(1)}, u32[]{:S(2)}, u32[]{:S(2)}) collective-permute-start(bf16[432,1280]{1,0:T(8,128)(2,1)S(1)} %add_convert_fusion.5), channel_id=1, source_target_pairs={{8,16},{16,8},{9,17},{17,9},{10,18},{18,10},{11,19},{19,11},{12,20... | collective-permute-start | bytes 3317768 | tf_op jit(solution)/shard_map/ppermute | solution.py:142
  443.5 10.9 %collective-permute-start.34 = (bf16[800,240]{1,0:T(8,128)(2,1)S(1)}, bf16[800,240]{1,0:T(8,128)(2,1)S(1)}, u32[]{:S(2)}, u32[]{:S(2)}) collective-permute-start(bf16[800,240]{1,0:T(8,128)(2,1)S(1)} %fusion.5), channel_id=1, source_target_pairs={{0,8},{24,16},{1,9},{25,17},{2,10},{26,18},{3,11},{27,19},{4,12},{... | collective-permute-start | bytes 1152008 | tf_op jit(solution)/shard_map/ppermute | solution.py:141
  447.9 21.5 %collective-permute-start.31 = (bf16[240,2048]{1,0:T(8,128)(2,1)S(1)}, bf16[240,2048]{1,0:T(8,128)(2,1)S(1)}, u32[]{:S(2)}, u32[]{:S(2)}) collective-permute-start(bf16[240,2048]{1,0:T(8,128)(2,1)S(1)} %maximum_select_fusion.5), channel_id=1, source_target_pairs={{0,2},{1,3},{2,0},{3,1},{4,6},{5,7},{6,4},{7,5},{8,10},{9,11},{10,... | collective-permute-start | bytes 2949128 | tf_op jit(solution)/shard_map/ppermute | solution.py:30
  455.5 41.8 %collective-permute-start.44 = (bf16[432,1280]{1,0:T(8,128)(2,1)S(1)}, bf16[432,1280]{1,0:T(8,128)(2,1)S(1)}, u32[]{:S(2)}, u32[]{:S(2)}) collective-permute-start(bf16[432,1280]{1,0:T(8,128)(2,1)S(1)} %add_convert_fusion.4), channel_id=1, source_target_pairs={{8,0},{16,24},{9,1},{17,25},{10,2},{18,26},{11,3},{19,27},{12,4},{... | collective-permute-start | bytes 3317768 | tf_op jit(solution)/shard_map/ppermute | solution.py:143
  457.3 39.0 %collective-permute-start.36 = (bf16[800,240]{1,0:T(8,128)(2,1)S(1)}, bf16[800,240]{1,0:T(8,128)(2,1)S(1)}, u32[]{:S(2)}, u32[]{:S(2)}) collective-permute-start(bf16[800,240]{1,0:T(8,128)(2,1)S(1)} %add_convert_fusion.10), channel_id=1, source_target_pairs={{8,0},{16,24},{9,1},{17,25},{10,2},{18,26},{11,3},{19,27},{12,4},{... | collective-permute-start | bytes 1152008 | tf_op jit(solution)/shard_map/ppermute | solution.py:143
  (37 other events, 406.6 us)

commit v3 on v2

--- a/solution.py
+++ b/solution.py
@@ -36,8 +36,54 @@
     )
 
 
+def add_kernel(left_ref, right_ref, out_ref):
+    out_ref[...] = (left_ref[...].astype(F32) + right_ref[...].astype(F32)).astype(BF)
+
+
 def add(left, right):
-    return (left.astype(F32) + right.astype(F32)).astype(BF)
+    width = left.shape[-1]
+    rows = left.size // width
+    if left.shape[-2] % 16:
+        return (left.astype(F32) + right.astype(F32)).astype(BF)
+    step = max(
+        size for size in range(16, 513, 16) if rows % size == 0
+    )
+    spec = pl.BlockSpec((step, width), lambda i: (i, 0))
+    return pl.pallas_call(
+        add_kernel,
+        grid=(rows // step,),
+        in_specs=[spec, spec],
+        out_specs=spec,
+        out_shape=jax.ShapeDtypeStruct((rows, width), BF),
+        compiler_params=pltpu.CompilerParams(vmem_limit_bytes=24 * 2**20),
+        cost_estimate=TINY,
+        name="add",
+    )(left.reshape(rows, width), right.reshape(rows, width)).reshape(left.shape)
+
+
+def add_pair_kernel(left_ref, right_ref, first_ref, second_ref):
+    for k, out_ref in enumerate((first_ref, second_ref)):
+        out_ref[...] = (left_ref[k].astype(F32) + right_ref[k].astype(F32)).astype(BF)
+
+
+def add_pair(left, right):
+    shape = left.shape[1:]
+    width = shape[-1]
+    rows = left.size // (2 * width)
+    step = max(size for size in range(16, 257, 16) if rows % size == 0)
+    spec = pl.BlockSpec((2, step, width), lambda i: (0, i, 0))
+    out = pl.BlockSpec((step, width), lambda i: (i, 0))
+    first, second = pl.pallas_call(
+        add_pair_kernel,
+        grid=(rows // step,),
+        in_specs=[spec, spec],
+        out_specs=[out, out],
+        out_shape=[jax.ShapeDtypeStruct((rows, width), BF)] * 2,
+        compiler_params=pltpu.CompilerParams(vmem_limit_bytes=24 * 2**20),
+        cost_estimate=TINY,
+        name="add_pair",
+    )(left.reshape(2, rows, width), right.reshape(2, rows, width))
+    return first.reshape(shape), second.reshape(shape)
 
 
 def frequencies():
@@ -90,7 +136,7 @@
     got = swap(sent, "gy", 1)
     near = ordered(full[:block], got[:block], me % 2, 1)
     far = ordered(full[2 * block : 3 * block], got[block:], me % 2, 1)
-    return near, swap(far, "gy", 2)
+    return near, far
 
 
 def assemble(near, far):
@@ -142,6 +188,20 @@
     total = add(inner, lax.ppermute(inner, "dp", [(1, 2), (2, 1)]))
     outer = lax.ppermute(total, "dp", [(1, 0), (2, 3)])
     return jnp.where((me == 0) | (me == 3), outer, total).astype(F32)
+
+
+def bit_z(by):
+    return (lax.axis_index("dp") // by) % 2
+
+
+def kept_z(value, by):
+    half = value.shape[0] // 2
+    return lax.dynamic_slice_in_dim(value, bit_z(by) * half, half, 0)
+
+
+def halve_z(value, by):
+    half = value.shape[0] // 2
+    return swap(lax.dynamic_slice_in_dim(value, (1 - bit_z(by)) * half, half, 0), "dp", by)
 
 
 def sum_all(value):
@@ -679,12 +739,14 @@
 
     shard = jnp.concatenate([w_qkv, w_out.T], axis=1)
     shard_far = swap(shard, "gy", 2)
-    inputs_far = tokens_far(tokens)
+    mate = swap(shard, "gy", 1)
+    inputs_far = tokens_far(after(tokens, mate))
     near_halves = attention_halves(shard, w_qkv.shape[1])
     far_halves = attention_halves(shard_far, w_qkv.shape[1])
     weights = []
-    for near, far in zip(near_halves, far_halves):
-        weights += [near, swap(near, "gy", 1), far, swap(far, "gy", 1)]
+    for half, (near, far) in enumerate(zip(near_halves, far_halves)):
+        near_mate = mate if pairs_x and half == 0 else swap(near, "gy", 1)
+        weights += [near, near_mate, far, swap(far, "gy", 1)]
     pieces = tokens_near(tokens, inputs_far)
 
     ff_shard = jnp.concatenate([w_gate, w_up, w_down.T], axis=0)
@@ -720,55 +782,126 @@
         [ff_own, ff_mate if pairs_x else swap(ff_own, "gy", 1)],
         [ff_other, swap(ff_other, "gy", 1)],
     ]
-    for blocks, far in zip(ff_blocks, ff_far_halves):
-        blocks += [far, swap(far, "gy", 1)]
+    ff_blocks[0] += [ff_far_halves[0], swap(ff_far_halves[0], "gy", 1)]
     near, got, far = tokens_near(cotangent, upstream_far)
     upstream = jnp.concatenate([near, got[:block], far, got[block:]], axis=0)
     middle, normed_two = branch(flip, inputs, mlp_gain, mixed, weights)
 
     made = mlp_chunk(normed_two, upstream, middle, None, ff_blocks[0])
+    ff_far_other = after(ff_far_halves[1], made[0])
+    ff_blocks[1] += [ff_far_other, swap(ff_far_other, "gy", 1)]
     later = mlp_chunk(normed_two, upstream, made[0], made[1], ff_blocks[1])
     result, normed_two_grad = later[0], later[1]
 
+    mid_grad, mixed_grad, gain_two, out_keep, out_send = branch_back(
+        flip, normed_two_grad, middle, upstream, mlp_gain, mixed, weights
+    )
+    result_near, result_sent = to_features(result)
+
     first_half = add(made[2], swap(made[3], "gy", 1))
     second_half = add(later[2], swap(later[3], "gy", 1))
-    split = 432
-    low = reduce_x([first_half[:, :split], second_half[:, :split]])
-    high_parts = [part[0, split:] for part in (first_half, second_half)]
-    high_far = [swap(part[1, split:], "gy", 2) for part in (first_half, second_half)]
-
-    mid_grad, mixed_grad, gain_two, out_keep, out_send = branch_back(
-        flip, normed_two_grad, middle, upstream, mlp_gain, mixed, weights
-    )
-    result_near, result_far = to_features(result)
     out_paired = add(out_keep, swap(out_send, "gy", 1))
-    mixed_grad = after(mixed_grad, first_half, second_half, out_paired)
-    out_far = swap(out_paired[1], "gx", 1) if pairs_x else out_paired[1]
-
-    dq, sent_grad, own_grad = attention_backward(
-        starts, cosine, sine, queries, prior_kv, own_kv, mixed, lse, mixed_grad
-    )
-    prior_grad = lax.ppermute(sent_grad, "gy", behind)
-    own_grad = after(own_grad, low, high_far)
-    out_far, result_far = after((out_far, result_far), dq)
-    out_both = (
-        add(out_paired[0], out_far) if pairs_x else reduce_x([out_paired[0], out_far])
-    )
-    sum_out = sum_z(add(out_both[0], swap(out_both[1], "gy", 2)))
-    low = add(low[0], swap(low[1], "gy", 2))
-    high = reduce_x([add(mine, theirs) for mine, theirs in zip(high_parts, high_far)])
-    ff_sum = jnp.concatenate([sum_z(low), sum_z(high)], axis=0)
-    grads, qkv_keep, qkv_send = qkv_grad(
-        flip, normed_one, dq, own_grad, prior_grad, cosine, sine
-    )
-    qkv_mate = swap(qkv_send, "gy", 1)
-    grads = after(grads, qkv_mate)
-    paired = add(qkv_keep, qkv_mate)
-    both = reduce_x([paired[0], paired[1]], -2)
-    sum_qkv = sum_z(add(both[0], swap(both[1], "gy", 2)))
-    in_grad, gain_one = input_grad(flip, grads, inputs, attn_gain, mid_grad, weights)
-    grad_near, grad_far = to_features(in_grad)
-    gains = sum_all(jnp.stack([reorder(gain_one[:, 0]), reorder(gain_two[:, 0])]))
+
+    def attend_back(mixed_grad, *earlier):
+        dq, sent_grad, own_grad = attention_backward(
+            starts, cosine, sine, queries, prior_kv, own_kv, mixed, lse, mixed_grad
+        )
+        prior_grad = lax.ppermute(sent_grad, "gy", behind)
+        own_grad = after(own_grad, *earlier)
+        grads, keep, send = qkv_grad(
+            flip, normed_one, dq, own_grad, prior_grad, cosine, sine
+        )
+        return grads, keep, swap(send, "gy", 1)
+
+    if not pairs_x:
+        grads, qkv_keep, qkv_mate = attend_back(mixed_grad)
+        ff_both = reduce_x([first_half, second_half])
+        ff_sum = sum_z(add(ff_both[0], swap(ff_both[1], "gy", 2)))
+        both = reduce_x([out_paired[0], out_paired[1]])
+        sum_out = sum_z(add(both[0], swap(both[1], "gy", 2)))
+        paired = add(qkv_keep, qkv_mate)
+        both = reduce_x([paired[0], paired[1]], -2)
+        sum_qkv = sum_z(add(both[0], swap(both[1], "gy", 2)))
+        in_grad, gain_one = input_grad(flip, grads, inputs, attn_gain, mid_grad, weights)
+        grad_near, grad_sent = to_features(in_grad)
+        grad_far = swap(grad_sent, "gy", 2)
+        result_far = swap(result_sent, "gy", 2)
+        gains = sum_all(jnp.stack([reorder(gain_one[:, 0]), reorder(gain_two[:, 0])]))
+    else:
+        split = 400
+        wide = first_half.shape[2]
+        out_rows = out_paired[0].size // (2 * wide)
+        filler = jnp.zeros((2, -(split + out_rows) % 64, wide), BF)
+        low_own, low_other = (
+            jnp.concatenate([half[:, :split], out_half.reshape(2, -1, wide), filler], axis=1)
+            for half, out_half in ((first_half, out_paired[0]), (second_half, out_paired[1]))
+        )
+        high_near, high_far = (
+            jnp.stack([first_half[k, split:], second_half[k, split:]]) for k in (0, 1)
+        )
+        mixed_grad = after(
+            mixed_grad, low_own, low_other, high_near, high_far, result_near, result_sent
+        )
+        low_got = swap(low_other, "gx", 1)
+        high_got = swap(high_far, "gy", 2)
+        grads, qkv_keep, qkv_mate = attend_back(mixed_grad, high_got)
+
+        high_near, high_sent = add_pair(high_near, after(high_got, grads))
+        qkv_near, qkv_sent = add_pair(qkv_keep, after(qkv_mate, high_near))
+        qkv_got = swap(qkv_sent, "gx", 1)
+        high_got = swap(after(high_sent, qkv_near), "gx", 1)
+        in_grad, gain_one = input_grad(
+            flip, after(grads, qkv_near), inputs, attn_gain, mid_grad, weights
+        )
+        low_near, low_sent = add_pair(low_own, after(low_got, in_grad))
+        low_got = swap(low_sent, "gy", 2)
+        qkv_near, qkv_sent = add_pair(qkv_near, after(qkv_got, low_near))
+        qkv_got = swap(qkv_sent, "gy", 2)
+        grad_near, grad_sent = to_features(after(in_grad, low_near))
+        grad_far = swap(grad_sent, "gy", 2)
+        result_far = swap(after(result_sent, grads), "gy", 2)
+        gains = jnp.stack([reorder(gain_one[:, 0]), reorder(gain_two[:, 0])])
+        gains_got = swap(gains, "gy", 1)
+        high = add(high_near, after(high_got, grad_near))
+        high_got = halve_z(high, 1)
+        gains = gains + after(gains_got, high)
+        gains_got = swap(gains, "gx", 1)
+        low = add(low_near, after(low_got, gains))
+        result_far = after(result_far, low)
+        low_got = halve_z(low, 1)
+        qkv_sum = add(qkv_near, after(qkv_got, low))
+        qkv_got = lax.ppermute(qkv_sum, "dp", [(0, 1), (3, 2)])
+        gains = gains + after(gains_got, qkv_sum)
+        gains_got = swap(gains, "gy", 2)
+        high = add(kept_z(high, 1), after(high_got, gains))
+        high_got = halve_z(high, 2)
+        qkv_sum = add(qkv_sum, after(qkv_got, high))
+        qkv_got = lax.ppermute(qkv_sum, "dp", [(1, 2), (2, 1)])
+        low = add(kept_z(low, 1), after(low_got, qkv_sum))
+        low_got = halve_z(low, 2)
+        gains = gains + after(gains_got, low)
+        gains_got = swap(gains, "dp", 1)
+        high = add(kept_z(high, 2), after(high_got, gains))
+        high_got = swap(high, "dp", 2)
+        qkv_sum = add(qkv_sum, after(qkv_got, high))
+        qkv_got = lax.ppermute(qkv_sum, "dp", [(1, 0), (2, 3)])
+        low = add(kept_z(low, 2), after(low_got, qkv_sum))
+        low_got = swap(low, "dp", 2)
+        gains = gains + after(gains_got, low)
+        gains_got = swap(gains, "dp", 2)
+        high = ordered(high, after(high_got, gains), bit_z(2), 0)
+        high_got = swap(high, "dp", 1)
+        low = ordered(low, after(low_got, high), bit_z(2), 0)
+        low_got = swap(low, "dp", 1)
+        at = lax.axis_index("dp")
+        sum_qkv = jnp.where(
+            (at == 0) | (at == 3), after(qkv_got, low), qkv_sum
+        ).astype(F32)
+        gains = gains + after(gains_got, sum_qkv)
+        high = ordered(high, after(high_got, gains), bit_z(1), 0).astype(F32)
+        low = ordered(low, after(low_got, high), bit_z(1), 0).astype(F32)
+        ff_sum = jnp.concatenate([low[:split], high], axis=0)
+        sum_out = low[split : split + out_rows].reshape(block, -1)
     return (
         assemble(result_near, result_far),
         assemble(grad_near, grad_far),

time: 507 us -> 514 us (1.014)
  Pallas kernels: 199 us -> 217 us
  local copies, waits for them, and re-layouts: 25.7 us -> 43.6 us
  starting transfers between devices: 62.5 us -> 49.8 us
  other arithmetic: 36.2 us -> 26.8 us
  waiting for transfers between devices: 174 us -> 168 us
    ppermute x13 -> x4, starting transfers between devices: 31.7 us -> 6.73 us  [the longest x1 3.48 us: on_device(): qkv_got = lax.ppermute(qkv_sum, 'dp', [(0, 1), (3, 2)])]
    convert_element_type x22 -> x3, other arithmetic: 20.2 us -> 1.54 us  [the longest x1 0.95 us: on_device(): sum_qkv = jnp.where((at == 0) | (at == 3), after(qkv_got, low), qkv_sum)....]
    pallas_call x0 -> x16, Pallas kernels: none -> 18.4 us  [the longest x4 9.51 us: add_pair(): pl.pallas_call(add_pair_kernel, grid=(rows // step,), in_specs=[spec, spe...]
    ppermute x13 -> x4, waiting for transfers between devices: 31.4 us -> 16.1 us  [the longest x1 7.88 us: on_device(): qkv_got = lax.ppermute(qkv_sum, 'dp', [(0, 1), (3, 2)])]
    ppermute x40 -> x45, starting transfers between devices: 28.3 us -> 40.9 us  [swap(): return lax.ppermute(value, axis, [(i, i ^ by) for i in range(peers)])]
    unnamed x65 -> x86, local copies, waits for them, and re-layouts: 4.47 us -> 16.2 us
    ppermute x40 -> x45, waiting for transfers between devices: 141 us -> 151 us  [swap(): return lax.ppermute(value, axis, [(i, i ^ by) for i in range(peers)])]
    another operation x0 -> x2, local copies, waits for them, and re-layouts: none -> 5.61 us  [on_device(): out_half.reshape(2, -1, wide)]
  transfers between devices with their start and end apart: 54 -> 50, of which waited for: 19 -> 20; matrix products, arithmetic and copies ran while one was open for 11% -> 9% of each run, Pallas kernels for 40% -> 42%
where the time goes in v3:
time: 514 us; the launch traced here: 507 us
  Pallas kernels  217 us (42%)
  waiting for transfers between devices  168 us (33%)
  starting transfers between devices  49.8 us (10%)
  local copies, waits for them, and re-layouts  43.6 us (8%)
  other arithmetic  26.8 us (5%)
    ppermute x45, waiting for transfers between devices, swap(): return lax.ppermute(value, axis, [(i, i ^ by) for i in range(peers)])  151 us
    pallas_call x2, Pallas kernels, mlp_chunk(): pl.pallas_call(functools.partial(mlp_kernel, first), grid=(size // tile,)...  68.7 us
    pallas_call x5, Pallas kernels, call_whole(): pl.pallas_call(kernel, in_specs=[SMEM] + [VMEM] * (len(ins) - 1), out_spe...  55.4 us
    ppermute x45, starting transfers between devices, swap(): return lax.ppermute(value, axis, [(i, i ^ by) for i in range(peers)])  40.9 us
    pallas_call x1, Pallas kernels, attention_backward(): pl.pallas_call(backward_kernel, grid=(KV_HEADS,), in_specs=[pl.BlockSpec(...  38.2 us
    pallas_call x1, Pallas kernels, attention_forward(): pl.pallas_call(forward_kernel, grid=(KV_HEADS,), in_specs=[pl.BlockSpec((...  36.5 us
    unnamed x86, local copies, waits for them, and re-layouts  16.2 us
  transfers between devices with their start and end apart: 50, of which 20 were waited for; matrix products, arithmetic and copies ran while one was open for 9% of the time, Pallas kernels for 42%

profile of v3, /device:TPU:0, one launch (start us, length us, event | category | flops | bytes accessed | tf_op | source)
XLA Modules:
  0.0 507.1 jit_solution(13043595755423745837)
XLA Ops:
  2.0 1.8 copy.22
  5.4 1.7 collective-permute-done.refs_1_
  8.2 2.9 collective-permute-start.1
  11.1 2.0 collective-permute-start.5
  13.0 2.0 constant_dynamic-slice_fusion.16
  15.1 31.3 %collective-permute-done.3.refs_2_ = bf16[240,1280]{1,0:T(8,128)(2,1)S(1)} collective-permute-done((bf16[240,1280]{1,0:T(8,128)(2,1)S(1)}, bf16[240,1280]{1,0:T(8,128)(2,1)S(1)}, u32[]{:S(2)}, u32[]{:S(2)}) %collective-permute-start.3) | collective-permute-done | bytes 614432 | tf_op jit(solution)/shard_map/ppermute | solution.py:30
  46.5 1.7 collective-permute-start.7
  48.2 2.0 constant_dynamic-slice_fusion.13
  53.2 8.6 %collective-permute-done.7.refs_6_ = bf16[240,1280]{1,0:T(8,128)(2,1)S(1)} collective-permute-done((bf16[240,1280]{1,0:T(8,128)(2,1)S(1)}, bf16[240,1280]{1,0:T(8,128)(2,1)S(1)}, u32[]{:S(2)}, u32[]{:S(2)}) %collective-permute-start.7) | collective-permute-done | bytes 614432 | tf_op jit(solution)/shard_map/ppermute | solution.py:30
  68.0 10.5 %project.1 = (bf16[960,1024]{1,0:T(8,128)(2,1)}, bf16[960,1024]{1,0:T(8,128)(2,1)}, bf16[960,1024]{1,0:T(8,128)(2,1)}, bf16[5,128,1024]{2,1,0:T(8,128)(2,1)}, bf16[5,128,512]{2,1,0:T(8,128)(2,1)}) custom-call(s32[1]{0:T(128)} %bitcast.flip_ref, bf16[240,1024]{1,0:T(8,128)(2,1)} %get-tuple-element.182.near_ref, ...), custom_call_target="tpu_custom_call" | custom-call | flops 1000 | bytes 1000 | tf_op jit(solution)/shard_map/project/pallas_call | solution.py:556
  79.2 2.2 collective-permute-start.9
  84.2 36.5 %attend_forward.1 = (bf16[960,1024]{1,0:T(8,128)(2,1)S(1)}, f32[5,8,1024]{2,1,0:T(8,128)S(1)}) custom-call(s32[1,1024]{1,0:T(1,128)S(1)} %bitcast.36, bf16[960,1024]{1,0:T(8,128)(2,1)S(1)} %copy-done.2, bf16[5,128,512]{2,1,0:T(8,128)(2,1)S(1)} %collective-permute-done.9.prior_ref, bf16[5,128,1024]{2,1,0:T(8,128)(2,1)S(1)} %copy-done.3), custom_call_target="tpu_custom_call" | custom-call | flops 1000 | bytes 1000 | tf_op jit(solution)/shard_map/attend_forward/pallas_call | solution.py:271
  120.7 5.0 collective-permute-done.12
  130.4 9.4 %branch.1 = (f32[960,1024]{1,0:T(8,128)}, bf16[960,1024]{1,0:T(8,128)(2,1)}) custom-call(s32[1]{0:T(128)} %bitcast.flip_ref, bf16[960,1024]{1,0:T(8,128)(2,1)} %get-tuple-element.85.x_ref, f32[960,1]{1,0:T(8,128)} %copy.25.gain_ref, bf16[960,1024]{1,0:T(8,128)(2,1)} %copy-done, bf16[240,1280]{1,0:T(8,128)(2,1)} %copy-done.17, bf16[240,1280]{1,0:T(8,128)(2,1)} %copy-done.18, ...), custom_call_target="tpu_custom_call" | custom-call | flops 1000 | bytes 1000 | tf_op jit(solution)/shard_map/branch/pallas_call | solution.py:556
  142.7 34.2 %feed_forward.2 = (f32[960,1024]{1,0:T(8,128)}, f32[960,1024]{1,0:T(8,128)}, bf16[2,720,1280]{2,1,0:T(8,128)(2,1)}, bf16[2,720,1280]{2,1,0:T(8,128)(2,1)}) custom-call(bf16[960,1024]{1,0:T(8,128)(2,1)} %get-tuple-element.90.refs_0_, bf16[960,1024]{1,0:T(8,128)(2,1)} %pad_maximum_fusion.refs_1_.up_ref, f32[960,1024]{1,0:T(8,128)} %get-tuple-element.94.refs_2_.middle_ref, ...), custom_call_target="tpu_custom_call" | custom-call | flops 1000 | bytes 1000 | tf_op jit(solution)/shard_map/feed_forward/pallas_call | solution.py:463
  177.5 3.8 collective-permute-done.18.refs_7_
  182.6 34.6 %feed_forward.3 = (bf16[960,1024]{1,0:T(8,128)(2,1)}, f32[960,1024]{1,0:T(8,128)}, bf16[2,720,1280]{2,1,0:T(8,128)(2,1)}, bf16[2,720,1280]{2,1,0:T(8,128)(2,1)}) custom-call(bf16[960,1024]{1,0:T(8,128)(2,1)} %get-tuple-element.90.refs_0_, bf16[960,1024]{1,0:T(8,128)(2,1)} %pad_maximum_fusion.refs_1_.up_ref, f32[960,1024]{1,0:T(8,128)} %get-tuple-element.96.refs_2_, ...), custom_call_target="tpu_custom_call" | custom-call | flops 1000 | bytes 1000 | tf_op jit(solution)/shard_map/feed_forward/pallas_call | solution.py:463
  217.4 13.6 %branch_back.1 = (f32[960,1024]{1,0:T(8,128)}, bf16[960,1024]{1,0:T(8,128)(2,1)}, f32[960,1]{1,0:T(8,128)}, bf16[2,2,240,480]{3,2,1,0:T(8,128)(2,1)}, bf16[2,2,240,480]{3,2,1,0:T(8,128)(2,1)}) custom-call(s32[1]{0:T(128)} %bitcast.flip_ref, f32[960,1024]{1,0:T(8,128)} %get-tuple-element.103.grad_ref, f32[960,1024]{1,0:T(8,128)} %get-tuple-element.94.refs_2_.middle_ref, ...), custom_call_target="tpu_custom_call" | custom-call | flops 1000 | bytes 1000 | tf_op jit(solution)/shard_map/branch_back/pallas_call | solution.py:556
  237.4 2.8 reshape_squeeze.6
  240.2 2.8 reshape_squeeze.7
  244.4 2.7 maximum_select_fusion.3
  247.1 3.2 add.191
  250.6 1.8 copy-done.6
  252.3 3.2 add.193
  257.6 4.9 maximum_maximum_fusion.1
  266.3 38.2 %attend_backward.1 = (bf16[960,1024]{1,0:T(8,128)(2,1)S(1)}, bf16[5,128,512]{2,1,0:T(8,128)(2,1)S(1)}, f32[5,128,1024]{2,1,0:T(8,128)}) custom-call(s32[1,1024]{1,0:T(1,128)S(1)} %bitcast.37, f32[32,1024]{1,0:T(8,128)S(1)} %copy-done.8, f32[32,1024]{1,0:T(8,128)S(1)} %copy-done.7, bf16[960,1024]{1,0:T(8,128)(2,1)S(1)} %copy-done.2, ...), custom_call_target="tpu_custom_call" | custom-call | flops 1000 | bytes 1000 | tf_op jit(solution)/shard_map/attend_backward/pallas_call | solution.py:370
  310.6 9.1 %qkv_grad.1 = (bf16[1600,1024]{1,0:T(8,128)(2,1)}, bf16[2,2,800,240]{3,2,1,0:T(8,128)(2,1)}, bf16[2,2,800,240]{3,2,1,0:T(8,128)(2,1)}) custom-call(s32[1]{0:T(128)} %bitcast.flip_ref, bf16[960,1024]{1,0:T(8,128)(2,1)} %get-tuple-element.101.normed_ref, bf16[960,1024]{1,0:T(8,128)(2,1)} %copy-done.9, f32[5,128,1024]{2,1,0:T(8,128)} %get-tuple-element.114.own_ref, ...), custom_call_target="tpu_custom_call" | custom-call | flops 1000 | bytes 1000 | tf_op jit(solution)/shard_map/qkv_grad/pallas_call | solution.py:556
  320.6 2.8 collective-permute-done.27
  323.4 3.5 add_pair.5
  326.9 12.8 %input_grad.1 = (bf16[960,1024]{1,0:T(8,128)(2,1)}, f32[960,1]{1,0:T(8,128)}) custom-call(s32[1]{0:T(128)} %bitcast.flip_ref, bf16[1600,1024]{1,0:T(8,128)(2,1)} %get-tuple-element.124.grads_ref, bf16[960,1024]{1,0:T(8,128)(2,1)} %get-tuple-element.85.x_ref, f32[960,1]{1,0:T(8,128)} %copy.24.gain_ref, f32[960,1024]{1,0:T(8,128)} %get-tuple-element.125.mid_grad_ref, ...), custom_call_target="tpu_custom_call" | custom-call | flops 1000 | bytes 1000 | tf_op jit(solution)/shard_map/input_grad/pallas_call | solution.py:556
  339.7 2.2 add_pair.6
  351.3 14.4 %collective-permute-done.33.right_ref = bf16[2,800,240]{2,1,0:T(8,128)(2,1)} collective-permute-done((bf16[2,800,240]{2,1,0:T(8,128)(2,1)}, bf16[2,800,240]{2,1,0:T(8,128)(2,1)}, u32[]{:S(2)}, u32[]{:S(2)}) %collective-permute-start.33) | collective-permute-done | bytes 768032 | tf_op jit(solution)/shard_map/ppermute | solution.py:30
  365.7 3.0 add_pair.7
  371.3 11.3 %collective-permute-done.30.right_ref = bf16[320,1280]{1,0:T(8,128)(2,1)S(1)} collective-permute-done((bf16[320,1280]{1,0:T(8,128)(2,1)}, bf16[320,1280]{1,0:T(8,128)(2,1)S(1)}, u32[]{:S(2)}, u32[]{:S(2)}) %collective-permute-start.30) | collective-permute-done | bytes 819232 | tf_op jit(solution)/shard_map/ppermute | solution.py:30
  387.4 20.9 %collective-permute-done.34.right_ref = bf16[800,240]{1,0:T(8,128)(2,1)S(1)} collective-permute-done((bf16[800,240]{1,0:T(8,128)(2,1)S(1)}, bf16[800,240]{1,0:T(8,128)(2,1)S(1)}, u32[]{:S(2)}, u32[]{:S(2)}) %collective-permute-start.34) | collective-permute-done | bytes 384032 | tf_op jit(solution)/shard_map/ppermute | solution.py:30
  409.3 3.5 collective-permute-start.35
  414.6 7.9 %collective-permute-done.35.right_ref = bf16[800,240]{1,0:T(8,128)(2,1)S(1)} collective-permute-done((bf16[800,240]{1,0:T(8,128)(2,1)S(1)}, bf16[800,240]{1,0:T(8,128)(2,1)S(1)}, u32[]{:S(2)}, u32[]{:S(2)}) %collective-permute-start.35) | collective-permute-done | bytes 384032 | tf_op jit(solution)/shard_map/ppermute | solution.py:873
  423.6 5.2 %collective-permute-start.43 = (bf16[128,1280]{1,0:T(8,128)(2,1)S(1)}, bf16[128,1280]{1,0:T(8,128)(2,1)S(1)}, u32[]{:S(2)}, u32[]{:S(2)}) collective-permute-start(bf16[128,1280]{1,0:T(8,128)(2,1)S(1)} %get-tuple-element.201), channel_id=1, source_target_pairs={{0,16},{8,24},{16,0},{24,8},{1,17},{9,25},{17,1},{25,9},{2,18},{10... | collective-permute-start | bytes 983048 | tf_op jit(solution)/shard_map/ppermute | solution.py:30
  428.8 2.0 maximum_select_fusion
  432.7 2.7 collective-permute-start.45
  435.4 19.6 %collective-permute-done.43.right_ref = bf16[128,1280]{1,0:T(8,128)(2,1)S(1)} collective-permute-done((bf16[128,1280]{1,0:T(8,128)(2,1)S(1)}, bf16[128,1280]{1,0:T(8,128)(2,1)S(1)}, u32[]{:S(2)}, u32[]{:S(2)}) %collective-permute-start.43) | collective-permute-done | bytes 327712 | tf_op jit(solution)/shard_map/ppermute | solution.py:30
  455.2 2.0 maximum_select_fusion.1
  458.5 3.0 collective-permute-start.49
  461.5 5.2 %collective-permute-done.45 = bf16[80,1280]{1,0:T(8,128)(2,1)S(1)} collective-permute-done((bf16[80,1280]{1,0:T(8,128)(2,1)S(1)}, bf16[80,1280]{1,0:T(8,128)(2,1)S(1)}, u32[]{:S(2)}, u32[]{:S(2)}) %collective-permute-start.45) | collective-permute-done | bytes 204832 | tf_op jit(solution)/shard_map/ppermute | solution.py:30
  466.8 6.3 %collective-permute-done.44 = bf16[128,1280]{1,0:T(8,128)(2,1)S(1)} collective-permute-done((bf16[128,1280]{1,0:T(8,128)(2,1)S(1)}, bf16[128,1280]{1,0:T(8,128)(2,1)S(1)}, u32[]{:S(2)}, u32[]{:S(2)}) %collective-permute-start.44) | collective-permute-done | bytes 327712 | tf_op jit(solution)/shard_map/ppermute | solution.py:30
  473.3 6.8 %collective-permute-done.42 = bf16[800,240]{1,0:T(8,128)(2,1)S(1)} collective-permute-done((bf16[800,240]{1,0:T(8,128)(2,1)S(1)}, bf16[800,240]{1,0:T(8,128)(2,1)S(1)}, u32[]{:S(2)}, u32[]{:S(2)}) %collective-permute-start.42) | collective-permute-done | bytes 384032 | tf_op jit(solution)/shard_map/ppermute | solution.py:887
  481.6 7.2 %collective-permute-done.48 = bf16[160,1280]{1,0:T(8,128)(2,1)S(1)} collective-permute-done((bf16[160,1280]{1,0:T(8,128)(2,1)S(1)}, bf16[160,1280]{1,0:T(8,128)(2,1)S(1)}, u32[]{:S(2)}, u32[]{:S(2)}) %collective-permute-start.48) | collective-permute-done | bytes 409632 | tf_op jit(solution)/shard_map/ppermute | solution.py:30
  489.0 12.0 %collective-permute-done.47 = bf16[256,1280]{1,0:T(8,128)(2,1)S(1)} collective-permute-done((bf16[256,1280]{1,0:T(8,128)(2,1)S(1)}, bf16[256,1280]{1,0:T(8,128)(2,1)S(1)}, u32[]{:S(2)}, u32[]{:S(2)}) %collective-permute-start.47) | collective-permute-done | bytes 655392 | tf_op jit(solution)/shard_map/ppermute | solution.py:30
  (234 shorter events, 79.1 us)
Async XLA Ops:
  8.2 40.0 %collective-permute-start.1 = (bf16[240,2048]{1,0:T(8,128)(2,1)}, bf16[240,2048]{1,0:T(8,128)(2,1)}, u32[]{:S(2)}, u32[]{:S(2)}) collective-permute-start(bf16[240,2048]{1,0:T(8,128)(2,1)} %constant_dynamic-slice_fusion.15), channel_id=1, source_target_pairs={{0,2},{1,3},{2,0},{3,1},{4,6},{5,7},{6,4},{7,5},{8,10},{9,11},{10,... | collective-permute-start | bytes 2949128 | tf_op jit(solution)/shard_map/ppermute | solution.py:30
  11.0 35.4 %collective-permute-start.3 = (bf16[240,1280]{1,0:T(8,128)(2,1)S(1)}, bf16[240,1280]{1,0:T(8,128)(2,1)S(1)}, u32[]{:S(2)}, u32[]{:S(2)}) collective-permute-start(bf16[240,1280]{1,0:T(8,128)(2,1)S(1)} %pad_maximum_fusion.9.refs_0_), channel_id=1, source_target_pairs={{0,2},{1,3},{2,0},{3,1},{4,6},{5,7},{6,4},{7,5},{8,10},{9,11},{10,... | collective-permute-start | bytes 1843208 | tf_op jit(solution)/shard_map/ppermute | solution.py:30
  11.1 42.1 %collective-permute-start.5 = (bf16[240,1280]{1,0:T(8,128)(2,1)S(1)}, bf16[240,1280]{1,0:T(8,128)(2,1)S(1)}, u32[]{:S(2)}, u32[]{:S(2)}) collective-permute-start(bf16[240,1280]{1,0:T(8,128)(2,1)S(1)} %pad_maximum_fusion.9.refs_0_), channel_id=1, source_target_pairs={{0,4},{4,0},{1,5},{5,1},{2,6},{6,2},{3,7},{7,3},{8,12},{12,8},{9,1... | collective-permute-start | bytes 1843208 | tf_op jit(solution)/shard_map/ppermute | solution.py:30
  46.5 15.4 %collective-permute-start.7 = (bf16[240,1280]{1,0:T(8,128)(2,1)S(1)}, bf16[240,1280]{1,0:T(8,128)(2,1)S(1)}, u32[]{:S(2)}, u32[]{:S(2)}) collective-permute-start(bf16[240,1280]{1,0:T(8,128)(2,1)S(1)} %collective-permute-done.3.refs_2_), channel_id=1, source_target_pairs={{0,4},{4,0},{1,5},{5,1},{2,6},{6,2},{3,7},{7,3},{8,12},{12,8},{9,1... | collective-permute-start | bytes 1843208 | tf_op jit(solution)/shard_map/ppermute | solution.py:30
  48.2 15.1 %collective-permute-start.4 = (bf16[240,1280]{1,0:T(8,128)(2,1)S(1)}, bf16[240,1280]{1,0:T(8,128)(2,1)S(1)}, u32[]{:S(2)}, u32[]{:S(2)}) collective-permute-start(bf16[240,1280]{1,0:T(8,128)(2,1)S(1)} %collective-permute-done.3.refs_2_), channel_id=1, source_target_pairs={{0,1},{1,0},{2,3},{3,2},{4,5},{5,4},{6,7},{7,6},{8,9},{9,8},{10,11... | collective-permute-start | bytes 1843208 | tf_op jit(solution)/shard_map/ppermute | solution.py:30
  51.2 15.9 %collective-permute-start.2 = (bf16[480,1024]{1,0:T(8,128)(2,1)}, bf16[480,1024]{1,0:T(8,128)(2,1)}, u32[]{:S(2)}, u32[]{:S(2)}) collective-permute-start(bf16[480,1024]{1,0:T(8,128)(2,1)} %pad_maximum_fusion.5), channel_id=1, source_target_pairs={{0,1},{1,0},{2,3},{3,2},{4,5},{5,4},{6,7},{7,6},{8,9},{9,8},{10,11... | collective-permute-start | bytes 2949128 | tf_op jit(solution)/shard_map/ppermute | solution.py:30
  53.2 13.9 %collective-permute-start.6 = (bf16[240,1280]{1,0:T(8,128)(2,1)S(1)}, bf16[240,1280]{1,0:T(8,128)(2,1)S(1)}, u32[]{:S(2)}, u32[]{:S(2)}) collective-permute-start(bf16[240,1280]{1,0:T(8,128)(2,1)S(1)} %collective-permute-done.5.refs_4_), channel_id=1, source_target_pairs={{0,1},{1,0},{2,3},{3,2},{4,5},{5,4},{6,7},{7,6},{8,9},{9,8},{10,11... | collective-permute-start | bytes 1843208 | tf_op jit(solution)/shard_map/ppermute | solution.py:30
  61.9 5.3 %collective-permute-start.8 = (bf16[240,1280]{1,0:T(8,128)(2,1)S(1)}, bf16[240,1280]{1,0:T(8,128)(2,1)}, u32[]{:S(2)}, u32[]{:S(2)}) collective-permute-start(bf16[240,1280]{1,0:T(8,128)(2,1)S(1)} %collective-permute-done.7.refs_6_), channel_id=1, source_target_pairs={{0,1},{1,0},{2,3},{3,2},{4,5},{5,4},{6,7},{7,6},{8,9},{9,8},{10,11... | collective-permute-start | bytes 1843208 | tf_op jit(solution)/shard_map/ppermute | solution.py:30
  61.9 58.8 %collective-permute-start.10 = (bf16[720,1280]{1,0:T(8,128)(2,1)}, bf16[720,1280]{1,0:T(8,128)(2,1)}, u32[]{:S(2)}, u32[]{:S(2)}) collective-permute-start(bf16[720,1280]{1,0:T(8,128)(2,1)} %pad_maximum_fusion.1.refs_3_), channel_id=1, source_target_pairs={{0,2},{1,3},{2,0},{3,1},{4,6},{5,7},{6,4},{7,5},{8,10},{9,11},{10,... | collective-permute-start | bytes 5529608 | tf_op jit(solution)/shard_map/ppermute | solution.py:30
  63.3 57.4 %collective-permute-start.11 = (bf16[720,1280]{1,0:T(8,128)(2,1)}, bf16[720,1280]{1,0:T(8,128)(2,1)}, u32[]{:S(2)}, u32[]{:S(2)}) collective-permute-start(bf16[720,1280]{1,0:T(8,128)(2,1)} %pad_maximum_fusion.1.refs_3_), channel_id=1, source_target_pairs={{0,4},{4,0},{1,5},{5,1},{2,6},{6,2},{3,7},{7,3},{8,12},{12,8},{9,1... | collective-permute-start | bytes 5529608 | tf_op jit(solution)/shard_map/ppermute | solution.py:30
  78.6 47.1 %collective-permute-start.12 = (bf16[240,2048]{1,0:T(8,128)(2,1)S(1)}, bf16[240,2048]{1,0:T(8,128)(2,1)S(1)}, u32[]{:S(2)}, u32[]{:S(2)}) collective-permute-start(bf16[240,2048]{1,0:T(8,128)(2,1)S(1)} %constant_dynamic-slice_fusion.10), channel_id=1, source_target_pairs={{0,2},{1,3},{2,0},{3,1},{4,6},{5,7},{6,4},{7,5},{8,10},{9,11},{10,... | collective-permute-start | bytes 2949128 | tf_op jit(solution)/shard_map/ppermute | solution.py:30
  79.2 3.6 collective-permute-start.9
  81.4 61.3 %collective-permute-start.14 = (bf16[720,1280]{1,0:T(8,128)(2,1)}, bf16[720,1280]{1,0:T(8,128)(2,1)}, u32[]{:S(2)}, u32[]{:S(2)}) collective-permute-start(bf16[720,1280]{1,0:T(8,128)(2,1)} %pad_maximum_fusion.1.refs_3_), channel_id=1, source_target_pairs={{0,1},{1,0},{2,3},{3,2},{4,5},{5,4},{6,7},{7,6},{8,9},{9,8},{10,11... | collective-permute-start | bytes 5529608 | tf_op jit(solution)/shard_map/ppermute | solution.py:30
  125.8 17.0 %collective-permute-start.15 = (bf16[720,1280]{1,0:T(8,128)(2,1)}, bf16[720,1280]{1,0:T(8,128)(2,1)}, u32[]{:S(2)}, u32[]{:S(2)}) collective-permute-start(bf16[720,1280]{1,0:T(8,128)(2,1)} %collective-permute-done.10.refs_5_), channel_id=1, source_target_pairs={{0,1},{1,0},{2,3},{3,2},{4,5},{5,4},{6,7},{7,6},{8,9},{9,8},{10,11... | collective-permute-start | bytes 5529608 | tf_op jit(solution)/shard_map/ppermute | solution.py:30
  125.8 51.2 %collective-permute-start.17 = (bf16[720,1280]{1,0:T(8,128)(2,1)}, bf16[720,1280]{1,0:T(8,128)(2,1)}, u32[]{:S(2)}, u32[]{:S(2)}) collective-permute-start(bf16[720,1280]{1,0:T(8,128)(2,1)} %collective-permute-done.10.refs_5_), channel_id=1, source_target_pairs={{0,4},{4,0},{1,5},{5,1},{2,6},{6,2},{3,7},{7,3},{8,12},{12,8},{9,1... | collective-permute-start | bytes 5529608 | tf_op jit(solution)/shard_map/ppermute | solution.py:30
  129.1 11.0 %collective-permute-start.13 = (bf16[480,1024]{1,0:T(8,128)(2,1)}, bf16[480,1024]{1,0:T(8,128)(2,1)}, u32[]{:S(2)}, u32[]{:S(2)}) collective-permute-start(bf16[480,1024]{1,0:T(8,128)(2,1)} %pad_maximum_fusion.6), channel_id=1, source_target_pairs={{0,1},{1,0},{2,3},{3,2},{4,5},{5,4},{6,7},{7,6},{8,9},{9,8},{10,11... | collective-permute-start | bytes 2949128 | tf_op jit(solution)/shard_map/ppermute | solution.py:30
  139.8 37.7 %collective-permute-start.16 = (bf16[720,1280]{1,0:T(8,128)(2,1)}, bf16[720,1280]{1,0:T(8,128)(2,1)S(1)}, u32[]{:S(2)}, u32[]{:S(2)}) collective-permute-start(bf16[720,1280]{1,0:T(8,128)(2,1)} %collective-permute-done.11.refs_4_), channel_id=1, source_target_pairs={{0,1},{1,0},{2,3},{3,2},{4,5},{5,4},{6,7},{7,6},{8,9},{9,8},{10,11... | collective-permute-start | bytes 5529608 | tf_op jit(solution)/shard_map/ppermute | solution.py:30
  176.9 4.4 collective-permute-start.18
  177.2 69.9 %collective-permute-start.20 = (bf16[2,720,1280]{2,1,0:T(8,128)(2,1)}, bf16[2,720,1280]{2,1,0:T(8,128)(2,1)}, u32[]{:S(2)}, u32[]{:S(2)}) collective-permute-start(bf16[2,720,1280]{2,1,0:T(8,128)(2,1)} %get-tuple-element.106), channel_id=1, source_target_pairs={{0,1},{1,0},{2,3},{3,2},{4,5},{5,4},{6,7},{7,6},{8,9},{9,8},{10,11... | collective-permute-start | bytes 11059208 | tf_op jit(solution)/shard_map/ppermute | solution.py:30
  217.1 33.4 %collective-permute-start.22 = (bf16[2,720,1280]{2,1,0:T(8,128)(2,1)}, bf16[2,720,1280]{2,1,0:T(8,128)(2,1)}, u32[]{:S(2)}, u32[]{:S(2)}) collective-permute-start(bf16[2,720,1280]{2,1,0:T(8,128)(2,1)} %get-tuple-element.110), channel_id=1, source_target_pairs={{0,1},{1,0},{2,3},{3,2},{4,5},{5,4},{6,7},{7,6},{8,9},{9,8},{10,11... | collective-permute-start | bytes 11059208 | tf_op jit(solution)/shard_map/ppermute | solution.py:30
  233.3 9.7 %collective-permute-start.19 = (bf16[480,1024]{1,0:T(8,128)(2,1)}, bf16[480,1024]{1,0:T(8,128)(2,1)}, u32[]{:S(2)}, u32[]{:S(2)}) collective-permute-start(bf16[480,1024]{1,0:T(8,128)(2,1)} %pad_maximum_fusion.7), channel_id=1, source_target_pairs={{0,1},{1,0},{2,3},{3,2},{4,5},{5,4},{6,7},{7,6},{8,9},{9,8},{10,11... | collective-permute-start | bytes 2949128 | tf_op jit(solution)/shard_map/ppermute | solution.py:30
  256.0 51.1 %collective-permute-start.23 = (bf16[2,320,1280]{2,1,0:T(8,128)(2,1)S(1)}, bf16[2,320,1280]{2,1,0:T(8,128)(2,1)S(1)}, u32[]{:S(2)}, u32[]{:S(2)}) collective-permute-start(bf16[2,320,1280]{2,1,0:T(8,128)(2,1)S(1)} %pad_maximum_fusion.3), channel_id=1, source_target_pairs={{0,2},{1,3},{2,0},{3,1},{4,6},{5,7},{6,4},{7,5},{8,10},{9,11},{10,... | collective-permute-start | bytes 4915208 | tf_op jit(solution)/shard_map/ppermute | solution.py:30
  262.5 77.3 %collective-permute-start.26 = (bf16[2,512,1280]{2,1,0:T(8,128)(2,1)}, bf16[2,512,1280]{2,1,0:T(8,128)(2,1)}, u32[]{:S(2)}, u32[]{:S(2)}) collective-permute-start(bf16[2,512,1280]{2,1,0:T(8,128)(2,1)} %get-tuple-element.219), channel_id=1, source_target_pairs={{0,4},{4,0},{1,5},{5,1},{2,6},{6,2},{3,7},{7,3},{8,12},{12,8},{9,1... | collective-permute-start | bytes 7864328 | tf_op jit(solution)/shard_map/ppermute | solution.py:30
  305.7 4.0 collective-permute-start.24
  319.7 3.7 collective-permute-start.27
  344.2 24.5 %collective-permute-start.31 = (bf16[480,1024]{1,0:T(8,128)(2,1)}, bf16[480,1024]{1,0:T(8,128)(2,1)}, u32[]{:S(2)}, u32[]{:S(2)}) collective-permute-start(bf16[480,1024]{1,0:T(8,128)(2,1)} %pad_maximum_fusion.8), channel_id=1, source_target_pairs={{0,1},{1,0},{2,3},{3,2},{4,5},{5,4},{6,7},{7,6},{8,9},{9,8},{10,11... | collective-permute-start | bytes 2949128 | tf_op jit(solution)/shard_map/ppermute | solution.py:30
  344.3 21.4 %collective-permute-start.33 = (bf16[2,800,240]{2,1,0:T(8,128)(2,1)}, bf16[2,800,240]{2,1,0:T(8,128)(2,1)}, u32[]{:S(2)}, u32[]{:S(2)}) collective-permute-start(bf16[2,800,240]{2,1,0:T(8,128)(2,1)} %bitcast.19), channel_id=1, source_target_pairs={{0,4},{4,0},{1,5},{5,1},{2,6},{6,2},{3,7},{7,3},{8,12},{12,8},{9,1... | collective-permute-start | bytes 2304008 | tf_op jit(solution)/shard_map/ppermute | solution.py:30
  347.1 35.5 %collective-permute-start.30 = (bf16[320,1280]{1,0:T(8,128)(2,1)}, bf16[320,1280]{1,0:T(8,128)(2,1)S(1)}, u32[]{:S(2)}, u32[]{:S(2)}) collective-permute-start(bf16[320,1280]{1,0:T(8,128)(2,1)} %copy-done.15), channel_id=1, source_target_pairs={{0,4},{4,0},{1,5},{5,1},{2,6},{6,2},{3,7},{7,3},{8,12},{12,8},{9,1... | collective-permute-start | bytes 2457608 | tf_op jit(solution)/shard_map/ppermute | solution.py:30
  347.7 38.3 %collective-permute-start.28 = (bf16[512,1280]{1,0:T(8,128)(2,1)}, bf16[512,1280]{1,0:T(8,128)(2,1)S(1)}, u32[]{:S(2)}, u32[]{:S(2)}) collective-permute-start(bf16[512,1280]{1,0:T(8,128)(2,1)} %copy-done.14), channel_id=1, source_target_pairs={{0,2},{1,3},{2,0},{3,1},{4,6},{5,7},{6,4},{7,5},{8,10},{9,11},{10,... | collective-permute-start | bytes 3932168 | tf_op jit(solution)/shard_map/ppermute | solution.py:30
  348.7 64.1 %collective-permute-start.25 = (bf16[240,2048]{1,0:T(8,128)(2,1)}, bf16[240,2048]{1,0:T(8,128)(2,1)S(1)}, u32[]{:S(2)}, u32[]{:S(2)}) collective-permute-start(bf16[240,2048]{1,0:T(8,128)(2,1)} %maximum_select_fusion.4), channel_id=1, source_target_pairs={{0,2},{1,3},{2,0},{3,1},{4,6},{5,7},{6,4},{7,5},{8,10},{9,11},{10,... | collective-permute-start | bytes 2949128 | tf_op jit(solution)/shard_map/ppermute | solution.py:30
  365.7 17.1 %collective-permute-start.29 = (f32[2,960]{1,0:T(2,128)S(1)}, f32[2,960]{1,0:T(2,128)S(1)}, u32[]{:S(2)}, u32[]{:S(2)}) collective-permute-start(f32[2,960]{1,0:T(2,128)S(1)} %pad_maximum_fusion.10), channel_id=1, source_target_pairs={{0,1},{1,0},{2,3},{3,2},{4,5},{5,4},{6,7},{7,6},{8,9},{9,8},{10,11... | collective-permute-start | bytes 23048 | tf_op jit(solution)/shard_map/ppermute | solution.py:30
  368.7 39.6 %collective-permute-start.34 = (bf16[800,240]{1,0:T(8,128)(2,1)S(1)}, bf16[800,240]{1,0:T(8,128)(2,1)S(1)}, u32[]{:S(2)}, u32[]{:S(2)}) collective-permute-start(bf16[800,240]{1,0:T(8,128)(2,1)S(1)} %get-tuple-element.142), channel_id=1, source_target_pairs={{0,2},{1,3},{2,0},{3,1},{4,6},{5,7},{6,4},{7,5},{8,10},{9,11},{10,... | collective-permute-start | bytes 1152008 | tf_op jit(solution)/shard_map/ppermute | solution.py:30
  382.9 26.5 %collective-permute-start.37 = (f32[2,960]{1,0:T(2,128)S(1)}, f32[2,960]{1,0:T(2,128)S(1)}, u32[]{:S(2)}, u32[]{:S(2)}) collective-permute-start(f32[2,960]{1,0:T(2,128)S(1)} %fusion.2), channel_id=1, source_target_pairs={{0,4},{4,0},{1,5},{5,1},{2,6},{6,2},{3,7},{7,3},{8,12},{12,8},{9,1... | collective-permute-start | bytes 23048 | tf_op jit(solution)/shard_map/ppermute | solution.py:30
  384.5 29.6 %collective-permute-start.36 = (bf16[160,1280]{1,0:T(8,128)(2,1)S(1)}, bf16[160,1280]{1,0:T(8,128)(2,1)S(1)}, u32[]{:S(2)}, u32[]{:S(2)}) collective-permute-start(bf16[160,1280]{1,0:T(8,128)(2,1)S(1)} %get-tuple-element.199), channel_id=1, source_target_pairs={{0,8},{8,0},{16,24},{24,16},{1,9},{9,1},{17,25},{25,17},{2,10},{10... | collective-permute-start | bytes 1228808 | tf_op jit(solution)/shard_map/ppermute | solution.py:30
  386.4 36.9 %collective-permute-start.41 = (bf16[256,1280]{1,0:T(8,128)(2,1)S(1)}, bf16[256,1280]{1,0:T(8,128)(2,1)S(1)}, u32[]{:S(2)}, u32[]{:S(2)}) collective-permute-start(bf16[256,1280]{1,0:T(8,128)(2,1)S(1)} %get-tuple-element.185), channel_id=1, source_target_pairs={{0,8},{8,0},{16,24},{24,16},{1,9},{9,1},{17,25},{25,17},{2,10},{10... | collective-permute-start | bytes 1966088 | tf_op jit(solution)/shard_map/ppermute | solution.py:30
  408.3 46.9 %collective-permute-start.32 = (bf16[240,2048]{1,0:T(8,128)(2,1)S(1)}, bf16[240,2048]{1,0:T(8,128)(2,1)S(1)}, u32[]{:S(2)}, u32[]{:S(2)}) collective-permute-start(bf16[240,2048]{1,0:T(8,128)(2,1)S(1)} %maximum_select_fusion.6), channel_id=1, source_target_pairs={{0,2},{1,3},{2,0},{3,1},{4,6},{5,7},{6,4},{7,5},{8,10},{9,11},{10,... | collective-permute-start | bytes 2949128 | tf_op jit(solution)/shard_map/ppermute | solution.py:30
  409.3 13.2 %collective-permute-start.35 = (bf16[800,240]{1,0:T(8,128)(2,1)S(1)}, bf16[800,240]{1,0:T(8,128)(2,1)S(1)}, u32[]{:S(2)}, u32[]{:S(2)}) collective-permute-start(bf16[800,240]{1,0:T(8,128)(2,1)S(1)} %add.196.left_ref), channel_id=1, source_target_pairs={{0,8},{24,16},{1,9},{25,17},{2,10},{26,18},{3,11},{27,19},{4,12},{... | collective-permute-start | bytes 1152008 | tf_op jit(solution)/shard_map/ppermute | solution.py:873
  412.9 18.2 %collective-permute-start.40 = (f32[2,960]{1,0:T(2,128)S(1)}, f32[2,960]{1,0:T(2,128)S(1)}, u32[]{:S(2)}, u32[]{:S(2)}) collective-permute-start(f32[2,960]{1,0:T(2,128)S(1)} %fusion.14), channel_id=1, source_target_pairs={{0,2},{1,3},{2,0},{3,1},{4,6},{5,7},{6,4},{7,5},{8,10},{9,11},{10,... | collective-permute-start | bytes 23048 | tf_op jit(solution)/shard_map/ppermute | solution.py:30
  414.2 18.4 %collective-permute-start.39 = (bf16[80,1280]{1,0:T(8,128)(2,1)S(1)}, bf16[80,1280]{1,0:T(8,128)(2,1)S(1)}, u32[]{:S(2)}, u32[]{:S(2)}) collective-permute-start(bf16[80,1280]{1,0:T(8,128)(2,1)S(1)} %get-tuple-element.203), channel_id=1, source_target_pairs={{0,16},{8,24},{16,0},{24,8},{1,17},{9,25},{17,1},{25,9},{2,18},{10... | collective-permute-start | bytes 614408 | tf_op jit(solution)/shard_map/ppermute | solution.py:30
  422.6 12.7 %collective-permute-start.38 = (bf16[800,240]{1,0:T(8,128)(2,1)S(1)}, bf16[800,240]{1,0:T(8,128)(2,1)S(1)}, u32[]{:S(2)}, u32[]{:S(2)}) collective-permute-start(bf16[800,240]{1,0:T(8,128)(2,1)S(1)} %add.198.left_ref), channel_id=1, source_target_pairs={{8,16},{16,8},{9,17},{17,9},{10,18},{18,10},{11,19},{19,11},{12,20... | collective-permute-start | bytes 1152008 | tf_op jit(solution)/shard_map/ppermute | solution.py:879
  423.6 31.4 %collective-permute-start.43 = (bf16[128,1280]{1,0:T(8,128)(2,1)S(1)}, bf16[128,1280]{1,0:T(8,128)(2,1)S(1)}, u32[]{:S(2)}, u32[]{:S(2)}) collective-permute-start(bf16[128,1280]{1,0:T(8,128)(2,1)S(1)} %get-tuple-element.201), channel_id=1, source_target_pairs={{0,16},{8,24},{16,0},{24,8},{1,17},{9,25},{17,1},{25,9},{2,18},{10... | collective-permute-start | bytes 983048 | tf_op jit(solution)/shard_map/ppermute | solution.py:30
  431.0 27.4 %collective-permute-start.46 = (f32[2,960]{1,0:T(2,128)S(1)}, f32[2,960]{1,0:T(2,128)S(1)}, u32[]{:S(2)}, u32[]{:S(2)}) collective-permute-start(f32[2,960]{1,0:T(2,128)S(1)} %add.171), channel_id=1, source_target_pairs={{0,8},{8,0},{16,24},{24,16},{1,9},{9,1},{17,25},{25,17},{2,10},{10... | collective-permute-start | bytes 23048 | tf_op jit(solution)/shard_map/ppermute | solution.py:30
  432.7 34.0 %collective-permute-start.45 = (bf16[80,1280]{1,0:T(8,128)(2,1)S(1)}, bf16[80,1280]{1,0:T(8,128)(2,1)S(1)}, u32[]{:S(2)}, u32[]{:S(2)}) collective-permute-start(bf16[80,1280]{1,0:T(8,128)(2,1)S(1)} %add.200), channel_id=1, source_target_pairs={{0,16},{8,24},{16,0},{24,8},{1,17},{9,25},{17,1},{25,9},{2,18},{10... | collective-permute-start | bytes 614408 | tf_op jit(solution)/shard_map/ppermute | solution.py:30
  455.1 18.0 %collective-permute-start.44 = (bf16[128,1280]{1,0:T(8,128)(2,1)S(1)}, bf16[128,1280]{1,0:T(8,128)(2,1)S(1)}, u32[]{:S(2)}, u32[]{:S(2)}) collective-permute-start(bf16[128,1280]{1,0:T(8,128)(2,1)S(1)} %add.202), channel_id=1, source_target_pairs={{0,16},{8,24},{16,0},{24,8},{1,17},{9,25},{17,1},{25,9},{2,18},{10... | collective-permute-start | bytes 983048 | tf_op jit(solution)/shard_map/ppermute | solution.py:30
  457.2 22.9 %collective-permute-start.42 = (bf16[800,240]{1,0:T(8,128)(2,1)S(1)}, bf16[800,240]{1,0:T(8,128)(2,1)S(1)}, u32[]{:S(2)}, u32[]{:S(2)}) collective-permute-start(bf16[800,240]{1,0:T(8,128)(2,1)S(1)} %add.201), channel_id=1, source_target_pairs={{8,0},{16,24},{9,1},{17,25},{10,2},{18,26},{11,3},{19,27},{12,4},{... | collective-permute-start | bytes 1152008 | tf_op jit(solution)/shard_map/ppermute | solution.py:887
  458.5 22.5 %collective-permute-start.49 = (f32[2,960]{1,0:T(2,128)S(1)}, f32[2,960]{1,0:T(2,128)S(1)}, u32[]{:S(2)}, u32[]{:S(2)}) collective-permute-start(f32[2,960]{1,0:T(2,128)S(1)} %add.174), channel_id=1, source_target_pairs={{0,16},{8,24},{16,0},{24,8},{1,17},{9,25},{17,1},{25,9},{2,18},{10... | collective-permute-start | bytes 23048 | tf_op jit(solution)/shard_map/ppermute | solution.py:30
  466.7 22.1 %collective-permute-start.48 = (bf16[160,1280]{1,0:T(8,128)(2,1)S(1)}, bf16[160,1280]{1,0:T(8,128)(2,1)S(1)}, u32[]{:S(2)}, u32[]{:S(2)}) collective-permute-start(bf16[160,1280]{1,0:T(8,128)(2,1)S(1)} %maximum_select_fusion.9), channel_id=1, source_target_pairs={{0,8},{8,0},{16,24},{24,16},{1,9},{9,1},{17,25},{25,17},{2,10},{10... | collective-permute-start | bytes 1228808 | tf_op jit(solution)/shard_map/ppermute | solution.py:30
  473.2 27.7 %collective-permute-start.47 = (bf16[256,1280]{1,0:T(8,128)(2,1)S(1)}, bf16[256,1280]{1,0:T(8,128)(2,1)S(1)}, u32[]{:S(2)}, u32[]{:S(2)}) collective-permute-start(bf16[256,1280]{1,0:T(8,128)(2,1)S(1)} %maximum_select_fusion.8), channel_id=1, source_target_pairs={{0,8},{8,0},{16,24},{24,16},{1,9},{9,1},{17,25},{25,17},{2,10},{10... | collective-permute-start | bytes 1966088 | tf_op jit(solution)/shard_map/ppermute | solution.py:30
  (45 other events, 382.4 us)

commit v4 on v3

--- a/solution.py
+++ b/solution.py
@@ -129,13 +129,11 @@
     )
 
 
-def to_features(full):
+def to_features(kept, got):
     me = lax.axis_index("gy")
-    block = full.shape[0] // 4
-    sent = jnp.concatenate([full[block : 2 * block], full[3 * block :]], axis=0)
-    got = swap(sent, "gy", 1)
-    near = ordered(full[:block], got[:block], me % 2, 1)
-    far = ordered(full[2 * block : 3 * block], got[block:], me % 2, 1)
+    block = kept.shape[0] // 2
+    near = ordered(kept[:block], got[:block], me % 2, 1)
+    far = ordered(kept[block:], got[block:], me % 2, 1)
     return near, far
 
 
@@ -188,6 +186,56 @@
     total = add(inner, lax.ppermute(inner, "dp", [(1, 2), (2, 1)]))
     outer = lax.ppermute(total, "dp", [(1, 0), (2, 3)])
     return jnp.where((me == 0) | (me == 3), outer, total).astype(F32)
+
+
+def unfold(rows, block):
+    return jnp.concatenate(
+        [rows[..., part * 256 : part * 256 + block] for part in range(5)], axis=-2
+    )
+
+
+LOW = 352
+HIGH_PAD = 16
+
+
+def pair_sums_kernel(keep_ref, got_ref, out_keep_ref, out_got_ref, low_ref, near_ref, far_ref):
+    def total(k, rows):
+        return (keep_ref[k, rows, :].astype(F32) + got_ref[k, rows, :].astype(F32)).astype(BF)
+
+    low_ref[:, LOW:, :] = (
+        out_keep_ref[0].astype(F32) + out_got_ref[...].astype(F32)
+    ).astype(BF)
+    for k, high_ref in enumerate((near_ref, far_ref)):
+        low_ref[k, :LOW, :] = total(k, slice(0, LOW))
+        size = high_ref.shape[0] - HIGH_PAD
+        high_ref[:size, :] = total(k, slice(LOW, LOW + size))
+        high_ref[size:, :] = jnp.zeros((HIGH_PAD, high_ref.shape[1]), BF)
+
+
+def pair_sums(keep, got, half, out_keep, out_got):
+    rows, width = keep.shape[1:]
+    out_rows = out_keep.shape[2]
+    out_block = pl.BlockSpec((1, 2, out_rows, 256), lambda i: (half, 0, 0, i))
+    high = rows - LOW + HIGH_PAD
+    tile = 256
+
+    def block(*dims):
+        return pl.BlockSpec((*dims, tile), lambda i: (*(0 for _ in dims), i))
+
+    return pl.pallas_call(
+        pair_sums_kernel,
+        grid=(width // tile,),
+        in_specs=[block(2, rows), block(2, rows), out_block, block(2, out_rows)],
+        out_specs=[block(2, LOW + out_rows), block(high), block(high)],
+        out_shape=[
+            jax.ShapeDtypeStruct((2, LOW + out_rows, width), BF),
+            jax.ShapeDtypeStruct((high, width), BF),
+            jax.ShapeDtypeStruct((high, width), BF),
+        ],
+        compiler_params=pltpu.CompilerParams(vmem_limit_bytes=32 * 2**20),
+        cost_estimate=TINY,
+        name="pair_sums",
+    )(keep, got, out_keep, out_got)
 
 
 def bit_z(by):
@@ -406,8 +454,9 @@
     refs = refs[3:]
     if not first:
         grad_in_ref, refs = refs[0], refs[1:]
-    blocks = refs[0:4]
-    out_ref, grad_out_ref, keep_ref, send_ref, total_ref, grad_total_ref = refs[4:]
+    blocks, refs = refs[:4], refs[4:]
+    out_refs, refs = (refs[:1], refs[1:]) if first else (refs[:2], refs[2:])
+    grad_out_ref, keep_ref, send_ref, total_ref, grad_total_ref = refs
     step = pl.program_id(0)
     last = pl.num_programs(0) - 1
 
@@ -447,7 +496,13 @@
 
     @pl.when(step == last)
     def _():
-        out_ref[...] = total_ref[...].astype(out_ref.dtype)
+        if first:
+            out_refs[0][...] = total_ref[...]
+        else:
+            for number in range(4):
+                rows = slice((number // 2) * block, (number // 2 + 1) * block)
+                source = slice(number * block, (number + 1) * block)
+                out_refs[number % 2][rows, :] = total_ref[source, :].astype(BF)
         grad_out_ref[...] = grad_total_ref[...]
 
 
@@ -457,6 +512,7 @@
     rows, size = blocks[0].shape
     tile = TILE
     whole = pl.BlockSpec((width, count), lambda i: (0, 0), pipeline_mode=pl.Buffered(1))
+    half = pl.BlockSpec((width // 2, count), lambda i: (0, 0), pipeline_mode=pl.Buffered(1))
     across = pl.BlockSpec((rows, tile), lambda i: (0, i))
     made = pl.BlockSpec((2, rows, tile), lambda i: (0, 0, i))
     operands = [normed, upstream, base] + ([] if first else [grad_in])
@@ -464,9 +520,13 @@
         functools.partial(mlp_kernel, first),
         grid=(size // tile,),
         in_specs=[whole] * len(operands) + [across] * 4,
-        out_specs=[whole, whole, made, made],
-        out_shape=[
-            jax.ShapeDtypeStruct((width, count), F32 if first else BF),
+        out_specs=([whole] if first else [half, half]) + [whole, made, made],
+        out_shape=(
+            [jax.ShapeDtypeStruct((width, count), F32)]
+            if first
+            else [jax.ShapeDtypeStruct((width // 2, count), BF)] * 2
+        )
+        + [
             jax.ShapeDtypeStruct((width, count), F32),
             jax.ShapeDtypeStruct((2, rows, size), BF),
             jax.ShapeDtypeStruct((2, rows, size), BF),
@@ -485,6 +545,7 @@
 QKV_WIDTH = Q_WIDTH + 2 * KV_WIDTH
 QKV_PART = QKV_WIDTH // 2
 OUT_PART = Q_WIDTH // 2
+OUT_ROWS = OUT_PART // 5
 
 
 def place_of(flip_ref, half, size):
@@ -604,17 +665,9 @@
     )
 
 
-def store_blocks(keep_ref, send_ref, half, made):
-    block = made.shape[0] // 4
-    keep_ref[half, 0] = made[:block]
-    send_ref[half, 0] = made[block : 2 * block]
-    keep_ref[half, 1] = made[2 * block : 3 * block]
-    send_ref[half, 1] = made[3 * block :]
-
-
 def branch_back_kernel(flip_ref, grad_ref, middle_ref, up_ref, gain_ref, mixed_ref, *refs):
     weights = refs[:8]
-    mid_grad_ref, mixed_grad_ref, gain_grad_ref, keep_ref, send_ref = refs[8:]
+    mid_grad_ref, mixed_grad_ref, gain_grad_ref, keep_ref, *send_refs = refs[8:]
     middle = middle_ref[...]
     mid_grad, gain_grad = norm_back(
         middle, norm_scale_of(middle), gain_ref[...], grad_ref[...]
@@ -623,17 +676,28 @@
     mid_grad = mid_grad + up_ref[...].astype(F32)
     mid_grad_ref[...] = mid_grad
     branch_grad = mid_grad.astype(BF)
+    block = branch_grad.shape[0] // 4
+    keep_ref[...] = jnp.zeros_like(keep_ref)
+    for send_ref in send_refs:
+        send_ref[...] = jnp.zeros_like(send_ref)
     for half in range(2):
         place = place_of(flip_ref, half, OUT_PART)
         weight = stacked(weights[4 * half : 4 * half + 4], OUT_COLUMNS)
         mixed_grad_ref[place, :] = dot(weight, branch_grad, 0, 0).astype(BF)
-        made = dot(branch_grad, mixed_ref[place, :], 1, 1).astype(BF)
-        store_blocks(keep_ref, send_ref, half, made)
+        heads = mixed_ref[place, :]
+        for number in range(4):
+            rows = branch_grad[number * block : (number + 1) * block]
+            made = dot(heads, rows, 1, 1).astype(BF)
+            target = send_refs[half] if number % 2 else keep_ref.at[half]
+            for part in range(5):
+                target[number // 2, :, part * 256 : part * 256 + block] = made[
+                    part * OUT_ROWS : (part + 1) * OUT_ROWS
+                ]
 
 
 def branch_back(flip, grad, middle, upstream, gain, mixed, weights):
     width, count = middle.shape
-    parts = (2, 2, width // 4, OUT_PART)
+    parts = (2, 2, OUT_ROWS, 5 * 256)
     return call_whole(
         branch_back_kernel,
         "branch_back",
@@ -643,7 +707,8 @@
             ((Q_WIDTH, count), BF),
             ((width, 1), F32),
             (parts, BF),
-            (parts, BF),
+            (parts[1:], BF),
+            (parts[1:], BF),
         ),
     )
 
@@ -688,7 +753,7 @@
 
 def input_grad_kernel(flip_ref, grads_ref, x_ref, gain_ref, mid_grad_ref, *refs):
     weights = refs[:8]
-    out_ref, gain_grad_ref = refs[8:]
+    keep_ref, send_ref, gain_grad_ref = refs[8:]
     total = jnp.zeros(x_ref.shape, F32)
     for half in range(2):
         weight = stacked(weights[4 * half : 4 * half + 4], QKV_COLUMNS)
@@ -696,7 +761,12 @@
     x = x_ref[...].astype(F32)
     grad, gain_grad = norm_back(x, norm_scale_of(x), gain_ref[...], total)
     gain_grad_ref[...] = gain_grad
-    out_ref[...] = (grad + mid_grad_ref[...]).astype(BF)
+    grad = (grad + mid_grad_ref[...]).astype(BF)
+    block = grad.shape[0] // 4
+    for number in range(4):
+        target = send_ref if number % 2 else keep_ref
+        rows = slice((number // 2) * block, (number // 2 + 1) * block)
+        target[rows, :] = grad[number * block : (number + 1) * block]
 
 
 def input_grad(flip, grads, inputs, gain, mid_grad, weights):
@@ -705,7 +775,7 @@
         input_grad_kernel,
         "input_grad",
         (flip, grads, inputs, gain, mid_grad, *weights),
-        (((width, count), BF), ((width, 1), F32)),
+        (((width // 2, count), BF), ((width // 2, count), BF), ((width, 1), F32)),
     )
 
 
@@ -740,8 +810,8 @@
     shard = jnp.concatenate([w_qkv, w_out.T], axis=1)
     shard_far = swap(shard, "gy", 2)
     mate = swap(shard, "gy", 1)
-    inputs_far = tokens_far(after(tokens, mate))
     near_halves = attention_halves(shard, w_qkv.shape[1])
+    inputs_far = tokens_far(after(tokens, shard_far, *near_halves))
     far_halves = attention_halves(shard_far, w_qkv.shape[1])
     weights = []
     for half, (near, far) in enumerate(zip(near_halves, far_halves)):
@@ -791,16 +861,23 @@
     ff_far_other = after(ff_far_halves[1], made[0])
     ff_blocks[1] += [ff_far_other, swap(ff_far_other, "gy", 1)]
     later = mlp_chunk(normed_two, upstream, made[0], made[1], ff_blocks[1])
-    result, normed_two_grad = later[0], later[1]
-
-    mid_grad, mixed_grad, gain_two, out_keep, out_send = branch_back(
-        flip, normed_two_grad, middle, upstream, mlp_gain, mixed, weights
-    )
-    result_near, result_sent = to_features(result)
-
-    first_half = add(made[2], swap(made[3], "gy", 1))
-    second_half = add(later[2], swap(later[3], "gy", 1))
-    out_paired = add(out_keep, swap(out_send, "gy", 1))
+    result_keep, result_send, normed_two_grad, later_keep, later_send = later
+    result_near, result_sent = to_features(result_keep, swap(result_send, "gy", 1))
+    result_far = swap(result_sent, "gy", 2)
+    first_got = swap(made[3], "gy", 1)
+    later_got = swap(later_send, "gy", 1)
+
+    mid_grad, mixed_grad, gain_two, out_keep, *out_sent = branch_back(
+        flip,
+        after(normed_two_grad, result_near, result_sent),
+        middle,
+        upstream,
+        mlp_gain,
+        mixed,
+        weights,
+    )
+    out_got = [swap(part, "gy", 1) for part in out_sent]
+    result_shard = assemble(result_near, result_far)
 
     def attend_back(mixed_grad, *earlier):
         dq, sent_grad, own_grad = attention_backward(
@@ -815,64 +892,59 @@
 
     if not pairs_x:
         grads, qkv_keep, qkv_mate = attend_back(mixed_grad)
-        ff_both = reduce_x([first_half, second_half])
+        ff_both = reduce_x([add(made[2], first_got), add(later_keep, later_got)])
         ff_sum = sum_z(add(ff_both[0], swap(ff_both[1], "gy", 2)))
-        both = reduce_x([out_paired[0], out_paired[1]])
+        paired = unfold(add(out_keep, jnp.stack(out_got)), block)
+        both = reduce_x([paired[0], paired[1]], -2)
         sum_out = sum_z(add(both[0], swap(both[1], "gy", 2)))
         paired = add(qkv_keep, qkv_mate)
         both = reduce_x([paired[0], paired[1]], -2)
         sum_qkv = sum_z(add(both[0], swap(both[1], "gy", 2)))
-        in_grad, gain_one = input_grad(flip, grads, inputs, attn_gain, mid_grad, weights)
-        grad_near, grad_sent = to_features(in_grad)
+        grad_keep, grad_send, gain_one = input_grad(
+            flip, grads, inputs, attn_gain, mid_grad, weights
+        )
+        grad_near, grad_sent = to_features(grad_keep, swap(grad_send, "gy", 1))
         grad_far = swap(grad_sent, "gy", 2)
-        result_far = swap(result_sent, "gy", 2)
         gains = sum_all(jnp.stack([reorder(gain_one[:, 0]), reorder(gain_two[:, 0])]))
     else:
-        split = 400
-        wide = first_half.shape[2]
-        out_rows = out_paired[0].size // (2 * wide)
-        filler = jnp.zeros((2, -(split + out_rows) % 64, wide), BF)
-        low_own, low_other = (
-            jnp.concatenate([half[:, :split], out_half.reshape(2, -1, wide), filler], axis=1)
-            for half, out_half in ((first_half, out_paired[0]), (second_half, out_paired[1]))
-        )
-        high_near, high_far = (
-            jnp.stack([first_half[k, split:], second_half[k, split:]]) for k in (0, 1)
+        low_own, near_own, far_own = pair_sums(made[2], first_got, 0, out_keep, out_got[0])
+        low_other, near_other, far_other = pair_sums(
+            later_keep, later_got, 1, out_keep, out_got[1]
         )
         mixed_grad = after(
-            mixed_grad, low_own, low_other, high_near, high_far, result_near, result_sent
+            mixed_grad, low_own, low_other, near_own, near_other, far_own, far_other, result_shard
         )
         low_got = swap(low_other, "gx", 1)
-        high_got = swap(high_far, "gy", 2)
-        grads, qkv_keep, qkv_mate = attend_back(mixed_grad, high_got)
-
-        high_near, high_sent = add_pair(high_near, after(high_got, grads))
-        qkv_near, qkv_sent = add_pair(qkv_keep, after(qkv_mate, high_near))
+        own_got = swap(far_own, "gy", 2)
+        other_got = swap(far_other, "gy", 2)
+        grads, qkv_keep, qkv_mate = attend_back(mixed_grad, own_got, other_got)
+
+        high_sent = add(near_other, after(other_got, grads))
+        high_near = add(near_own, after(own_got, high_sent))
+        low_near, low_sent = add_pair(low_own, after(low_got, high_near))
+        low_got = swap(low_sent, "gy", 2)
+        qkv_near, qkv_sent = add_pair(qkv_keep, after(qkv_mate, low_near))
         qkv_got = swap(qkv_sent, "gx", 1)
         high_got = swap(after(high_sent, qkv_near), "gx", 1)
-        in_grad, gain_one = input_grad(
+        grad_keep, grad_send, gain_one = input_grad(
             flip, after(grads, qkv_near), inputs, attn_gain, mid_grad, weights
         )
-        low_near, low_sent = add_pair(low_own, after(low_got, in_grad))
-        low_got = swap(low_sent, "gy", 2)
-        qkv_near, qkv_sent = add_pair(qkv_near, after(qkv_got, low_near))
+        grad_got = swap(grad_send, "gy", 1)
+        qkv_near, qkv_sent = add_pair(qkv_near, after(qkv_got, grad_keep))
         qkv_got = swap(qkv_sent, "gy", 2)
-        grad_near, grad_sent = to_features(after(in_grad, low_near))
+        low = add(low_near, after(low_got, qkv_near))
+        low_got = halve_z(low, 1)
+        grad_near, grad_sent = to_features(grad_keep, after(grad_got, low))
         grad_far = swap(grad_sent, "gy", 2)
-        result_far = swap(after(result_sent, grads), "gy", 2)
-        gains = jnp.stack([reorder(gain_one[:, 0]), reorder(gain_two[:, 0])])
-        gains_got = swap(gains, "gy", 1)
         high = add(high_near, after(high_got, grad_near))
         high_got = halve_z(high, 1)
-        gains = gains + after(gains_got, high)
+        gain_one, gain_two = after((gain_one, gain_two), high)
+        gains = jnp.stack([reorder(gain_one[:, 0]), reorder(gain_two[:, 0])])
         gains_got = swap(gains, "gx", 1)
-        low = add(low_near, after(low_got, gains))
-        result_far = after(result_far, low)
-        low_got = halve_z(low, 1)
-        qkv_sum = add(qkv_near, after(qkv_got, low))
+        qkv_sum = add(qkv_near, after(qkv_got, high))
         qkv_got = lax.ppermute(qkv_sum, "dp", [(0, 1), (3, 2)])
         gains = gains + after(gains_got, qkv_sum)
-        gains_got = swap(gains, "gy", 2)
+        gains_got = swap(gains, "gy", 1)
         high = add(kept_z(high, 1), after(high_got, gains))
         high_got = halve_z(high, 2)
         qkv_sum = add(qkv_sum, after(qkv_got, high))
@@ -880,7 +952,7 @@
         low = add(kept_z(low, 1), after(low_got, qkv_sum))
         low_got = halve_z(low, 2)
         gains = gains + after(gains_got, low)
-        gains_got = swap(gains, "dp", 1)
+        gains_got = swap(gains, "gy", 2)
         high = add(kept_z(high, 2), after(high_got, gains))
         high_got = swap(high, "dp", 2)
         qkv_sum = add(qkv_sum, after(qkv_got, high))
@@ -888,25 +960,27 @@
         low = add(kept_z(low, 2), after(low_got, qkv_sum))
         low_got = swap(low, "dp", 2)
         gains = gains + after(gains_got, low)
-        gains_got = swap(gains, "dp", 2)
-        high = ordered(high, after(high_got, gains), bit_z(2), 0)
+        gains_got = swap(gains, "dp", 1)
+        high = ordered(high, after(high_got, low), bit_z(2), 0)
         high_got = swap(high, "dp", 1)
         low = ordered(low, after(low_got, high), bit_z(2), 0)
         low_got = swap(low, "dp", 1)
+        gains = gains + after(gains_got, low)
+        gains_got = swap(gains, "dp", 2)
         at = lax.axis_index("dp")
         sum_qkv = jnp.where(
             (at == 0) | (at == 3), after(qkv_got, low), qkv_sum
         ).astype(F32)
-        gains = gains + after(gains_got, sum_qkv)
-        high = ordered(high, after(high_got, gains), bit_z(1), 0).astype(F32)
+        high = ordered(high, after(high_got, sum_qkv), bit_z(1), 0).astype(F32)
         low = ordered(low, after(low_got, high), bit_z(1), 0).astype(F32)
-        ff_sum = jnp.concatenate([low[:split], high], axis=0)
-        sum_out = low[split : split + out_rows].reshape(block, -1)
+        gains = gains + after(gains_got, low)
+        ff_sum = jnp.concatenate([low[:LOW], high[: high.shape[0] - HIGH_PAD]], axis=0)
+        sum_out = unfold(low[LOW:], block)
     return (
-        assemble(result_near, result_far),
+        result_shard,
         assemble(grad_near, grad_far),
         sum_qkv.T,
-        sum_out.T,
+        sum_out,
         ff_sum[:block],
         ff_sum[block : 2 * block],
         ff_sum[2 * block :].T,

time: 514 us -> 472 us (0.918)
  waiting for transfers between devices: 168 us -> 137 us
  other arithmetic: 26.8 us -> 20.9 us
  local copies, waits for them, and re-layouts: 43.6 us -> 37.9 us
    ppermute x45 -> x47, waiting for transfers between devices: 151 us -> 129 us  [swap(): return lax.ppermute(value, axis, [(i, i ^ by) for i in range(peers)])]
    pallas_call x0 -> x2, Pallas kernels: none -> 9.69 us  [pair_sums(): pl.pallas_call(pair_sums_kernel, grid=(width // tile,), in_specs=[block(2...]
    pallas_call x12 -> x11, Pallas kernels: 8.9 us -> 1.68 us  [add(): pl.pallas_call(add_kernel, grid=(rows // step,), in_specs=[spec, spec], o...]
    ppermute x1, waiting for transfers between devices: 6.75 us -> 0.01 us  [on_device(): qkv_got = lax.ppermute(qkv_sum, 'dp', [(1, 0), (2, 3)])]
    concatenate x3 -> x1, other arithmetic: 6.9 us -> 1.19 us  [on_device(): jnp.concatenate([low[:LOW], high[:high.shape[0] - HIGH_PAD]], axis=0)]
    another operation x2 -> x0, local copies, waits for them, and re-layouts: 5.61 us -> none  [on_device(): out_half.reshape(2, -1, wide)]
    unnamed x86 -> x96, local copies, waits for them, and re-layouts: 16.2 us -> 18.2 us
    ppermute x45 -> x47, starting transfers between devices: 40.9 us -> 41.5 us  [swap(): return lax.ppermute(value, axis, [(i, i ^ by) for i in range(peers)])]
  transfers between devices with their start and end apart: 50 -> 52, of which waited for: 20 -> 19; matrix products, arithmetic and copies ran while one was open for 9% -> 8% of each run, Pallas kernels for 42% -> 47%
where the time goes in v4:
time: 472 us; the launch traced here: 465 us
  Pallas kernels  219 us (46%)
  waiting for transfers between devices  137 us (29%)
  starting transfers between devices  49 us (10%)
  local copies, waits for them, and re-layouts  37.9 us (8%)
  other arithmetic  20.9 us (4%)
    ppermute x47, waiting for transfers between devices, swap(): return lax.ppermute(value, axis, [(i, i ^ by) for i in range(peers)])  129 us
    pallas_call x2, Pallas kernels, mlp_chunk(): pl.pallas_call(functools.partial(mlp_kernel, first), grid=(size // tile,)...  68.9 us
    pallas_call x5, Pallas kernels, call_whole(): pl.pallas_call(kernel, in_specs=[SMEM] + [VMEM] * (len(ins) - 1), out_spe...  55.5 us
    ppermute x47, starting transfers between devices, swap(): return lax.ppermute(value, axis, [(i, i ^ by) for i in range(peers)])  41.5 us
    pallas_call x1, Pallas kernels, attention_backward(): pl.pallas_call(backward_kernel, grid=(KV_HEADS,), in_specs=[pl.BlockSpec(...  38.3 us
    pallas_call x1, Pallas kernels, attention_forward(): pl.pallas_call(forward_kernel, grid=(KV_HEADS,), in_specs=[pl.BlockSpec((...  36.4 us
    unnamed x96, local copies, waits for them, and re-layouts  18.2 us
    select_n x8, other arithmetic, ordered(): jnp.where(bit == 0, jnp.concatenate([mine, theirs], axis=axis), jnp.conca...  11.7 us
  transfers between devices with their start and end apart: 52, of which 19 were waited for; matrix products, arithmetic and copies ran while one was open for 8% of the time, Pallas kernels for 47%

profile of v4, /device:TPU:0, one launch (start us, length us, event | category | flops | bytes accessed | tf_op | source)
XLA Modules:
  0.0 465.1 jit_solution(6646195956107723567)
XLA Ops:
  3.1 3.0 collective-permute-start
  6.1 1.5 collective-permute-start.1
  7.6 12.4 %collective-permute-done.refs_2_ = bf16[240,1280]{1,0:T(8,128)(2,1)S(1)} collective-permute-done((bf16[240,1280]{1,0:T(8,128)(2,1)S(1)}, bf16[240,1280]{1,0:T(8,128)(2,1)S(1)}, u32[]{:S(2)}, u32[]{:S(2)}) %collective-permute-start) | collective-permute-done | bytes 614432 | tf_op jit(solution)/shard_map/ppermute | solution.py:30
  21.5 2.5 constant_dynamic-slice_fusion.15
  24.4 2.0 constant_dynamic-slice_fusion.16
  26.5 1.5 collective-permute-start.7
  28.3 18.3 %collective-permute-done.2 = bf16[240,2048]{1,0:T(8,128)(2,1)} collective-permute-done((bf16[240,2048]{1,0:T(8,128)(2,1)}, bf16[240,2048]{1,0:T(8,128)(2,1)}, u32[]{:S(2)}, u32[]{:S(2)}) %collective-permute-start.2) | collective-permute-done | bytes 983072 | tf_op jit(solution)/shard_map/ppermute | solution.py:30
  46.5 2.0 constant_dynamic-slice_fusion.13
  57.2 10.5 %project.1 = (bf16[960,1024]{1,0:T(8,128)(2,1)}, bf16[960,1024]{1,0:T(8,128)(2,1)}, bf16[960,1024]{1,0:T(8,128)(2,1)}, bf16[5,128,1024]{2,1,0:T(8,128)(2,1)}, bf16[5,128,512]{2,1,0:T(8,128)(2,1)}) custom-call(s32[1]{0:T(128)} %bitcast.flip_ref, bf16[240,1024]{1,0:T(8,128)(2,1)} %get-tuple-element.188.near_ref, ...), custom_call_target="tpu_custom_call" | custom-call | flops 1000 | bytes 1000 | tf_op jit(solution)/shard_map/project/pallas_call | solution.py:617
  69.1 1.7 collective-permute-start.9
  70.9 1.6 collective-permute-done.9.prior_ref
  73.8 36.4 %attend_forward.1 = (bf16[960,1024]{1,0:T(8,128)(2,1)S(1)}, f32[5,8,1024]{2,1,0:T(8,128)S(1)}) custom-call(s32[1,1024]{1,0:T(1,128)S(1)} %bitcast.20, bf16[960,1024]{1,0:T(8,128)(2,1)S(1)} %copy-done.2, bf16[5,128,512]{2,1,0:T(8,128)(2,1)S(1)} %collective-permute-done.9.prior_ref, bf16[5,128,1024]{2,1,0:T(8,128)(2,1)S(1)} %copy-done.3), custom_call_target="tpu_custom_call" | custom-call | flops 1000 | bytes 1000 | tf_op jit(solution)/shard_map/attend_forward/pallas_call | solution.py:319
  110.3 5.2 %collective-permute-done.12 = bf16[240,2048]{1,0:T(8,128)(2,1)S(1)} collective-permute-done((bf16[240,2048]{1,0:T(8,128)(2,1)S(1)}, bf16[240,2048]{1,0:T(8,128)(2,1)S(1)}, u32[]{:S(2)}, u32[]{:S(2)}) %collective-permute-start.12) | collective-permute-done | bytes 983072 | tf_op jit(solution)/shard_map/ppermute | solution.py:30
  115.5 1.5 collective-permute-start.17
  120.3 9.4 %branch.1 = (f32[960,1024]{1,0:T(8,128)}, bf16[960,1024]{1,0:T(8,128)(2,1)}) custom-call(s32[1]{0:T(128)} %bitcast.flip_ref, bf16[960,1024]{1,0:T(8,128)(2,1)} %get-tuple-element.94.x_ref, f32[960,1]{1,0:T(8,128)} %copy.24.gain_ref, bf16[960,1024]{1,0:T(8,128)(2,1)} %copy-done, bf16[240,1280]{1,0:T(8,128)(2,1)} %copy-done.23, bf16[240,1280]{1,0:T(8,128)(2,1)} %copy-done.27, ...), custom_call_target="tpu_custom_call" | custom-call | flops 1000 | bytes 1000 | tf_op jit(solution)/shard_map/branch/pallas_call | solution.py:617
  132.6 34.3 %feed_forward.2 = (f32[960,1024]{1,0:T(8,128)}, f32[960,1024]{1,0:T(8,128)}, bf16[2,720,1280]{2,1,0:T(8,128)(2,1)}, bf16[2,720,1280]{2,1,0:T(8,128)(2,1)}) custom-call(bf16[960,1024]{1,0:T(8,128)(2,1)} %get-tuple-element.99.refs_0_, bf16[960,1024]{1,0:T(8,128)(2,1)} %pad_maximum_fusion.refs_1_.up_ref, f32[960,1024]{1,0:T(8,128)} %get-tuple-element.103.refs_2_.middle_ref, ...), custom_call_target="tpu_custom_call" | custom-call | flops 1000 | bytes 1000 | tf_op jit(solution)/shard_map/feed_forward/pallas_call | solution.py:519
  167.5 4.0 collective-permute-done.18.refs_7_
  172.8 34.6 %feed_forward.3 = (bf16[480,1024]{1,0:T(8,128)(2,1)}, bf16[480,1024]{1,0:T(8,128)(2,1)}, f32[960,1024]{1,0:T(8,128)}, bf16[2,720,1280]{2,1,0:T(8,128)(2,1)}, bf16[2,720,1280]{2,1,0:T(8,128)(2,1)}) custom-call(bf16[960,1024]{1,0:T(8,128)(2,1)} %get-tuple-element.99.refs_0_, bf16[960,1024]{1,0:T(8,128)(2,1)} %pad_maximum_fusion.refs_1_.up_ref, ...), custom_call_target="tpu_custom_call" | custom-call | flops 1000 | bytes 1000 | tf_op jit(solution)/shard_map/feed_forward/pallas_call | solution.py:519
  209.2 6.4 %collective-permute-done.19 = bf16[480,1024]{1,0:T(8,128)(2,1)} collective-permute-done((bf16[480,1024]{1,0:T(8,128)(2,1)}, bf16[480,1024]{1,0:T(8,128)(2,1)}, u32[]{:S(2)}, u32[]{:S(2)}) %collective-permute-start.19) | collective-permute-done | bytes 983072 | tf_op jit(solution)/shard_map/ppermute | solution.py:30
  220.3 13.6 %branch_back.1 = (f32[960,1024]{1,0:T(8,128)}, bf16[960,1024]{1,0:T(8,128)(2,1)}, f32[960,1]{1,0:T(8,128)}, bf16[2,2,96,1280]{3,2,1,0:T(8,128)(2,1)}, bf16[2,96,...) custom-call(s32[1]{0:T(128)} %bitcast.flip_ref, f32[960,1024]{1,0:T(8,128)} %get-tuple-element.114.grad_ref, ...), custom_call_target="tpu_custom_call" | custom-call | flops 1000 | bytes 1000 | tf_op jit(solution)/shard_map/branch_back/pallas_call | solution.py:617
  234.5 1.7 collective-permute-done.22.out_got_ref
  237.4 2.0 copy-done.6
  239.4 4.5 pair_sums.2
  246.1 5.2 %pair_sums.3 = (bf16[2,448,1280]{2,1,0:T(8,128)(2,1)}, bf16[384,1280]{1,0:T(8,128)(2,1)S(1)}, bf16[384,1280]{1,0:T(8,128)(2,1)S(1)}) custom-call(bf16[2,720,1280]{2,1,0:T(8,128)(2,1)S(1)} %copy-done.7, bf16[2,720,1280]{2,1,0:T(8,128)(2,1)} %collective-permute-done.23.got_ref, bf16[2,2,96,1280]{3,2,1,0:T(8,128)(2,1)S(1)} %copy-done.5, ...), custom_call_target="tpu_custom_call" | custom-call | flops 1000 | bytes 1000 | tf_op jit(solution)/shard_map/pair_sums/pallas_call | solution.py:225
  253.6 3.8 maximum_select_fusion
  257.4 38.3 %attend_backward.1 = (bf16[960,1024]{1,0:T(8,128)(2,1)S(1)}, bf16[5,128,512]{2,1,0:T(8,128)(2,1)S(1)}, f32[5,128,1024]{2,1,0:T(8,128)}) custom-call(s32[1,1024]{1,0:T(1,128)S(1)} %bitcast.21, f32[32,1024]{1,0:T(8,128)S(1)} %copy-done.9, f32[32,1024]{1,0:T(8,128)S(1)} %copy-done.8, bf16[960,1024]{1,0:T(8,128)(2,1)S(1)} %copy-done.2, ...), custom_call_target="tpu_custom_call" | custom-call | flops 1000 | bytes 1000 | tf_op jit(solution)/shard_map/attend_backward/pallas_call | solution.py:418
  301.9 9.1 %qkv_grad.1 = (bf16[1600,1024]{1,0:T(8,128)(2,1)}, bf16[2,2,800,240]{3,2,1,0:T(8,128)(2,1)}, bf16[2,2,800,240]{3,2,1,0:T(8,128)(2,1)}) custom-call(s32[1]{0:T(128)} %bitcast.flip_ref, bf16[960,1024]{1,0:T(8,128)(2,1)} %get-tuple-element.111.normed_ref, bf16[960,1024]{1,0:T(8,128)(2,1)} %copy-done.10, f32[5,128,1024]{2,1,0:T(8,128)} %get-tuple-element.132.own_ref, ...), custom_call_target="tpu_custom_call" | custom-call | flops 1000 | bytes 1000 | tf_op jit(solution)/shard_map/qkv_grad/pallas_call | solution.py:617
  313.5 1.8 add_pair.3
  316.4 3.5 add_pair.4
  322.2 12.9 %input_grad.1 = (bf16[480,1024]{1,0:T(8,128)(2,1)}, bf16[480,1024]{1,0:T(8,128)(2,1)}, f32[960,1]{1,0:T(8,128)}) custom-call(s32[1]{0:T(128)} %bitcast.flip_ref, bf16[1600,1024]{1,0:T(8,128)(2,1)} %get-tuple-element.143.grads_ref, bf16[960,1024]{1,0:T(8,128)(2,1)} %get-tuple-element.94.x_ref, f32[960,1]{1,0:T(8,128)} %copy.23.gain_ref, ...), custom_call_target="tpu_custom_call" | custom-call | flops 1000 | bytes 1000 | tf_op jit(solution)/shard_map/input_grad/pallas_call | solution.py:617
  337.1 5.1 %collective-permute-done.32.right_ref = bf16[2,800,240]{2,1,0:T(8,128)(2,1)} collective-permute-done((bf16[2,800,240]{2,1,0:T(8,128)(2,1)}, bf16[2,800,240]{2,1,0:T(8,128)(2,1)}, u32[]{:S(2)}, u32[]{:S(2)}) %collective-permute-start.32) | collective-permute-done | bytes 768032 | tf_op jit(solution)/shard_map/ppermute | solution.py:30
  342.2 3.0 add_pair.5
  346.6 1.7 collective-permute-start.42
  349.8 12.4 %collective-permute-done.35.right_ref = bf16[384,1280]{1,0:T(8,128)(2,1)S(1)} collective-permute-done((bf16[384,1280]{1,0:T(8,128)(2,1)}, bf16[384,1280]{1,0:T(8,128)(2,1)S(1)}, u32[]{:S(2)}, u32[]{:S(2)}) %collective-permute-start.35) | collective-permute-done | bytes 983072 | tf_op jit(solution)/shard_map/ppermute | solution.py:30
  362.6 1.8 collective-permute-start.37
  368.5 2.5 collective-permute-start.36
  371.1 4.9 %collective-permute-done.37.right_ref = bf16[192,1280]{1,0:T(8,128)(2,1)S(1)} collective-permute-done((bf16[192,1280]{1,0:T(8,128)(2,1)S(1)}, bf16[192,1280]{1,0:T(8,128)(2,1)S(1)}, u32[]{:S(2)}, u32[]{:S(2)}) %collective-permute-start.37) | collective-permute-done | bytes 491552 | tf_op jit(solution)/shard_map/ppermute | solution.py:30
  376.2 3.7 collective-permute-start.40
  379.9 4.9 %collective-permute-done.36.right_ref = bf16[800,240]{1,0:T(8,128)(2,1)S(1)} collective-permute-done((bf16[800,240]{1,0:T(8,128)(2,1)S(1)}, bf16[800,240]{1,0:T(8,128)(2,1)S(1)}, u32[]{:S(2)}, u32[]{:S(2)}) %collective-permute-start.36) | collective-permute-done | bytes 384032 | tf_op jit(solution)/shard_map/ppermute | solution.py:945
  385.8 5.2 %collective-permute-start.44 = (bf16[112,1280]{1,0:T(8,128)(2,1)S(1)}, bf16[112,1280]{1,0:T(8,128)(2,1)S(1)}, u32[]{:S(2)}, u32[]{:S(2)}) collective-permute-start(bf16[112,1280]{1,0:T(8,128)(2,1)S(1)} %get-tuple-element.207), channel_id=1, source_target_pairs={{0,16},{8,24},{16,0},{24,8},{1,17},{9,25},{17,1},{25,9},{2,18},{10... | collective-permute-start | bytes 860168 | tf_op jit(solution)/shard_map/ppermute | solution.py:30
  394.9 23.0 %collective-permute-done.44.right_ref = bf16[112,1280]{1,0:T(8,128)(2,1)S(1)} collective-permute-done((bf16[112,1280]{1,0:T(8,128)(2,1)S(1)}, bf16[112,1280]{1,0:T(8,128)(2,1)S(1)}, u32[]{:S(2)}, u32[]{:S(2)}) %collective-permute-start.44) | collective-permute-done | bytes 286752 | tf_op jit(solution)/shard_map/ppermute | solution.py:30
  418.1 1.8 collective-permute-start.50
  419.9 9.5 %collective-permute-done.46 = bf16[96,1280]{1,0:T(8,128)(2,1)S(1)} collective-permute-done((bf16[96,1280]{1,0:T(8,128)(2,1)S(1)}, bf16[96,1280]{1,0:T(8,128)(2,1)S(1)}, u32[]{:S(2)}, u32[]{:S(2)}) %collective-permute-start.46) | collective-permute-done | bytes 245792 | tf_op jit(solution)/shard_map/ppermute | solution.py:30
  429.5 3.5 maximum_select_fusion.1
  433.0 2.4 collective-permute-done.45
  435.6 2.5 collective-permute-done.50
  439.1 9.7 %collective-permute-done.48 = bf16[192,1280]{1,0:T(8,128)(2,1)S(1)} collective-permute-done((bf16[192,1280]{1,0:T(8,128)(2,1)S(1)}, bf16[192,1280]{1,0:T(8,128)(2,1)S(1)}, u32[]{:S(2)}, u32[]{:S(2)}) %collective-permute-start.48) | collective-permute-done | bytes 491552 | tf_op jit(solution)/shard_map/ppermute | solution.py:30
  450.8 10.3 %collective-permute-done.47 = bf16[224,1280]{1,0:T(8,128)(2,1)S(1)} collective-permute-done((bf16[224,1280]{1,0:T(8,128)(2,1)S(1)}, bf16[224,1280]{1,0:T(8,128)(2,1)S(1)}, u32[]{:S(2)}, u32[]{:S(2)}) %collective-permute-start.47) | collective-permute-done | bytes 573472 | tf_op jit(solution)/shard_map/ppermute | solution.py:30
  (234 shorter events, 70.0 us)
Async XLA Ops:
  3.1 16.9 %collective-permute-start = (bf16[240,1280]{1,0:T(8,128)(2,1)S(1)}, bf16[240,1280]{1,0:T(8,128)(2,1)S(1)}, u32[]{:S(2)}, u32[]{:S(2)}) collective-permute-start(bf16[240,1280]{1,0:T(8,128)(2,1)S(1)} %pad_maximum_fusion.5.refs_0_), channel_id=1, source_target_pairs={{0,2},{1,3},{2,0},{3,1},{4,6},{5,7},{6,4},{7,5},{8,10},{9,11},{10,... | collective-permute-start | bytes 1843208 | tf_op jit(solution)/shard_map/ppermute | solution.py:30
  6.1 15.3 %collective-permute-start.1 = (bf16[240,1280]{1,0:T(8,128)(2,1)S(1)}, bf16[240,1280]{1,0:T(8,128)(2,1)S(1)}, u32[]{:S(2)}, u32[]{:S(2)}) collective-permute-start(bf16[240,1280]{1,0:T(8,128)(2,1)S(1)} %pad_maximum_fusion.5.refs_0_), channel_id=1, source_target_pairs={{0,4},{4,0},{1,5},{5,1},{2,6},{6,2},{3,7},{7,3},{8,12},{12,8},{9,1... | collective-permute-start | bytes 1843208 | tf_op jit(solution)/shard_map/ppermute | solution.py:30
  23.9 22.6 %collective-permute-start.2 = (bf16[240,2048]{1,0:T(8,128)(2,1)}, bf16[240,2048]{1,0:T(8,128)(2,1)}, u32[]{:S(2)}, u32[]{:S(2)}) collective-permute-start(bf16[240,2048]{1,0:T(8,128)(2,1)} %constant_dynamic-slice_fusion.15), channel_id=1, source_target_pairs={{0,2},{1,3},{2,0},{3,1},{4,6},{5,7},{6,4},{7,5},{8,10},{9,11},{10,... | collective-permute-start | bytes 2949128 | tf_op jit(solution)/shard_map/ppermute | solution.py:30
  24.4 27.2 %collective-permute-start.4 = (bf16[240,1280]{1,0:T(8,128)(2,1)S(1)}, bf16[240,1280]{1,0:T(8,128)(2,1)S(1)}, u32[]{:S(2)}, u32[]{:S(2)}) collective-permute-start(bf16[240,1280]{1,0:T(8,128)(2,1)S(1)} %pad_maximum_fusion.5.refs_0_), channel_id=1, source_target_pairs={{0,1},{1,0},{2,3},{3,2},{4,5},{5,4},{6,7},{7,6},{8,9},{9,8},{10,11... | collective-permute-start | bytes 1843208 | tf_op jit(solution)/shard_map/ppermute | solution.py:30
  26.5 25.1 %collective-permute-start.7 = (bf16[240,1280]{1,0:T(8,128)(2,1)S(1)}, bf16[240,1280]{1,0:T(8,128)(2,1)S(1)}, u32[]{:S(2)}, u32[]{:S(2)}) collective-permute-start(bf16[240,1280]{1,0:T(8,128)(2,1)S(1)} %collective-permute-done.refs_2_), channel_id=1, source_target_pairs={{0,4},{4,0},{1,5},{5,1},{2,6},{6,2},{3,7},{7,3},{8,12},{12,8},{9,1... | collective-permute-start | bytes 1843208 | tf_op jit(solution)/shard_map/ppermute | solution.py:30
  28.0 24.4 %collective-permute-start.5 = (bf16[240,1280]{1,0:T(8,128)(2,1)S(1)}, bf16[240,1280]{1,0:T(8,128)(2,1)S(1)}, u32[]{:S(2)}, u32[]{:S(2)}) collective-permute-start(bf16[240,1280]{1,0:T(8,128)(2,1)S(1)} %collective-permute-done.refs_2_), channel_id=1, source_target_pairs={{0,1},{1,0},{2,3},{3,2},{4,5},{5,4},{6,7},{7,6},{8,9},{9,8},{10,11... | collective-permute-start | bytes 1843208 | tf_op jit(solution)/shard_map/ppermute | solution.py:30
  49.6 7.6 %collective-permute-start.3 = (bf16[480,1024]{1,0:T(8,128)(2,1)}, bf16[480,1024]{1,0:T(8,128)(2,1)}, u32[]{:S(2)}, u32[]{:S(2)}) collective-permute-start(bf16[480,1024]{1,0:T(8,128)(2,1)} %pad_maximum_fusion.3), channel_id=1, source_target_pairs={{0,1},{1,0},{2,3},{3,2},{4,5},{5,4},{6,7},{7,6},{8,9},{9,8},{10,11... | collective-permute-start | bytes 2949128 | tf_op jit(solution)/shard_map/ppermute | solution.py:30
  51.0 6.1 %collective-permute-start.6 = (bf16[240,1280]{1,0:T(8,128)(2,1)S(1)}, bf16[240,1280]{1,0:T(8,128)(2,1)}, u32[]{:S(2)}, u32[]{:S(2)}) collective-permute-start(bf16[240,1280]{1,0:T(8,128)(2,1)S(1)} %collective-permute-done.1.refs_4_), channel_id=1, source_target_pairs={{0,1},{1,0},{2,3},{3,2},{4,5},{5,4},{6,7},{7,6},{8,9},{9,8},{10,11... | collective-permute-start | bytes 1843208 | tf_op jit(solution)/shard_map/ppermute | solution.py:30
  51.5 5.6 %collective-permute-start.8 = (bf16[240,1280]{1,0:T(8,128)(2,1)S(1)}, bf16[240,1280]{1,0:T(8,128)(2,1)}, u32[]{:S(2)}, u32[]{:S(2)}) collective-permute-start(bf16[240,1280]{1,0:T(8,128)(2,1)S(1)} %collective-permute-done.7.refs_6_), channel_id=1, source_target_pairs={{0,1},{1,0},{2,3},{3,2},{4,5},{5,4},{6,7},{7,6},{8,9},{9,8},{10,11... | collective-permute-start | bytes 1843208 | tf_op jit(solution)/shard_map/ppermute | solution.py:30
  51.6 58.6 %collective-permute-start.10 = (bf16[720,1280]{1,0:T(8,128)(2,1)}, bf16[720,1280]{1,0:T(8,128)(2,1)}, u32[]{:S(2)}, u32[]{:S(2)}) collective-permute-start(bf16[720,1280]{1,0:T(8,128)(2,1)} %pad_maximum_fusion.1.refs_3_), channel_id=1, source_target_pairs={{0,2},{1,3},{2,0},{3,1},{4,6},{5,7},{6,4},{7,5},{8,10},{9,11},{10,... | collective-permute-start | bytes 5529608 | tf_op jit(solution)/shard_map/ppermute | solution.py:30
  53.3 57.0 %collective-permute-start.11 = (bf16[720,1280]{1,0:T(8,128)(2,1)}, bf16[720,1280]{1,0:T(8,128)(2,1)}, u32[]{:S(2)}, u32[]{:S(2)}) collective-permute-start(bf16[720,1280]{1,0:T(8,128)(2,1)} %pad_maximum_fusion.1.refs_3_), channel_id=1, source_target_pairs={{0,4},{4,0},{1,5},{5,1},{2,6},{6,2},{3,7},{7,3},{8,12},{12,8},{9,1... | collective-permute-start | bytes 5529608 | tf_op jit(solution)/shard_map/ppermute | solution.py:30
  67.8 47.6 %collective-permute-start.12 = (bf16[240,2048]{1,0:T(8,128)(2,1)S(1)}, bf16[240,2048]{1,0:T(8,128)(2,1)S(1)}, u32[]{:S(2)}, u32[]{:S(2)}) collective-permute-start(bf16[240,2048]{1,0:T(8,128)(2,1)S(1)} %constant_dynamic-slice_fusion.10), channel_id=1, source_target_pairs={{0,2},{1,3},{2,0},{3,1},{4,6},{5,7},{6,4},{7,5},{8,10},{9,11},{10,... | collective-permute-start | bytes 2949128 | tf_op jit(solution)/shard_map/ppermute | solution.py:30
  70.8 61.8 %collective-permute-start.14 = (bf16[720,1280]{1,0:T(8,128)(2,1)}, bf16[720,1280]{1,0:T(8,128)(2,1)}, u32[]{:S(2)}, u32[]{:S(2)}) collective-permute-start(bf16[720,1280]{1,0:T(8,128)(2,1)} %pad_maximum_fusion.1.refs_3_), channel_id=1, source_target_pairs={{0,1},{1,0},{2,3},{3,2},{4,5},{5,4},{6,7},{7,6},{8,9},{9,8},{10,11... | collective-permute-start | bytes 5529608 | tf_op jit(solution)/shard_map/ppermute | solution.py:30
  115.5 17.2 %collective-permute-start.15 = (bf16[720,1280]{1,0:T(8,128)(2,1)}, bf16[720,1280]{1,0:T(8,128)(2,1)}, u32[]{:S(2)}, u32[]{:S(2)}) collective-permute-start(bf16[720,1280]{1,0:T(8,128)(2,1)} %collective-permute-done.10.refs_5_), channel_id=1, source_target_pairs={{0,1},{1,0},{2,3},{3,2},{4,5},{5,4},{6,7},{7,6},{8,9},{9,8},{10,11... | collective-permute-start | bytes 5529608 | tf_op jit(solution)/shard_map/ppermute | solution.py:30
  115.5 51.5 %collective-permute-start.17 = (bf16[720,1280]{1,0:T(8,128)(2,1)}, bf16[720,1280]{1,0:T(8,128)(2,1)}, u32[]{:S(2)}, u32[]{:S(2)}) collective-permute-start(bf16[720,1280]{1,0:T(8,128)(2,1)} %collective-permute-done.10.refs_5_), channel_id=1, source_target_pairs={{0,4},{4,0},{1,5},{5,1},{2,6},{6,2},{3,7},{7,3},{8,12},{12,8},{9,1... | collective-permute-start | bytes 5529608 | tf_op jit(solution)/shard_map/ppermute | solution.py:30
  118.9 11.0 %collective-permute-start.13 = (bf16[480,1024]{1,0:T(8,128)(2,1)}, bf16[480,1024]{1,0:T(8,128)(2,1)}, u32[]{:S(2)}, u32[]{:S(2)}) collective-permute-start(bf16[480,1024]{1,0:T(8,128)(2,1)} %pad_maximum_fusion.4), channel_id=1, source_target_pairs={{0,1},{1,0},{2,3},{3,2},{4,5},{5,4},{6,7},{7,6},{8,9},{9,8},{10,11... | collective-permute-start | bytes 2949128 | tf_op jit(solution)/shard_map/ppermute | solution.py:30
  129.7 37.9 %collective-permute-start.16 = (bf16[720,1280]{1,0:T(8,128)(2,1)}, bf16[720,1280]{1,0:T(8,128)(2,1)S(1)}, u32[]{:S(2)}, u32[]{:S(2)}) collective-permute-start(bf16[720,1280]{1,0:T(8,128)(2,1)} %collective-permute-done.11.refs_4_), channel_id=1, source_target_pairs={{0,1},{1,0},{2,3},{3,2},{4,5},{5,4},{6,7},{7,6},{8,9},{9,8},{10,11... | collective-permute-start | bytes 5529608 | tf_op jit(solution)/shard_map/ppermute | solution.py:30
  167.2 69.0 %collective-permute-start.21 = (bf16[2,720,1280]{2,1,0:T(8,128)(2,1)}, bf16[2,720,1280]{2,1,0:T(8,128)(2,1)}, u32[]{:S(2)}, u32[]{:S(2)}) collective-permute-start(bf16[2,720,1280]{2,1,0:T(8,128)(2,1)} %get-tuple-element.117), channel_id=1, source_target_pairs={{0,1},{1,0},{2,3},{3,2},{4,5},{5,4},{6,7},{7,6},{8,9},{9,8},{10,11... | collective-permute-start | bytes 11059208 | tf_op jit(solution)/shard_map/ppermute | solution.py:30
  207.4 38.7 %collective-permute-start.23 = (bf16[2,720,1280]{2,1,0:T(8,128)(2,1)}, bf16[2,720,1280]{2,1,0:T(8,128)(2,1)}, u32[]{:S(2)}, u32[]{:S(2)}) collective-permute-start(bf16[2,720,1280]{2,1,0:T(8,128)(2,1)} %get-tuple-element.122), channel_id=1, source_target_pairs={{0,1},{1,0},{2,3},{3,2},{4,5},{5,4},{6,7},{7,6},{8,9},{9,8},{10,11... | collective-permute-start | bytes 11059208 | tf_op jit(solution)/shard_map/ppermute | solution.py:30
  207.6 8.0 %collective-permute-start.19 = (bf16[480,1024]{1,0:T(8,128)(2,1)}, bf16[480,1024]{1,0:T(8,128)(2,1)}, u32[]{:S(2)}, u32[]{:S(2)}) collective-permute-start(bf16[480,1024]{1,0:T(8,128)(2,1)} %get-tuple-element.110), channel_id=1, source_target_pairs={{0,1},{1,0},{2,3},{3,2},{4,5},{5,4},{6,7},{7,6},{8,9},{9,8},{10,11... | collective-permute-start | bytes 2949128 | tf_op jit(solution)/shard_map/ppermute | solution.py:30
  218.2 35.4 %collective-permute-start.20 = (bf16[240,2048]{1,0:T(8,128)(2,1)}, bf16[240,2048]{1,0:T(8,128)(2,1)}, u32[]{:S(2)}, u32[]{:S(2)}) collective-permute-start(bf16[240,2048]{1,0:T(8,128)(2,1)} %maximum_select_fusion.4), channel_id=1, source_target_pairs={{0,2},{1,3},{2,0},{3,1},{4,6},{5,7},{6,4},{7,5},{8,10},{9,11},{10,... | collective-permute-start | bytes 2949128 | tf_op jit(solution)/shard_map/ppermute | solution.py:30
  234.0 12.1 %collective-permute-start.24 = (bf16[2,96,1280]{2,1,0:T(8,128)(2,1)}, bf16[2,96,1280]{2,1,0:T(8,128)(2,1)S(1)}, u32[]{:S(2)}, u32[]{:S(2)}) collective-permute-start(bf16[2,96,1280]{2,1,0:T(8,128)(2,1)} %get-tuple-element.123), channel_id=1, source_target_pairs={{0,1},{1,0},{2,3},{3,2},{4,5},{5,4},{6,7},{7,6},{8,9},{9,8},{10,11... | collective-permute-start | bytes 1474568 | tf_op jit(solution)/shard_map/ppermute | solution.py:30
  244.8 53.5 %collective-permute-start.25 = (bf16[384,1280]{1,0:T(8,128)(2,1)S(1)}, bf16[384,1280]{1,0:T(8,128)(2,1)S(1)}, u32[]{:S(2)}, u32[]{:S(2)}) collective-permute-start(bf16[384,1280]{1,0:T(8,128)(2,1)S(1)} %get-tuple-element.127), channel_id=1, source_target_pairs={{0,2},{1,3},{2,0},{3,1},{4,6},{5,7},{6,4},{7,5},{8,10},{9,11},{10,... | collective-permute-start | bytes 2949128 | tf_op jit(solution)/shard_map/ppermute | solution.py:30
  252.3 47.1 %collective-permute-start.26 = (bf16[384,1280]{1,0:T(8,128)(2,1)S(1)}, bf16[384,1280]{1,0:T(8,128)(2,1)S(1)}, u32[]{:S(2)}, u32[]{:S(2)}) collective-permute-start(bf16[384,1280]{1,0:T(8,128)(2,1)S(1)} %get-tuple-element.128), channel_id=1, source_target_pairs={{0,2},{1,3},{2,0},{3,1},{4,6},{5,7},{6,4},{7,5},{8,10},{9,11},{10,... | collective-permute-start | bytes 2949128 | tf_op jit(solution)/shard_map/ppermute | solution.py:30
  253.1 60.3 %collective-permute-start.29 = (bf16[2,448,1280]{2,1,0:T(8,128)(2,1)}, bf16[2,448,1280]{2,1,0:T(8,128)(2,1)S(1)}, u32[]{:S(2)}, u32[]{:S(2)}) collective-permute-start(bf16[2,448,1280]{2,1,0:T(8,128)(2,1)} %get-tuple-element.124), channel_id=1, source_target_pairs={{0,4},{4,0},{1,5},{5,1},{2,6},{6,2},{3,7},{7,3},{8,12},{12,8},{9,1... | collective-permute-start | bytes 6881288 | tf_op jit(solution)/shard_map/ppermute | solution.py:30
  311.0 5.4 %collective-permute-start.28 = (bf16[2,2,800,240]{3,2,1,0:T(8,128)(2,1)}, bf16[2,2,800,240]{3,2,1,0:T(8,128)(2,1)S(1)}, u32[]{:S(2)}, u32[]{:S(2)}) collective-permute-start(bf16[2,2,800,240]{3,2,1,0:T(8,128)(2,1)} %get-tuple-element.136), channel_id=1, source_target_pairs={{0,1},{1,0},{2,3},{3,2},{4,5},{5,4},{6,7},{7,6},{8,9},{9,8},{10,11... | collective-permute-start | bytes 4608008 | tf_op jit(solution)/shard_map/ppermute | solution.py:30
  315.3 30.9 %collective-permute-start.31 = (bf16[448,1280]{1,0:T(8,128)(2,1)}, bf16[448,1280]{1,0:T(8,128)(2,1)S(1)}, u32[]{:S(2)}, u32[]{:S(2)}) collective-permute-start(bf16[448,1280]{1,0:T(8,128)(2,1)} %get-tuple-element.147), channel_id=1, source_target_pairs={{0,2},{1,3},{2,0},{3,1},{4,6},{5,7},{6,4},{7,5},{8,10},{9,11},{10,... | collective-permute-start | bytes 3440648 | tf_op jit(solution)/shard_map/ppermute | solution.py:30
  320.8 21.4 %collective-permute-start.32 = (bf16[2,800,240]{2,1,0:T(8,128)(2,1)}, bf16[2,800,240]{2,1,0:T(8,128)(2,1)}, u32[]{:S(2)}, u32[]{:S(2)}) collective-permute-start(bf16[2,800,240]{2,1,0:T(8,128)(2,1)} %bitcast.9), channel_id=1, source_target_pairs={{0,4},{4,0},{1,5},{5,1},{2,6},{6,2},{3,7},{7,3},{8,12},{12,8},{9,1... | collective-permute-start | bytes 2304008 | tf_op jit(solution)/shard_map/ppermute | solution.py:30
  335.2 13.0 %collective-permute-start.30 = (bf16[480,1024]{1,0:T(8,128)(2,1)}, bf16[480,1024]{1,0:T(8,128)(2,1)}, u32[]{:S(2)}, u32[]{:S(2)}) collective-permute-start(bf16[480,1024]{1,0:T(8,128)(2,1)} %get-tuple-element.146), channel_id=1, source_target_pairs={{0,1},{1,0},{2,3},{3,2},{4,5},{5,4},{6,7},{7,6},{8,9},{9,8},{10,11... | collective-permute-start | bytes 2949128 | tf_op jit(solution)/shard_map/ppermute | solution.py:30
  335.2 27.1 %collective-permute-start.35 = (bf16[384,1280]{1,0:T(8,128)(2,1)}, bf16[384,1280]{1,0:T(8,128)(2,1)S(1)}, u32[]{:S(2)}, u32[]{:S(2)}) collective-permute-start(bf16[384,1280]{1,0:T(8,128)(2,1)} %copy-done.12), channel_id=1, source_target_pairs={{0,4},{4,0},{1,5},{5,1},{2,6},{6,2},{3,7},{7,3},{8,12},{12,8},{9,1... | collective-permute-start | bytes 2949128 | tf_op jit(solution)/shard_map/ppermute | solution.py:30
  345.2 23.2 %collective-permute-start.34 = (bf16[800,240]{1,0:T(8,128)(2,1)S(1)}, bf16[800,240]{1,0:T(8,128)(2,1)S(1)}, u32[]{:S(2)}, u32[]{:S(2)}) collective-permute-start(bf16[800,240]{1,0:T(8,128)(2,1)S(1)} %get-tuple-element.153), channel_id=1, source_target_pairs={{0,2},{1,3},{2,0},{3,1},{4,6},{5,7},{6,4},{7,5},{8,10},{9,11},{10,... | collective-permute-start | bytes 1152008 | tf_op jit(solution)/shard_map/ppermute | solution.py:30
  346.6 39.1 %collective-permute-start.42 = (bf16[224,1280]{1,0:T(8,128)(2,1)S(1)}, bf16[224,1280]{1,0:T(8,128)(2,1)S(1)}, u32[]{:S(2)}, u32[]{:S(2)}) collective-permute-start(bf16[224,1280]{1,0:T(8,128)(2,1)S(1)} %get-tuple-element.189), channel_id=1, source_target_pairs={{0,8},{8,0},{16,24},{24,16},{1,9},{9,1},{17,25},{25,17},{2,10},{10... | collective-permute-start | bytes 1720328 | tf_op jit(solution)/shard_map/ppermute | solution.py:30
  362.6 13.4 %collective-permute-start.37 = (bf16[192,1280]{1,0:T(8,128)(2,1)S(1)}, bf16[192,1280]{1,0:T(8,128)(2,1)S(1)}, u32[]{:S(2)}, u32[]{:S(2)}) collective-permute-start(bf16[192,1280]{1,0:T(8,128)(2,1)S(1)} %get-tuple-element.191), channel_id=1, source_target_pairs={{0,8},{8,0},{16,24},{24,16},{1,9},{9,1},{17,25},{25,17},{2,10},{10... | collective-permute-start | bytes 1474568 | tf_op jit(solution)/shard_map/ppermute | solution.py:30
  364.9 6.1 %collective-permute-start.38 = (f32[2,960]{1,0:T(2,128)S(1)}, f32[2,960]{1,0:T(2,128)S(1)}, u32[]{:S(2)}, u32[]{:S(2)}) collective-permute-start(f32[2,960]{1,0:T(2,128)S(1)} %pad_maximum_fusion.6), channel_id=1, source_target_pairs={{0,4},{4,0},{1,5},{5,1},{2,6},{6,2},{3,7},{7,3},{8,12},{12,8},{9,1... | collective-permute-start | bytes 23048 | tf_op jit(solution)/shard_map/ppermute | solution.py:30
  367.6 61.9 %collective-permute-start.33 = (bf16[240,2048]{1,0:T(8,128)(2,1)}, bf16[240,2048]{1,0:T(8,128)(2,1)}, u32[]{:S(2)}, u32[]{:S(2)}) collective-permute-start(bf16[240,2048]{1,0:T(8,128)(2,1)} %maximum_select_fusion.6), channel_id=1, source_target_pairs={{0,2},{1,3},{2,0},{3,1},{4,6},{5,7},{6,4},{7,5},{8,10},{9,11},{10,... | collective-permute-start | bytes 2949128 | tf_op jit(solution)/shard_map/ppermute | solution.py:30
  368.5 16.3 %collective-permute-start.36 = (bf16[800,240]{1,0:T(8,128)(2,1)S(1)}, bf16[800,240]{1,0:T(8,128)(2,1)S(1)}, u32[]{:S(2)}, u32[]{:S(2)}) collective-permute-start(bf16[800,240]{1,0:T(8,128)(2,1)S(1)} %add.194.left_ref), channel_id=1, source_target_pairs={{0,8},{24,16},{1,9},{25,17},{2,10},{26,18},{3,11},{27,19},{4,12},{... | collective-permute-start | bytes 1152008 | tf_op jit(solution)/shard_map/ppermute | solution.py:945
  371.1 20.0 %collective-permute-start.41 = (f32[2,960]{1,0:T(2,128)S(1)}, f32[2,960]{1,0:T(2,128)S(1)}, u32[]{:S(2)}, u32[]{:S(2)}) collective-permute-start(f32[2,960]{1,0:T(2,128)S(1)} %fusion.2), channel_id=1, source_target_pairs={{0,1},{1,0},{2,3},{3,2},{4,5},{5,4},{6,7},{7,6},{8,9},{9,8},{10,11... | collective-permute-start | bytes 23048 | tf_op jit(solution)/shard_map/ppermute | solution.py:30
  376.2 14.9 %collective-permute-start.40 = (bf16[96,1280]{1,0:T(8,128)(2,1)S(1)}, bf16[96,1280]{1,0:T(8,128)(2,1)S(1)}, u32[]{:S(2)}, u32[]{:S(2)}) collective-permute-start(bf16[96,1280]{1,0:T(8,128)(2,1)S(1)} %get-tuple-element.209), channel_id=1, source_target_pairs={{0,16},{8,24},{16,0},{24,8},{1,17},{9,25},{17,1},{25,9},{2,18},{10... | collective-permute-start | bytes 737288 | tf_op jit(solution)/shard_map/ppermute | solution.py:30
  384.9 8.5 %collective-permute-start.39 = (bf16[800,240]{1,0:T(8,128)(2,1)S(1)}, bf16[800,240]{1,0:T(8,128)(2,1)S(1)}, u32[]{:S(2)}, u32[]{:S(2)}) collective-permute-start(bf16[800,240]{1,0:T(8,128)(2,1)S(1)} %add.196.left_ref), channel_id=1, source_target_pairs={{8,16},{16,8},{9,17},{17,9},{10,18},{18,10},{11,19},{19,11},{12,20... | collective-permute-start | bytes 1152008 | tf_op jit(solution)/shard_map/ppermute | solution.py:951
  385.8 32.1 %collective-permute-start.44 = (bf16[112,1280]{1,0:T(8,128)(2,1)S(1)}, bf16[112,1280]{1,0:T(8,128)(2,1)S(1)}, u32[]{:S(2)}, u32[]{:S(2)}) collective-permute-start(bf16[112,1280]{1,0:T(8,128)(2,1)S(1)} %get-tuple-element.207), channel_id=1, source_target_pairs={{0,16},{8,24},{16,0},{24,8},{1,17},{9,25},{17,1},{25,9},{2,18},{10... | collective-permute-start | bytes 860168 | tf_op jit(solution)/shard_map/ppermute | solution.py:30
  391.2 38.2 %collective-permute-start.46 = (bf16[96,1280]{1,0:T(8,128)(2,1)S(1)}, bf16[96,1280]{1,0:T(8,128)(2,1)S(1)}, u32[]{:S(2)}, u32[]{:S(2)}) collective-permute-start(bf16[96,1280]{1,0:T(8,128)(2,1)S(1)} %add.198), channel_id=1, source_target_pairs={{0,16},{8,24},{16,0},{24,8},{1,17},{9,25},{17,1},{25,9},{2,18},{10... | collective-permute-start | bytes 737288 | tf_op jit(solution)/shard_map/ppermute | solution.py:30
  392.6 25.5 %collective-permute-start.49 = (f32[2,960]{1,0:T(2,128)S(1)}, f32[2,960]{1,0:T(2,128)S(1)}, u32[]{:S(2)}, u32[]{:S(2)}) collective-permute-start(f32[2,960]{1,0:T(2,128)S(1)} %fusion.11), channel_id=1, source_target_pairs={{0,2},{1,3},{2,0},{3,1},{4,6},{5,7},{6,4},{7,5},{8,10},{9,11},{10,... | collective-permute-start | bytes 23048 | tf_op jit(solution)/shard_map/ppermute | solution.py:30
  393.6 44.6 %collective-permute-start.43 = (bf16[800,240]{1,0:T(8,128)(2,1)S(1)}, bf16[800,240]{1,0:T(8,128)(2,1)S(1)}, u32[]{:S(2)}, u32[]{:S(2)}) collective-permute-start(bf16[800,240]{1,0:T(8,128)(2,1)S(1)} %add.199), channel_id=1, source_target_pairs={{8,0},{16,24},{9,1},{17,25},{10,2},{18,26},{11,3},{19,27},{12,4},{... | collective-permute-start | bytes 1152008 | tf_op jit(solution)/shard_map/ppermute | solution.py:959
  418.0 17.4 %collective-permute-start.45 = (bf16[112,1280]{1,0:T(8,128)(2,1)S(1)}, bf16[112,1280]{1,0:T(8,128)(2,1)S(1)}, u32[]{:S(2)}, u32[]{:S(2)}) collective-permute-start(bf16[112,1280]{1,0:T(8,128)(2,1)S(1)} %add.200), channel_id=1, source_target_pairs={{0,16},{8,24},{16,0},{24,8},{1,17},{9,25},{17,1},{25,9},{2,18},{10... | collective-permute-start | bytes 860168 | tf_op jit(solution)/shard_map/ppermute | solution.py:30
  418.1 20.1 %collective-permute-start.50 = (f32[2,960]{1,0:T(2,128)S(1)}, f32[2,960]{1,0:T(2,128)S(1)}, u32[]{:S(2)}, u32[]{:S(2)}) collective-permute-start(f32[2,960]{1,0:T(2,128)S(1)} %add.172), channel_id=1, source_target_pairs={{0,8},{8,0},{16,24},{24,16},{1,9},{9,1},{17,25},{25,17},{2,10},{10... | collective-permute-start | bytes 23048 | tf_op jit(solution)/shard_map/ppermute | solution.py:30
  429.4 19.4 %collective-permute-start.48 = (bf16[192,1280]{1,0:T(8,128)(2,1)S(1)}, bf16[192,1280]{1,0:T(8,128)(2,1)S(1)}, u32[]{:S(2)}, u32[]{:S(2)}) collective-permute-start(bf16[192,1280]{1,0:T(8,128)(2,1)S(1)} %maximum_select_fusion.9), channel_id=1, source_target_pairs={{0,8},{8,0},{16,24},{24,16},{1,9},{9,1},{17,25},{25,17},{2,10},{10... | collective-permute-start | bytes 1474568 | tf_op jit(solution)/shard_map/ppermute | solution.py:30
  435.5 25.5 %collective-permute-start.47 = (bf16[224,1280]{1,0:T(8,128)(2,1)S(1)}, bf16[224,1280]{1,0:T(8,128)(2,1)S(1)}, u32[]{:S(2)}, u32[]{:S(2)}) collective-permute-start(bf16[224,1280]{1,0:T(8,128)(2,1)S(1)} %maximum_select_fusion.8), channel_id=1, source_target_pairs={{0,8},{8,0},{16,24},{24,16},{1,9},{9,1},{17,25},{25,17},{2,10},{10... | collective-permute-start | bytes 1720328 | tf_op jit(solution)/shard_map/ppermute | solution.py:30
  438.1 24.5 %collective-permute-start.51 = (f32[2,960]{1,0:T(2,128)S(1)}, f32[2,960]{1,0:T(2,128)S(1)}, u32[]{:S(2)}, u32[]{:S(2)}) collective-permute-start(f32[2,960]{1,0:T(2,128)S(1)} %add.173), channel_id=1, source_target_pairs={{0,16},{8,24},{16,0},{24,8},{1,17},{9,25},{17,1},{25,9},{2,18},{10... | collective-permute-start | bytes 23048 | tf_op jit(solution)/shard_map/ppermute | solution.py:30
  (50 other events, 327.3 us)

commit v5 on v4

--- a/solution.py
+++ b/solution.py
@@ -188,34 +188,23 @@
     return jnp.where((me == 0) | (me == 3), outer, total).astype(F32)
 
 
-def unfold(rows, block):
-    return jnp.concatenate(
-        [rows[..., part * 256 : part * 256 + block] for part in range(5)], axis=-2
-    )
-
-
-LOW = 352
-HIGH_PAD = 16
-
-
-def pair_sums_kernel(keep_ref, got_ref, out_keep_ref, out_got_ref, low_ref, near_ref, far_ref):
+LOW = 448
+HIGH_PAD = 48
+
+
+def pair_sums_kernel(keep_ref, got_ref, low_ref, near_ref, far_ref):
     def total(k, rows):
         return (keep_ref[k, rows, :].astype(F32) + got_ref[k, rows, :].astype(F32)).astype(BF)
 
-    low_ref[:, LOW:, :] = (
-        out_keep_ref[0].astype(F32) + out_got_ref[...].astype(F32)
-    ).astype(BF)
     for k, high_ref in enumerate((near_ref, far_ref)):
-        low_ref[k, :LOW, :] = total(k, slice(0, LOW))
+        low_ref[k] = total(k, slice(0, LOW))
         size = high_ref.shape[0] - HIGH_PAD
         high_ref[:size, :] = total(k, slice(LOW, LOW + size))
         high_ref[size:, :] = jnp.zeros((HIGH_PAD, high_ref.shape[1]), BF)
 
 
-def pair_sums(keep, got, half, out_keep, out_got):
+def pair_sums(keep, got):
     rows, width = keep.shape[1:]
-    out_rows = out_keep.shape[2]
-    out_block = pl.BlockSpec((1, 2, out_rows, 256), lambda i: (half, 0, 0, i))
     high = rows - LOW + HIGH_PAD
     tile = 256
 
@@ -225,17 +214,17 @@
     return pl.pallas_call(
         pair_sums_kernel,
         grid=(width // tile,),
-        in_specs=[block(2, rows), block(2, rows), out_block, block(2, out_rows)],
-        out_specs=[block(2, LOW + out_rows), block(high), block(high)],
+        in_specs=[block(2, rows), block(2, rows)],
+        out_specs=[block(2, LOW), block(high), block(high)],
         out_shape=[
-            jax.ShapeDtypeStruct((2, LOW + out_rows, width), BF),
+            jax.ShapeDtypeStruct((2, LOW, width), BF),
             jax.ShapeDtypeStruct((high, width), BF),
             jax.ShapeDtypeStruct((high, width), BF),
         ],
         compiler_params=pltpu.CompilerParams(vmem_limit_bytes=32 * 2**20),
         cost_estimate=TINY,
         name="pair_sums",
-    )(keep, got, out_keep, out_got)
+    )(keep, got)
 
 
 def bit_z(by):
@@ -545,7 +534,7 @@
 QKV_WIDTH = Q_WIDTH + 2 * KV_WIDTH
 QKV_PART = QKV_WIDTH // 2
 OUT_PART = Q_WIDTH // 2
-OUT_ROWS = OUT_PART // 5
+WIDE = 256
 
 
 def place_of(flip_ref, half, size):
@@ -667,7 +656,7 @@
 
 def branch_back_kernel(flip_ref, grad_ref, middle_ref, up_ref, gain_ref, mixed_ref, *refs):
     weights = refs[:8]
-    mid_grad_ref, mixed_grad_ref, gain_grad_ref, keep_ref, *send_refs = refs[8:]
+    mid_grad_ref, mixed_grad_ref, gain_grad_ref, keep_ref, send_ref = refs[8:]
     middle = middle_ref[...]
     mid_grad, gain_grad = norm_back(
         middle, norm_scale_of(middle), gain_ref[...], grad_ref[...]
@@ -677,9 +666,6 @@
     mid_grad_ref[...] = mid_grad
     branch_grad = mid_grad.astype(BF)
     block = branch_grad.shape[0] // 4
-    keep_ref[...] = jnp.zeros_like(keep_ref)
-    for send_ref in send_refs:
-        send_ref[...] = jnp.zeros_like(send_ref)
     for half in range(2):
         place = place_of(flip_ref, half, OUT_PART)
         weight = stacked(weights[4 * half : 4 * half + 4], OUT_COLUMNS)
@@ -687,17 +673,13 @@
         heads = mixed_ref[place, :]
         for number in range(4):
             rows = branch_grad[number * block : (number + 1) * block]
-            made = dot(heads, rows, 1, 1).astype(BF)
-            target = send_refs[half] if number % 2 else keep_ref.at[half]
-            for part in range(5):
-                target[number // 2, :, part * 256 : part * 256 + block] = made[
-                    part * OUT_ROWS : (part + 1) * OUT_ROWS
-                ]
+            target = send_ref if number % 2 else keep_ref
+            target[half, number // 2] = dot(heads, rows, 1, 1).astype(BF)
 
 
 def branch_back(flip, grad, middle, upstream, gain, mixed, weights):
     width, count = middle.shape
-    parts = (2, 2, OUT_ROWS, 5 * 256)
+    parts = (2, 2, OUT_PART, width // 4)
     return call_whole(
         branch_back_kernel,
         "branch_back",
@@ -707,15 +689,29 @@
             ((Q_WIDTH, count), BF),
             ((width, 1), F32),
             (parts, BF),
-            (parts[1:], BF),
-            (parts[1:], BF),
+            (parts, BF),
         ),
     )
 
 
 def qkv_grad_kernel(
-    flip_ref, normed_ref, dq_ref, own_ref, prior_ref, cos_ref, sin_ref, made_ref, keep_ref, send_ref
+    flip_ref,
+    normed_ref,
+    dq_ref,
+    own_ref,
+    prior_ref,
+    cos_ref,
+    sin_ref,
+    out_keep_ref,
+    out_send_ref,
+    made_ref,
+    keep_ref,
+    send_ref,
 ):
+    block = out_keep_ref.shape[3]
+    for target, source in ((keep_ref, out_keep_ref), (send_ref, out_send_ref)):
+        target[:, :, :, block:] = jnp.zeros((*target.shape[:3], WIDE - block), BF)
+        target[:, :, QKV_PART:, :block] = source[...]
     made_ref[:Q_WIDTH, :] = dq_ref[...]
     count = own_ref.shape[2]
     cosine, sine = cos_ref[...], sin_ref[...]
@@ -737,16 +733,16 @@
         for number in range(4):
             rows = normed[number * block : (number + 1) * block]
             target = send_ref if number % 2 else keep_ref
-            target[half, number // 2] = dot(grads, rows, 1, 1).astype(BF)
-
-
-def qkv_grad(flip, normed, dq, own, prior, cosine, sine):
+            target[half, number // 2, :QKV_PART, :block] = dot(grads, rows, 1, 1).astype(BF)
+
+
+def qkv_grad(flip, normed, dq, own, prior, cosine, sine, out_keep, out_send):
     width, count = normed.shape
-    parts = (2, 2, QKV_PART, width // 4)
+    parts = (2, 2, QKV_PART + OUT_PART, WIDE)
     return call_whole(
         qkv_grad_kernel,
         "qkv_grad",
-        (flip, normed, dq, own, prior, cosine, sine),
+        (flip, normed, dq, own, prior, cosine, sine, out_keep, out_send),
         (((QKV_WIDTH, count), BF), (parts, BF), (parts, BF)),
     )
 
@@ -867,17 +863,19 @@
     first_got = swap(made[3], "gy", 1)
     later_got = swap(later_send, "gy", 1)
 
-    mid_grad, mixed_grad, gain_two, out_keep, *out_sent = branch_back(
-        flip,
-        after(normed_two_grad, result_near, result_sent),
-        middle,
-        upstream,
-        mlp_gain,
-        mixed,
-        weights,
-    )
-    out_got = [swap(part, "gy", 1) for part in out_sent]
-    result_shard = assemble(result_near, result_far)
+    early = (result_near, result_sent)
+    if pairs_x:
+        low_own, near_own, far_own = pair_sums(made[2], first_got)
+        low_other, near_other, far_other = pair_sums(
+            later_keep, after(later_got, near_own)
+        )
+        early += (low_own, near_own, far_own, low_other, near_other, far_other)
+        low_got = swap(low_other, "gx", 1)
+        own_got = swap(far_own, "gy", 2)
+        other_got = swap(far_other, "gy", 2)
+    mid_grad, mixed_grad, gain_two, out_keep, out_send = branch_back(
+        flip, after(normed_two_grad, *early), middle, upstream, mlp_gain, mixed, weights
+    )
 
     def attend_back(mixed_grad, *earlier):
         dq, sent_grad, own_grad = attention_backward(
@@ -886,7 +884,7 @@
         prior_grad = lax.ppermute(sent_grad, "gy", behind)
         own_grad = after(own_grad, *earlier)
         grads, keep, send = qkv_grad(
-            flip, normed_one, dq, own_grad, prior_grad, cosine, sine
+            flip, normed_one, dq, own_grad, prior_grad, cosine, sine, out_keep, out_send
         )
         return grads, keep, swap(send, "gy", 1)
 
@@ -894,12 +892,13 @@
         grads, qkv_keep, qkv_mate = attend_back(mixed_grad)
         ff_both = reduce_x([add(made[2], first_got), add(later_keep, later_got)])
         ff_sum = sum_z(add(ff_both[0], swap(ff_both[1], "gy", 2)))
-        paired = unfold(add(out_keep, jnp.stack(out_got)), block)
-        both = reduce_x([paired[0], paired[1]], -2)
-        sum_out = sum_z(add(both[0], swap(both[1], "gy", 2)))
-        paired = add(qkv_keep, qkv_mate)
-        both = reduce_x([paired[0], paired[1]], -2)
-        sum_qkv = sum_z(add(both[0], swap(both[1], "gy", 2)))
+        paired = add(qkv_keep, qkv_mate)[..., :block]
+        sums = [
+            reduce_x([paired[0, :, rows], paired[1, :, rows]], -2)
+            for rows in (slice(0, QKV_PART), slice(QKV_PART, None))
+        ]
+        sum_qkv, sum_out = (sum_z(add(both[0], swap(both[1], "gy", 2))) for both in sums)
+        result_shard = assemble(result_near, result_far)
         grad_keep, grad_send, gain_one = input_grad(
             flip, grads, inputs, attn_gain, mid_grad, weights
         )
@@ -907,17 +906,9 @@
         grad_far = swap(grad_sent, "gy", 2)
         gains = sum_all(jnp.stack([reorder(gain_one[:, 0]), reorder(gain_two[:, 0])]))
     else:
-        low_own, near_own, far_own = pair_sums(made[2], first_got, 0, out_keep, out_got[0])
-        low_other, near_other, far_other = pair_sums(
-            later_keep, later_got, 1, out_keep, out_got[1]
+        grads, qkv_keep, qkv_mate = attend_back(
+            mixed_grad, own_got, other_got, result_far, low_got
         )
-        mixed_grad = after(
-            mixed_grad, low_own, low_other, near_own, near_other, far_own, far_other, result_shard
-        )
-        low_got = swap(low_other, "gx", 1)
-        own_got = swap(far_own, "gy", 2)
-        other_got = swap(far_other, "gy", 2)
-        grads, qkv_keep, qkv_mate = attend_back(mixed_grad, own_got, other_got)
 
         high_sent = add(near_other, after(other_got, grads))
         high_near = add(near_own, after(own_got, high_sent))
@@ -936,46 +927,46 @@
         low_got = halve_z(low, 1)
         grad_near, grad_sent = to_features(grad_keep, after(grad_got, low))
         grad_far = swap(grad_sent, "gy", 2)
-        high = add(high_near, after(high_got, grad_near))
+        result_shard = assemble(result_near, after(result_far, grad_near))
+        low = add(kept_z(low, 1), after(low_got, result_shard))
+        low_got = halve_z(low, 2)
+        qkv_sum = add(qkv_near, after(qkv_got, low))
+        qkv_got = halve_z(qkv_sum, 1)
+        high = add(high_near, after(high_got, qkv_sum))
         high_got = halve_z(high, 1)
         gain_one, gain_two = after((gain_one, gain_two), high)
         gains = jnp.stack([reorder(gain_one[:, 0]), reorder(gain_two[:, 0])])
         gains_got = swap(gains, "gx", 1)
-        qkv_sum = add(qkv_near, after(qkv_got, high))
-        qkv_got = lax.ppermute(qkv_sum, "dp", [(0, 1), (3, 2)])
+        low = add(kept_z(low, 2), after(low_got, gains))
+        low_got = swap(low, "dp", 2)
+        qkv_sum = add(kept_z(qkv_sum, 1), after(qkv_got, low))
+        qkv_got = halve_z(qkv_sum, 2)
         gains = gains + after(gains_got, qkv_sum)
         gains_got = swap(gains, "gy", 1)
         high = add(kept_z(high, 1), after(high_got, gains))
         high_got = halve_z(high, 2)
-        qkv_sum = add(qkv_sum, after(qkv_got, high))
-        qkv_got = lax.ppermute(qkv_sum, "dp", [(1, 2), (2, 1)])
-        low = add(kept_z(low, 1), after(low_got, qkv_sum))
-        low_got = halve_z(low, 2)
-        gains = gains + after(gains_got, low)
+        gains = gains + after(gains_got, high)
         gains_got = swap(gains, "gy", 2)
-        high = add(kept_z(high, 2), after(high_got, gains))
+        qkv_sum = add(kept_z(qkv_sum, 2), after(qkv_got, gains))
+        qkv_got = swap(qkv_sum, "dp", 2)
+        low = ordered(low, after(low_got, qkv_sum), bit_z(2), 0)
+        low_got = swap(low, "dp", 1)
+        high = add(kept_z(high, 2), after(high_got, low))
         high_got = swap(high, "dp", 2)
-        qkv_sum = add(qkv_sum, after(qkv_got, high))
-        qkv_got = lax.ppermute(qkv_sum, "dp", [(1, 0), (2, 3)])
-        low = add(kept_z(low, 2), after(low_got, qkv_sum))
-        low_got = swap(low, "dp", 2)
-        gains = gains + after(gains_got, low)
+        gains = gains + after(gains_got, high)
         gains_got = swap(gains, "dp", 1)
+        qkv_sum = ordered(qkv_sum, after(qkv_got, gains), bit_z(2), 0)
+        qkv_got = swap(qkv_sum, "dp", 1)
+        low = ordered(low, after(low_got, qkv_sum), bit_z(1), 0).astype(F32)
         high = ordered(high, after(high_got, low), bit_z(2), 0)
         high_got = swap(high, "dp", 1)
-        low = ordered(low, after(low_got, high), bit_z(2), 0)
-        low_got = swap(low, "dp", 1)
-        gains = gains + after(gains_got, low)
+        gains = gains + after(gains_got, high)
         gains_got = swap(gains, "dp", 2)
-        at = lax.axis_index("dp")
-        sum_qkv = jnp.where(
-            (at == 0) | (at == 3), after(qkv_got, low), qkv_sum
-        ).astype(F32)
-        high = ordered(high, after(high_got, sum_qkv), bit_z(1), 0).astype(F32)
-        low = ordered(low, after(low_got, high), bit_z(1), 0).astype(F32)
-        gains = gains + after(gains_got, low)
-        ff_sum = jnp.concatenate([low[:LOW], high[: high.shape[0] - HIGH_PAD]], axis=0)
-        sum_out = unfold(low[LOW:], block)
+        qkv_sum = ordered(qkv_sum, after(qkv_got, gains), bit_z(1), 0).astype(F32)
+        sum_qkv, sum_out = qkv_sum[:QKV_PART, :block], qkv_sum[QKV_PART:, :block]
+        high = ordered(high, after(high_got, qkv_sum), bit_z(1), 0).astype(F32)
+        gains = gains + after(gains_got, high)
+        ff_sum = jnp.concatenate([low, high[: high.shape[0] - HIGH_PAD]], axis=0)
     return (
         result_shard,
         assemble(grad_near, grad_far),

time: 472 us -> 457 us (0.968)
  waiting for transfers between devices: 137 us -> 128 us
  local copies, waits for them, and re-layouts: 37.9 us -> 31.5 us
    unnamed x96 -> x82, local copies, waits for them, and re-layouts: 18.2 us -> 11.2 us
    ppermute x47 -> x49, waiting for transfers between devices: 129 us -> 123 us  [swap(): return lax.ppermute(value, axis, [(i, i ^ by) for i in range(peers)])]
    ppermute x3 -> x0, waiting for transfers between devices: 4.89 us -> none  [the longest x1 4.89 us: on_device(): qkv_got = lax.ppermute(qkv_sum, 'dp', [(0, 1), (3, 2)])]
    ppermute x47 -> x49, starting transfers between devices: 41.5 us -> 45.5 us  [swap(): return lax.ppermute(value, axis, [(i, i ^ by) for i in range(peers)])]
    select_n x8 -> x9, other arithmetic: 11.7 us -> 9.11 us  [ordered(): jnp.where(bit == 0, jnp.concatenate([mine, theirs], axis=axis), jnp.conca...]
  transfers between devices with their start and end apart: 52 -> 51, of which waited for: 19 -> 20; matrix products, arithmetic and copies ran while one was open for 8% -> 7% of each run, Pallas kernels for 47% -> 46%
where the time goes in v5:
time: 457 us; the launch traced here: 450 us
  Pallas kernels  223 us (49%)
  waiting for transfers between devices  128 us (28%)
  starting transfers between devices  48.5 us (11%)
  local copies, waits for them, and re-layouts  31.5 us (7%)
  other arithmetic  17.9 us (4%)
    ppermute x49, waiting for transfers between devices, swap(): return lax.ppermute(value, axis, [(i, i ^ by) for i in range(peers)])  123 us
    pallas_call x2, Pallas kernels, mlp_chunk(): pl.pallas_call(functools.partial(mlp_kernel, first), grid=(size // tile,)...  68.9 us
    pallas_call x5, Pallas kernels, call_whole(): pl.pallas_call(kernel, in_specs=[SMEM] + [VMEM] * (len(ins) - 1), out_spe...  57.3 us
    ppermute x49, starting transfers between devices, swap(): return lax.ppermute(value, axis, [(i, i ^ by) for i in range(peers)])  45.5 us
    pallas_call x1, Pallas kernels, attention_backward(): pl.pallas_call(backward_kernel, grid=(KV_HEADS,), in_specs=[pl.BlockSpec(...  38.3 us
    pallas_call x1, Pallas kernels, attention_forward(): pl.pallas_call(forward_kernel, grid=(KV_HEADS,), in_specs=[pl.BlockSpec((...  36.4 us
    unnamed x82, local copies, waits for them, and re-layouts  11.2 us
  transfers between devices with their start and end apart: 51, of which 20 were waited for; matrix products, arithmetic and copies ran while one was open for 7% of the time, Pallas kernels for 46%

profile of v5, /device:TPU:0, one launch (start us, length us, event | category | flops | bytes accessed | tf_op | source)
XLA Modules:
  0.0 450.0 jit_solution(2523615865125277323)
XLA Ops:
  3.1 3.0 collective-permute-start
  6.1 1.5 collective-permute-start.1
  7.6 12.4 %collective-permute-done.refs_2_ = bf16[240,1280]{1,0:T(8,128)(2,1)S(1)} collective-permute-done((bf16[240,1280]{1,0:T(8,128)(2,1)S(1)}, bf16[240,1280]{1,0:T(8,128)(2,1)S(1)}, u32[]{:S(2)}, u32[]{:S(2)}) %collective-permute-start) | collective-permute-done | bytes 614432 | tf_op jit(solution)/shard_map/ppermute | solution.py:30
  21.5 2.5 constant_dynamic-slice_fusion.19
  24.4 2.0 constant_dynamic-slice_fusion.20
  26.5 1.5 collective-permute-start.7
  28.3 18.3 %collective-permute-done.2 = bf16[240,2048]{1,0:T(8,128)(2,1)} collective-permute-done((bf16[240,2048]{1,0:T(8,128)(2,1)}, bf16[240,2048]{1,0:T(8,128)(2,1)}, u32[]{:S(2)}, u32[]{:S(2)}) %collective-permute-start.2) | collective-permute-done | bytes 983072 | tf_op jit(solution)/shard_map/ppermute | solution.py:30
  46.5 2.0 constant_dynamic-slice_fusion.17
  53.3 1.5 collective-permute-start.11
  57.2 10.5 %project.1 = (bf16[960,1024]{1,0:T(8,128)(2,1)}, bf16[960,1024]{1,0:T(8,128)(2,1)}, bf16[960,1024]{1,0:T(8,128)(2,1)}, bf16[5,128,1024]{2,1,0:T(8,128)(2,1)}, bf16[5,128,512]{2,1,0:T(8,128)(2,1)}) custom-call(s32[1]{0:T(128)} %bitcast.flip_ref, bf16[240,1024]{1,0:T(8,128)(2,1)} %get-tuple-element.192.near_ref, ...), custom_call_target="tpu_custom_call" | custom-call | flops 1000 | bytes 1000 | tf_op jit(solution)/shard_map/project/pallas_call | solution.py:606
  69.1 1.7 collective-permute-start.9
  70.9 1.6 collective-permute-done.9.prior_ref
  73.8 36.4 %attend_forward.1 = (bf16[960,1024]{1,0:T(8,128)(2,1)S(1)}, f32[5,8,1024]{2,1,0:T(8,128)S(1)}) custom-call(s32[1,1024]{1,0:T(1,128)S(1)} %bitcast.21, bf16[960,1024]{1,0:T(8,128)(2,1)S(1)} %copy-done.2, bf16[5,128,512]{2,1,0:T(8,128)(2,1)S(1)} %collective-permute-done.9.prior_ref, bf16[5,128,1024]{2,1,0:T(8,128)(2,1)S(1)} %copy-done.3), custom_call_target="tpu_custom_call" | custom-call | flops 1000 | bytes 1000 | tf_op jit(solution)/shard_map/attend_forward/pallas_call | solution.py:308
  110.3 5.2 %collective-permute-done.12 = bf16[240,2048]{1,0:T(8,128)(2,1)S(1)} collective-permute-done((bf16[240,2048]{1,0:T(8,128)(2,1)S(1)}, bf16[240,2048]{1,0:T(8,128)(2,1)S(1)}, u32[]{:S(2)}, u32[]{:S(2)}) %collective-permute-start.12) | collective-permute-done | bytes 983072 | tf_op jit(solution)/shard_map/ppermute | solution.py:30
  115.4 1.5 collective-permute-start.17
  120.3 9.4 %branch.1 = (f32[960,1024]{1,0:T(8,128)}, bf16[960,1024]{1,0:T(8,128)(2,1)}) custom-call(s32[1]{0:T(128)} %bitcast.flip_ref, bf16[960,1024]{1,0:T(8,128)(2,1)} %get-tuple-element.95.x_ref, f32[960,1]{1,0:T(8,128)} %copy.24.gain_ref, bf16[960,1024]{1,0:T(8,128)(2,1)} %copy-done, bf16[240,1280]{1,0:T(8,128)(2,1)} %copy-done.20, bf16[240,1280]{1,0:T(8,128)(2,1)} %copy-done.23, ...), custom_call_target="tpu_custom_call" | custom-call | flops 1000 | bytes 1000 | tf_op jit(solution)/shard_map/branch/pallas_call | solution.py:606
  132.7 34.3 %feed_forward.2 = (f32[960,1024]{1,0:T(8,128)}, f32[960,1024]{1,0:T(8,128)}, bf16[2,720,1280]{2,1,0:T(8,128)(2,1)}, bf16[2,720,1280]{2,1,0:T(8,128)(2,1)}) custom-call(bf16[960,1024]{1,0:T(8,128)(2,1)} %get-tuple-element.100.refs_0_, bf16[960,1024]{1,0:T(8,128)(2,1)} %pad_maximum_fusion.refs_1_.up_ref, f32[960,1024]{1,0:T(8,128)} %get-tuple-element.104.refs_2_.middle_ref, ...), custom_call_target="tpu_custom_call" | custom-call | flops 1000 | bytes 1000 | tf_op jit(solution)/shard_map/feed_forward/pallas_call | solution.py:508
  167.5 3.8 collective-permute-done.18.refs_7_
  172.6 34.6 %feed_forward.3 = (bf16[480,1024]{1,0:T(8,128)(2,1)}, bf16[480,1024]{1,0:T(8,128)(2,1)}, f32[960,1024]{1,0:T(8,128)}, bf16[2,720,1280]{2,1,0:T(8,128)(2,1)}, bf16[2,720,1280]{2,1,0:T(8,128)(2,1)}) custom-call(bf16[960,1024]{1,0:T(8,128)(2,1)} %get-tuple-element.100.refs_0_, bf16[960,1024]{1,0:T(8,128)(2,1)} %pad_maximum_fusion.refs_1_.up_ref, ...), custom_call_target="tpu_custom_call" | custom-call | flops 1000 | bytes 1000 | tf_op jit(solution)/shard_map/feed_forward/pallas_call | solution.py:508
  207.7 5.1 %pair_sums.2 = (bf16[2,448,1280]{2,1,0:T(8,128)(2,1)S(1)}, bf16[320,1280]{1,0:T(8,128)(2,1)S(1)}, bf16[320,1280]{1,0:T(8,128)(2,1)}) custom-call(bf16[2,720,1280]{2,1,0:T(8,128)(2,1)S(1)} %copy-done.5, bf16[2,720,1280]{2,1,0:T(8,128)(2,1)} %collective-permute-done.21.got_ref), custom_call_target="tpu_custom_call" | custom-call | flops 1000 | bytes 1000 | tf_op jit(solution)/shard_map/pair_sums/pallas_call | solution.py:214
  215.2 3.5 pair_sums.3
  228.3 13.8 %branch_back.1 = (f32[960,1024]{1,0:T(8,128)}, bf16[960,1024]{1,0:T(8,128)(2,1)}, f32[960,1]{1,0:T(8,128)}, bf16[2,2,480,240]{3,2,1,0:T(8,128)(2,1)}, bf16[2,2,480,240]{3,2,1,0:T(8,128)(2,1)}) custom-call(s32[1]{0:T(128)} %bitcast.flip_ref, f32[960,1024]{1,0:T(8,128)} %get-tuple-element.126.grad_ref, f32[960,1024]{1,0:T(8,128)} %get-tuple-element.104.refs_2_.middle_ref, ...), custom_call_target="tpu_custom_call" | custom-call | flops 1000 | bytes 1000 | tf_op jit(solution)/shard_map/branch_back/pallas_call | solution.py:606
  242.1 38.3 %attend_backward.1 = (bf16[960,1024]{1,0:T(8,128)(2,1)S(1)}, bf16[5,128,512]{2,1,0:T(8,128)(2,1)S(1)}, f32[5,128,1024]{2,1,0:T(8,128)}) custom-call(s32[1,1024]{1,0:T(1,128)S(1)} %bitcast.22, f32[32,1024]{1,0:T(8,128)S(1)} %copy-done.11, f32[32,1024]{1,0:T(8,128)S(1)} %copy-done.10, bf16[960,1024]{1,0:T(8,128)(2,1)S(1)} %copy-done.2, ...), custom_call_target="tpu_custom_call" | custom-call | flops 1000 | bytes 1000 | tf_op jit(solution)/shard_map/attend_backward/pallas_call | solution.py:407
  283.1 2.6 collective-permute-done.26.prior_ref
  286.5 10.7 %qkv_grad.1 = (bf16[1600,1024]{1,0:T(8,128)(2,1)}, bf16[2,2,1280,256]{3,2,1,0:T(8,128)(2,1)}, bf16[2,2,1280,256]{3,2,1,0:T(8,128)(2,1)}) custom-call(s32[1]{0:T(128)} %bitcast.flip_ref, bf16[960,1024]{1,0:T(8,128)(2,1)} %get-tuple-element.112.normed_ref, bf16[960,1024]{1,0:T(8,128)(2,1)} %copy-done.12, f32[5,128,1024]{2,1,0:T(8,128)} %get-tuple-element.130.own_ref, ...), custom_call_target="tpu_custom_call" | custom-call | flops 1000 | bytes 1000 | tf_op jit(solution)/shard_map/qkv_grad/pallas_call | solution.py:606
  297.3 1.5 add.212
  301.1 3.1 add_pair.3
  304.2 3.9 add_pair.4
  310.8 13.0 %input_grad.1 = (bf16[480,1024]{1,0:T(8,128)(2,1)}, bf16[480,1024]{1,0:T(8,128)(2,1)}, f32[960,1]{1,0:T(8,128)}) custom-call(s32[1]{0:T(128)} %bitcast.flip_ref, bf16[1600,1024]{1,0:T(8,128)(2,1)} %get-tuple-element.143.grads_ref, bf16[960,1024]{1,0:T(8,128)(2,1)} %get-tuple-element.95.x_ref, f32[960,1]{1,0:T(8,128)} %copy.23.gain_ref, ...), custom_call_target="tpu_custom_call" | custom-call | flops 1000 | bytes 1000 | tf_op jit(solution)/shard_map/input_grad/pallas_call | solution.py:606
  325.8 14.2 %collective-permute-done.30.right_ref = bf16[2,1280,256]{2,1,0:T(8,128)(2,1)S(1)} collective-permute-done((bf16[2,1280,256]{2,1,0:T(8,128)(2,1)}, bf16[2,1280,256]{2,1,0:T(8,128)(2,1)S(1)}, u32[]{:S(2)}, u32[]{:S(2)}) %collective-permute-start.30) | collective-permute-done | bytes 1310752 | tf_op jit(solution)/shard_map/ppermute | solution.py:30
  340.6 1.5 add.214
  343.4 1.6 collective-permute-start.33
  346.6 3.5 maximum_select_fusion
  350.1 7.3 %collective-permute-done.33.right_ref = bf16[224,1280]{1,0:T(8,128)(2,1)S(1)} collective-permute-done((bf16[224,1280]{1,0:T(8,128)(2,1)S(1)}, bf16[224,1280]{1,0:T(8,128)(2,1)S(1)}, u32[]{:S(2)}, u32[]{:S(2)}) %collective-permute-start.33) | collective-permute-done | bytes 573472 | tf_op jit(solution)/shard_map/ppermute | solution.py:30
  357.6 2.6 collective-permute-start.35
  367.3 4.3 collective-permute-done.35.right_ref
  371.8 17.0 %collective-permute-done.34.right_ref = bf16[640,256]{1,0:T(8,128)(2,1)S(1)} collective-permute-done((bf16[640,256]{1,0:T(8,128)(2,1)S(1)}, bf16[640,256]{1,0:T(8,128)(2,1)S(1)}, u32[]{:S(2)}, u32[]{:S(2)}) %collective-permute-start.34) | collective-permute-done | bytes 327712 | tf_op jit(solution)/shard_map/ppermute | solution.py:30
  389.4 1.6 collective-permute-start.37
  393.9 11.3 %collective-permute-done.37.right_ref = bf16[320,256]{1,0:T(8,128)(2,1)S(1)} collective-permute-done((bf16[320,256]{1,0:T(8,128)(2,1)S(1)}, bf16[320,256]{1,0:T(8,128)(2,1)S(1)}, u32[]{:S(2)}, u32[]{:S(2)}) %collective-permute-start.37) | collective-permute-done | bytes 163872 | tf_op jit(solution)/shard_map/ppermute | solution.py:30
  405.5 2.7 collective-permute-start.48
  408.2 2.0 maximum_select_fusion.1
  410.2 3.1 collective-permute-done.43.right_ref
  413.4 2.7 collective-permute-start.46
  416.9 13.7 %collective-permute-done.48 = bf16[224,1280]{1,0:T(8,128)(2,1)S(1)} collective-permute-done((bf16[224,1280]{1,0:T(8,128)(2,1)S(1)}, bf16[224,1280]{1,0:T(8,128)(2,1)S(1)}, u32[]{:S(2)}, u32[]{:S(2)}) %collective-permute-start.48) | collective-permute-done | bytes 573472 | tf_op jit(solution)/shard_map/ppermute | solution.py:30
  431.2 3.8 collective-permute-start.50
  435.0 3.0 collective-permute-done.45
  440.0 5.9 %collective-permute-done.49 = bf16[160,1280]{1,0:T(8,128)(2,1)S(1)} collective-permute-done((bf16[160,1280]{1,0:T(8,128)(2,1)S(1)}, bf16[160,1280]{1,0:T(8,128)(2,1)S(1)}, u32[]{:S(2)}, u32[]{:S(2)}) %collective-permute-start.49) | collective-permute-done | bytes 409632 | tf_op jit(solution)/shard_map/ppermute | solution.py:30
  447.9 1.6 pad_maximum_fusion.2
  (219 shorter events, 65.3 us)
Async XLA Ops:
  3.1 16.9 %collective-permute-start = (bf16[240,1280]{1,0:T(8,128)(2,1)S(1)}, bf16[240,1280]{1,0:T(8,128)(2,1)S(1)}, u32[]{:S(2)}, u32[]{:S(2)}) collective-permute-start(bf16[240,1280]{1,0:T(8,128)(2,1)S(1)} %pad_maximum_fusion.5.refs_0_), channel_id=1, source_target_pairs={{0,2},{1,3},{2,0},{3,1},{4,6},{5,7},{6,4},{7,5},{8,10},{9,11},{10,... | collective-permute-start | bytes 1843208 | tf_op jit(solution)/shard_map/ppermute | solution.py:30
  6.1 15.3 %collective-permute-start.1 = (bf16[240,1280]{1,0:T(8,128)(2,1)S(1)}, bf16[240,1280]{1,0:T(8,128)(2,1)S(1)}, u32[]{:S(2)}, u32[]{:S(2)}) collective-permute-start(bf16[240,1280]{1,0:T(8,128)(2,1)S(1)} %pad_maximum_fusion.5.refs_0_), channel_id=1, source_target_pairs={{0,4},{4,0},{1,5},{5,1},{2,6},{6,2},{3,7},{7,3},{8,12},{12,8},{9,1... | collective-permute-start | bytes 1843208 | tf_op jit(solution)/shard_map/ppermute | solution.py:30
  23.9 22.6 %collective-permute-start.2 = (bf16[240,2048]{1,0:T(8,128)(2,1)}, bf16[240,2048]{1,0:T(8,128)(2,1)}, u32[]{:S(2)}, u32[]{:S(2)}) collective-permute-start(bf16[240,2048]{1,0:T(8,128)(2,1)} %constant_dynamic-slice_fusion.19), channel_id=1, source_target_pairs={{0,2},{1,3},{2,0},{3,1},{4,6},{5,7},{6,4},{7,5},{8,10},{9,11},{10,... | collective-permute-start | bytes 2949128 | tf_op jit(solution)/shard_map/ppermute | solution.py:30
  24.4 27.2 %collective-permute-start.4 = (bf16[240,1280]{1,0:T(8,128)(2,1)S(1)}, bf16[240,1280]{1,0:T(8,128)(2,1)S(1)}, u32[]{:S(2)}, u32[]{:S(2)}) collective-permute-start(bf16[240,1280]{1,0:T(8,128)(2,1)S(1)} %pad_maximum_fusion.5.refs_0_), channel_id=1, source_target_pairs={{0,1},{1,0},{2,3},{3,2},{4,5},{5,4},{6,7},{7,6},{8,9},{9,8},{10,11... | collective-permute-start | bytes 1843208 | tf_op jit(solution)/shard_map/ppermute | solution.py:30
  26.5 25.0 %collective-permute-start.7 = (bf16[240,1280]{1,0:T(8,128)(2,1)S(1)}, bf16[240,1280]{1,0:T(8,128)(2,1)S(1)}, u32[]{:S(2)}, u32[]{:S(2)}) collective-permute-start(bf16[240,1280]{1,0:T(8,128)(2,1)S(1)} %collective-permute-done.refs_2_), channel_id=1, source_target_pairs={{0,4},{4,0},{1,5},{5,1},{2,6},{6,2},{3,7},{7,3},{8,12},{12,8},{9,1... | collective-permute-start | bytes 1843208 | tf_op jit(solution)/shard_map/ppermute | solution.py:30
  28.0 24.4 %collective-permute-start.5 = (bf16[240,1280]{1,0:T(8,128)(2,1)S(1)}, bf16[240,1280]{1,0:T(8,128)(2,1)S(1)}, u32[]{:S(2)}, u32[]{:S(2)}) collective-permute-start(bf16[240,1280]{1,0:T(8,128)(2,1)S(1)} %collective-permute-done.refs_2_), channel_id=1, source_target_pairs={{0,1},{1,0},{2,3},{3,2},{4,5},{5,4},{6,7},{7,6},{8,9},{9,8},{10,11... | collective-permute-start | bytes 1843208 | tf_op jit(solution)/shard_map/ppermute | solution.py:30
  49.6 7.6 %collective-permute-start.3 = (bf16[480,1024]{1,0:T(8,128)(2,1)}, bf16[480,1024]{1,0:T(8,128)(2,1)}, u32[]{:S(2)}, u32[]{:S(2)}) collective-permute-start(bf16[480,1024]{1,0:T(8,128)(2,1)} %pad_maximum_fusion.3), channel_id=1, source_target_pairs={{0,1},{1,0},{2,3},{3,2},{4,5},{5,4},{6,7},{7,6},{8,9},{9,8},{10,11... | collective-permute-start | bytes 2949128 | tf_op jit(solution)/shard_map/ppermute | solution.py:30
  51.0 6.1 %collective-permute-start.6 = (bf16[240,1280]{1,0:T(8,128)(2,1)S(1)}, bf16[240,1280]{1,0:T(8,128)(2,1)}, u32[]{:S(2)}, u32[]{:S(2)}) collective-permute-start(bf16[240,1280]{1,0:T(8,128)(2,1)S(1)} %collective-permute-done.1.refs_4_), channel_id=1, source_target_pairs={{0,1},{1,0},{2,3},{3,2},{4,5},{5,4},{6,7},{7,6},{8,9},{9,8},{10,11... | collective-permute-start | bytes 1843208 | tf_op jit(solution)/shard_map/ppermute | solution.py:30
  51.5 5.6 %collective-permute-start.8 = (bf16[240,1280]{1,0:T(8,128)(2,1)S(1)}, bf16[240,1280]{1,0:T(8,128)(2,1)}, u32[]{:S(2)}, u32[]{:S(2)}) collective-permute-start(bf16[240,1280]{1,0:T(8,128)(2,1)S(1)} %collective-permute-done.7.refs_6_), channel_id=1, source_target_pairs={{0,1},{1,0},{2,3},{3,2},{4,5},{5,4},{6,7},{7,6},{8,9},{9,8},{10,11... | collective-permute-start | bytes 1843208 | tf_op jit(solution)/shard_map/ppermute | solution.py:30
  51.6 58.6 %collective-permute-start.10 = (bf16[720,1280]{1,0:T(8,128)(2,1)}, bf16[720,1280]{1,0:T(8,128)(2,1)}, u32[]{:S(2)}, u32[]{:S(2)}) collective-permute-start(bf16[720,1280]{1,0:T(8,128)(2,1)} %pad_maximum_fusion.1.refs_3_), channel_id=1, source_target_pairs={{0,2},{1,3},{2,0},{3,1},{4,6},{5,7},{6,4},{7,5},{8,10},{9,11},{10,... | collective-permute-start | bytes 5529608 | tf_op jit(solution)/shard_map/ppermute | solution.py:30
  53.3 57.0 %collective-permute-start.11 = (bf16[720,1280]{1,0:T(8,128)(2,1)}, bf16[720,1280]{1,0:T(8,128)(2,1)}, u32[]{:S(2)}, u32[]{:S(2)}) collective-permute-start(bf16[720,1280]{1,0:T(8,128)(2,1)} %pad_maximum_fusion.1.refs_3_), channel_id=1, source_target_pairs={{0,4},{4,0},{1,5},{5,1},{2,6},{6,2},{3,7},{7,3},{8,12},{12,8},{9,1... | collective-permute-start | bytes 5529608 | tf_op jit(solution)/shard_map/ppermute | solution.py:30
  67.8 47.6 %collective-permute-start.12 = (bf16[240,2048]{1,0:T(8,128)(2,1)S(1)}, bf16[240,2048]{1,0:T(8,128)(2,1)S(1)}, u32[]{:S(2)}, u32[]{:S(2)}) collective-permute-start(bf16[240,2048]{1,0:T(8,128)(2,1)S(1)} %constant_dynamic-slice_fusion.14), channel_id=1, source_target_pairs={{0,2},{1,3},{2,0},{3,1},{4,6},{5,7},{6,4},{7,5},{8,10},{9,11},{10,... | collective-permute-start | bytes 2949128 | tf_op jit(solution)/shard_map/ppermute | solution.py:30
  70.8 61.9 %collective-permute-start.14 = (bf16[720,1280]{1,0:T(8,128)(2,1)}, bf16[720,1280]{1,0:T(8,128)(2,1)}, u32[]{:S(2)}, u32[]{:S(2)}) collective-permute-start(bf16[720,1280]{1,0:T(8,128)(2,1)} %pad_maximum_fusion.1.refs_3_), channel_id=1, source_target_pairs={{0,1},{1,0},{2,3},{3,2},{4,5},{5,4},{6,7},{7,6},{8,9},{9,8},{10,11... | collective-permute-start | bytes 5529608 | tf_op jit(solution)/shard_map/ppermute | solution.py:30
  115.4 17.2 %collective-permute-start.15 = (bf16[720,1280]{1,0:T(8,128)(2,1)}, bf16[720,1280]{1,0:T(8,128)(2,1)}, u32[]{:S(2)}, u32[]{:S(2)}) collective-permute-start(bf16[720,1280]{1,0:T(8,128)(2,1)} %collective-permute-done.10.refs_5_), channel_id=1, source_target_pairs={{0,1},{1,0},{2,3},{3,2},{4,5},{5,4},{6,7},{7,6},{8,9},{9,8},{10,11... | collective-permute-start | bytes 5529608 | tf_op jit(solution)/shard_map/ppermute | solution.py:30
  115.4 51.5 %collective-permute-start.17 = (bf16[720,1280]{1,0:T(8,128)(2,1)}, bf16[720,1280]{1,0:T(8,128)(2,1)}, u32[]{:S(2)}, u32[]{:S(2)}) collective-permute-start(bf16[720,1280]{1,0:T(8,128)(2,1)} %collective-permute-done.10.refs_5_), channel_id=1, source_target_pairs={{0,4},{4,0},{1,5},{5,1},{2,6},{6,2},{3,7},{7,3},{8,12},{12,8},{9,1... | collective-permute-start | bytes 5529608 | tf_op jit(solution)/shard_map/ppermute | solution.py:30
  118.9 11.1 %collective-permute-start.13 = (bf16[480,1024]{1,0:T(8,128)(2,1)}, bf16[480,1024]{1,0:T(8,128)(2,1)}, u32[]{:S(2)}, u32[]{:S(2)}) collective-permute-start(bf16[480,1024]{1,0:T(8,128)(2,1)} %pad_maximum_fusion.4), channel_id=1, source_target_pairs={{0,1},{1,0},{2,3},{3,2},{4,5},{5,4},{6,7},{7,6},{8,9},{9,8},{10,11... | collective-permute-start | bytes 2949128 | tf_op jit(solution)/shard_map/ppermute | solution.py:30
  129.7 37.9 %collective-permute-start.16 = (bf16[720,1280]{1,0:T(8,128)(2,1)}, bf16[720,1280]{1,0:T(8,128)(2,1)S(1)}, u32[]{:S(2)}, u32[]{:S(2)}) collective-permute-start(bf16[720,1280]{1,0:T(8,128)(2,1)} %collective-permute-done.11.refs_4_), channel_id=1, source_target_pairs={{0,1},{1,0},{2,3},{3,2},{4,5},{5,4},{6,7},{7,6},{8,9},{9,8},{10,11... | collective-permute-start | bytes 5529608 | tf_op jit(solution)/shard_map/ppermute | solution.py:30
  167.0 4.4 collective-permute-start.18
  167.3 40.4 %collective-permute-start.21 = (bf16[2,720,1280]{2,1,0:T(8,128)(2,1)}, bf16[2,720,1280]{2,1,0:T(8,128)(2,1)}, u32[]{:S(2)}, u32[]{:S(2)}) collective-permute-start(bf16[2,720,1280]{2,1,0:T(8,128)(2,1)} %get-tuple-element.116), channel_id=1, source_target_pairs={{0,1},{1,0},{2,3},{3,2},{4,5},{5,4},{6,7},{7,6},{8,9},{9,8},{10,11... | collective-permute-start | bytes 11059208 | tf_op jit(solution)/shard_map/ppermute | solution.py:30
  207.2 8.1 %collective-permute-start.22 = (bf16[2,720,1280]{2,1,0:T(8,128)(2,1)}, bf16[2,720,1280]{2,1,0:T(8,128)(2,1)S(1)}, u32[]{:S(2)}, u32[]{:S(2)}) collective-permute-start(bf16[2,720,1280]{2,1,0:T(8,128)(2,1)} %get-tuple-element.121), channel_id=1, source_target_pairs={{0,1},{1,0},{2,3},{3,2},{4,5},{5,4},{6,7},{7,6},{8,9},{9,8},{10,11... | collective-permute-start | bytes 11059208 | tf_op jit(solution)/shard_map/ppermute | solution.py:30
  207.3 14.3 %collective-permute-start.19 = (bf16[480,1024]{1,0:T(8,128)(2,1)}, bf16[480,1024]{1,0:T(8,128)(2,1)}, u32[]{:S(2)}, u32[]{:S(2)}) collective-permute-start(bf16[480,1024]{1,0:T(8,128)(2,1)} %get-tuple-element.111), channel_id=1, source_target_pairs={{0,1},{1,0},{2,3},{3,2},{4,5},{5,4},{6,7},{7,6},{8,9},{9,8},{10,11... | collective-permute-start | bytes 2949128 | tf_op jit(solution)/shard_map/ppermute | solution.py:30
  219.7 63.4 %collective-permute-start.25 = (bf16[2,448,1280]{2,1,0:T(8,128)(2,1)}, bf16[2,448,1280]{2,1,0:T(8,128)(2,1)}, u32[]{:S(2)}, u32[]{:S(2)}) collective-permute-start(bf16[2,448,1280]{2,1,0:T(8,128)(2,1)} %get-tuple-element.123), channel_id=1, source_target_pairs={{0,4},{4,0},{1,5},{5,1},{2,6},{6,2},{3,7},{7,3},{8,12},{12,8},{9,1... | collective-permute-start | bytes 6881288 | tf_op jit(solution)/shard_map/ppermute | solution.py:30
  224.1 58.9 %collective-permute-start.20 = (bf16[240,2048]{1,0:T(8,128)(2,1)}, bf16[240,2048]{1,0:T(8,128)(2,1)}, u32[]{:S(2)}, u32[]{:S(2)}) collective-permute-start(bf16[240,2048]{1,0:T(8,128)(2,1)} %maximum_select_fusion.4), channel_id=1, source_target_pairs={{0,2},{1,3},{2,0},{3,1},{4,6},{5,7},{6,4},{7,5},{8,10},{9,11},{10,... | collective-permute-start | bytes 2949128 | tf_op jit(solution)/shard_map/ppermute | solution.py:30
  224.9 58.1 %collective-permute-start.23 = (bf16[320,1280]{1,0:T(8,128)(2,1)}, bf16[320,1280]{1,0:T(8,128)(2,1)}, u32[]{:S(2)}, u32[]{:S(2)}) collective-permute-start(bf16[320,1280]{1,0:T(8,128)(2,1)} %get-tuple-element.119), channel_id=1, source_target_pairs={{0,2},{1,3},{2,0},{3,1},{4,6},{5,7},{6,4},{7,5},{8,10},{9,11},{10,... | collective-permute-start | bytes 2457608 | tf_op jit(solution)/shard_map/ppermute | solution.py:30
  226.2 56.9 %collective-permute-start.24 = (bf16[320,1280]{1,0:T(8,128)(2,1)}, bf16[320,1280]{1,0:T(8,128)(2,1)}, u32[]{:S(2)}, u32[]{:S(2)}) collective-permute-start(bf16[320,1280]{1,0:T(8,128)(2,1)} %get-tuple-element.125), channel_id=1, source_target_pairs={{0,2},{1,3},{2,0},{3,1},{4,6},{5,7},{6,4},{7,5},{8,10},{9,11},{10,... | collective-permute-start | bytes 2457608 | tf_op jit(solution)/shard_map/ppermute | solution.py:30
  297.2 7.0 %collective-permute-start.27 = (bf16[2,2,1280,256]{3,2,1,0:T(8,128)(2,1)}, bf16[2,2,1280,256]{3,2,1,0:T(8,128)(2,1)S(1)}, u32[]{:S(2)}, u32[]{:S(2)}) collective-permute-start(bf16[2,2,1280,256]{3,2,1,0:T(8,128)(2,1)} %get-tuple-element.136), channel_id=1, source_target_pairs={{0,1},{1,0},{2,3},{3,2},{4,5},{5,4},{6,7},{7,6},{8,9},{9,8},{10,11... | collective-permute-start | bytes 7864328 | tf_op jit(solution)/shard_map/ppermute | solution.py:30
  308.1 31.8 %collective-permute-start.30 = (bf16[2,1280,256]{2,1,0:T(8,128)(2,1)}, bf16[2,1280,256]{2,1,0:T(8,128)(2,1)S(1)}, u32[]{:S(2)}, u32[]{:S(2)}) collective-permute-start(bf16[2,1280,256]{2,1,0:T(8,128)(2,1)} %bitcast.9), channel_id=1, source_target_pairs={{0,4},{4,0},{1,5},{5,1},{2,6},{6,2},{3,7},{7,3},{8,12},{12,8},{9,1... | collective-permute-start | bytes 3932168 | tf_op jit(solution)/shard_map/ppermute | solution.py:30
  309.6 31.0 %collective-permute-start.29 = (bf16[448,1280]{1,0:T(8,128)(2,1)}, bf16[448,1280]{1,0:T(8,128)(2,1)}, u32[]{:S(2)}, u32[]{:S(2)}) collective-permute-start(bf16[448,1280]{1,0:T(8,128)(2,1)} %get-tuple-element.147), channel_id=1, source_target_pairs={{0,2},{1,3},{2,0},{3,1},{4,6},{5,7},{6,4},{7,5},{8,10},{9,11},{10,... | collective-permute-start | bytes 3440648 | tf_op jit(solution)/shard_map/ppermute | solution.py:30
  323.8 18.3 %collective-permute-start.28 = (bf16[480,1024]{1,0:T(8,128)(2,1)}, bf16[480,1024]{1,0:T(8,128)(2,1)}, u32[]{:S(2)}, u32[]{:S(2)}) collective-permute-start(bf16[480,1024]{1,0:T(8,128)(2,1)} %get-tuple-element.146), channel_id=1, source_target_pairs={{0,1},{1,0},{2,3},{3,2},{4,5},{5,4},{6,7},{7,6},{8,9},{9,8},{10,11... | collective-permute-start | bytes 2949128 | tf_op jit(solution)/shard_map/ppermute | solution.py:30
  323.8 37.3 %collective-permute-start.36 = (bf16[320,1280]{1,0:T(8,128)(2,1)}, bf16[320,1280]{1,0:T(8,128)(2,1)S(1)}, u32[]{:S(2)}, u32[]{:S(2)}) collective-permute-start(bf16[320,1280]{1,0:T(8,128)(2,1)} %copy-done.15), channel_id=1, source_target_pairs={{0,4},{4,0},{1,5},{5,1},{2,6},{6,2},{3,7},{7,3},{8,12},{12,8},{9,1... | collective-permute-start | bytes 2457608 | tf_op jit(solution)/shard_map/ppermute | solution.py:30
  343.4 13.9 %collective-permute-start.33 = (bf16[224,1280]{1,0:T(8,128)(2,1)S(1)}, bf16[224,1280]{1,0:T(8,128)(2,1)S(1)}, u32[]{:S(2)}, u32[]{:S(2)}) collective-permute-start(bf16[224,1280]{1,0:T(8,128)(2,1)S(1)} %get-tuple-element.193), channel_id=1, source_target_pairs={{0,8},{8,0},{16,24},{24,16},{1,9},{9,1},{17,25},{25,17},{2,10},{10... | collective-permute-start | bytes 1720328 | tf_op jit(solution)/shard_map/ppermute | solution.py:30
  345.4 15.4 %collective-permute-start.32 = (bf16[1280,256]{1,0:T(8,128)(2,1)S(1)}, bf16[1280,256]{1,0:T(8,128)(2,1)S(1)}, u32[]{:S(2)}, u32[]{:S(2)}) collective-permute-start(bf16[1280,256]{1,0:T(8,128)(2,1)S(1)} %get-tuple-element.154), channel_id=1, source_target_pairs={{0,2},{1,3},{2,0},{3,1},{4,6},{5,7},{6,4},{7,5},{8,10},{9,11},{10,... | collective-permute-start | bytes 1966088 | tf_op jit(solution)/shard_map/ppermute | solution.py:30
  357.6 14.0 %collective-permute-start.35 = (bf16[112,1280]{1,0:T(8,128)(2,1)S(1)}, bf16[112,1280]{1,0:T(8,128)(2,1)S(1)}, u32[]{:S(2)}, u32[]{:S(2)}) collective-permute-start(bf16[112,1280]{1,0:T(8,128)(2,1)S(1)} %get-tuple-element.213), channel_id=1, source_target_pairs={{0,16},{8,24},{16,0},{24,8},{1,17},{9,25},{17,1},{25,9},{2,18},{10... | collective-permute-start | bytes 860168 | tf_op jit(solution)/shard_map/ppermute | solution.py:30
  361.4 29.6 %collective-permute-start.40 = (bf16[160,1280]{1,0:T(8,128)(2,1)S(1)}, bf16[160,1280]{1,0:T(8,128)(2,1)S(1)}, u32[]{:S(2)}, u32[]{:S(2)}) collective-permute-start(bf16[160,1280]{1,0:T(8,128)(2,1)S(1)} %get-tuple-element.209), channel_id=1, source_target_pairs={{0,8},{8,0},{16,24},{24,16},{1,9},{9,1},{17,25},{25,17},{2,10},{10... | collective-permute-start | bytes 1228808 | tf_op jit(solution)/shard_map/ppermute | solution.py:30
  362.4 26.4 %collective-permute-start.34 = (bf16[640,256]{1,0:T(8,128)(2,1)S(1)}, bf16[640,256]{1,0:T(8,128)(2,1)S(1)}, u32[]{:S(2)}, u32[]{:S(2)}) collective-permute-start(bf16[640,256]{1,0:T(8,128)(2,1)S(1)} %get-tuple-element.211), channel_id=1, source_target_pairs={{0,8},{8,0},{16,24},{24,16},{1,9},{9,1},{17,25},{25,17},{2,10},{10... | collective-permute-start | bytes 983048 | tf_op jit(solution)/shard_map/ppermute | solution.py:30
  364.1 25.1 %collective-permute-start.38 = (f32[2,960]{1,0:T(2,128)S(1)}, f32[2,960]{1,0:T(2,128)S(1)}, u32[]{:S(2)}, u32[]{:S(2)}) collective-permute-start(f32[2,960]{1,0:T(2,128)S(1)} %pad_maximum_fusion.6), channel_id=1, source_target_pairs={{0,4},{4,0},{1,5},{5,1},{2,6},{6,2},{3,7},{7,3},{8,12},{12,8},{9,1... | collective-permute-start | bytes 23048 | tf_op jit(solution)/shard_map/ppermute | solution.py:30
  366.0 42.2 %collective-permute-start.31 = (bf16[240,2048]{1,0:T(8,128)(2,1)S(1)}, bf16[240,2048]{1,0:T(8,128)(2,1)S(1)}, u32[]{:S(2)}, u32[]{:S(2)}) collective-permute-start(bf16[240,2048]{1,0:T(8,128)(2,1)S(1)} %maximum_select_fusion.6), channel_id=1, source_target_pairs={{0,2},{1,3},{2,0},{3,1},{4,6},{5,7},{6,4},{7,5},{8,10},{9,11},{10,... | collective-permute-start | bytes 2949128 | tf_op jit(solution)/shard_map/ppermute | solution.py:30
  371.7 33.7 %collective-permute-start.44 = (bf16[112,1280]{1,0:T(8,128)(2,1)S(1)}, bf16[112,1280]{1,0:T(8,128)(2,1)S(1)}, u32[]{:S(2)}, u32[]{:S(2)}) collective-permute-start(bf16[112,1280]{1,0:T(8,128)(2,1)S(1)} %add.218), channel_id=1, source_target_pairs={{0,16},{8,24},{16,0},{24,8},{1,17},{9,25},{17,1},{25,9},{2,18},{10... | collective-permute-start | bytes 860168 | tf_op jit(solution)/shard_map/ppermute | solution.py:30
  389.4 15.9 %collective-permute-start.37 = (bf16[320,256]{1,0:T(8,128)(2,1)S(1)}, bf16[320,256]{1,0:T(8,128)(2,1)S(1)}, u32[]{:S(2)}, u32[]{:S(2)}) collective-permute-start(bf16[320,256]{1,0:T(8,128)(2,1)S(1)} %get-tuple-element.217), channel_id=1, source_target_pairs={{0,16},{8,24},{16,0},{24,8},{1,17},{9,25},{17,1},{25,9},{2,18},{10... | collective-permute-start | bytes 491528 | tf_op jit(solution)/shard_map/ppermute | solution.py:30
  391.2 22.1 %collective-permute-start.43 = (bf16[80,1280]{1,0:T(8,128)(2,1)S(1)}, bf16[80,1280]{1,0:T(8,128)(2,1)S(1)}, u32[]{:S(2)}, u32[]{:S(2)}) collective-permute-start(bf16[80,1280]{1,0:T(8,128)(2,1)S(1)} %get-tuple-element.215), channel_id=1, source_target_pairs={{0,16},{8,24},{16,0},{24,8},{1,17},{9,25},{17,1},{25,9},{2,18},{10... | collective-permute-start | bytes 614408 | tf_op jit(solution)/shard_map/ppermute | solution.py:30
  392.6 20.8 %collective-permute-start.42 = (f32[2,960]{1,0:T(2,128)S(1)}, f32[2,960]{1,0:T(2,128)S(1)}, u32[]{:S(2)}, u32[]{:S(2)}) collective-permute-start(f32[2,960]{1,0:T(2,128)S(1)} %fusion.12), channel_id=1, source_target_pairs={{0,2},{1,3},{2,0},{3,1},{4,6},{5,7},{6,4},{7,5},{8,10},{9,11},{10,... | collective-permute-start | bytes 23048 | tf_op jit(solution)/shard_map/ppermute | solution.py:30
  405.3 11.5 %collective-permute-start.41 = (bf16[320,256]{1,0:T(8,128)(2,1)S(1)}, bf16[320,256]{1,0:T(8,128)(2,1)S(1)}, u32[]{:S(2)}, u32[]{:S(2)}) collective-permute-start(bf16[320,256]{1,0:T(8,128)(2,1)S(1)} %add.221), channel_id=1, source_target_pairs={{0,16},{8,24},{16,0},{24,8},{1,17},{9,25},{17,1},{25,9},{2,18},{10... | collective-permute-start | bytes 491528 | tf_op jit(solution)/shard_map/ppermute | solution.py:30
  405.5 25.2 %collective-permute-start.48 = (bf16[224,1280]{1,0:T(8,128)(2,1)S(1)}, bf16[224,1280]{1,0:T(8,128)(2,1)S(1)}, u32[]{:S(2)}, u32[]{:S(2)}) collective-permute-start(bf16[224,1280]{1,0:T(8,128)(2,1)S(1)} %maximum_select_fusion.9), channel_id=1, source_target_pairs={{0,8},{8,0},{16,24},{24,16},{1,9},{9,1},{17,25},{25,17},{2,10},{10... | collective-permute-start | bytes 1720328 | tf_op jit(solution)/shard_map/ppermute | solution.py:30
  413.3 17.7 %collective-permute-start.47 = (bf16[80,1280]{1,0:T(8,128)(2,1)S(1)}, bf16[80,1280]{1,0:T(8,128)(2,1)S(1)}, u32[]{:S(2)}, u32[]{:S(2)}) collective-permute-start(bf16[80,1280]{1,0:T(8,128)(2,1)S(1)} %add.222), channel_id=1, source_target_pairs={{0,16},{8,24},{16,0},{24,8},{1,17},{9,25},{17,1},{25,9},{2,18},{10... | collective-permute-start | bytes 614408 | tf_op jit(solution)/shard_map/ppermute | solution.py:30
  413.4 17.8 %collective-permute-start.46 = (f32[2,960]{1,0:T(2,128)S(1)}, f32[2,960]{1,0:T(2,128)S(1)}, u32[]{:S(2)}, u32[]{:S(2)}) collective-permute-start(f32[2,960]{1,0:T(2,128)S(1)} %add.194), channel_id=1, source_target_pairs={{0,8},{8,0},{16,24},{24,16},{1,9},{9,1},{17,25},{25,17},{2,10},{10... | collective-permute-start | bytes 23048 | tf_op jit(solution)/shard_map/ppermute | solution.py:30
  416.9 21.2 %collective-permute-start.45 = (bf16[640,256]{1,0:T(8,128)(2,1)S(1)}, bf16[640,256]{1,0:T(8,128)(2,1)S(1)}, u32[]{:S(2)}, u32[]{:S(2)}) collective-permute-start(bf16[640,256]{1,0:T(8,128)(2,1)S(1)} %maximum_select_fusion.11), channel_id=1, source_target_pairs={{0,8},{8,0},{16,24},{24,16},{1,9},{9,1},{17,25},{25,17},{2,10},{10... | collective-permute-start | bytes 983048 | tf_op jit(solution)/shard_map/ppermute | solution.py:30
  431.1 14.8 %collective-permute-start.49 = (bf16[160,1280]{1,0:T(8,128)(2,1)S(1)}, bf16[160,1280]{1,0:T(8,128)(2,1)S(1)}, u32[]{:S(2)}, u32[]{:S(2)}) collective-permute-start(bf16[160,1280]{1,0:T(8,128)(2,1)S(1)} %maximum_select_fusion.10), channel_id=1, source_target_pairs={{0,8},{8,0},{16,24},{24,16},{1,9},{9,1},{17,25},{25,17},{2,10},{10... | collective-permute-start | bytes 1228808 | tf_op jit(solution)/shard_map/ppermute | solution.py:30
  431.2 16.1 %collective-permute-start.50 = (f32[2,960]{1,0:T(2,128)S(1)}, f32[2,960]{1,0:T(2,128)S(1)}, u32[]{:S(2)}, u32[]{:S(2)}) collective-permute-start(f32[2,960]{1,0:T(2,128)S(1)} %add.195), channel_id=1, source_target_pairs={{0,16},{8,24},{16,0},{24,8},{1,17},{9,25},{17,1},{25,9},{2,18},{10... | collective-permute-start | bytes 23048 | tf_op jit(solution)/shard_map/ppermute | solution.py:30
  (43 other events, 384.5 us)

commit v6 on v5

--- a/solution.py
+++ b/solution.py
@@ -192,18 +192,21 @@
 HIGH_PAD = 48
 
 
-def pair_sums_kernel(keep_ref, got_ref, low_ref, near_ref, far_ref):
+def pair_sums_kernel(bit_ref, keep_ref, got_ref, low_ref, low_sent_ref, near_ref, far_ref):
+    half = LOW // 2
+
     def total(k, rows):
         return (keep_ref[k, rows, :].astype(F32) + got_ref[k, rows, :].astype(F32)).astype(BF)
 
     for k, high_ref in enumerate((near_ref, far_ref)):
-        low_ref[k] = total(k, slice(0, LOW))
+        for target, bit in ((low_ref, bit_ref[0]), (low_sent_ref, 1 - bit_ref[0])):
+            target[k] = total(k, pl.ds(pl.multiple_of(bit * half, 16), half))
         size = high_ref.shape[0] - HIGH_PAD
         high_ref[:size, :] = total(k, slice(LOW, LOW + size))
         high_ref[size:, :] = jnp.zeros((HIGH_PAD, high_ref.shape[1]), BF)
 
 
-def pair_sums(keep, got):
+def pair_sums(bit, keep, got):
     rows, width = keep.shape[1:]
     high = rows - LOW + HIGH_PAD
     tile = 256
@@ -214,17 +217,18 @@
     return pl.pallas_call(
         pair_sums_kernel,
         grid=(width // tile,),
-        in_specs=[block(2, rows), block(2, rows)],
-        out_specs=[block(2, LOW), block(high), block(high)],
+        in_specs=[SMEM, block(2, rows), block(2, rows)],
+        out_specs=[block(2, LOW // 2), block(2, LOW // 2), block(high), block(high)],
         out_shape=[
-            jax.ShapeDtypeStruct((2, LOW, width), BF),
+            jax.ShapeDtypeStruct((2, LOW // 2, width), BF),
+            jax.ShapeDtypeStruct((2, LOW // 2, width), BF),
             jax.ShapeDtypeStruct((high, width), BF),
             jax.ShapeDtypeStruct((high, width), BF),
         ],
         compiler_params=pltpu.CompilerParams(vmem_limit_bytes=32 * 2**20),
         cost_estimate=TINY,
         name="pair_sums",
-    )(keep, got)
+    )(bit, keep, got)
 
 
 def bit_z(by):
@@ -865,31 +869,34 @@
 
     early = (result_near, result_sent)
     if pairs_x:
-        low_own, near_own, far_own = pair_sums(made[2], first_got)
-        low_other, near_other, far_other = pair_sums(
-            later_keep, after(later_got, near_own)
-        )
-        early += (low_own, near_own, far_own, low_other, near_other, far_other)
-        low_got = swap(low_other, "gx", 1)
+        bit = jnp.reshape(bit_z(1), (1,)).astype(jnp.int32)
+        first_sums = pair_sums(bit, made[2], first_got)
+        low_own, low_own_sent, near_own, far_own = first_sums
+        later_sums = pair_sums(bit, later_keep, after(later_got, near_own))
+        low_other, low_other_sent, near_other, far_other = later_sums
+        early += (*first_sums, *later_sums)
+        own_halved = swap(low_own_sent, "dp", 1)
+        other_halved = swap(low_other_sent, "dp", 1)
         own_got = swap(far_own, "gy", 2)
         other_got = swap(far_other, "gy", 2)
     mid_grad, mixed_grad, gain_two, out_keep, out_send = branch_back(
         flip, after(normed_two_grad, *early), middle, upstream, mlp_gain, mixed, weights
     )
 
-    def attend_back(mixed_grad, *earlier):
+    def attend_back(mixed_grad, between=lambda dq: ()):
         dq, sent_grad, own_grad = attention_backward(
             starts, cosine, sine, queries, prior_kv, own_kv, mixed, lse, mixed_grad
         )
         prior_grad = lax.ppermute(sent_grad, "gy", behind)
+        earlier = between(dq)
         own_grad = after(own_grad, *earlier)
         grads, keep, send = qkv_grad(
             flip, normed_one, dq, own_grad, prior_grad, cosine, sine, out_keep, out_send
         )
-        return grads, keep, swap(send, "gy", 1)
+        return earlier, grads, keep, swap(send, "gy", 1)
 
     if not pairs_x:
-        grads, qkv_keep, qkv_mate = attend_back(mixed_grad)
+        _, grads, qkv_keep, qkv_mate = attend_back(mixed_grad)
         ff_both = reduce_x([add(made[2], first_got), add(later_keep, later_got)])
         ff_sum = sum_z(add(ff_both[0], swap(ff_both[1], "gy", 2)))
         paired = add(qkv_keep, qkv_mate)[..., :block]
@@ -906,31 +913,35 @@
         grad_far = swap(grad_sent, "gy", 2)
         gains = sum_all(jnp.stack([reorder(gain_one[:, 0]), reorder(gain_two[:, 0])]))
     else:
-        grads, qkv_keep, qkv_mate = attend_back(
-            mixed_grad, own_got, other_got, result_far, low_got
-        )
+
+        def between(dq):
+            own = add(low_own, after(own_halved, dq))
+            other = add(low_other, after(other_halved, dq))
+            return own, other, own_got, other_got, result_far
+
+        earlier, grads, qkv_keep, qkv_mate = attend_back(mixed_grad, between)
+        summed_own, summed_other = earlier[:2]
+        low_got = swap(summed_other, "gx", 1)
 
         high_sent = add(near_other, after(other_got, grads))
         high_near = add(near_own, after(own_got, high_sent))
-        low_near, low_sent = add_pair(low_own, after(low_got, high_near))
-        low_got = swap(low_sent, "gy", 2)
-        qkv_near, qkv_sent = add_pair(qkv_keep, after(qkv_mate, low_near))
+        qkv_near, qkv_sent = add_pair(qkv_keep, after(qkv_mate, high_near))
         qkv_got = swap(qkv_sent, "gx", 1)
         high_got = swap(after(high_sent, qkv_near), "gx", 1)
         grad_keep, grad_send, gain_one = input_grad(
             flip, after(grads, qkv_near), inputs, attn_gain, mid_grad, weights
         )
         grad_got = swap(grad_send, "gy", 1)
-        qkv_near, qkv_sent = add_pair(qkv_near, after(qkv_got, grad_keep))
+        low_near, low_sent = add_pair(summed_own, after(low_got, grad_keep))
+        low_got = swap(low_sent, "gy", 2)
+        qkv_near, qkv_sent = add_pair(qkv_near, after(qkv_got, low_near))
         qkv_got = swap(qkv_sent, "gy", 2)
         low = add(low_near, after(low_got, qkv_near))
-        low_got = halve_z(low, 1)
+        low_got = halve_z(low, 2)
         grad_near, grad_sent = to_features(grad_keep, after(grad_got, low))
         grad_far = swap(grad_sent, "gy", 2)
         result_shard = assemble(result_near, after(result_far, grad_near))
-        low = add(kept_z(low, 1), after(low_got, result_shard))
-        low_got = halve_z(low, 2)
-        qkv_sum = add(qkv_near, after(qkv_got, low))
+        qkv_sum = add(qkv_near, after(qkv_got, result_shard))
         qkv_got = halve_z(qkv_sum, 1)
         high = add(high_near, after(high_got, qkv_sum))
         high_got = halve_z(high, 1)

time: 457 us -> 469 us (1.026)
  Pallas kernels: 223 us -> 228 us
    ppermute x49 -> x50, waiting for transfers between devices: 123 us -> 129 us  [swap(): return lax.ppermute(value, axis, [(i, i ^ by) for i in range(peers)])]
    pallas_call x11 -> x12, Pallas kernels: 5.51 us -> 9.45 us  [add(): pl.pallas_call(add_kernel, grid=(rows // step,), in_specs=[spec, spec], o...]
    ppermute x49 -> x50, starting transfers between devices: 45.5 us -> 47.9 us  [swap(): return lax.ppermute(value, axis, [(i, i ^ by) for i in range(peers)])]
    unnamed x82 -> x86, local copies, waits for them, and re-layouts: 11.2 us -> 11.4 us
  transfers between devices with their start and end apart: 51 -> 52, of which waited for: 20 -> 17; matrix products, arithmetic and copies ran while one was open for 7% -> 7% of each run, Pallas kernels for 46% -> 47%
where the time goes in v6:
time: 469 us; the launch traced here: 462 us
  Pallas kernels  228 us (49%)
  waiting for transfers between devices  131 us (28%)
  starting transfers between devices  51.5 us (11%)
  local copies, waits for them, and re-layouts  31.6 us (7%)
  other arithmetic  18.1 us (4%)
    ppermute x50, waiting for transfers between devices, swap(): return lax.ppermute(value, axis, [(i, i ^ by) for i in range(peers)])  129 us
    pallas_call x2, Pallas kernels, mlp_chunk(): pl.pallas_call(functools.partial(mlp_kernel, first), grid=(size // tile,)...  68.9 us
    pallas_call x5, Pallas kernels, call_whole(): pl.pallas_call(kernel, in_specs=[SMEM] + [VMEM] * (len(ins) - 1), out_spe...  57.1 us
    ppermute x50, starting transfers between devices, swap(): return lax.ppermute(value, axis, [(i, i ^ by) for i in range(peers)])  47.9 us
    pallas_call x1, Pallas kernels, attention_backward(): pl.pallas_call(backward_kernel, grid=(KV_HEADS,), in_specs=[pl.BlockSpec(...  38.4 us
    pallas_call x1, Pallas kernels, attention_forward(): pl.pallas_call(forward_kernel, grid=(KV_HEADS,), in_specs=[pl.BlockSpec((...  36.4 us
    unnamed x86, local copies, waits for them, and re-layouts  11.4 us
    pallas_call x2, Pallas kernels, pair_sums(): pl.pallas_call(pair_sums_kernel, grid=(width // tile,), in_specs=[SMEM, b...  10.6 us
  transfers between devices with their start and end apart: 52, of which 17 were waited for; matrix products, arithmetic and copies ran while one was open for 7% of the time, Pallas kernels for 47%

profile of v6, /device:TPU:0, one launch (start us, length us, event | category | flops | bytes accessed | tf_op | source)
XLA Modules:
  0.0 461.6 jit_solution(13099316025568557360)
XLA Ops:
  3.1 3.0 collective-permute-start
  7.6 12.4 %collective-permute-done.refs_2_ = bf16[240,1280]{1,0:T(8,128)(2,1)S(1)} collective-permute-done((bf16[240,1280]{1,0:T(8,128)(2,1)S(1)}, bf16[240,1280]{1,0:T(8,128)(2,1)S(1)}, u32[]{:S(2)}, u32[]{:S(2)}) %collective-permute-start) | collective-permute-done | bytes 614432 | tf_op jit(solution)/shard_map/ppermute | solution.py:30
  21.5 2.5 constant_dynamic-slice_fusion.17
  24.4 2.0 constant_dynamic-slice_fusion.18
  26.5 1.5 collective-permute-start.7
  28.3 18.3 %collective-permute-done.2 = bf16[240,2048]{1,0:T(8,128)(2,1)} collective-permute-done((bf16[240,2048]{1,0:T(8,128)(2,1)}, bf16[240,2048]{1,0:T(8,128)(2,1)}, u32[]{:S(2)}, u32[]{:S(2)}) %collective-permute-start.2) | collective-permute-done | bytes 983072 | tf_op jit(solution)/shard_map/ppermute | solution.py:30
  46.5 2.0 constant_dynamic-slice_fusion.15
  57.2 10.5 %project.1 = (bf16[960,1024]{1,0:T(8,128)(2,1)}, bf16[960,1024]{1,0:T(8,128)(2,1)}, bf16[960,1024]{1,0:T(8,128)(2,1)}, bf16[5,128,1024]{2,1,0:T(8,128)(2,1)}, bf16[5,128,512]{2,1,0:T(8,128)(2,1)}) custom-call(s32[1]{0:T(128)} %bitcast.flip_ref, bf16[240,1024]{1,0:T(8,128)(2,1)} %get-tuple-element.198.near_ref, ...), custom_call_target="tpu_custom_call" | custom-call | flops 1000 | bytes 1000 | tf_op jit(solution)/shard_map/project/pallas_call | solution.py:610
  69.0 1.7 collective-permute-start.9
  70.9 1.6 collective-permute-done.9.prior_ref
  73.8 36.4 %attend_forward.1 = (bf16[960,1024]{1,0:T(8,128)(2,1)S(1)}, f32[5,8,1024]{2,1,0:T(8,128)S(1)}) custom-call(s32[1,1024]{1,0:T(1,128)S(1)} %bitcast.31, bf16[960,1024]{1,0:T(8,128)(2,1)S(1)} %copy-done.2, bf16[5,128,512]{2,1,0:T(8,128)(2,1)S(1)} %collective-permute-done.9.prior_ref, bf16[5,128,1024]{2,1,0:T(8,128)(2,1)S(1)} %copy-done.3), custom_call_target="tpu_custom_call" | custom-call | flops 1000 | bytes 1000 | tf_op jit(solution)/shard_map/attend_forward/pallas_call | solution.py:312
  110.3 5.2 %collective-permute-done.12 = bf16[240,2048]{1,0:T(8,128)(2,1)S(1)} collective-permute-done((bf16[240,2048]{1,0:T(8,128)(2,1)S(1)}, bf16[240,2048]{1,0:T(8,128)(2,1)S(1)}, u32[]{:S(2)}, u32[]{:S(2)}) %collective-permute-start.12) | collective-permute-done | bytes 983072 | tf_op jit(solution)/shard_map/ppermute | solution.py:30
  120.3 9.3 %branch.1 = (f32[960,1024]{1,0:T(8,128)}, bf16[960,1024]{1,0:T(8,128)(2,1)}) custom-call(s32[1]{0:T(128)} %bitcast.flip_ref, bf16[960,1024]{1,0:T(8,128)(2,1)} %get-tuple-element.98.x_ref, f32[960,1]{1,0:T(8,128)} %copy.24.gain_ref, bf16[960,1024]{1,0:T(8,128)(2,1)} %copy-done, bf16[240,1280]{1,0:T(8,128)(2,1)} %copy-done.22, bf16[240,1280]{1,0:T(8,128)(2,1)} %copy-done.25, ...), custom_call_target="tpu_custom_call" | custom-call | flops 1000 | bytes 1000 | tf_op jit(solution)/shard_map/branch/pallas_call | solution.py:610
  132.6 34.4 %feed_forward.2 = (f32[960,1024]{1,0:T(8,128)}, f32[960,1024]{1,0:T(8,128)}, bf16[2,720,1280]{2,1,0:T(8,128)(2,1)}, bf16[2,720,1280]{2,1,0:T(8,128)(2,1)}) custom-call(bf16[960,1024]{1,0:T(8,128)(2,1)} %get-tuple-element.103.refs_0_, bf16[960,1024]{1,0:T(8,128)(2,1)} %pad_maximum_fusion.refs_1_.up_ref, f32[960,1024]{1,0:T(8,128)} %get-tuple-element.107.refs_2_.middle_ref, ...), custom_call_target="tpu_custom_call" | custom-call | flops 1000 | bytes 1000 | tf_op jit(solution)/shard_map/feed_forward/pallas_call | solution.py:512
  167.6 3.8 collective-permute-done.18.refs_7_
  172.6 34.5 %feed_forward.3 = (bf16[480,1024]{1,0:T(8,128)(2,1)}, bf16[480,1024]{1,0:T(8,128)(2,1)}, f32[960,1024]{1,0:T(8,128)}, bf16[2,720,1280]{2,1,0:T(8,128)(2,1)}, bf16[2,720,1280]{2,1,0:T(8,128)(2,1)}) custom-call(bf16[960,1024]{1,0:T(8,128)(2,1)} %get-tuple-element.103.refs_0_, bf16[960,1024]{1,0:T(8,128)(2,1)} %pad_maximum_fusion.refs_1_.up_ref, ...), custom_call_target="tpu_custom_call" | custom-call | flops 1000 | bytes 1000 | tf_op jit(solution)/shard_map/feed_forward/pallas_call | solution.py:512
  207.7 2.0 copy-done.6
  209.7 5.3 %pair_sums.2 = (bf16[2,224,1280]{2,1,0:T(8,128)(2,1)S(1)}, bf16[2,224,1280]{2,1,0:T(8,128)(2,1)}, bf16[320,1280]{1,0:T(8,128)(2,1)S(1)}, bf16[320,1280]{1,0:T(8,128)(2,1)}) custom-call(s32[1]{0:T(128)} %bitcast.6.bit_ref, bf16[2,720,1280]{2,1,0:T(8,128)(2,1)S(1)} %copy-done.6, bf16[2,720,1280]{2,1,0:T(8,128)(2,1)} %collective-permute-done.21.got_ref), custom_call_target="tpu_custom_call" | custom-call | flops 1000 | bytes 1000 | tf_op jit(solution)/shard_map/pair_sums/pallas_call | solution.py:217
  216.1 1.6 collective-permute-start.23
  220.3 5.2 %pair_sums.3 = (bf16[2,224,1280]{2,1,0:T(8,128)(2,1)S(1)}, bf16[2,224,1280]{2,1,0:T(8,128)(2,1)}, bf16[320,1280]{1,0:T(8,128)(2,1)S(1)}, bf16[320,1280]{1,0:T(8,128)(2,1)}) custom-call(s32[1]{0:T(128)} %bitcast.6.bit_ref, bf16[2,720,1280]{2,1,0:T(8,128)(2,1)S(1)} %copy-done.5, bf16[2,720,1280]{2,1,0:T(8,128)(2,1)} %collective-permute-done.22.got_ref), custom_call_target="tpu_custom_call" | custom-call | flops 1000 | bytes 1000 | tf_op jit(solution)/shard_map/pair_sums/pallas_call | solution.py:217
  231.6 13.7 %branch_back.1 = (f32[960,1024]{1,0:T(8,128)}, bf16[960,1024]{1,0:T(8,128)(2,1)}, f32[960,1]{1,0:T(8,128)}, bf16[2,2,480,240]{3,2,1,0:T(8,128)(2,1)}, bf16[2,2,480,240]{3,2,1,0:T(8,128)(2,1)}) custom-call(s32[1]{0:T(128)} %bitcast.flip_ref, f32[960,1024]{1,0:T(8,128)} %get-tuple-element.131.grad_ref, f32[960,1024]{1,0:T(8,128)} %get-tuple-element.107.refs_2_.middle_ref, ...), custom_call_target="tpu_custom_call" | custom-call | flops 1000 | bytes 1000 | tf_op jit(solution)/shard_map/branch_back/pallas_call | solution.py:610
  246.3 38.4 %attend_backward.1 = (bf16[960,1024]{1,0:T(8,128)(2,1)S(1)}, bf16[5,128,512]{2,1,0:T(8,128)(2,1)S(1)}, f32[5,128,1024]{2,1,0:T(8,128)}) custom-call(s32[1,1024]{1,0:T(1,128)S(1)} %bitcast.32, f32[32,1024]{1,0:T(8,128)S(1)} %copy-done.9, f32[32,1024]{1,0:T(8,128)S(1)} %copy-done.8, bf16[960,1024]{1,0:T(8,128)(2,1)S(1)} %copy-done.2, ...), custom_call_target="tpu_custom_call" | custom-call | flops 1000 | bytes 1000 | tf_op jit(solution)/shard_map/attend_backward/pallas_call | solution.py:411
  284.8 1.8 collective-permute-start.27
  288.1 2.5 add.205
  291.5 10.5 %qkv_grad.1 = (bf16[1600,1024]{1,0:T(8,128)(2,1)}, bf16[2,2,1280,256]{3,2,1,0:T(8,128)(2,1)}, bf16[2,2,1280,256]{3,2,1,0:T(8,128)(2,1)}) custom-call(s32[1]{0:T(128)} %bitcast.flip_ref, bf16[960,1024]{1,0:T(8,128)(2,1)} %get-tuple-element.115.normed_ref, bf16[960,1024]{1,0:T(8,128)(2,1)} %copy-done.10, f32[5,128,1024]{2,1,0:T(8,128)} %get-tuple-element.137.own_ref, ...), custom_call_target="tpu_custom_call" | custom-call | flops 1000 | bytes 1000 | tf_op jit(solution)/shard_map/qkv_grad/pallas_call | solution.py:610
  305.2 1.6 add.207.left_ref
  308.0 4.0 add_pair.3
  312.5 13.0 %input_grad.1 = (bf16[480,1024]{1,0:T(8,128)(2,1)}, bf16[480,1024]{1,0:T(8,128)(2,1)}, f32[960,1]{1,0:T(8,128)}) custom-call(s32[1]{0:T(128)} %bitcast.flip_ref, bf16[1600,1024]{1,0:T(8,128)(2,1)} %get-tuple-element.148.grads_ref, bf16[960,1024]{1,0:T(8,128)(2,1)} %get-tuple-element.98.x_ref, f32[960,1]{1,0:T(8,128)} %copy.23.gain_ref, ...), custom_call_target="tpu_custom_call" | custom-call | flops 1000 | bytes 1000 | tf_op jit(solution)/shard_map/input_grad/pallas_call | solution.py:610
  325.6 6.1 %collective-permute-done.30.right_ref = bf16[2,224,1280]{2,1,0:T(8,128)(2,1)} collective-permute-done((bf16[2,224,1280]{2,1,0:T(8,128)(2,1)}, bf16[2,224,1280]{2,1,0:T(8,128)(2,1)}, u32[]{:S(2)}, u32[]{:S(2)}) %collective-permute-start.30) | collective-permute-done | bytes 1146912 | tf_op jit(solution)/shard_map/ppermute | solution.py:30
  331.7 2.2 add_pair.4
  337.7 22.0 %collective-permute-done.32.right_ref = bf16[2,1280,256]{2,1,0:T(8,128)(2,1)S(1)} collective-permute-done((bf16[2,1280,256]{2,1,0:T(8,128)(2,1)}, bf16[2,1280,256]{2,1,0:T(8,128)(2,1)S(1)}, u32[]{:S(2)}, u32[]{:S(2)}) %collective-permute-start.32) | collective-permute-done | bytes 1310752 | tf_op jit(solution)/shard_map/ppermute | solution.py:30
  364.3 2.7 collective-permute-start.36
  367.1 3.5 maximum_select_fusion
  370.6 7.4 %collective-permute-done.34.right_ref = bf16[1280,256]{1,0:T(8,128)(2,1)S(1)} collective-permute-done((bf16[1280,256]{1,0:T(8,128)(2,1)S(1)}, bf16[1280,256]{1,0:T(8,128)(2,1)S(1)}, u32[]{:S(2)}, u32[]{:S(2)}) %collective-permute-start.34) | collective-permute-done | bytes 655392 | tf_op jit(solution)/shard_map/ppermute | solution.py:30
  378.5 1.6 collective-permute-start.41
  383.6 2.6 collective-permute-start.45
  386.2 14.2 %collective-permute-done.35.right_ref = bf16[640,256]{1,0:T(8,128)(2,1)S(1)} collective-permute-done((bf16[640,256]{1,0:T(8,128)(2,1)S(1)}, bf16[640,256]{1,0:T(8,128)(2,1)S(1)}, u32[]{:S(2)}, u32[]{:S(2)}) %collective-permute-start.35) | collective-permute-done | bytes 327712 | tf_op jit(solution)/shard_map/ppermute | solution.py:30
  401.0 1.8 collective-permute-start.38
  405.4 11.4 %collective-permute-done.38.right_ref = bf16[320,256]{1,0:T(8,128)(2,1)S(1)} collective-permute-done((bf16[320,256]{1,0:T(8,128)(2,1)S(1)}, bf16[320,256]{1,0:T(8,128)(2,1)S(1)}, u32[]{:S(2)}, u32[]{:S(2)}) %collective-permute-start.38) | collective-permute-done | bytes 163872 | tf_op jit(solution)/shard_map/ppermute | solution.py:30
  417.1 2.8 collective-permute-start.49
  419.9 2.1 maximum_select_fusion.1
  422.0 2.8 collective-permute-done.44.right_ref
  425.0 2.8 collective-permute-start.47
  428.6 13.7 %collective-permute-done.49 = bf16[224,1280]{1,0:T(8,128)(2,1)S(1)} collective-permute-done((bf16[224,1280]{1,0:T(8,128)(2,1)S(1)}, bf16[224,1280]{1,0:T(8,128)(2,1)S(1)}, u32[]{:S(2)}, u32[]{:S(2)}) %collective-permute-start.49) | collective-permute-done | bytes 573472 | tf_op jit(solution)/shard_map/ppermute | solution.py:30
  442.8 3.9 collective-permute-start.51
  446.7 2.9 collective-permute-done.46
  451.6 5.9 %collective-permute-done.50 = bf16[160,1280]{1,0:T(8,128)(2,1)S(1)} collective-permute-done((bf16[160,1280]{1,0:T(8,128)(2,1)S(1)}, bf16[160,1280]{1,0:T(8,128)(2,1)S(1)}, u32[]{:S(2)}, u32[]{:S(2)}) %collective-permute-start.50) | collective-permute-done | bytes 409632 | tf_op jit(solution)/shard_map/ppermute | solution.py:30
  459.5 1.6 pad_maximum_fusion.2
  (225 shorter events, 66.5 us)
Async XLA Ops:
  3.1 16.9 %collective-permute-start = (bf16[240,1280]{1,0:T(8,128)(2,1)S(1)}, bf16[240,1280]{1,0:T(8,128)(2,1)S(1)}, u32[]{:S(2)}, u32[]{:S(2)}) collective-permute-start(bf16[240,1280]{1,0:T(8,128)(2,1)S(1)} %pad_maximum_fusion.5.refs_0_), channel_id=1, source_target_pairs={{0,2},{1,3},{2,0},{3,1},{4,6},{5,7},{6,4},{7,5},{8,10},{9,11},{10,... | collective-permute-start | bytes 1843208 | tf_op jit(solution)/shard_map/ppermute | solution.py:30
  6.1 15.3 %collective-permute-start.1 = (bf16[240,1280]{1,0:T(8,128)(2,1)S(1)}, bf16[240,1280]{1,0:T(8,128)(2,1)S(1)}, u32[]{:S(2)}, u32[]{:S(2)}) collective-permute-start(bf16[240,1280]{1,0:T(8,128)(2,1)S(1)} %pad_maximum_fusion.5.refs_0_), channel_id=1, source_target_pairs={{0,4},{4,0},{1,5},{5,1},{2,6},{6,2},{3,7},{7,3},{8,12},{12,8},{9,1... | collective-permute-start | bytes 1843208 | tf_op jit(solution)/shard_map/ppermute | solution.py:30
  23.9 22.6 %collective-permute-start.2 = (bf16[240,2048]{1,0:T(8,128)(2,1)}, bf16[240,2048]{1,0:T(8,128)(2,1)}, u32[]{:S(2)}, u32[]{:S(2)}) collective-permute-start(bf16[240,2048]{1,0:T(8,128)(2,1)} %constant_dynamic-slice_fusion.17), channel_id=1, source_target_pairs={{0,2},{1,3},{2,0},{3,1},{4,6},{5,7},{6,4},{7,5},{8,10},{9,11},{10,... | collective-permute-start | bytes 2949128 | tf_op jit(solution)/shard_map/ppermute | solution.py:30
  24.4 27.2 %collective-permute-start.4 = (bf16[240,1280]{1,0:T(8,128)(2,1)S(1)}, bf16[240,1280]{1,0:T(8,128)(2,1)S(1)}, u32[]{:S(2)}, u32[]{:S(2)}) collective-permute-start(bf16[240,1280]{1,0:T(8,128)(2,1)S(1)} %pad_maximum_fusion.5.refs_0_), channel_id=1, source_target_pairs={{0,1},{1,0},{2,3},{3,2},{4,5},{5,4},{6,7},{7,6},{8,9},{9,8},{10,11... | collective-permute-start | bytes 1843208 | tf_op jit(solution)/shard_map/ppermute | solution.py:30
  26.5 25.0 %collective-permute-start.7 = (bf16[240,1280]{1,0:T(8,128)(2,1)S(1)}, bf16[240,1280]{1,0:T(8,128)(2,1)S(1)}, u32[]{:S(2)}, u32[]{:S(2)}) collective-permute-start(bf16[240,1280]{1,0:T(8,128)(2,1)S(1)} %collective-permute-done.refs_2_), channel_id=1, source_target_pairs={{0,4},{4,0},{1,5},{5,1},{2,6},{6,2},{3,7},{7,3},{8,12},{12,8},{9,1... | collective-permute-start | bytes 1843208 | tf_op jit(solution)/shard_map/ppermute | solution.py:30
  28.0 24.4 %collective-permute-start.5 = (bf16[240,1280]{1,0:T(8,128)(2,1)S(1)}, bf16[240,1280]{1,0:T(8,128)(2,1)S(1)}, u32[]{:S(2)}, u32[]{:S(2)}) collective-permute-start(bf16[240,1280]{1,0:T(8,128)(2,1)S(1)} %collective-permute-done.refs_2_), channel_id=1, source_target_pairs={{0,1},{1,0},{2,3},{3,2},{4,5},{5,4},{6,7},{7,6},{8,9},{9,8},{10,11... | collective-permute-start | bytes 1843208 | tf_op jit(solution)/shard_map/ppermute | solution.py:30
  49.6 7.6 %collective-permute-start.3 = (bf16[480,1024]{1,0:T(8,128)(2,1)}, bf16[480,1024]{1,0:T(8,128)(2,1)}, u32[]{:S(2)}, u32[]{:S(2)}) collective-permute-start(bf16[480,1024]{1,0:T(8,128)(2,1)} %pad_maximum_fusion.3), channel_id=1, source_target_pairs={{0,1},{1,0},{2,3},{3,2},{4,5},{5,4},{6,7},{7,6},{8,9},{9,8},{10,11... | collective-permute-start | bytes 2949128 | tf_op jit(solution)/shard_map/ppermute | solution.py:30
  51.0 6.1 %collective-permute-start.6 = (bf16[240,1280]{1,0:T(8,128)(2,1)S(1)}, bf16[240,1280]{1,0:T(8,128)(2,1)}, u32[]{:S(2)}, u32[]{:S(2)}) collective-permute-start(bf16[240,1280]{1,0:T(8,128)(2,1)S(1)} %collective-permute-done.1.refs_4_), channel_id=1, source_target_pairs={{0,1},{1,0},{2,3},{3,2},{4,5},{5,4},{6,7},{7,6},{8,9},{9,8},{10,11... | collective-permute-start | bytes 1843208 | tf_op jit(solution)/shard_map/ppermute | solution.py:30
  51.6 58.6 %collective-permute-start.10 = (bf16[720,1280]{1,0:T(8,128)(2,1)}, bf16[720,1280]{1,0:T(8,128)(2,1)}, u32[]{:S(2)}, u32[]{:S(2)}) collective-permute-start(bf16[720,1280]{1,0:T(8,128)(2,1)} %pad_maximum_fusion.1.refs_3_), channel_id=1, source_target_pairs={{0,2},{1,3},{2,0},{3,1},{4,6},{5,7},{6,4},{7,5},{8,10},{9,11},{10,... | collective-permute-start | bytes 5529608 | tf_op jit(solution)/shard_map/ppermute | solution.py:30
  53.3 57.0 %collective-permute-start.11 = (bf16[720,1280]{1,0:T(8,128)(2,1)}, bf16[720,1280]{1,0:T(8,128)(2,1)}, u32[]{:S(2)}, u32[]{:S(2)}) collective-permute-start(bf16[720,1280]{1,0:T(8,128)(2,1)} %pad_maximum_fusion.1.refs_3_), channel_id=1, source_target_pairs={{0,4},{4,0},{1,5},{5,1},{2,6},{6,2},{3,7},{7,3},{8,12},{12,8},{9,1... | collective-permute-start | bytes 5529608 | tf_op jit(solution)/shard_map/ppermute | solution.py:30
  67.8 47.7 %collective-permute-start.12 = (bf16[240,2048]{1,0:T(8,128)(2,1)S(1)}, bf16[240,2048]{1,0:T(8,128)(2,1)S(1)}, u32[]{:S(2)}, u32[]{:S(2)}) collective-permute-start(bf16[240,2048]{1,0:T(8,128)(2,1)S(1)} %constant_dynamic-slice_fusion.12), channel_id=1, source_target_pairs={{0,2},{1,3},{2,0},{3,1},{4,6},{5,7},{6,4},{7,5},{8,10},{9,11},{10,... | collective-permute-start | bytes 2949128 | tf_op jit(solution)/shard_map/ppermute | solution.py:30
  70.8 61.8 %collective-permute-start.14 = (bf16[720,1280]{1,0:T(8,128)(2,1)}, bf16[720,1280]{1,0:T(8,128)(2,1)}, u32[]{:S(2)}, u32[]{:S(2)}) collective-permute-start(bf16[720,1280]{1,0:T(8,128)(2,1)} %pad_maximum_fusion.1.refs_3_), channel_id=1, source_target_pairs={{0,1},{1,0},{2,3},{3,2},{4,5},{5,4},{6,7},{7,6},{8,9},{9,8},{10,11... | collective-permute-start | bytes 5529608 | tf_op jit(solution)/shard_map/ppermute | solution.py:30
  115.4 17.2 %collective-permute-start.15 = (bf16[720,1280]{1,0:T(8,128)(2,1)}, bf16[720,1280]{1,0:T(8,128)(2,1)}, u32[]{:S(2)}, u32[]{:S(2)}) collective-permute-start(bf16[720,1280]{1,0:T(8,128)(2,1)} %collective-permute-done.10.refs_5_), channel_id=1, source_target_pairs={{0,1},{1,0},{2,3},{3,2},{4,5},{5,4},{6,7},{7,6},{8,9},{9,8},{10,11... | collective-permute-start | bytes 5529608 | tf_op jit(solution)/shard_map/ppermute | solution.py:30
  115.5 51.6 %collective-permute-start.17 = (bf16[720,1280]{1,0:T(8,128)(2,1)}, bf16[720,1280]{1,0:T(8,128)(2,1)}, u32[]{:S(2)}, u32[]{:S(2)}) collective-permute-start(bf16[720,1280]{1,0:T(8,128)(2,1)} %collective-permute-done.10.refs_5_), channel_id=1, source_target_pairs={{0,4},{4,0},{1,5},{5,1},{2,6},{6,2},{3,7},{7,3},{8,12},{12,8},{9,1... | collective-permute-start | bytes 5529608 | tf_op jit(solution)/shard_map/ppermute | solution.py:30
  118.9 11.0 %collective-permute-start.13 = (bf16[480,1024]{1,0:T(8,128)(2,1)}, bf16[480,1024]{1,0:T(8,128)(2,1)}, u32[]{:S(2)}, u32[]{:S(2)}) collective-permute-start(bf16[480,1024]{1,0:T(8,128)(2,1)} %pad_maximum_fusion.4), channel_id=1, source_target_pairs={{0,1},{1,0},{2,3},{3,2},{4,5},{5,4},{6,7},{7,6},{8,9},{9,8},{10,11... | collective-permute-start | bytes 2949128 | tf_op jit(solution)/shard_map/ppermute | solution.py:30
  129.7 37.9 %collective-permute-start.16 = (bf16[720,1280]{1,0:T(8,128)(2,1)}, bf16[720,1280]{1,0:T(8,128)(2,1)S(1)}, u32[]{:S(2)}, u32[]{:S(2)}) collective-permute-start(bf16[720,1280]{1,0:T(8,128)(2,1)} %collective-permute-done.11.refs_4_), channel_id=1, source_target_pairs={{0,1},{1,0},{2,3},{3,2},{4,5},{5,4},{6,7},{7,6},{8,9},{9,8},{10,11... | collective-permute-start | bytes 5529608 | tf_op jit(solution)/shard_map/ppermute | solution.py:30
  167.3 40.3 %collective-permute-start.21 = (bf16[2,720,1280]{2,1,0:T(8,128)(2,1)}, bf16[2,720,1280]{2,1,0:T(8,128)(2,1)}, u32[]{:S(2)}, u32[]{:S(2)}) collective-permute-start(bf16[2,720,1280]{2,1,0:T(8,128)(2,1)} %get-tuple-element.119), channel_id=1, source_target_pairs={{0,1},{1,0},{2,3},{3,2},{4,5},{5,4},{6,7},{7,6},{8,9},{9,8},{10,11... | collective-permute-start | bytes 11059208 | tf_op jit(solution)/shard_map/ppermute | solution.py:30
  207.1 13.2 %collective-permute-start.22 = (bf16[2,720,1280]{2,1,0:T(8,128)(2,1)}, bf16[2,720,1280]{2,1,0:T(8,128)(2,1)}, u32[]{:S(2)}, u32[]{:S(2)}) collective-permute-start(bf16[2,720,1280]{2,1,0:T(8,128)(2,1)} %get-tuple-element.125), channel_id=1, source_target_pairs={{0,1},{1,0},{2,3},{3,2},{4,5},{5,4},{6,7},{7,6},{8,9},{9,8},{10,11... | collective-permute-start | bytes 11059208 | tf_op jit(solution)/shard_map/ppermute | solution.py:30
  207.3 11.8 %collective-permute-start.19 = (bf16[480,1024]{1,0:T(8,128)(2,1)}, bf16[480,1024]{1,0:T(8,128)(2,1)}, u32[]{:S(2)}, u32[]{:S(2)}) collective-permute-start(bf16[480,1024]{1,0:T(8,128)(2,1)} %get-tuple-element.114), channel_id=1, source_target_pairs={{0,1},{1,0},{2,3},{3,2},{4,5},{5,4},{6,7},{7,6},{8,9},{9,8},{10,11... | collective-permute-start | bytes 2949128 | tf_op jit(solution)/shard_map/ppermute | solution.py:30
  216.1 68.7 %collective-permute-start.23 = (bf16[2,224,1280]{2,1,0:T(8,128)(2,1)}, bf16[2,224,1280]{2,1,0:T(8,128)(2,1)}, u32[]{:S(2)}, u32[]{:S(2)}) collective-permute-start(bf16[2,224,1280]{2,1,0:T(8,128)(2,1)} %get-tuple-element.121), channel_id=1, source_target_pairs={{0,8},{8,0},{16,24},{24,16},{1,9},{9,1},{17,25},{25,17},{2,10},{10... | collective-permute-start | bytes 3440648 | tf_op jit(solution)/shard_map/ppermute | solution.py:30
  225.5 62.6 %collective-permute-start.24 = (bf16[2,224,1280]{2,1,0:T(8,128)(2,1)}, bf16[2,224,1280]{2,1,0:T(8,128)(2,1)}, u32[]{:S(2)}, u32[]{:S(2)}) collective-permute-start(bf16[2,224,1280]{2,1,0:T(8,128)(2,1)} %get-tuple-element.128), channel_id=1, source_target_pairs={{0,8},{8,0},{16,24},{24,16},{1,9},{9,1},{17,25},{25,17},{2,10},{10... | collective-permute-start | bytes 3440648 | tf_op jit(solution)/shard_map/ppermute | solution.py:30
  227.4 63.3 %collective-permute-start.20 = (bf16[240,2048]{1,0:T(8,128)(2,1)}, bf16[240,2048]{1,0:T(8,128)(2,1)}, u32[]{:S(2)}, u32[]{:S(2)}) collective-permute-start(bf16[240,2048]{1,0:T(8,128)(2,1)} %maximum_select_fusion.4), channel_id=1, source_target_pairs={{0,2},{1,3},{2,0},{3,1},{4,6},{5,7},{6,4},{7,5},{8,10},{9,11},{10,... | collective-permute-start | bytes 2949128 | tf_op jit(solution)/shard_map/ppermute | solution.py:30
  228.2 62.4 %collective-permute-start.25 = (bf16[320,1280]{1,0:T(8,128)(2,1)}, bf16[320,1280]{1,0:T(8,128)(2,1)}, u32[]{:S(2)}, u32[]{:S(2)}) collective-permute-start(bf16[320,1280]{1,0:T(8,128)(2,1)} %get-tuple-element.123), channel_id=1, source_target_pairs={{0,2},{1,3},{2,0},{3,1},{4,6},{5,7},{6,4},{7,5},{8,10},{9,11},{10,... | collective-permute-start | bytes 2457608 | tf_op jit(solution)/shard_map/ppermute | solution.py:30
  229.4 61.3 %collective-permute-start.26 = (bf16[320,1280]{1,0:T(8,128)(2,1)}, bf16[320,1280]{1,0:T(8,128)(2,1)}, u32[]{:S(2)}, u32[]{:S(2)}) collective-permute-start(bf16[320,1280]{1,0:T(8,128)(2,1)} %get-tuple-element.130), channel_id=1, source_target_pairs={{0,2},{1,3},{2,0},{3,1},{4,6},{5,7},{6,4},{7,5},{8,10},{9,11},{10,... | collective-permute-start | bytes 2457608 | tf_op jit(solution)/shard_map/ppermute | solution.py:30
  284.8 5.9 %collective-permute-start.27 = (bf16[5,128,512]{2,1,0:T(8,128)(2,1)S(1)}, bf16[5,128,512]{2,1,0:T(8,128)(2,1)S(1)}, u32[]{:S(2)}, u32[]{:S(2)}) collective-permute-start(bf16[5,128,512]{2,1,0:T(8,128)(2,1)S(1)} %get-tuple-element.138), channel_id=1, source_target_pairs={{1,0},{3,2},{5,4},{7,6},{9,8},{11,10},{13,12},{15,14},{17,16},{19,... | collective-permute-start | bytes 1966088 | tf_op jit(solution)/shard_map/ppermute | solution.py:890
  302.1 5.9 %collective-permute-start.28 = (bf16[2,2,1280,256]{3,2,1,0:T(8,128)(2,1)}, bf16[2,2,1280,256]{3,2,1,0:T(8,128)(2,1)S(1)}, u32[]{:S(2)}, u32[]{:S(2)}) collective-permute-start(bf16[2,2,1280,256]{3,2,1,0:T(8,128)(2,1)} %get-tuple-element.143), channel_id=1, source_target_pairs={{0,1},{1,0},{2,3},{3,2},{4,5},{5,4},{6,7},{7,6},{8,9},{9,8},{10,11... | collective-permute-start | bytes 7864328 | tf_op jit(solution)/shard_map/ppermute | solution.py:30
  303.2 28.4 %collective-permute-start.30 = (bf16[2,224,1280]{2,1,0:T(8,128)(2,1)}, bf16[2,224,1280]{2,1,0:T(8,128)(2,1)}, u32[]{:S(2)}, u32[]{:S(2)}) collective-permute-start(bf16[2,224,1280]{2,1,0:T(8,128)(2,1)} %bitcast.12), channel_id=1, source_target_pairs={{0,4},{4,0},{1,5},{5,1},{2,6},{6,2},{3,7},{7,3},{8,12},{12,8},{9,1... | collective-permute-start | bytes 3440648 | tf_op jit(solution)/shard_map/ppermute | solution.py:30
  312.0 47.7 %collective-permute-start.32 = (bf16[2,1280,256]{2,1,0:T(8,128)(2,1)}, bf16[2,1280,256]{2,1,0:T(8,128)(2,1)S(1)}, u32[]{:S(2)}, u32[]{:S(2)}) collective-permute-start(bf16[2,1280,256]{2,1,0:T(8,128)(2,1)} %bitcast.16), channel_id=1, source_target_pairs={{0,4},{4,0},{1,5},{5,1},{2,6},{6,2},{3,7},{7,3},{8,12},{12,8},{9,1... | collective-permute-start | bytes 3932168 | tf_op jit(solution)/shard_map/ppermute | solution.py:30
  325.5 36.0 %collective-permute-start.29 = (bf16[480,1024]{1,0:T(8,128)(2,1)}, bf16[480,1024]{1,0:T(8,128)(2,1)}, u32[]{:S(2)}, u32[]{:S(2)}) collective-permute-start(bf16[480,1024]{1,0:T(8,128)(2,1)} %get-tuple-element.151), channel_id=1, source_target_pairs={{0,1},{1,0},{2,3},{3,2},{4,5},{5,4},{6,7},{7,6},{8,9},{9,8},{10,11... | collective-permute-start | bytes 2949128 | tf_op jit(solution)/shard_map/ppermute | solution.py:30
  334.7 25.6 %collective-permute-start.31 = (bf16[224,1280]{1,0:T(8,128)(2,1)}, bf16[224,1280]{1,0:T(8,128)(2,1)}, u32[]{:S(2)}, u32[]{:S(2)}) collective-permute-start(bf16[224,1280]{1,0:T(8,128)(2,1)} %get-tuple-element.154), channel_id=1, source_target_pairs={{0,2},{1,3},{2,0},{3,1},{4,6},{5,7},{6,4},{7,5},{8,10},{9,11},{10,... | collective-permute-start | bytes 1720328 | tf_op jit(solution)/shard_map/ppermute | solution.py:30
  335.8 42.3 %collective-permute-start.37 = (bf16[320,1280]{1,0:T(8,128)(2,1)}, bf16[320,1280]{1,0:T(8,128)(2,1)S(1)}, u32[]{:S(2)}, u32[]{:S(2)}) collective-permute-start(bf16[320,1280]{1,0:T(8,128)(2,1)} %copy-done.15), channel_id=1, source_target_pairs={{0,4},{4,0},{1,5},{5,1},{2,6},{6,2},{3,7},{7,3},{8,12},{12,8},{9,1... | collective-permute-start | bytes 2457608 | tf_op jit(solution)/shard_map/ppermute | solution.py:30
  363.1 14.9 %collective-permute-start.34 = (bf16[1280,256]{1,0:T(8,128)(2,1)S(1)}, bf16[1280,256]{1,0:T(8,128)(2,1)S(1)}, u32[]{:S(2)}, u32[]{:S(2)}) collective-permute-start(bf16[1280,256]{1,0:T(8,128)(2,1)S(1)} %get-tuple-element.161), channel_id=1, source_target_pairs={{0,2},{1,3},{2,0},{3,1},{4,6},{5,7},{6,4},{7,5},{8,10},{9,11},{10,... | collective-permute-start | bytes 1966088 | tf_op jit(solution)/shard_map/ppermute | solution.py:30
  364.3 19.1 %collective-permute-start.36 = (bf16[112,1280]{1,0:T(8,128)(2,1)S(1)}, bf16[112,1280]{1,0:T(8,128)(2,1)S(1)}, u32[]{:S(2)}, u32[]{:S(2)}) collective-permute-start(bf16[112,1280]{1,0:T(8,128)(2,1)S(1)} %get-tuple-element.217), channel_id=1, source_target_pairs={{0,16},{8,24},{16,0},{24,8},{1,17},{9,25},{17,1},{25,9},{2,18},{10... | collective-permute-start | bytes 860168 | tf_op jit(solution)/shard_map/ppermute | solution.py:30
  378.5 24.2 %collective-permute-start.41 = (bf16[160,1280]{1,0:T(8,128)(2,1)S(1)}, bf16[160,1280]{1,0:T(8,128)(2,1)S(1)}, u32[]{:S(2)}, u32[]{:S(2)}) collective-permute-start(bf16[160,1280]{1,0:T(8,128)(2,1)S(1)} %get-tuple-element.213), channel_id=1, source_target_pairs={{0,8},{8,0},{16,24},{24,16},{1,9},{9,1},{17,25},{25,17},{2,10},{10... | collective-permute-start | bytes 1228808 | tf_op jit(solution)/shard_map/ppermute | solution.py:30
  380.2 20.2 %collective-permute-start.35 = (bf16[640,256]{1,0:T(8,128)(2,1)S(1)}, bf16[640,256]{1,0:T(8,128)(2,1)S(1)}, u32[]{:S(2)}, u32[]{:S(2)}) collective-permute-start(bf16[640,256]{1,0:T(8,128)(2,1)S(1)} %get-tuple-element.215), channel_id=1, source_target_pairs={{0,8},{8,0},{16,24},{24,16},{1,9},{9,1},{17,25},{25,17},{2,10},{10... | collective-permute-start | bytes 983048 | tf_op jit(solution)/shard_map/ppermute | solution.py:30
  381.3 19.6 %collective-permute-start.39 = (f32[2,960]{1,0:T(2,128)S(1)}, f32[2,960]{1,0:T(2,128)S(1)}, u32[]{:S(2)}, u32[]{:S(2)}) collective-permute-start(f32[2,960]{1,0:T(2,128)S(1)} %pad_maximum_fusion.6), channel_id=1, source_target_pairs={{0,4},{4,0},{1,5},{5,1},{2,6},{6,2},{3,7},{7,3},{8,12},{12,8},{9,1... | collective-permute-start | bytes 23048 | tf_op jit(solution)/shard_map/ppermute | solution.py:30
  382.2 37.7 %collective-permute-start.33 = (bf16[240,2048]{1,0:T(8,128)(2,1)S(1)}, bf16[240,2048]{1,0:T(8,128)(2,1)S(1)}, u32[]{:S(2)}, u32[]{:S(2)}) collective-permute-start(bf16[240,2048]{1,0:T(8,128)(2,1)S(1)} %maximum_select_fusion.6), channel_id=1, source_target_pairs={{0,2},{1,3},{2,0},{3,1},{4,6},{5,7},{6,4},{7,5},{8,10},{9,11},{10,... | collective-permute-start | bytes 2949128 | tf_op jit(solution)/shard_map/ppermute | solution.py:30
  383.6 33.4 %collective-permute-start.45 = (bf16[112,1280]{1,0:T(8,128)(2,1)S(1)}, bf16[112,1280]{1,0:T(8,128)(2,1)S(1)}, u32[]{:S(2)}, u32[]{:S(2)}) collective-permute-start(bf16[112,1280]{1,0:T(8,128)(2,1)S(1)} %add.211), channel_id=1, source_target_pairs={{0,16},{8,24},{16,0},{24,8},{1,17},{9,25},{17,1},{25,9},{2,18},{10... | collective-permute-start | bytes 860168 | tf_op jit(solution)/shard_map/ppermute | solution.py:30
  401.0 15.9 %collective-permute-start.38 = (bf16[320,256]{1,0:T(8,128)(2,1)S(1)}, bf16[320,256]{1,0:T(8,128)(2,1)S(1)}, u32[]{:S(2)}, u32[]{:S(2)}) collective-permute-start(bf16[320,256]{1,0:T(8,128)(2,1)S(1)} %get-tuple-element.221), channel_id=1, source_target_pairs={{0,16},{8,24},{16,0},{24,8},{1,17},{9,25},{17,1},{25,9},{2,18},{10... | collective-permute-start | bytes 491528 | tf_op jit(solution)/shard_map/ppermute | solution.py:30
  402.9 21.9 %collective-permute-start.44 = (bf16[80,1280]{1,0:T(8,128)(2,1)S(1)}, bf16[80,1280]{1,0:T(8,128)(2,1)S(1)}, u32[]{:S(2)}, u32[]{:S(2)}) collective-permute-start(bf16[80,1280]{1,0:T(8,128)(2,1)S(1)} %get-tuple-element.219), channel_id=1, source_target_pairs={{0,16},{8,24},{16,0},{24,8},{1,17},{9,25},{17,1},{25,9},{2,18},{10... | collective-permute-start | bytes 614408 | tf_op jit(solution)/shard_map/ppermute | solution.py:30
  404.2 20.8 %collective-permute-start.43 = (f32[2,960]{1,0:T(2,128)S(1)}, f32[2,960]{1,0:T(2,128)S(1)}, u32[]{:S(2)}, u32[]{:S(2)}) collective-permute-start(f32[2,960]{1,0:T(2,128)S(1)} %fusion.12), channel_id=1, source_target_pairs={{0,2},{1,3},{2,0},{3,1},{4,6},{5,7},{6,4},{7,5},{8,10},{9,11},{10,... | collective-permute-start | bytes 23048 | tf_op jit(solution)/shard_map/ppermute | solution.py:30
  416.9 11.5 %collective-permute-start.42 = (bf16[320,256]{1,0:T(8,128)(2,1)S(1)}, bf16[320,256]{1,0:T(8,128)(2,1)S(1)}, u32[]{:S(2)}, u32[]{:S(2)}) collective-permute-start(bf16[320,256]{1,0:T(8,128)(2,1)S(1)} %add.214), channel_id=1, source_target_pairs={{0,16},{8,24},{16,0},{24,8},{1,17},{9,25},{17,1},{25,9},{2,18},{10... | collective-permute-start | bytes 491528 | tf_op jit(solution)/shard_map/ppermute | solution.py:30
  417.1 25.2 %collective-permute-start.49 = (bf16[224,1280]{1,0:T(8,128)(2,1)S(1)}, bf16[224,1280]{1,0:T(8,128)(2,1)S(1)}, u32[]{:S(2)}, u32[]{:S(2)}) collective-permute-start(bf16[224,1280]{1,0:T(8,128)(2,1)S(1)} %maximum_select_fusion.9), channel_id=1, source_target_pairs={{0,8},{8,0},{16,24},{24,16},{1,9},{9,1},{17,25},{25,17},{2,10},{10... | collective-permute-start | bytes 1720328 | tf_op jit(solution)/shard_map/ppermute | solution.py:30
  424.9 17.7 %collective-permute-start.48 = (bf16[80,1280]{1,0:T(8,128)(2,1)S(1)}, bf16[80,1280]{1,0:T(8,128)(2,1)S(1)}, u32[]{:S(2)}, u32[]{:S(2)}) collective-permute-start(bf16[80,1280]{1,0:T(8,128)(2,1)S(1)} %add.215), channel_id=1, source_target_pairs={{0,16},{8,24},{16,0},{24,8},{1,17},{9,25},{17,1},{25,9},{2,18},{10... | collective-permute-start | bytes 614408 | tf_op jit(solution)/shard_map/ppermute | solution.py:30
  425.0 17.8 %collective-permute-start.47 = (f32[2,960]{1,0:T(2,128)S(1)}, f32[2,960]{1,0:T(2,128)S(1)}, u32[]{:S(2)}, u32[]{:S(2)}) collective-permute-start(f32[2,960]{1,0:T(2,128)S(1)} %add.186), channel_id=1, source_target_pairs={{0,8},{8,0},{16,24},{24,16},{1,9},{9,1},{17,25},{25,17},{2,10},{10... | collective-permute-start | bytes 23048 | tf_op jit(solution)/shard_map/ppermute | solution.py:30
  428.5 21.2 %collective-permute-start.46 = (bf16[640,256]{1,0:T(8,128)(2,1)S(1)}, bf16[640,256]{1,0:T(8,128)(2,1)S(1)}, u32[]{:S(2)}, u32[]{:S(2)}) collective-permute-start(bf16[640,256]{1,0:T(8,128)(2,1)S(1)} %maximum_select_fusion.11), channel_id=1, source_target_pairs={{0,8},{8,0},{16,24},{24,16},{1,9},{9,1},{17,25},{25,17},{2,10},{10... | collective-permute-start | bytes 983048 | tf_op jit(solution)/shard_map/ppermute | solution.py:30
  442.7 14.8 %collective-permute-start.50 = (bf16[160,1280]{1,0:T(8,128)(2,1)S(1)}, bf16[160,1280]{1,0:T(8,128)(2,1)S(1)}, u32[]{:S(2)}, u32[]{:S(2)}) collective-permute-start(bf16[160,1280]{1,0:T(8,128)(2,1)S(1)} %maximum_select_fusion.10), channel_id=1, source_target_pairs={{0,8},{8,0},{16,24},{24,16},{1,9},{9,1},{17,25},{25,17},{2,10},{10... | collective-permute-start | bytes 1228808 | tf_op jit(solution)/shard_map/ppermute | solution.py:30
  442.8 16.1 %collective-permute-start.51 = (f32[2,960]{1,0:T(2,128)S(1)}, f32[2,960]{1,0:T(2,128)S(1)}, u32[]{:S(2)}, u32[]{:S(2)}) collective-permute-start(f32[2,960]{1,0:T(2,128)S(1)} %add.187), channel_id=1, source_target_pairs={{0,16},{8,24},{16,0},{24,8},{1,17},{9,25},{17,1},{25,9},{2,18},{10... | collective-permute-start | bytes 23048 | tf_op jit(solution)/shard_map/ppermute | solution.py:30
  (46 other events, 409.5 us)

commit v7 on v6

--- a/solution.py
+++ b/solution.py
@@ -915,13 +915,14 @@
     else:
 
         def between(dq):
-            own = add(low_own, after(own_halved, dq))
-            other = add(low_other, after(other_halved, dq))
-            return own, other, own_got, other_got, result_far
+            own = add_pair(first_sums[0], after(own_halved, dq))
+            other = add_pair(later_sums[0], after(other_halved, dq))
+            return *own, *other, own_got, other_got, result_far
 
         earlier, grads, qkv_keep, qkv_mate = attend_back(mixed_grad, between)
-        summed_own, summed_other = earlier[:2]
-        low_got = swap(summed_other, "gx", 1)
+        low_near, low_far, low_other, low_other_far = earlier[:4]
+        low_got = swap(low_far, "gy", 2)
+        low_other_got = swap(low_other_far, "gy", 2)
 
         high_sent = add(near_other, after(other_got, grads))
         high_near = add(near_own, after(own_got, high_sent))
@@ -932,8 +933,9 @@
             flip, after(grads, qkv_near), inputs, attn_gain, mid_grad, weights
         )
         grad_got = swap(grad_send, "gy", 1)
-        low_near, low_sent = add_pair(summed_own, after(low_got, grad_keep))
-        low_got = swap(low_sent, "gy", 2)
+        low_other = add(low_other, after(low_other_got, grad_keep))
+        low_near = add(low_near, after(low_got, low_other))
+        low_got = swap(low_other, "gx", 1)
         qkv_near, qkv_sent = add_pair(qkv_near, after(qkv_got, low_near))
         qkv_got = swap(qkv_sent, "gy", 2)
         low = add(low_near, after(low_got, qkv_near))

time: 469 us -> 466 us (level)
    ppermute x50 -> x51, waiting for transfers between devices: 129 us -> 126 us  [swap(): return lax.ppermute(value, axis, [(i, i ^ by) for i in range(peers)])]
    ppermute x50 -> x51, starting transfers between devices: 47.9 us -> 49.5 us  [swap(): return lax.ppermute(value, axis, [(i, i ^ by) for i in range(peers)])]
    unnamed x86 -> x88, local copies, waits for them, and re-layouts: 11.4 us -> 11.7 us
  transfers between devices with their start and end apart: 52 -> 53, of which waited for: 17 -> 18; matrix products, arithmetic and copies ran while one was open for 7% -> 7% of each run, Pallas kernels for 47% -> 46%
where the time goes in v7:
time: 466 us; the launch traced here: 459 us
  Pallas kernels  227 us (49%)
  waiting for transfers between devices  128 us (27%)
  starting transfers between devices  53.1 us (11%)
  local copies, waits for them, and re-layouts  30.7 us (7%)
  other arithmetic  18.1 us (4%)
    ppermute x51, waiting for transfers between devices, swap(): return lax.ppermute(value, axis, [(i, i ^ by) for i in range(peers)])  126 us
    pallas_call x2, Pallas kernels, mlp_chunk(): pl.pallas_call(functools.partial(mlp_kernel, first), grid=(size // tile,)...  68.8 us
    pallas_call x5, Pallas kernels, call_whole(): pl.pallas_call(kernel, in_specs=[SMEM] + [VMEM] * (len(ins) - 1), out_spe...  57 us
    ppermute x51, starting transfers between devices, swap(): return lax.ppermute(value, axis, [(i, i ^ by) for i in range(peers)])  49.5 us
    pallas_call x1, Pallas kernels, attention_backward(): pl.pallas_call(backward_kernel, grid=(KV_HEADS,), in_specs=[pl.BlockSpec(...  38.4 us
    pallas_call x1, Pallas kernels, attention_forward(): pl.pallas_call(forward_kernel, grid=(KV_HEADS,), in_specs=[pl.BlockSpec((...  36.4 us
    unnamed x88, local copies, waits for them, and re-layouts  11.7 us
    pallas_call x2, Pallas kernels, pair_sums(): pl.pallas_call(pair_sums_kernel, grid=(width // tile,), in_specs=[SMEM, b...  10.6 us
  transfers between devices with their start and end apart: 53, of which 18 were waited for; matrix products, arithmetic and copies ran while one was open for 7% of the time, Pallas kernels for 46%

profile of v7, /device:TPU:0, one launch (start us, length us, event | category | flops | bytes accessed | tf_op | source)
XLA Modules:
  0.0 458.8 jit_solution(1428663678376720578)
XLA Ops:
  3.1 3.0 collective-permute-start
  7.6 12.4 %collective-permute-done.refs_2_ = bf16[240,1280]{1,0:T(8,128)(2,1)S(1)} collective-permute-done((bf16[240,1280]{1,0:T(8,128)(2,1)S(1)}, bf16[240,1280]{1,0:T(8,128)(2,1)S(1)}, u32[]{:S(2)}, u32[]{:S(2)}) %collective-permute-start) | collective-permute-done | bytes 614432 | tf_op jit(solution)/shard_map/ppermute | solution.py:30
  21.5 2.5 constant_dynamic-slice_fusion.17
  24.4 2.0 constant_dynamic-slice_fusion.18
  26.5 1.5 collective-permute-start.7
  28.3 18.3 %collective-permute-done.2 = bf16[240,2048]{1,0:T(8,128)(2,1)} collective-permute-done((bf16[240,2048]{1,0:T(8,128)(2,1)}, bf16[240,2048]{1,0:T(8,128)(2,1)}, u32[]{:S(2)}, u32[]{:S(2)}) %collective-permute-start.2) | collective-permute-done | bytes 983072 | tf_op jit(solution)/shard_map/ppermute | solution.py:30
  46.5 2.0 constant_dynamic-slice_fusion.15
  57.2 10.5 %project.1 = (bf16[960,1024]{1,0:T(8,128)(2,1)}, bf16[960,1024]{1,0:T(8,128)(2,1)}, bf16[960,1024]{1,0:T(8,128)(2,1)}, bf16[5,128,1024]{2,1,0:T(8,128)(2,1)}, bf16[5,128,512]{2,1,0:T(8,128)(2,1)}) custom-call(s32[1]{0:T(128)} %bitcast.flip_ref, bf16[240,1024]{1,0:T(8,128)(2,1)} %get-tuple-element.204.near_ref, ...), custom_call_target="tpu_custom_call" | custom-call | flops 1000 | bytes 1000 | tf_op jit(solution)/shard_map/project/pallas_call | solution.py:610
  69.1 1.7 collective-permute-start.9
  70.9 1.6 collective-permute-done.9.prior_ref
  73.8 36.4 %attend_forward.1 = (bf16[960,1024]{1,0:T(8,128)(2,1)S(1)}, f32[5,8,1024]{2,1,0:T(8,128)S(1)}) custom-call(s32[1,1024]{1,0:T(1,128)S(1)} %bitcast.22, bf16[960,1024]{1,0:T(8,128)(2,1)S(1)} %copy-done.2, bf16[5,128,512]{2,1,0:T(8,128)(2,1)S(1)} %collective-permute-done.9.prior_ref, bf16[5,128,1024]{2,1,0:T(8,128)(2,1)S(1)} %copy-done.3), custom_call_target="tpu_custom_call" | custom-call | flops 1000 | bytes 1000 | tf_op jit(solution)/shard_map/attend_forward/pallas_call | solution.py:312
  110.3 5.2 %collective-permute-done.12 = bf16[240,2048]{1,0:T(8,128)(2,1)S(1)} collective-permute-done((bf16[240,2048]{1,0:T(8,128)(2,1)S(1)}, bf16[240,2048]{1,0:T(8,128)(2,1)S(1)}, u32[]{:S(2)}, u32[]{:S(2)}) %collective-permute-start.12) | collective-permute-done | bytes 983072 | tf_op jit(solution)/shard_map/ppermute | solution.py:30
  120.3 9.4 %branch.1 = (f32[960,1024]{1,0:T(8,128)}, bf16[960,1024]{1,0:T(8,128)(2,1)}) custom-call(s32[1]{0:T(128)} %bitcast.flip_ref, bf16[960,1024]{1,0:T(8,128)(2,1)} %get-tuple-element.101.x_ref, f32[960,1]{1,0:T(8,128)} %copy.24.gain_ref, bf16[960,1024]{1,0:T(8,128)(2,1)} %copy-done, bf16[240,1280]{1,0:T(8,128)(2,1)} %copy-done.22, bf16[240,1280]{1,0:T(8,128)(2,1)} %copy-done.25, ...), custom_call_target="tpu_custom_call" | custom-call | flops 1000 | bytes 1000 | tf_op jit(solution)/shard_map/branch/pallas_call | solution.py:610
  132.7 34.3 %feed_forward.2 = (f32[960,1024]{1,0:T(8,128)}, f32[960,1024]{1,0:T(8,128)}, bf16[2,720,1280]{2,1,0:T(8,128)(2,1)}, bf16[2,720,1280]{2,1,0:T(8,128)(2,1)}) custom-call(bf16[960,1024]{1,0:T(8,128)(2,1)} %get-tuple-element.106.refs_0_, bf16[960,1024]{1,0:T(8,128)(2,1)} %pad_maximum_fusion.refs_1_.up_ref, f32[960,1024]{1,0:T(8,128)} %get-tuple-element.110.refs_2_.middle_ref, ...), custom_call_target="tpu_custom_call" | custom-call | flops 1000 | bytes 1000 | tf_op jit(solution)/shard_map/feed_forward/pallas_call | solution.py:512
  167.6 3.7 collective-permute-done.18.refs_7_
  172.6 34.5 %feed_forward.3 = (bf16[480,1024]{1,0:T(8,128)(2,1)}, bf16[480,1024]{1,0:T(8,128)(2,1)}, f32[960,1024]{1,0:T(8,128)}, bf16[2,720,1280]{2,1,0:T(8,128)(2,1)}, bf16[2,720,1280]{2,1,0:T(8,128)(2,1)}) custom-call(bf16[960,1024]{1,0:T(8,128)(2,1)} %get-tuple-element.106.refs_0_, bf16[960,1024]{1,0:T(8,128)(2,1)} %pad_maximum_fusion.refs_1_.up_ref, ...), custom_call_target="tpu_custom_call" | custom-call | flops 1000 | bytes 1000 | tf_op jit(solution)/shard_map/feed_forward/pallas_call | solution.py:512
  207.6 2.0 copy-done.6
  209.6 5.3 %pair_sums.2 = (bf16[2,224,1280]{2,1,0:T(8,128)(2,1)S(1)}, bf16[2,224,1280]{2,1,0:T(8,128)(2,1)}, bf16[320,1280]{1,0:T(8,128)(2,1)S(1)}, bf16[320,1280]{1,0:T(8,128)(2,1)}) custom-call(s32[1]{0:T(128)} %bitcast.6.bit_ref, bf16[2,720,1280]{2,1,0:T(8,128)(2,1)S(1)} %copy-done.6, bf16[2,720,1280]{2,1,0:T(8,128)(2,1)} %collective-permute-done.21.got_ref), custom_call_target="tpu_custom_call" | custom-call | flops 1000 | bytes 1000 | tf_op jit(solution)/shard_map/pair_sums/pallas_call | solution.py:217
  216.0 1.6 collective-permute-start.23
  220.3 5.3 %pair_sums.3 = (bf16[2,224,1280]{2,1,0:T(8,128)(2,1)S(1)}, bf16[2,224,1280]{2,1,0:T(8,128)(2,1)}, bf16[320,1280]{1,0:T(8,128)(2,1)S(1)}, bf16[320,1280]{1,0:T(8,128)(2,1)}) custom-call(s32[1]{0:T(128)} %bitcast.6.bit_ref, bf16[2,720,1280]{2,1,0:T(8,128)(2,1)S(1)} %copy-done.5, bf16[2,720,1280]{2,1,0:T(8,128)(2,1)} %collective-permute-done.22.got_ref), custom_call_target="tpu_custom_call" | custom-call | flops 1000 | bytes 1000 | tf_op jit(solution)/shard_map/pair_sums/pallas_call | solution.py:217
  231.7 13.7 %branch_back.1 = (f32[960,1024]{1,0:T(8,128)}, bf16[960,1024]{1,0:T(8,128)(2,1)}, f32[960,1]{1,0:T(8,128)}, bf16[2,2,480,240]{3,2,1,0:T(8,128)(2,1)}, bf16[2,2,480,240]{3,2,1,0:T(8,128)(2,1)}) custom-call(s32[1]{0:T(128)} %bitcast.flip_ref, f32[960,1024]{1,0:T(8,128)} %get-tuple-element.134.grad_ref, f32[960,1024]{1,0:T(8,128)} %get-tuple-element.110.refs_2_.middle_ref, ...), custom_call_target="tpu_custom_call" | custom-call | flops 1000 | bytes 1000 | tf_op jit(solution)/shard_map/branch_back/pallas_call | solution.py:610
  245.5 38.4 %attend_backward.1 = (bf16[960,1024]{1,0:T(8,128)(2,1)S(1)}, bf16[5,128,512]{2,1,0:T(8,128)(2,1)S(1)}, f32[5,128,1024]{2,1,0:T(8,128)}) custom-call(s32[1,1024]{1,0:T(1,128)S(1)} %bitcast.23, f32[32,1024]{1,0:T(8,128)S(1)} %copy-done.9, f32[32,1024]{1,0:T(8,128)S(1)} %copy-done.8, bf16[960,1024]{1,0:T(8,128)(2,1)S(1)} %copy-done.2, ...), custom_call_target="tpu_custom_call" | custom-call | flops 1000 | bytes 1000 | tf_op jit(solution)/shard_map/attend_backward/pallas_call | solution.py:411
  283.9 1.8 collective-permute-start.27
  285.7 2.2 add_pair.4
  291.1 10.5 %qkv_grad.1 = (bf16[1600,1024]{1,0:T(8,128)(2,1)}, bf16[2,2,1280,256]{3,2,1,0:T(8,128)(2,1)}, bf16[2,2,1280,256]{3,2,1,0:T(8,128)(2,1)}) custom-call(s32[1]{0:T(128)} %bitcast.flip_ref, bf16[960,1024]{1,0:T(8,128)(2,1)} %get-tuple-element.118.normed_ref, bf16[960,1024]{1,0:T(8,128)(2,1)} %copy-done.10, f32[5,128,1024]{2,1,0:T(8,128)} %get-tuple-element.144.own_ref, ...), custom_call_target="tpu_custom_call" | custom-call | flops 1000 | bytes 1000 | tf_op jit(solution)/shard_map/qkv_grad/pallas_call | solution.py:610
  304.3 1.6 add.205.left_ref
  306.0 1.6 collective-permute-done.28
  307.6 4.0 add_pair.6
  313.3 12.8 %input_grad.1 = (bf16[480,1024]{1,0:T(8,128)(2,1)}, bf16[480,1024]{1,0:T(8,128)(2,1)}, f32[960,1]{1,0:T(8,128)}) custom-call(s32[1]{0:T(128)} %bitcast.flip_ref, bf16[1600,1024]{1,0:T(8,128)(2,1)} %get-tuple-element.155.grads_ref, bf16[960,1024]{1,0:T(8,128)(2,1)} %get-tuple-element.101.x_ref, f32[960,1]{1,0:T(8,128)} %copy.23.gain_ref, ...), custom_call_target="tpu_custom_call" | custom-call | flops 1000 | bytes 1000 | tf_op jit(solution)/shard_map/input_grad/pallas_call | solution.py:610
  330.0 11.8 %collective-permute-done.30.right_ref = bf16[224,1280]{1,0:T(8,128)(2,1)} collective-permute-done((bf16[224,1280]{1,0:T(8,128)(2,1)}, bf16[224,1280]{1,0:T(8,128)(2,1)}, u32[]{:S(2)}, u32[]{:S(2)}) %collective-permute-start.30) | collective-permute-done | bytes 573472 | tf_op jit(solution)/shard_map/ppermute | solution.py:30
  345.0 10.9 %collective-permute-done.32.right_ref = bf16[224,1280]{1,0:T(8,128)(2,1)} collective-permute-done((bf16[224,1280]{1,0:T(8,128)(2,1)}, bf16[224,1280]{1,0:T(8,128)(2,1)}, u32[]{:S(2)}, u32[]{:S(2)}) %collective-permute-start.32) | collective-permute-done | bytes 573472 | tf_op jit(solution)/shard_map/ppermute | solution.py:30
  359.8 2.8 collective-permute-start.37
  362.6 3.5 maximum_select_fusion
  366.1 8.2 %collective-permute-done.35.right_ref = bf16[1280,256]{1,0:T(8,128)(2,1)S(1)} collective-permute-done((bf16[1280,256]{1,0:T(8,128)(2,1)S(1)}, bf16[1280,256]{1,0:T(8,128)(2,1)S(1)}, u32[]{:S(2)}, u32[]{:S(2)}) %collective-permute-start.35) | collective-permute-done | bytes 655392 | tf_op jit(solution)/shard_map/ppermute | solution.py:30
  374.9 1.6 collective-permute-start.42
  379.9 2.7 collective-permute-start.46
  382.6 15.0 %collective-permute-done.36.right_ref = bf16[640,256]{1,0:T(8,128)(2,1)S(1)} collective-permute-done((bf16[640,256]{1,0:T(8,128)(2,1)S(1)}, bf16[640,256]{1,0:T(8,128)(2,1)S(1)}, u32[]{:S(2)}, u32[]{:S(2)}) %collective-permute-start.36) | collective-permute-done | bytes 327712 | tf_op jit(solution)/shard_map/ppermute | solution.py:30
  398.2 1.7 collective-permute-start.39
  402.5 11.5 %collective-permute-done.39.right_ref = bf16[320,256]{1,0:T(8,128)(2,1)S(1)} collective-permute-done((bf16[320,256]{1,0:T(8,128)(2,1)S(1)}, bf16[320,256]{1,0:T(8,128)(2,1)S(1)}, u32[]{:S(2)}, u32[]{:S(2)}) %collective-permute-start.39) | collective-permute-done | bytes 163872 | tf_op jit(solution)/shard_map/ppermute | solution.py:30
  414.3 2.8 collective-permute-start.50
  417.1 2.1 maximum_select_fusion.1
  419.2 2.8 collective-permute-done.45.right_ref
  422.2 2.8 collective-permute-start.48
  425.7 13.7 %collective-permute-done.50 = bf16[224,1280]{1,0:T(8,128)(2,1)S(1)} collective-permute-done((bf16[224,1280]{1,0:T(8,128)(2,1)S(1)}, bf16[224,1280]{1,0:T(8,128)(2,1)S(1)}, u32[]{:S(2)}, u32[]{:S(2)}) %collective-permute-start.50) | collective-permute-done | bytes 573472 | tf_op jit(solution)/shard_map/ppermute | solution.py:30
  440.0 3.9 collective-permute-start.52
  443.9 3.0 collective-permute-done.47
  448.8 5.9 %collective-permute-done.51 = bf16[160,1280]{1,0:T(8,128)(2,1)S(1)} collective-permute-done((bf16[160,1280]{1,0:T(8,128)(2,1)S(1)}, bf16[160,1280]{1,0:T(8,128)(2,1)S(1)}, u32[]{:S(2)}, u32[]{:S(2)}) %collective-permute-start.51) | collective-permute-done | bytes 409632 | tf_op jit(solution)/shard_map/ppermute | solution.py:30
  456.7 1.6 pad_maximum_fusion.2
  (230 shorter events, 68.4 us)
Async XLA Ops:
  3.1 16.9 %collective-permute-start = (bf16[240,1280]{1,0:T(8,128)(2,1)S(1)}, bf16[240,1280]{1,0:T(8,128)(2,1)S(1)}, u32[]{:S(2)}, u32[]{:S(2)}) collective-permute-start(bf16[240,1280]{1,0:T(8,128)(2,1)S(1)} %pad_maximum_fusion.5.refs_0_), channel_id=1, source_target_pairs={{0,2},{1,3},{2,0},{3,1},{4,6},{5,7},{6,4},{7,5},{8,10},{9,11},{10,... | collective-permute-start | bytes 1843208 | tf_op jit(solution)/shard_map/ppermute | solution.py:30
  6.1 15.3 %collective-permute-start.1 = (bf16[240,1280]{1,0:T(8,128)(2,1)S(1)}, bf16[240,1280]{1,0:T(8,128)(2,1)S(1)}, u32[]{:S(2)}, u32[]{:S(2)}) collective-permute-start(bf16[240,1280]{1,0:T(8,128)(2,1)S(1)} %pad_maximum_fusion.5.refs_0_), channel_id=1, source_target_pairs={{0,4},{4,0},{1,5},{5,1},{2,6},{6,2},{3,7},{7,3},{8,12},{12,8},{9,1... | collective-permute-start | bytes 1843208 | tf_op jit(solution)/shard_map/ppermute | solution.py:30
  23.9 22.6 %collective-permute-start.2 = (bf16[240,2048]{1,0:T(8,128)(2,1)}, bf16[240,2048]{1,0:T(8,128)(2,1)}, u32[]{:S(2)}, u32[]{:S(2)}) collective-permute-start(bf16[240,2048]{1,0:T(8,128)(2,1)} %constant_dynamic-slice_fusion.17), channel_id=1, source_target_pairs={{0,2},{1,3},{2,0},{3,1},{4,6},{5,7},{6,4},{7,5},{8,10},{9,11},{10,... | collective-permute-start | bytes 2949128 | tf_op jit(solution)/shard_map/ppermute | solution.py:30
  24.4 27.2 %collective-permute-start.4 = (bf16[240,1280]{1,0:T(8,128)(2,1)S(1)}, bf16[240,1280]{1,0:T(8,128)(2,1)S(1)}, u32[]{:S(2)}, u32[]{:S(2)}) collective-permute-start(bf16[240,1280]{1,0:T(8,128)(2,1)S(1)} %pad_maximum_fusion.5.refs_0_), channel_id=1, source_target_pairs={{0,1},{1,0},{2,3},{3,2},{4,5},{5,4},{6,7},{7,6},{8,9},{9,8},{10,11... | collective-permute-start | bytes 1843208 | tf_op jit(solution)/shard_map/ppermute | solution.py:30
  26.5 25.1 %collective-permute-start.7 = (bf16[240,1280]{1,0:T(8,128)(2,1)S(1)}, bf16[240,1280]{1,0:T(8,128)(2,1)S(1)}, u32[]{:S(2)}, u32[]{:S(2)}) collective-permute-start(bf16[240,1280]{1,0:T(8,128)(2,1)S(1)} %collective-permute-done.refs_2_), channel_id=1, source_target_pairs={{0,4},{4,0},{1,5},{5,1},{2,6},{6,2},{3,7},{7,3},{8,12},{12,8},{9,1... | collective-permute-start | bytes 1843208 | tf_op jit(solution)/shard_map/ppermute | solution.py:30
  28.0 24.4 %collective-permute-start.5 = (bf16[240,1280]{1,0:T(8,128)(2,1)S(1)}, bf16[240,1280]{1,0:T(8,128)(2,1)S(1)}, u32[]{:S(2)}, u32[]{:S(2)}) collective-permute-start(bf16[240,1280]{1,0:T(8,128)(2,1)S(1)} %collective-permute-done.refs_2_), channel_id=1, source_target_pairs={{0,1},{1,0},{2,3},{3,2},{4,5},{5,4},{6,7},{7,6},{8,9},{9,8},{10,11... | collective-permute-start | bytes 1843208 | tf_op jit(solution)/shard_map/ppermute | solution.py:30
  49.6 7.6 %collective-permute-start.3 = (bf16[480,1024]{1,0:T(8,128)(2,1)}, bf16[480,1024]{1,0:T(8,128)(2,1)}, u32[]{:S(2)}, u32[]{:S(2)}) collective-permute-start(bf16[480,1024]{1,0:T(8,128)(2,1)} %pad_maximum_fusion.3), channel_id=1, source_target_pairs={{0,1},{1,0},{2,3},{3,2},{4,5},{5,4},{6,7},{7,6},{8,9},{9,8},{10,11... | collective-permute-start | bytes 2949128 | tf_op jit(solution)/shard_map/ppermute | solution.py:30
  51.0 6.1 %collective-permute-start.6 = (bf16[240,1280]{1,0:T(8,128)(2,1)S(1)}, bf16[240,1280]{1,0:T(8,128)(2,1)}, u32[]{:S(2)}, u32[]{:S(2)}) collective-permute-start(bf16[240,1280]{1,0:T(8,128)(2,1)S(1)} %collective-permute-done.1.refs_4_), channel_id=1, source_target_pairs={{0,1},{1,0},{2,3},{3,2},{4,5},{5,4},{6,7},{7,6},{8,9},{9,8},{10,11... | collective-permute-start | bytes 1843208 | tf_op jit(solution)/shard_map/ppermute | solution.py:30
  51.6 58.6 %collective-permute-start.10 = (bf16[720,1280]{1,0:T(8,128)(2,1)}, bf16[720,1280]{1,0:T(8,128)(2,1)}, u32[]{:S(2)}, u32[]{:S(2)}) collective-permute-start(bf16[720,1280]{1,0:T(8,128)(2,1)} %pad_maximum_fusion.1.refs_3_), channel_id=1, source_target_pairs={{0,2},{1,3},{2,0},{3,1},{4,6},{5,7},{6,4},{7,5},{8,10},{9,11},{10,... | collective-permute-start | bytes 5529608 | tf_op jit(solution)/shard_map/ppermute | solution.py:30
  53.3 57.0 %collective-permute-start.11 = (bf16[720,1280]{1,0:T(8,128)(2,1)}, bf16[720,1280]{1,0:T(8,128)(2,1)}, u32[]{:S(2)}, u32[]{:S(2)}) collective-permute-start(bf16[720,1280]{1,0:T(8,128)(2,1)} %pad_maximum_fusion.1.refs_3_), channel_id=1, source_target_pairs={{0,4},{4,0},{1,5},{5,1},{2,6},{6,2},{3,7},{7,3},{8,12},{12,8},{9,1... | collective-permute-start | bytes 5529608 | tf_op jit(solution)/shard_map/ppermute | solution.py:30
  67.8 47.6 %collective-permute-start.12 = (bf16[240,2048]{1,0:T(8,128)(2,1)S(1)}, bf16[240,2048]{1,0:T(8,128)(2,1)S(1)}, u32[]{:S(2)}, u32[]{:S(2)}) collective-permute-start(bf16[240,2048]{1,0:T(8,128)(2,1)S(1)} %constant_dynamic-slice_fusion.12), channel_id=1, source_target_pairs={{0,2},{1,3},{2,0},{3,1},{4,6},{5,7},{6,4},{7,5},{8,10},{9,11},{10,... | collective-permute-start | bytes 2949128 | tf_op jit(solution)/shard_map/ppermute | solution.py:30
  70.8 61.9 %collective-permute-start.14 = (bf16[720,1280]{1,0:T(8,128)(2,1)}, bf16[720,1280]{1,0:T(8,128)(2,1)}, u32[]{:S(2)}, u32[]{:S(2)}) collective-permute-start(bf16[720,1280]{1,0:T(8,128)(2,1)} %pad_maximum_fusion.1.refs_3_), channel_id=1, source_target_pairs={{0,1},{1,0},{2,3},{3,2},{4,5},{5,4},{6,7},{7,6},{8,9},{9,8},{10,11... | collective-permute-start | bytes 5529608 | tf_op jit(solution)/shard_map/ppermute | solution.py:30
  115.5 17.3 %collective-permute-start.15 = (bf16[720,1280]{1,0:T(8,128)(2,1)}, bf16[720,1280]{1,0:T(8,128)(2,1)}, u32[]{:S(2)}, u32[]{:S(2)}) collective-permute-start(bf16[720,1280]{1,0:T(8,128)(2,1)} %collective-permute-done.10.refs_5_), channel_id=1, source_target_pairs={{0,1},{1,0},{2,3},{3,2},{4,5},{5,4},{6,7},{7,6},{8,9},{9,8},{10,11... | collective-permute-start | bytes 5529608 | tf_op jit(solution)/shard_map/ppermute | solution.py:30
  115.5 51.6 %collective-permute-start.17 = (bf16[720,1280]{1,0:T(8,128)(2,1)}, bf16[720,1280]{1,0:T(8,128)(2,1)}, u32[]{:S(2)}, u32[]{:S(2)}) collective-permute-start(bf16[720,1280]{1,0:T(8,128)(2,1)} %collective-permute-done.10.refs_5_), channel_id=1, source_target_pairs={{0,4},{4,0},{1,5},{5,1},{2,6},{6,2},{3,7},{7,3},{8,12},{12,8},{9,1... | collective-permute-start | bytes 5529608 | tf_op jit(solution)/shard_map/ppermute | solution.py:30
  118.9 11.1 %collective-permute-start.13 = (bf16[480,1024]{1,0:T(8,128)(2,1)}, bf16[480,1024]{1,0:T(8,128)(2,1)}, u32[]{:S(2)}, u32[]{:S(2)}) collective-permute-start(bf16[480,1024]{1,0:T(8,128)(2,1)} %pad_maximum_fusion.4), channel_id=1, source_target_pairs={{0,1},{1,0},{2,3},{3,2},{4,5},{5,4},{6,7},{7,6},{8,9},{9,8},{10,11... | collective-permute-start | bytes 2949128 | tf_op jit(solution)/shard_map/ppermute | solution.py:30
  129.7 37.9 %collective-permute-start.16 = (bf16[720,1280]{1,0:T(8,128)(2,1)}, bf16[720,1280]{1,0:T(8,128)(2,1)S(1)}, u32[]{:S(2)}, u32[]{:S(2)}) collective-permute-start(bf16[720,1280]{1,0:T(8,128)(2,1)} %collective-permute-done.11.refs_4_), channel_id=1, source_target_pairs={{0,1},{1,0},{2,3},{3,2},{4,5},{5,4},{6,7},{7,6},{8,9},{9,8},{10,11... | collective-permute-start | bytes 5529608 | tf_op jit(solution)/shard_map/ppermute | solution.py:30
  167.3 40.3 %collective-permute-start.21 = (bf16[2,720,1280]{2,1,0:T(8,128)(2,1)}, bf16[2,720,1280]{2,1,0:T(8,128)(2,1)}, u32[]{:S(2)}, u32[]{:S(2)}) collective-permute-start(bf16[2,720,1280]{2,1,0:T(8,128)(2,1)} %get-tuple-element.122), channel_id=1, source_target_pairs={{0,1},{1,0},{2,3},{3,2},{4,5},{5,4},{6,7},{7,6},{8,9},{9,8},{10,11... | collective-permute-start | bytes 11059208 | tf_op jit(solution)/shard_map/ppermute | solution.py:30
  207.1 13.2 %collective-permute-start.22 = (bf16[2,720,1280]{2,1,0:T(8,128)(2,1)}, bf16[2,720,1280]{2,1,0:T(8,128)(2,1)}, u32[]{:S(2)}, u32[]{:S(2)}) collective-permute-start(bf16[2,720,1280]{2,1,0:T(8,128)(2,1)} %get-tuple-element.128), channel_id=1, source_target_pairs={{0,1},{1,0},{2,3},{3,2},{4,5},{5,4},{6,7},{7,6},{8,9},{9,8},{10,11... | collective-permute-start | bytes 11059208 | tf_op jit(solution)/shard_map/ppermute | solution.py:30
  207.2 11.7 %collective-permute-start.19 = (bf16[480,1024]{1,0:T(8,128)(2,1)}, bf16[480,1024]{1,0:T(8,128)(2,1)}, u32[]{:S(2)}, u32[]{:S(2)}) collective-permute-start(bf16[480,1024]{1,0:T(8,128)(2,1)} %get-tuple-element.117), channel_id=1, source_target_pairs={{0,1},{1,0},{2,3},{3,2},{4,5},{5,4},{6,7},{7,6},{8,9},{9,8},{10,11... | collective-permute-start | bytes 2949128 | tf_op jit(solution)/shard_map/ppermute | solution.py:30
  216.0 67.9 %collective-permute-start.23 = (bf16[2,224,1280]{2,1,0:T(8,128)(2,1)}, bf16[2,224,1280]{2,1,0:T(8,128)(2,1)}, u32[]{:S(2)}, u32[]{:S(2)}) collective-permute-start(bf16[2,224,1280]{2,1,0:T(8,128)(2,1)} %get-tuple-element.124), channel_id=1, source_target_pairs={{0,8},{8,0},{16,24},{24,16},{1,9},{9,1},{17,25},{25,17},{2,10},{10... | collective-permute-start | bytes 3440648 | tf_op jit(solution)/shard_map/ppermute | solution.py:30
  225.5 63.2 %collective-permute-start.24 = (bf16[2,224,1280]{2,1,0:T(8,128)(2,1)}, bf16[2,224,1280]{2,1,0:T(8,128)(2,1)}, u32[]{:S(2)}, u32[]{:S(2)}) collective-permute-start(bf16[2,224,1280]{2,1,0:T(8,128)(2,1)} %get-tuple-element.131), channel_id=1, source_target_pairs={{0,8},{8,0},{16,24},{24,16},{1,9},{9,1},{17,25},{25,17},{2,10},{10... | collective-permute-start | bytes 3440648 | tf_op jit(solution)/shard_map/ppermute | solution.py:30
  227.3 62.9 %collective-permute-start.20 = (bf16[240,2048]{1,0:T(8,128)(2,1)}, bf16[240,2048]{1,0:T(8,128)(2,1)}, u32[]{:S(2)}, u32[]{:S(2)}) collective-permute-start(bf16[240,2048]{1,0:T(8,128)(2,1)} %maximum_select_fusion.4), channel_id=1, source_target_pairs={{0,2},{1,3},{2,0},{3,1},{4,6},{5,7},{6,4},{7,5},{8,10},{9,11},{10,... | collective-permute-start | bytes 2949128 | tf_op jit(solution)/shard_map/ppermute | solution.py:30
  228.2 62.0 %collective-permute-start.25 = (bf16[320,1280]{1,0:T(8,128)(2,1)}, bf16[320,1280]{1,0:T(8,128)(2,1)}, u32[]{:S(2)}, u32[]{:S(2)}) collective-permute-start(bf16[320,1280]{1,0:T(8,128)(2,1)} %get-tuple-element.126), channel_id=1, source_target_pairs={{0,2},{1,3},{2,0},{3,1},{4,6},{5,7},{6,4},{7,5},{8,10},{9,11},{10,... | collective-permute-start | bytes 2457608 | tf_op jit(solution)/shard_map/ppermute | solution.py:30
  229.3 60.9 %collective-permute-start.26 = (bf16[320,1280]{1,0:T(8,128)(2,1)}, bf16[320,1280]{1,0:T(8,128)(2,1)}, u32[]{:S(2)}, u32[]{:S(2)}) collective-permute-start(bf16[320,1280]{1,0:T(8,128)(2,1)} %get-tuple-element.133), channel_id=1, source_target_pairs={{0,2},{1,3},{2,0},{3,1},{4,6},{5,7},{6,4},{7,5},{8,10},{9,11},{10,... | collective-permute-start | bytes 2457608 | tf_op jit(solution)/shard_map/ppermute | solution.py:30
  283.9 6.4 %collective-permute-start.27 = (bf16[5,128,512]{2,1,0:T(8,128)(2,1)S(1)}, bf16[5,128,512]{2,1,0:T(8,128)(2,1)S(1)}, u32[]{:S(2)}, u32[]{:S(2)}) collective-permute-start(bf16[5,128,512]{2,1,0:T(8,128)(2,1)S(1)} %get-tuple-element.145), channel_id=1, source_target_pairs={{1,0},{3,2},{5,4},{7,6},{9,8},{11,10},{13,12},{15,14},{17,16},{19,... | collective-permute-start | bytes 1966088 | tf_op jit(solution)/shard_map/ppermute | solution.py:890
  311.6 32.7 %collective-permute-start.33 = (bf16[2,1280,256]{2,1,0:T(8,128)(2,1)}, bf16[2,1280,256]{2,1,0:T(8,128)(2,1)S(1)}, u32[]{:S(2)}, u32[]{:S(2)}) collective-permute-start(bf16[2,1280,256]{2,1,0:T(8,128)(2,1)} %bitcast.10), channel_id=1, source_target_pairs={{0,4},{4,0},{1,5},{5,1},{2,6},{6,2},{3,7},{7,3},{8,12},{12,8},{9,1... | collective-permute-start | bytes 3932168 | tf_op jit(solution)/shard_map/ppermute | solution.py:30
  312.1 15.0 %collective-permute-start.31 = (bf16[224,1280]{1,0:T(8,128)(2,1)S(1)}, bf16[224,1280]{1,0:T(8,128)(2,1)S(1)}, u32[]{:S(2)}, u32[]{:S(2)}) collective-permute-start(bf16[224,1280]{1,0:T(8,128)(2,1)S(1)} %get-tuple-element.143), channel_id=1, source_target_pairs={{0,2},{1,3},{2,0},{3,1},{4,6},{5,7},{6,4},{7,5},{8,10},{9,11},{10,... | collective-permute-start | bytes 1720328 | tf_op jit(solution)/shard_map/ppermute | solution.py:30
  326.1 30.9 %collective-permute-start.29 = (bf16[480,1024]{1,0:T(8,128)(2,1)}, bf16[480,1024]{1,0:T(8,128)(2,1)}, u32[]{:S(2)}, u32[]{:S(2)}) collective-permute-start(bf16[480,1024]{1,0:T(8,128)(2,1)} %get-tuple-element.158), channel_id=1, source_target_pairs={{0,1},{1,0},{2,3},{3,2},{4,5},{5,4},{6,7},{7,6},{8,9},{9,8},{10,11... | collective-permute-start | bytes 2949128 | tf_op jit(solution)/shard_map/ppermute | solution.py:30
  326.1 15.7 %collective-permute-start.30 = (bf16[224,1280]{1,0:T(8,128)(2,1)}, bf16[224,1280]{1,0:T(8,128)(2,1)}, u32[]{:S(2)}, u32[]{:S(2)}) collective-permute-start(bf16[224,1280]{1,0:T(8,128)(2,1)} %get-tuple-element.140), channel_id=1, source_target_pairs={{0,2},{1,3},{2,0},{3,1},{4,6},{5,7},{6,4},{7,5},{8,10},{9,11},{10,... | collective-permute-start | bytes 1720328 | tf_op jit(solution)/shard_map/ppermute | solution.py:30
  328.0 27.8 %collective-permute-start.32 = (bf16[224,1280]{1,0:T(8,128)(2,1)}, bf16[224,1280]{1,0:T(8,128)(2,1)}, u32[]{:S(2)}, u32[]{:S(2)}) collective-permute-start(bf16[224,1280]{1,0:T(8,128)(2,1)} %add.206), channel_id=1, source_target_pairs={{0,4},{4,0},{1,5},{5,1},{2,6},{6,2},{3,7},{7,3},{8,12},{12,8},{9,1... | collective-permute-start | bytes 1720328 | tf_op jit(solution)/shard_map/ppermute | solution.py:30
  329.6 45.0 %collective-permute-start.38 = (bf16[320,1280]{1,0:T(8,128)(2,1)}, bf16[320,1280]{1,0:T(8,128)(2,1)S(1)}, u32[]{:S(2)}, u32[]{:S(2)}) collective-permute-start(bf16[320,1280]{1,0:T(8,128)(2,1)} %copy-done.15), channel_id=1, source_target_pairs={{0,4},{4,0},{1,5},{5,1},{2,6},{6,2},{3,7},{7,3},{8,12},{12,8},{9,1... | collective-permute-start | bytes 2457608 | tf_op jit(solution)/shard_map/ppermute | solution.py:30
  358.6 15.7 %collective-permute-start.35 = (bf16[1280,256]{1,0:T(8,128)(2,1)S(1)}, bf16[1280,256]{1,0:T(8,128)(2,1)S(1)}, u32[]{:S(2)}, u32[]{:S(2)}) collective-permute-start(bf16[1280,256]{1,0:T(8,128)(2,1)S(1)} %get-tuple-element.167), channel_id=1, source_target_pairs={{0,2},{1,3},{2,0},{3,1},{4,6},{5,7},{6,4},{7,5},{8,10},{9,11},{10,... | collective-permute-start | bytes 1966088 | tf_op jit(solution)/shard_map/ppermute | solution.py:30
  359.8 20.0 %collective-permute-start.37 = (bf16[112,1280]{1,0:T(8,128)(2,1)S(1)}, bf16[112,1280]{1,0:T(8,128)(2,1)S(1)}, u32[]{:S(2)}, u32[]{:S(2)}) collective-permute-start(bf16[112,1280]{1,0:T(8,128)(2,1)S(1)} %get-tuple-element.223), channel_id=1, source_target_pairs={{0,16},{8,24},{16,0},{24,8},{1,17},{9,25},{17,1},{25,9},{2,18},{10... | collective-permute-start | bytes 860168 | tf_op jit(solution)/shard_map/ppermute | solution.py:30
  374.9 25.0 %collective-permute-start.42 = (bf16[160,1280]{1,0:T(8,128)(2,1)S(1)}, bf16[160,1280]{1,0:T(8,128)(2,1)S(1)}, u32[]{:S(2)}, u32[]{:S(2)}) collective-permute-start(bf16[160,1280]{1,0:T(8,128)(2,1)S(1)} %get-tuple-element.219), channel_id=1, source_target_pairs={{0,8},{8,0},{16,24},{24,16},{1,9},{9,1},{17,25},{25,17},{2,10},{10... | collective-permute-start | bytes 1228808 | tf_op jit(solution)/shard_map/ppermute | solution.py:30
  376.5 21.0 %collective-permute-start.36 = (bf16[640,256]{1,0:T(8,128)(2,1)S(1)}, bf16[640,256]{1,0:T(8,128)(2,1)S(1)}, u32[]{:S(2)}, u32[]{:S(2)}) collective-permute-start(bf16[640,256]{1,0:T(8,128)(2,1)S(1)} %get-tuple-element.221), channel_id=1, source_target_pairs={{0,8},{8,0},{16,24},{24,16},{1,9},{9,1},{17,25},{25,17},{2,10},{10... | collective-permute-start | bytes 983048 | tf_op jit(solution)/shard_map/ppermute | solution.py:30
  377.6 20.4 %collective-permute-start.40 = (f32[2,960]{1,0:T(2,128)S(1)}, f32[2,960]{1,0:T(2,128)S(1)}, u32[]{:S(2)}, u32[]{:S(2)}) collective-permute-start(f32[2,960]{1,0:T(2,128)S(1)} %pad_maximum_fusion.6), channel_id=1, source_target_pairs={{0,4},{4,0},{1,5},{5,1},{2,6},{6,2},{3,7},{7,3},{8,12},{12,8},{9,1... | collective-permute-start | bytes 23048 | tf_op jit(solution)/shard_map/ppermute | solution.py:30
  378.6 38.5 %collective-permute-start.34 = (bf16[240,2048]{1,0:T(8,128)(2,1)S(1)}, bf16[240,2048]{1,0:T(8,128)(2,1)S(1)}, u32[]{:S(2)}, u32[]{:S(2)}) collective-permute-start(bf16[240,2048]{1,0:T(8,128)(2,1)S(1)} %maximum_select_fusion.6), channel_id=1, source_target_pairs={{0,2},{1,3},{2,0},{3,1},{4,6},{5,7},{6,4},{7,5},{8,10},{9,11},{10,... | collective-permute-start | bytes 2949128 | tf_op jit(solution)/shard_map/ppermute | solution.py:30
  379.9 34.2 %collective-permute-start.46 = (bf16[112,1280]{1,0:T(8,128)(2,1)S(1)}, bf16[112,1280]{1,0:T(8,128)(2,1)S(1)}, u32[]{:S(2)}, u32[]{:S(2)}) collective-permute-start(bf16[112,1280]{1,0:T(8,128)(2,1)S(1)} %add.211), channel_id=1, source_target_pairs={{0,16},{8,24},{16,0},{24,8},{1,17},{9,25},{17,1},{25,9},{2,18},{10... | collective-permute-start | bytes 860168 | tf_op jit(solution)/shard_map/ppermute | solution.py:30
  398.2 15.9 %collective-permute-start.39 = (bf16[320,256]{1,0:T(8,128)(2,1)S(1)}, bf16[320,256]{1,0:T(8,128)(2,1)S(1)}, u32[]{:S(2)}, u32[]{:S(2)}) collective-permute-start(bf16[320,256]{1,0:T(8,128)(2,1)S(1)} %get-tuple-element.227), channel_id=1, source_target_pairs={{0,16},{8,24},{16,0},{24,8},{1,17},{9,25},{17,1},{25,9},{2,18},{10... | collective-permute-start | bytes 491528 | tf_op jit(solution)/shard_map/ppermute | solution.py:30
  400.1 22.0 %collective-permute-start.45 = (bf16[80,1280]{1,0:T(8,128)(2,1)S(1)}, bf16[80,1280]{1,0:T(8,128)(2,1)S(1)}, u32[]{:S(2)}, u32[]{:S(2)}) collective-permute-start(bf16[80,1280]{1,0:T(8,128)(2,1)S(1)} %get-tuple-element.225), channel_id=1, source_target_pairs={{0,16},{8,24},{16,0},{24,8},{1,17},{9,25},{17,1},{25,9},{2,18},{10... | collective-permute-start | bytes 614408 | tf_op jit(solution)/shard_map/ppermute | solution.py:30
  401.4 20.8 %collective-permute-start.44 = (f32[2,960]{1,0:T(2,128)S(1)}, f32[2,960]{1,0:T(2,128)S(1)}, u32[]{:S(2)}, u32[]{:S(2)}) collective-permute-start(f32[2,960]{1,0:T(2,128)S(1)} %fusion.12), channel_id=1, source_target_pairs={{0,2},{1,3},{2,0},{3,1},{4,6},{5,7},{6,4},{7,5},{8,10},{9,11},{10,... | collective-permute-start | bytes 23048 | tf_op jit(solution)/shard_map/ppermute | solution.py:30
  414.1 11.5 %collective-permute-start.43 = (bf16[320,256]{1,0:T(8,128)(2,1)S(1)}, bf16[320,256]{1,0:T(8,128)(2,1)S(1)}, u32[]{:S(2)}, u32[]{:S(2)}) collective-permute-start(bf16[320,256]{1,0:T(8,128)(2,1)S(1)} %add.214), channel_id=1, source_target_pairs={{0,16},{8,24},{16,0},{24,8},{1,17},{9,25},{17,1},{25,9},{2,18},{10... | collective-permute-start | bytes 491528 | tf_op jit(solution)/shard_map/ppermute | solution.py:30
  414.3 25.2 %collective-permute-start.50 = (bf16[224,1280]{1,0:T(8,128)(2,1)S(1)}, bf16[224,1280]{1,0:T(8,128)(2,1)S(1)}, u32[]{:S(2)}, u32[]{:S(2)}) collective-permute-start(bf16[224,1280]{1,0:T(8,128)(2,1)S(1)} %maximum_select_fusion.9), channel_id=1, source_target_pairs={{0,8},{8,0},{16,24},{24,16},{1,9},{9,1},{17,25},{25,17},{2,10},{10... | collective-permute-start | bytes 1720328 | tf_op jit(solution)/shard_map/ppermute | solution.py:30
  422.1 17.7 %collective-permute-start.49 = (bf16[80,1280]{1,0:T(8,128)(2,1)S(1)}, bf16[80,1280]{1,0:T(8,128)(2,1)S(1)}, u32[]{:S(2)}, u32[]{:S(2)}) collective-permute-start(bf16[80,1280]{1,0:T(8,128)(2,1)S(1)} %add.215), channel_id=1, source_target_pairs={{0,16},{8,24},{16,0},{24,8},{1,17},{9,25},{17,1},{25,9},{2,18},{10... | collective-permute-start | bytes 614408 | tf_op jit(solution)/shard_map/ppermute | solution.py:30
  422.2 17.8 %collective-permute-start.48 = (f32[2,960]{1,0:T(2,128)S(1)}, f32[2,960]{1,0:T(2,128)S(1)}, u32[]{:S(2)}, u32[]{:S(2)}) collective-permute-start(f32[2,960]{1,0:T(2,128)S(1)} %add.186), channel_id=1, source_target_pairs={{0,8},{8,0},{16,24},{24,16},{1,9},{9,1},{17,25},{25,17},{2,10},{10... | collective-permute-start | bytes 23048 | tf_op jit(solution)/shard_map/ppermute | solution.py:30
  425.7 21.2 %collective-permute-start.47 = (bf16[640,256]{1,0:T(8,128)(2,1)S(1)}, bf16[640,256]{1,0:T(8,128)(2,1)S(1)}, u32[]{:S(2)}, u32[]{:S(2)}) collective-permute-start(bf16[640,256]{1,0:T(8,128)(2,1)S(1)} %maximum_select_fusion.11), channel_id=1, source_target_pairs={{0,8},{8,0},{16,24},{24,16},{1,9},{9,1},{17,25},{25,17},{2,10},{10... | collective-permute-start | bytes 983048 | tf_op jit(solution)/shard_map/ppermute | solution.py:30
  439.9 14.8 %collective-permute-start.51 = (bf16[160,1280]{1,0:T(8,128)(2,1)S(1)}, bf16[160,1280]{1,0:T(8,128)(2,1)S(1)}, u32[]{:S(2)}, u32[]{:S(2)}) collective-permute-start(bf16[160,1280]{1,0:T(8,128)(2,1)S(1)} %maximum_select_fusion.10), channel_id=1, source_target_pairs={{0,8},{8,0},{16,24},{24,16},{1,9},{9,1},{17,25},{25,17},{2,10},{10... | collective-permute-start | bytes 1228808 | tf_op jit(solution)/shard_map/ppermute | solution.py:30
  440.0 16.1 %collective-permute-start.52 = (f32[2,960]{1,0:T(2,128)S(1)}, f32[2,960]{1,0:T(2,128)S(1)}, u32[]{:S(2)}, u32[]{:S(2)}) collective-permute-start(f32[2,960]{1,0:T(2,128)S(1)} %add.187), channel_id=1, source_target_pairs={{0,16},{8,24},{16,0},{24,8},{1,17},{9,25},{17,1},{25,9},{2,18},{10... | collective-permute-start | bytes 23048 | tf_op jit(solution)/shard_map/ppermute | solution.py:30
  (48 other events, 408.8 us)
